TPU v7x, 32 devices: a whole 2x2x4 slice. The times are simulated.
32 devices in a mesh: dp: 8 (over z, core), seq: 4 (over y, x).
Axes of the slice: x: 2, y: 2, z: 4, core: 2. Of those that a mesh axis runs over, the one named last changes fastest.
Arguments:
- tokens: bfloat16 [2, 8192, 2048], P(None, ('dp', 'seq')), may hold values from -6 to 6
- cotangent: bfloat16 [2, 8192, 2048], P(None, ('dp', 'seq')), may hold values from -6 to 6
- segments: int32 [2, 8192], P(None, 'dp'), may hold values from 0 to 3, as said below
- in_weight: float32 [2048, 8512], P(('dp', 'seq')), may hold values from -0.125 to 0.125
- in_m: float32 [2048, 8512], P(('dp', 'seq')), may hold values from -0.0014648438 to 0.0014648438
- in_v: float32 [2048, 8512], P(('dp', 'seq')), may hold values from 1e-09 to 1e-07
- conv_weight: float32 [5, 4352], P(None, ('dp', 'seq')), may hold values from -3 to 3
- conv_m: float32 [5, 4352], P(None, ('dp', 'seq')), may hold values from -0.0014648438 to 0.0014648438
- conv_v: float32 [5, 4352], P(None, ('dp', 'seq')), may hold values from 1e-09 to 1e-07
- out_weight: float32 [4096, 2048], P(None, ('dp', 'seq')), may hold values from -0.09375 to 0.09375
- out_m: float32 [4096, 2048], P(None, ('dp', 'seq')), may hold values from -0.0014648438 to 0.0014648438
- out_v: float32 [4096, 2048], P(None, ('dp', 'seq')), may hold values from 1e-09 to 1e-07
- packed: float32 [6336], replicated, may hold values from -7 to 2, as said below
- packed_m: float32 [6336], replicated, may hold values from -0.0014648438 to 0.0014648438
- packed_v: float32 [6336], replicated, may hold values from 1e-09 to 1e-07
Outputs:
- output: bfloat16 [2, 8192, 2048], P(None, ('dp', 'seq'))
- input_grad: bfloat16 [2, 8192, 2048], P(None, ('dp', 'seq'))
- grad_norm: float32 [], replicated
- in_weight_new: float32 [2048, 8512], P(('dp', 'seq'))
- in_m_new: float32 [2048, 8512], P(('dp', 'seq'))
- in_v_new: float32 [2048, 8512], P(('dp', 'seq'))
- conv_weight_step: float32 [5, 4352], P(None, ('dp', 'seq'))
- conv_m_new: float32 [5, 4352], P(None, ('dp', 'seq'))
- conv_v_new: float32 [5, 4352], P(None, ('dp', 'seq'))
- out_weight_new: float32 [4096, 2048], P(None, ('dp', 'seq'))
- out_m_new: float32 [4096, 2048], P(None, ('dp', 'seq'))
- out_v_new: float32 [4096, 2048], P(None, ('dp', 'seq'))
- packed_step: float32 [6336], replicated
- packed_m_new: float32 [6336], replicated
- packed_v_new: float32 [6336], replicated
Inputs may be any that keep to these rules, and one draw needn't show every extreme that they name: `segments`: for each micro-batch and each index of dp the ids of its 1024 tokens start at 0 and never fall; id 1 begins within the first 256 tokens and ends within the last 256; ids 2 and 3 follow it. `packed`: gains and skip factors are positive.
All inputs are finite; a program needn't handle non-finite values.
Results may differ from a plain program's by a relative error of at most 0.015.
Values may be sent and summed in bfloat16 or wider, within the bound.
No kernel may reach another device: no remote copies, remote signals or barrier semaphores. Data moves between devices by JAX's collectives and lax.ppermute only.
A program may use at most 448 MiB of HBM per device.

v0:
```python
from functools import partial

import jax
import jax.numpy as jnp
from jax import lax
from jax.sharding import PartitionSpec as P

D = 2048
HEADS = 64
HEADDIM = 64
STATE = 128
CONV = 4
BLOCK = 256
MICRO = 2
INNER = 4096
CH = 4352
PIECE = 256


NORM_EPS = 1e-05
LEARN_RATE = 0.004
BETA_ONE = 0.9
BETA_TWO = 0.95
FIX_ONE = 1.0 - 0.9**10
FIX_TWO = 1.0 - 0.95**10
ADAM_EPS = 1e-08
WEIGHT_DECAY = 0.1
CLIP_NORM = 1.0


def from_behind(array, axis, by):
    count = lax.axis_size(axis)
    pairs = [(i, i + by) for i in range(count) if 0 <= i + by < count]
    return lax.ppermute(array, axis, pairs)


def entering_2(part, axis, combine, identity, reverse):
    count = lax.axis_size(axis)
    place = lax.axis_index(axis)
    ahead = count - 1 - place if reverse else place
    gathered = jax.tree.map(lambda a: lax.all_gather(a, axis), part)
    state = jax.tree.map(lambda a, e: jnp.zeros_like(a) + jnp.asarray(e, a.dtype), part, identity)

    def one(turn, state):
        source = count - 1 - turn if reverse else turn
        return combine(
            state, jax.tree.map(lambda a: lax.dynamic_index_in_dim(a, source, 0, False), gathered)
        )

    return lax.fori_loop(0, ahead, one, state)


def to_bfloat(value):
    return lax.optimization_barrier(value.astype(jnp.bfloat16)).astype(jnp.float32)


def rounding_pair():

    def value_plain(value):
        return to_bfloat(value)

    def value_keep(value):
        return (to_bfloat(value), None)

    def value_pass(kept, grad):
        return (grad,)

    def grad_plain(value):
        return value

    def grad_keep(value):
        return (value, None)

    def grad_round(kept, grad):
        return (to_bfloat(grad),)

    value_op = jax.custom_vjp(value_plain)
    value_op.defvjp(value_keep, value_pass)
    grad_op = jax.custom_vjp(grad_plain)
    grad_op.defvjp(grad_keep, grad_round)
    return (value_op, grad_op)


def value_lower(value):
    return rounding_pair()[0](value)


def grad_lower(value):
    return rounding_pair()[1](value)


def unpack_vector(packed):
    return (
        packed[:HEADS],
        packed[HEADS : 2 * HEADS],
        packed[2 * HEADS : 3 * HEADS],
        packed[3 * HEADS : 3 * HEADS + D],
        packed[3 * HEADS + D :],
    )


def pre_norm(row_x, gain_in):
    return row_x * lax.rsqrt(jnp.mean(row_x * row_x, axis=-1, keepdims=True) + NORM_EPS) * gain_in


def gated_norm(mixed_y, gate_z, gain_out):
    gated_y = mixed_y * jax.nn.silu(gate_z)
    return (
        gated_y
        * lax.rsqrt(jnp.mean(gated_y * gated_y, axis=-1, keepdims=True) + NORM_EPS)
        * gain_out
    )


def causal_conv(padded, seg_padded, conv_w, length):
    tap_count = conv_w.shape[0] - 1
    segment = seg_padded[tap_count - 1 :]
    summed = conv_w[tap_count][None, :] + jnp.zeros_like(padded[:length])
    for tap_at in range(tap_count):
        valid = (seg_padded[tap_at : tap_at + length] == segment).astype(padded.dtype)
        summed = (
            summed + conv_w[tap_at][None, :] * padded[tap_at : tap_at + length] * valid[:, None]
        )
    return summed


def block_parts(x_heads, b_proj, c_proj, step_dt, a_neg, segment, seg_prev):
    width = x_heads.shape[0]
    cumulative = jnp.cumsum(step_dt * a_neg[None, :], axis=0)
    positions = jnp.arange(width)
    same_doc = (
        (segment[:, None] == segment[None, :]) & (positions[:, None] >= positions[None, :])
    ).astype(step_dt.dtype)
    cum_heads = cumulative.T
    gaps_log = cum_heads[:, :, None] - cum_heads[:, None, :]
    decay_mask = jnp.exp(jnp.minimum(gaps_log, 0.0)) * same_doc[None]
    inner_cb = jnp.einsum("tn,sn->ts", c_proj, b_proj)
    mixing = grad_lower(value_lower(inner_cb[None] * decay_mask * step_dt.T[:, None, :]))
    y_intra = jnp.einsum("hts,shp->thp", mixing, x_heads)
    end_weight = (
        jnp.exp(cumulative[-1][None, :] - cumulative)
        * (segment == segment[-1]).astype(step_dt.dtype)[:, None]
    )
    weighted = grad_lower(value_lower(x_heads * (end_weight * step_dt)[:, :, None]))
    s_block = jnp.einsum("shp,sn->hpn", weighted, b_proj)
    a_block = jnp.exp(cumulative[-1]) * (segment[-1] == seg_prev).astype(step_dt.dtype)
    entry_decay = jnp.exp(cumulative) * (segment == seg_prev).astype(step_dt.dtype)[:, None]
    return (y_intra, s_block, a_block, entry_decay)


def norm_part(row_x, packed):
    return pre_norm(row_x, unpack_vector(packed)[3])


def mixer_front(conv_in, dt_raw, tail, conv_w, packed, seg_window):
    a_log, skip_gain, dt_bias, gain_in, gain_out = unpack_vector(packed)
    length = conv_in.shape[0]
    padded = jnp.concatenate([tail, conv_in], axis=0)
    activated = grad_lower(
        value_lower(jax.nn.silu(causal_conv(padded, seg_window, conv_w, length)))
    )
    x_heads = activated[:, :INNER].reshape(length, HEADS, HEADDIM)
    b_proj = activated[:, INNER : INNER + STATE]
    c_proj = activated[:, INNER + STATE :]
    step_dt = jax.nn.softplus(dt_raw + dt_bias[None, :])
    a_neg = -jnp.exp(a_log)
    segment = seg_window[CONV - 1 :]
    running = jnp.zeros((HEADS, HEADDIM, STATE), jnp.float32)
    decay_run = jnp.ones((HEADS,), jnp.float32)
    last_row = BLOCK
    seg_prev = seg_window[CONV - 2]
    y_intra, s_block, a_block, entry_decay = block_parts(
        x_heads[0:last_row],
        b_proj[0:last_row],
        c_proj[0:last_row],
        step_dt,
        a_neg,
        segment,
        seg_prev,
    )
    intra_list = [y_intra]
    entry_list = [entry_decay]
    prefix_list = [running]
    factor_list = [decay_run]
    running = a_block[:, None, None] * running + s_block
    decay_run = a_block * decay_run
    mids = (
        jnp.concatenate(intra_list, axis=0),
        jnp.concatenate(entry_list, axis=0),
        jnp.stack(prefix_list),
        jnp.stack(factor_list),
        c_proj,
        x_heads,
    )
    return (running, decay_run, mids)


def mixer_rear(mids, gate_z, packed, s_in):
    y_intra, entry_decay, prefixes, factors, c_proj, x_heads = mids
    a_log, skip_gain, dt_bias, gain_in, gain_out = unpack_vector(packed)
    length = y_intra.shape[0]
    pieces = []
    for block_at in range(length // BLOCK):
        first_row = block_at * BLOCK
        last_row = first_row + BLOCK
        entering = prefixes[block_at] + factors[block_at][:, None, None] * s_in
        y_state = entry_decay[first_row:last_row][:, :, None] * jnp.einsum(
            "tn,hpn->thp", c_proj[first_row:last_row], value_lower(entering)
        )
        pieces.append(
            y_intra[first_row:last_row]
            + y_state
            + skip_gain[None, :, None] * x_heads[first_row:last_row]
        )
    mixed_y = grad_lower(jnp.concatenate(pieces, axis=0).reshape(length, INNER))
    return gated_norm(mixed_y, gate_z, gain_out)


def chain_step(earlier, later):
    return (earlier[0] * later[0], later[0][:, None, None] * earlier[1] + later[1])


def adamw(master, gradient, first_moment, second_moment, clip_scale, decay):
    clipped = gradient * clip_scale
    first_new = BETA_ONE * first_moment + (1.0 - BETA_ONE) * clipped
    second_new = BETA_TWO * second_moment + (1.0 - BETA_TWO) * clipped * clipped
    update = first_new / FIX_ONE / (jnp.sqrt(second_new / FIX_TWO) + ADAM_EPS) + decay * master
    return (-LEARN_RATE * update, first_new, second_new)


def per_device(
    tokens,
    cotangent,
    segments,
    in_weight,
    in_m,
    in_v,
    conv_weight,
    conv_m,
    conv_v,
    out_weight,
    out_m,
    out_v,
    packed,
    packed_m,
    packed_v,
):
    in_low = in_weight.astype(jnp.bfloat16)
    conv_low = conv_weight.astype(jnp.bfloat16)
    out_low = out_weight.astype(jnp.bfloat16)
    w_in, w_conv, w_out = (
        lax.all_gather(in_low, ("dp", "seq"), axis=0, tiled=True),
        lax.all_gather(conv_low, ("dp", "seq"), axis=1, tiled=True),
        lax.all_gather(out_low, ("dp", "seq"), axis=1, tiled=True),
    )
    conv_full = w_conv.astype(jnp.float32)
    offset = lax.axis_index("seq") * PIECE
    grad_in = jnp.zeros(w_in.shape, jnp.float32)
    grad_conv = jnp.zeros(w_conv.shape, jnp.float32)
    grad_out = jnp.zeros(w_out.shape, jnp.float32)
    grad_vec = jnp.zeros_like(packed)
    result_list = []
    dx_list = []
    for micro_at in range(MICRO):
        tok_f = tokens[micro_at].astype(jnp.float32)
        cot_b = cotangent[micro_at]
        seg_pad = jnp.concatenate([jnp.full((CONV - 1,), -1, jnp.int32), segments[micro_at]])
        seg_window = lax.dynamic_slice_in_dim(seg_pad, offset, PIECE + CONV - 1)
        hidden_f, norm_pull = jax.vjp(norm_part, tok_f, packed)
        hidden_b = hidden_f.astype(jnp.bfloat16)
        proj_b = jnp.dot(hidden_b, w_in, preferred_element_type=jnp.float32).astype(jnp.bfloat16)
        proj_f = proj_b.astype(jnp.float32)
        gate_z = proj_f[:, :INNER]
        conv_in = proj_f[:, INNER : INNER + CH]
        dt_raw = proj_f[:, INNER + CH :]
        tail_b = from_behind(proj_b[PIECE - (CONV - 1) :, INNER : INNER + CH], "seq", 1)
        front_fn = partial(mixer_front, seg_window=seg_window)
        (s_loc, decay_dev, mids), pull_front = jax.vjp(
            front_fn, conv_in, dt_raw, tail_b.astype(jnp.float32), conv_full, packed
        )
        s_in = entering_2(
            (decay_dev, s_loc),
            "seq",
            chain_step,
            (jnp.ones_like(decay_dev), jnp.zeros_like(s_loc)),
            False,
        )[1]
        normed, pull_rear = jax.vjp(mixer_rear, mids, gate_z, packed, s_in)
        normed_b = normed.astype(jnp.bfloat16)
        result = tok_f + jnp.dot(normed_b, w_out, preferred_element_type=jnp.float32)
        result_list.append(result.astype(jnp.bfloat16))
        grad_out = grad_out + jnp.einsum(
            "ti,td->id", normed_b, cot_b, preferred_element_type=jnp.float32
        )
        d_normed = jnp.einsum("td,id->ti", cot_b, w_out, preferred_element_type=jnp.float32)
        d_mids, d_gate, d_vec_rear, d_sin = pull_rear(d_normed)
        later_grad = entering_2(
            (decay_dev, d_sin),
            "seq",
            chain_step,
            (jnp.ones_like(decay_dev), jnp.zeros_like(d_sin)),
            True,
        )[1]
        d_decay = jnp.sum(later_grad * s_in, axis=(1, 2))
        d_conv_in, d_dt_raw, d_tail, d_conv, d_vec_front = pull_front((later_grad, d_decay, d_mids))
        tail_back = from_behind(d_tail.astype(jnp.bfloat16), "seq", -1).astype(d_tail.dtype)
        d_conv_in = jnp.concatenate(
            [d_conv_in[: PIECE - (CONV - 1)], d_conv_in[PIECE - (CONV - 1) :] + tail_back], axis=0
        )
        d_proj_b = jnp.concatenate([d_gate, d_conv_in, d_dt_raw], axis=1).astype(jnp.bfloat16)
        grad_in = grad_in + jnp.einsum(
            "td,tf->df", hidden_b, d_proj_b, preferred_element_type=jnp.float32
        )
        d_hidden = jnp.einsum("tf,df->td", d_proj_b, w_in, preferred_element_type=jnp.float32)
        d_tok, d_vec_norm = norm_pull(d_hidden)
        dx_list.append((cot_b.astype(jnp.float32) + d_tok).astype(jnp.bfloat16))
        grad_conv = grad_conv + d_conv
        grad_vec = grad_vec + d_vec_front + d_vec_rear + d_vec_norm
    shard_in, shard_conv, shard_out = (
        lax.psum_scatter(grad_in, ("dp", "seq"), scatter_dimension=0, tiled=True),
        lax.psum_scatter(grad_conv, ("dp", "seq"), scatter_dimension=1, tiled=True),
        lax.psum_scatter(grad_out, ("dp", "seq"), scatter_dimension=1, tiled=True),
    )
    partial_sq = (
        jnp.sum(shard_in * shard_in)
        + jnp.sum(shard_conv * shard_conv)
        + jnp.sum(shard_out * shard_out)
    )
    total_sq, vec_total = lax.psum((partial_sq, grad_vec), ("dp", "seq"))
    grad_norm = jnp.sqrt(total_sq + jnp.sum(vec_total * vec_total))
    clip_scale = jnp.minimum(1.0, CLIP_NORM / (grad_norm + 1e-06))
    in_new = adamw(in_weight, shard_in, in_m, in_v, clip_scale, WEIGHT_DECAY)
    conv_new = adamw(conv_weight, shard_conv, conv_m, conv_v, clip_scale, WEIGHT_DECAY)
    out_new = adamw(out_weight, shard_out, out_m, out_v, clip_scale, WEIGHT_DECAY)
    vec_new = adamw(packed, vec_total, packed_m, packed_v, clip_scale, 0.0)
    return (
        jnp.stack(result_list),
        jnp.stack(dx_list),
        grad_norm,
        in_weight + in_new[0],
        in_new[1],
        in_new[2],
        conv_new[0],
        conv_new[1],
        conv_new[2],
        out_weight + out_new[0],
        out_new[1],
        out_new[2],
        vec_new[0],
        vec_new[1],
        vec_new[2],
    )


def solution(mesh):
    return jax.shard_map(
        per_device,
        mesh=mesh,
        in_specs=(
            P(None, ("dp", "seq"), None),
            P(None, ("dp", "seq"), None),
            P(None, "dp"),
            P(("dp", "seq"), None),
            P(("dp", "seq"), None),
            P(("dp", "seq"), None),
            P(None, ("dp", "seq")),
            P(None, ("dp", "seq")),
            P(None, ("dp", "seq")),
            P(None, ("dp", "seq")),
            P(None, ("dp", "seq")),
            P(None, ("dp", "seq")),
            P(),
            P(),
            P(),
        ),
        out_specs=(
            P(None, ("dp", "seq"), None),
            P(None, ("dp", "seq"), None),
            P(),
            P(("dp", "seq"), None),
            P(("dp", "seq"), None),
            P(("dp", "seq"), None),
            P(None, ("dp", "seq")),
            P(None, ("dp", "seq")),
            P(None, ("dp", "seq")),
            P(None, ("dp", "seq")),
            P(None, ("dp", "seq")),
            P(None, ("dp", "seq")),
            P(),
            P(),
            P(),
        ),
        check_vma=False,
    )
```

profile of v0, /device:TPU:0, one launch (start us, length us, event | category | flops | bytes accessed | tf_op | source)
XLA Modules:
  0.0 3206.4 jit_solution(1549719020050024516)
XLA Ops:
  11.3 72.7 %all-gather.4 = bf16[32,136,5]{1,2,0:T(8,128)(2,1)S(1)} all-gather(bf16[1,136,5]{1,2,0:T(8,128)(2,1)S(1)} %convert_bitcast_fusion), channel_id=1, replica_groups=mesh['dp'=8,'seq'=4] {'dp','seq'}, dimensions={0}, use_global_device_ids=true | all-gather | bytes 44880 | tf_op jit(solution)/shard_map/all_gather | solution.py:253
  92.3 125.3 %all-gather.14.cloned.1.call-done = bf16[2048,8512]{1,0:T(8,128)(2,1)} async-done(((bf16[64,8512]{1,0:T(8,128)(2,1)}), bf16[2048,8512]{1,0:T(8,128)(2,1)}) %all-gather.14.cloned.1.call-update) | async-done | bytes 34865168 | tf_op jit(solution)/shard_map/all_gather | solution.py:252
  217.6 19.0 fusion.194
  241.0 19.1 fusion.193
  270.4 10.0 multiply_convert_fusion
  284.5 6.0 copy.275
  306.2 9.9 multiply_convert_fusion.1
  319.4 5.6 copy.264
  334.9 12.7 fusion.95
  350.9 7.1 all-gather.6
  358.0 7.7 all-gather.5
  370.0 6.4 fusion.23
  380.7 6.5 fusion.18
  387.2 36.0 %all-gather.20.cloned.1.call-done = f32[256,64,128]{2,1,0:T(8,128)} async-done(((f32[64,64,128]{2,1,0:T(8,128)}), f32[256,64,128]{2,1,0:T(8,128)}) %all-gather.20.cloned.1.call-update) | async-done | bytes 8388624 | tf_op jit(solution)/shard_map/all_gather | solution.py:41
  427.8 8.7 fusion.48
  436.5 5.8 copy.277
  442.3 6.7 multiply_reduce_fusion.16
  449.0 64.1 %all-gather.18.cloned.1.call-done = f32[256,64,128]{2,1,0:T(8,128)} async-done(((f32[64,64,128]{2,1,0:T(8,128)}), f32[256,64,128]{2,1,0:T(8,128)}) %all-gather.18.cloned.1.call-update) | async-done | bytes 8388624 | tf_op jit(solution)/shard_map/all_gather | solution.py:41
  517.6 8.8 fusion.49
  540.0 11.8 multiply_reduce_fusion.11
  551.8 13.0 fusion.44
  593.4 5.8 convolution_convert_fusion.2
  600.2 18.3 fusion.27
  621.1 16.4 fusion.25
  638.6 14.9 fusion.97
  653.4 14.3 all-gather.24.cloned.1.call-done
  668.0 8.1 while.55
  681.7 75.3 %all-gather.22.cloned.1.call-done = f32[256,64,128]{2,1,0:T(8,128)} async-done(((f32[64,64,128]{2,1,0:T(8,128)}), f32[256,64,128]{2,1,0:T(8,128)}) %all-gather.22.cloned.1.call-update) | async-done | bytes 8388624 | tf_op jit(solution)/shard_map/all_gather | solution.py:41
  758.7 11.4 while.54
  776.4 7.9 fusion.40
  784.3 5.8 copy.293
  795.8 7.9 fusion.37
  803.7 5.6 copy.281
  813.2 11.9 multiply_reduce_fusion.2
  825.8 6.3 multiply_reduce_fusion.6
  833.1 26.3 convolution_add_fusion.1
  895.8 11.5 broadcast_multiply_fusion
  907.3 7.0 fusion.183
  932.5 26.7 fusion.106
  959.2 47.0 %convolution_add_fusion = f32[2048,8512]{1,0:T(8,128)} fusion(f32[2048,8512]{1,0:T(8,128)} %fusion.106, bf16[256,64]{1,0:T(8,128)(2,1)S(1)} %get-tuple-element.403, bf16[3,4352]{1,0:T(4,128)(2,1)S(1)} %fusion.128, bf16[253,4352]{1,0:T(8,128)(2,1)} %slice.316, bf16[256,4096]{1,0:T(8,128)(2,1)} %get-tuple-element.441, f32[256]{0:T(256)S(1)} %copy-done.75, ...), kind=kOutput, calls=%fused_computation.8 | convolution fusion | flops 8962441216 | bytes 144918016 | tf_op jit(solution)/shard_map/td,tf->df/dot_general | solution.py:311
  1012.0 12.0 fusion.66
  1024.0 12.7 fusion.67
  1039.5 18.5 fusion.107
  1058.0 20.0 fusion.70
  1084.0 581.0 %reduce-scatter.6.cloned.1.call-done = f32[4096,64]{0,1:T(8,128)} async-done(((f32[4096,2048]{0,1:T(8,128)}), f32[4096,64]{0,1:T(8,128)}) %reduce-scatter.6.cloned.1.call-update) | async-done | bytes 1048592 | tf_op jit(solution)/shard_map/reduce_scatter | solution.py:322
  1667.1 1470.3 %reduce-scatter.4.cloned.1.call-done = f32[64,8512]{1,0:T(8,128)} async-done(((f32[2048,8512]{1,0:T(8,128)}), f32[64,8512]{1,0:T(8,128)}) %reduce-scatter.4.cloned.1.call-update) | async-done | bytes 2179088 | tf_op jit(solution)/shard_map/reduce_scatter | solution.py:320
  3144.9 40.3 %all-reduce.41 = (f32[]{:T(128)}, f32[6336]{0:T(1024)S(1)}) all-reduce(f32[]{:T(128)S(6)} %add.449, f32[6336]{0:T(1024)S(1)} %pad_add_fusion.2), channel_id=1, replica_groups=mesh['dp'=8,'seq'=4] {'dp','seq'}, use_global_device_ids=true, to_apply=%region_58.60 | all-reduce | flops 6337 | bytes 50696 | tf_op jit(solution)/shard_map/psum | solution.py:329
  3187.9 7.0 multiply_add_fusion.2
  (518 shorter events, 249.5 us)
Async XLA Ops:
  7.2 76.9 %copy-start.136 = (s32[2,1024]{1,0:T(2,128)S(1)}, s32[2,1024]{1,0:T(2,128)}, u32[]{:S(2)}) copy-start(s32[2,1024]{1,0:T(2,128)} %param.26) | copy-start | bytes 24580
  7.2 81.1 %copy-start.18 = (bf16[2,256,2048]{2,1,0:T(8,128)(2,1)S(1)}, bf16[2,256,2048]{2,1,0:T(8,128)(2,1)}, u32[]{:S(2)}) copy-start(bf16[2,256,2048]{2,1,0:T(8,128)(2,1)} %param.24) | copy-start | bytes 6291460
  7.2 210.4 %all-gather.14.cloned.1.call-start = ((), (), s32[]{:S(2)}) async-start(), calls=%async_computation.2 | async-start | bytes 36225024 | tf_op jit(solution)/shard_map/all_gather | solution.py:252
  10.2 324.7 %all-gather.16.cloned.1.call-start = ((), (), s32[]{:S(2)}) async-start(), calls=%async_computation.3 | async-start | bytes 17301504 | tf_op jit(solution)/shard_map/all_gather | solution.py:254
  11.1 412.0 %all-gather.20.cloned.1.call-start = ((), (), s32[]{:S(2)}) async-start(), calls=%async_computation.7 | async-start | bytes 10485760 | tf_op jit(solution)/shard_map/all_gather | solution.py:41
  11.3 229.7 %copy-start.45 = (f32[2048]{0:T(1024)}, f32[2048]{0:T(1024)S(1)}, u32[]{:S(2)}) copy-start(f32[2048]{0:T(1024)S(1)} %slice.221) | copy-start | bytes 24580
  88.4 217.8 %copy-start.78 = (f32[4352]{0:T(1024)}, f32[4352]{0:T(1024)S(1)}, u32[]{:S(2)}) copy-start(f32[4352]{0:T(1024)S(1)} %get-tuple-element.318) | copy-start | bytes 52228
  88.4 217.8 %copy-start.80 = (f32[4352]{0:T(1024)}, f32[4352]{0:T(1024)S(1)}, u32[]{:S(2)}) copy-start(f32[4352]{0:T(1024)S(1)} %get-tuple-element.319) | copy-start | bytes 52228
  88.4 217.8 %copy-start.82 = (f32[4352]{0:T(1024)}, f32[4352]{0:T(1024)S(1)}, u32[]{:S(2)}) copy-start(f32[4352]{0:T(1024)S(1)} %get-tuple-element.320) | copy-start | bytes 52228
  88.4 217.8 %copy-start.83 = (f32[4352]{0:T(1024)}, f32[4352]{0:T(1024)S(1)}, u32[]{:S(2)}) copy-start(f32[4352]{0:T(1024)S(1)} %get-tuple-element.321) | copy-start | bytes 52228
  88.9 147.7 %copy-start.74 = (f32[256]{0:T(256)}, f32[256]{0:T(256)S(1)}, u32[]{:S(2)}) copy-start(f32[256]{0:T(256)S(1)} %fusion.162) | copy-start | bytes 3076
  89.5 151.5 %copy-start.76 = (f32[256]{0:T(256)}, f32[256]{0:T(256)S(1)}, u32[]{:S(2)}) copy-start(f32[256]{0:T(256)S(1)} %fusion.160) | copy-start | bytes 3076
  89.5 170.5 %copy-start.137 = (f32[64]{0:T(128)}, f32[64]{0:T(128)S(1)}, u32[]{:S(2)}) copy-start(f32[64]{0:T(128)S(1)} %get-tuple-element.438) | copy-start | bytes 772
  89.5 174.6 %copy-start.106 = (f32[64]{0:T(128)}, f32[64]{0:T(128)S(1)}, u32[]{:S(2)}) copy-start(f32[64]{0:T(128)S(1)} %get-tuple-element.439) | copy-start | bytes 772
  90.9 173.2 %copy-start.102 = (f32[256]{0:T(256)}, f32[256]{0:T(256)S(1)}, u32[]{:S(2)}) copy-start(f32[256]{0:T(256)S(1)} %get-tuple-element.454) | copy-start | bytes 3076
  90.9 173.2 %copy-start.132 = (f32[256]{0:T(256)}, f32[256]{0:T(256)S(1)}, u32[]{:S(2)}) copy-start(f32[256]{0:T(256)S(1)} %get-tuple-element.453) | copy-start | bytes 3076
  90.9 179.4 %copy-start.108 = (f32[256]{0:T(256)}, f32[256]{0:T(256)S(1)}, u32[]{:S(2)}) copy-start(f32[256]{0:T(256)S(1)} %get-tuple-element.455) | copy-start | bytes 3076
  90.9 179.4 %copy-start.110 = (f32[256]{0:T(256)}, f32[256]{0:T(256)S(1)}, u32[]{:S(2)}) copy-start(f32[256]{0:T(256)S(1)} %get-tuple-element.456) | copy-start | bytes 3076
  90.9 179.4 %copy-start.112 = (f32[256]{0:T(256)}, f32[256]{0:T(256)S(1)}, u32[]{:S(2)}) copy-start(f32[256]{0:T(256)S(1)} %get-tuple-element.457) | copy-start | bytes 3076
  92.3 171.8 %copy-start.104 = (f32[256]{0:T(256)}, f32[256]{0:T(256)S(1)}, u32[]{:S(2)}) copy-start(f32[256]{0:T(256)S(1)} %get-tuple-element.447) | copy-start | bytes 3076
  92.3 171.8 %copy-start.133 = (f32[256]{0:T(256)}, f32[256]{0:T(256)S(1)}, u32[]{:S(2)}) copy-start(f32[256]{0:T(256)S(1)} %get-tuple-element.446) | copy-start | bytes 3076
  92.3 213.8 %copy-start.114 = (f32[256]{0:T(256)}, f32[256]{0:T(256)S(1)}, u32[]{:S(2)}) copy-start(f32[256]{0:T(256)S(1)} %get-tuple-element.448) | copy-start | bytes 3076
  92.3 213.8 %copy-start.116 = (f32[256]{0:T(256)}, f32[256]{0:T(256)S(1)}, u32[]{:S(2)}) copy-start(f32[256]{0:T(256)S(1)} %get-tuple-element.449) | copy-start | bytes 3076
  92.3 213.8 %copy-start.118 = (f32[256]{0:T(256)}, f32[256]{0:T(256)S(1)}, u32[]{:S(2)}) copy-start(f32[256]{0:T(256)S(1)} %get-tuple-element.450) | copy-start | bytes 3076
  237.5 32.8 %collective-permute-start.1 = (bf16[3,4352]{1,0:T(4,128)(2,1)S(1)}, bf16[3,4352]{1,0:T(4,128)(2,1)S(1)}, u32[]{:S(2)}, u32[]{:S(2)}) collective-permute-start(bf16[3,4352]{1,0:T(4,128)(2,1)S(1)} %slice.300), channel_id=1, source_target_pairs={{0,1},{1,2},{2,3},{4,5},{5,6},{6,7},{8,9},{9,10},{10,11},{12,13},{... | collective-permute-start | bytes 78344 | tf_op jit(solution)/shard_map/ppermute | solution.py:34
  262.9 84.7 %copy-start.37 = (f32[64,2,128]{0,2,1:T(8,128)}, f32[64,2,128]{0,2,1:T(8,128)S(1)}, u32[]{:S(2)}) copy-start(f32[64,2,128]{0,2,1:T(8,128)S(1)} %copy.270) | copy-start | bytes 196612
  264.1 85.7 %copy-start.39 = (f32[64,2,128]{0,2,1:T(8,128)}, f32[64,2,128]{0,2,1:T(8,128)S(1)}, u32[]{:S(2)}) copy-start(f32[64,2,128]{0,2,1:T(8,128)S(1)} %copy.259) | copy-start | bytes 196612
  270.3 20.2 copy-start.63
  280.4 89.4 %copy-start.16 = (bf16[256,4352]{1,0:T(8,128)(2,1)}, bf16[256,4352]{1,0:T(8,128)(2,1)S(1)}, u32[]{:S(2)}) copy-start(bf16[256,4352]{1,0:T(8,128)(2,1)S(1)} %get-tuple-element.396) | copy-start | bytes 6684676
  296.8 216.2 %all-gather.18.cloned.1.call-start = ((), (), s32[]{:S(2)}) async-start(), calls=%async_computation.6 | async-start | bytes 10485760 | tf_op jit(solution)/shard_map/all_gather | solution.py:41
  297.8 8.3 collective-permute-start
  332.2 335.5 %all-gather.24.cloned.1.call-start = ((), (), s32[]{:S(2)}) async-start(), calls=%async_computation.9 | async-start | bytes 10485760 | tf_op jit(solution)/shard_map/all_gather | solution.py:41
  332.6 37.4 %copy-start.47 = (f32[256,256]{1,0:T(8,128)}, f32[256,256]{1,0:T(8,128)S(1)}, u32[]{:S(2)}) copy-start(f32[256,256]{1,0:T(8,128)S(1)} %fusion.113) | copy-start | bytes 786436
  347.7 28.8 copy-start.69
  348.8 220.9 %copy-start.55 = (f32[256,64]{0,1:T(8,128)}, f32[256,64]{0,1:T(8,128)S(1)}, u32[]{:S(2)}) copy-start(f32[256,64]{0,1:T(8,128)S(1)} %copy.274) | copy-start | bytes 196612
  349.8 30.2 copy-start.67
  536.9 101.6 %copy-start.100 = (f32[256]{0:T(256)}, f32[256]{0:T(256)S(1)}, u32[]{:S(2)}) copy-start(f32[256]{0:T(256)S(1)} %fusion.161) | copy-start | bytes 3076
  573.9 183.2 %all-gather.22.cloned.1.call-start = ((), (), s32[]{:S(2)}) async-start(), calls=%async_computation.8 | async-start | bytes 10485760 | tf_op jit(solution)/shard_map/all_gather | solution.py:41
  581.3 501.2 %all-reduce.44.cloned.1.call-start = ((), (), s32[]{:S(2)}) async-start(), calls=%async_computation.10 | async-start | bytes 278528
  833.0 831.9 %reduce-scatter.6.cloned.1.call-start = ((), (), s32[]{:S(2)}) async-start(), calls=%async_computation.5 | async-start | bytes 34603008 | tf_op jit(solution)/shard_map/reduce_scatter | solution.py:322
  859.4 2278.0 %reduce-scatter.4.cloned.1.call-start = ((), (), s32[]{:S(2)}) async-start(), calls=%async_computation.4 | async-start | bytes 72450048 | tf_op jit(solution)/shard_map/reduce_scatter | solution.py:320
  914.4 12.0 collective-permute-start.2
  921.2 38.0 %copy-start.90 = (bf16[256,64]{1,0:T(8,128)(2,1)}, bf16[256,64]{1,0:T(8,128)(2,1)S(1)}, u32[]{:S(2)}) copy-start(bf16[256,64]{1,0:T(8,128)(2,1)S(1)} %get-tuple-element.403) | copy-start | bytes 98308
  925.0 6.4 collective-permute-start.3
  932.5 26.7 copy-start.75
  1082.4 2104.7 %copy-start.98 = (f32[6336]{0:T(1024)S(1)}, f32[6336]{0:T(1024)}, u32[]{:S(2)}) copy-start(f32[6336]{0:T(1024)} %param.37) | copy-start | bytes 76036
  1082.4 2104.7 %copy-start.99 = (f32[6336]{0:T(1024)S(1)}, f32[6336]{0:T(1024)}, u32[]{:S(2)}) copy-start(f32[6336]{0:T(1024)} %param.38) | copy-start | bytes 76036
  1082.4 2105.4 %copy-start.34 = (f32[64,8512]{1,0:T(8,128)S(1)}, f32[64,8512]{1,0:T(8,128)}, u32[]{:S(2)}) copy-start(f32[64,8512]{1,0:T(8,128)} %param.27) | copy-start | bytes 6537220
  (115 other events, 833.0 us)
Sparse Core Ops, SparseCore 0:
  11.5 206.0 all-gather.13
  221.1 113.8 all-gather.15
  337.3 85.7 all-gather.19
  425.4 87.5 all-gather.17
  574.1 93.6 all-gather.23
  669.4 87.5 all-gather.21
  833.2 119.2 all-reduce.43
  954.8 710.1 reduce-scatter.5
  1667.4 1470.0 reduce-scatter.3
where the time goes:
time: 3210 us
  waiting for transfers between devices  2370 us (74%)
  matrix products  321 us (10%)
  other arithmetic  251 us (8%)
  blocking collectives  128 us (4%)
  local copies, waits for them, and re-layouts  96.8 us (3%)
    reduce_scatter x1, waiting for transfers between devices, per_device(): lax.psum_scatter(grad_in, ('dp', 'seq'), scatter_dimension=0, tiled=True)  1470 us
    reduce_scatter x1, waiting for transfers between devices, per_device(): lax.psum_scatter(grad_out, ('dp', 'seq'), scatter_dimension=1, tiled=True)  581 us
    all_gather x4, waiting for transfers between devices, entering_2(): gathered = jax.tree.map(lambda a: lax.all_gather(a, axis), part)  190 us
    all_gather x1, waiting for transfers between devices, per_device(): lax.all_gather(in_low, ('dp', 'seq'), axis=0, tiled=True)  125 us
    dot_general x2, matrix products, per_device(): jnp.einsum('td,tf->df', hidden_b, d_proj_b, preferred_element_type=jnp.fl...  73.7 us
    all_gather x1, blocking collectives, per_device(): lax.all_gather(conv_low, ('dp', 'seq'), axis=1, tiled=True)  72.7 us
  transfers between devices with their start and end apart: 13, of which 9 were waited for; matrix products, arithmetic and copies ran while one was open for 16% of the time, Pallas kernels for 0%

commit v1 on v0

v1 whole, which is shorter than its diff:
```python
import jax
import jax.numpy as jnp
from jax import lax
from jax.sharding import PartitionSpec as P

D = 2048
HEADS = 64
HEADDIM = 64
STATE = 128
CONV = 4
BLOCK = 256
MICRO = 2
INNER = 4096
CH = 4352
NORM_EPS = 1e-05
LEARN_RATE = 0.004
BETA_ONE = 0.9
BETA_TWO = 0.95
FIX_ONE = 1.0 - 0.9**10
FIX_TWO = 1.0 - 0.95**10
ADAM_EPS = 1e-08
WEIGHT_DECAY = 0.1
CLIP_NORM = 1.0
BF = jnp.bfloat16
F32 = jnp.float32
ALL = ("dp", "seq")


def to_bfloat(value):
    return value.astype(BF).astype(F32)


def rounding_pair():
    def value_plain(value):
        return to_bfloat(value)

    def value_keep(value):
        return (to_bfloat(value), None)

    def value_pass(kept, grad):
        return (grad,)

    def grad_plain(value):
        return value

    def grad_keep(value):
        return (value, None)

    def grad_round(kept, grad):
        return (to_bfloat(grad),)

    value_op = jax.custom_vjp(value_plain)
    value_op.defvjp(value_keep, value_pass)
    grad_op = jax.custom_vjp(grad_plain)
    grad_op.defvjp(grad_keep, grad_round)
    return (value_op, grad_op)


value_lower, grad_lower = rounding_pair()


def causal_conv(padded, seg_padded, conv_w, length):
    segment = seg_padded[CONV - 1 :]
    summed = conv_w[CONV][None, :] + jnp.zeros_like(padded[:length])
    for tap in range(CONV):
        valid = (seg_padded[tap : tap + length] == segment).astype(padded.dtype)
        summed = summed + conv_w[tap][None, :] * padded[tap : tap + length] * valid[:, None]
    return summed


def block_parts(xh, bm, cm, dt, a_neg, seg, seg_prev):
    width = xh.shape[0]
    cum = jnp.cumsum(dt * a_neg[None, :], axis=0)
    pos = jnp.arange(width)
    same = ((seg[:, None] == seg[None, :]) & (pos[:, None] >= pos[None, :])).astype(F32)
    ch = cum.T
    decay = jnp.exp(jnp.minimum(ch[:, :, None] - ch[:, None, :], 0.0)) * same[None]
    inner = jnp.einsum("tn,sn->ts", cm, bm)
    mix = grad_lower(value_lower(inner[None] * decay * dt.T[:, None, :]))
    y_intra = jnp.einsum("hts,shp->thp", mix, xh)
    end_w = jnp.exp(cum[-1][None, :] - cum) * (seg == seg[-1]).astype(F32)[:, None]
    weighted = grad_lower(value_lower(xh * (end_w * dt)[:, :, None]))
    s_block = jnp.einsum("shp,sn->hpn", weighted, bm)
    a_block = jnp.exp(cum[-1]) * (seg[-1] == seg_prev).astype(F32)
    entry = jnp.exp(cum) * (seg == seg_prev).astype(F32)[:, None]
    return (y_intra, s_block, a_block, entry)


def mixer(conv_in, dt_raw, conv_w, a_log, skip, dt_bias, seg):
    length = conv_in.shape[0]
    hl = dt_raw.shape[1]
    xw = hl * HEADDIM
    nb = length // BLOCK
    padded = jnp.concatenate([jnp.zeros((CONV - 1, conv_in.shape[1]), F32), conv_in], axis=0)
    seg_pad = jnp.concatenate([jnp.full((CONV - 1,), -1, jnp.int32), seg])
    act = grad_lower(value_lower(jax.nn.silu(causal_conv(padded, seg_pad, conv_w, length))))
    xh = act[:, :xw].reshape(nb, BLOCK, hl, HEADDIM)
    bm = act[:, xw : xw + STATE].reshape(nb, BLOCK, STATE)
    cm = act[:, xw + STATE :].reshape(nb, BLOCK, STATE)
    dt = jax.nn.softplus(dt_raw + dt_bias[None, :]).reshape(nb, BLOCK, hl)
    a_neg = -jnp.exp(a_log)
    segb = seg.reshape(nb, BLOCK)
    seg_prev = jnp.concatenate([jnp.full((1,), -1, jnp.int32), segb[:-1, -1]])

    def step(state, ins):
        x_c, b_c, c_c, dt_c, s_c, p_c = ins
        y_in, s_blk, a_blk, entry = block_parts(x_c, b_c, c_c, dt_c, a_neg, s_c, p_c)
        y_st = entry[:, :, None] * jnp.einsum("tn,hpn->thp", c_c, value_lower(state))
        y = y_in + y_st + skip[None, :, None] * x_c
        return (a_blk[:, None, None] * state + s_blk, y)

    start = jnp.zeros((hl, HEADDIM, STATE), F32)
    _, y = lax.scan(jax.checkpoint(step), start, (xh, bm, cm, dt, segb, seg_prev))
    return grad_lower(y.reshape(length, xw))


def adamw(master, gradient, first, second, clip, decay):
    clipped = gradient * clip
    first_new = BETA_ONE * first + (1.0 - BETA_ONE) * clipped
    second_new = BETA_TWO * second + (1.0 - BETA_TWO) * clipped * clipped
    update = first_new / FIX_ONE / (jnp.sqrt(second_new / FIX_TWO) + ADAM_EPS) + decay * master
    return (-LEARN_RATE * update, first_new, second_new)


def dot(a, b, dims, out=F32):
    return lax.dot_general(a, b, (dims, ((), ())), preferred_element_type=out)


NN = ((1,), (0,))
NT = ((1,), (1,))
TN = ((0,), (0,))


def per_device(tokens, cotangent, segments, in_weight, in_m, in_v, conv_weight, conv_m, conv_v,
               out_weight, out_m, out_v, packed, packed_m, packed_v):
    n = lax.axis_size("seq")
    rank = lax.axis_index("seq")
    ndev = n * lax.axis_size("dp")
    hl = HEADS // n
    xw = hl * HEADDIM
    rows = D // ndev
    piece = tokens.shape[1]
    length = piece * n

    in_low = in_weight.astype(BF)
    out_low = out_weight.astype(BF).T
    xs = INNER + INNER
    parts_z = in_low[:, :INNER].reshape(rows, n, xw).transpose(1, 0, 2)
    parts_x = in_low[:, INNER:xs].reshape(rows, n, xw).transpose(1, 0, 2)
    parts_bc = jnp.broadcast_to(in_low[None, :, xs : xs + 2 * STATE], (n, rows, 2 * STATE))
    parts_dt = jnp.pad(in_low[:, xs + 2 * STATE :].reshape(rows, n, hl).transpose(1, 0, 2), ((0, 0), (0, 0), (0, 128 - hl)))
    parts_o = out_low.reshape(rows, n, xw).transpose(1, 0, 2)
    send = jnp.concatenate([parts_x, parts_bc, parts_dt, parts_z, parts_o], axis=2)
    got = lax.all_to_all(send, "seq", 0, 0).reshape(n * rows, -1)
    xc = xw + 2 * STATE + 128
    w_x = lax.all_gather(got[:, :xc], "dp", axis=0, tiled=True)
    w_z = lax.all_gather(got[:, xc : xc + xw], "dp", axis=0, tiled=True)
    w_o = lax.all_gather(got[:, xc + xw :], "dp", axis=0, tiled=True)
    conv_full = lax.all_gather(conv_weight.astype(BF), ALL, axis=1, tiled=True)
    conv_loc = jnp.concatenate([lax.dynamic_slice_in_dim(conv_full, rank * xw, xw, 1), conv_full[:, INNER:]], axis=1).astype(F32)

    a_log = lax.dynamic_slice_in_dim(packed, rank * hl, hl)
    skip = lax.dynamic_slice_in_dim(packed, HEADS + rank * hl, hl)
    dt_bias = lax.dynamic_slice_in_dim(packed, 2 * HEADS + rank * hl, hl)
    gain_in = packed[3 * HEADS : 3 * HEADS + D]
    gain_out = lax.dynamic_slice_in_dim(packed, 3 * HEADS + D + rank * xw, xw)

    tok = tokens.astype(F32)
    r_in = lax.rsqrt(jnp.mean(tok * tok, axis=-1, keepdims=True) + NORM_EPS)
    hidden_own = (tok * r_in * gain_in).astype(BF)
    hidden = lax.all_gather(hidden_own, "seq", axis=1, tiled=True).reshape(MICRO * length, D)
    cot = lax.all_gather(cotangent, "seq", axis=1, tiled=True).reshape(MICRO * length, D)

    proj_x = dot(hidden, w_x, NN).astype(BF)
    proj_z = dot(hidden, w_z, NN).astype(BF)
    conv_in = proj_x[:, : xw + 2 * STATE].astype(F32).reshape(MICRO, length, -1)
    dt_raw = proj_x[:, xw + 2 * STATE : xw + 2 * STATE + hl].astype(F32).reshape(MICRO, length, hl)
    mix_fn = lambda ci, dr, cw, al, sk, db: jax.vmap(mixer, (0, 0, None, None, None, None, 0))(ci, dr, cw, al, sk, db, segments)
    y, pull = jax.vjp(mix_fn, conv_in, dt_raw, conv_loc, a_log, skip, dt_bias)
    y = y.reshape(MICRO * length, xw)
    z = proj_z.astype(F32)
    sig = jax.nn.sigmoid(z)
    gz = y * z * sig
    dnr = dot(cot, w_o, NN)
    dng = dnr * gain_out
    sums = lax.psum(jnp.stack([jnp.sum(gz * gz, axis=1), jnp.sum(dng * gz, axis=1)]), "seq")
    r = lax.rsqrt(sums[0] / INNER + NORM_EPS)
    normed = (gz * r[:, None] * gain_out).astype(BF)
    d_gz = r[:, None] * dng - gz * (r * r * r * sums[1] / INNER)[:, None]
    d_gain_out = jnp.sum(dnr * gz * r[:, None], axis=0)
    dy = d_gz * z * sig
    dz = (d_gz * y * (sig * (1.0 + z * (1.0 - sig)))).astype(BF)

    out_part = dot(normed, w_o, NT).astype(BF).reshape(MICRO, length, D)
    out_sum = lax.psum_scatter(out_part, "seq", scatter_dimension=1, tiled=True)
    output = (tok + out_sum.astype(F32)).astype(BF)
    dw_o = lax.psum_scatter(dot(cot, normed, TN).astype(BF), "dp", scatter_dimension=0, tiled=True)
    dw_z = lax.psum_scatter(dot(hidden, dz, TN).astype(BF), "dp", scatter_dimension=0, tiled=True)

    d_ci, d_dr, d_conv, d_alog, d_skip, d_dtb = pull(dy.reshape(MICRO, length, xw))
    d_px = jnp.concatenate([d_ci.reshape(MICRO * length, -1), jnp.pad(d_dr.reshape(MICRO * length, hl), ((0, 0), (0, 128 - hl)))], axis=1).astype(BF)
    d_hid = (dot(dz, w_z, NT) + dot(d_px, w_x, NT)).astype(BF).reshape(MICRO, length, D)
    d_hidden = lax.psum_scatter(d_hid, "seq", scatter_dimension=1, tiled=True).astype(F32)
    dw_x = lax.psum_scatter(dot(hidden, d_px, TN).astype(BF), "dp", scatter_dimension=0, tiled=True)

    grad_piece = jnp.concatenate([dw_x, dw_z, dw_o], axis=1).reshape(n, rows, -1)
    grad_got = lax.all_to_all(grad_piece, "seq", 0, 0)
    flat = lambda a: a.transpose(1, 0, 2).reshape(rows, -1)
    g_x = flat(grad_got[:, :, :xw]).astype(F32)
    g_bc = jnp.sum(grad_got[:, :, xw : xw + 2 * STATE].astype(F32), axis=0)
    g_dt = flat(grad_got[:, :, xw + 2 * STATE : xw + 2 * STATE + hl]).astype(F32)
    g_z = flat(grad_got[:, :, xc : xc + xw]).astype(F32)
    shard_in = jnp.concatenate([g_z, g_x, g_bc, g_dt], axis=1)
    shard_out = flat(grad_got[:, :, xc + xw :]).astype(F32).T

    dh = d_hidden * gain_in
    d_gain_in = jnp.sum(d_hidden * tok * r_in, axis=(0, 1))
    d_tok = r_in * (dh - tok * (r_in * r_in) * jnp.mean(dh * tok, axis=-1, keepdims=True))
    input_grad = (cotangent.astype(F32) + d_tok).astype(BF)

    conv_part = jnp.zeros((CONV + 1, CH), F32)
    conv_part = lax.dynamic_update_slice(conv_part, d_conv[:, :xw], (0, rank * xw))
    conv_part = conv_part.at[:, INNER:].set(d_conv[:, xw:])
    vec_part = jnp.zeros((packed.shape[0],), F32)
    vec_part = lax.dynamic_update_slice(vec_part, d_alog, (rank * hl,))
    vec_part = lax.dynamic_update_slice(vec_part, d_skip, (HEADS + rank * hl,))
    vec_part = lax.dynamic_update_slice(vec_part, d_dtb, (2 * HEADS + rank * hl,))
    vec_part = lax.dynamic_update_slice(vec_part, d_gain_in, (3 * HEADS,))
    vec_part = lax.dynamic_update_slice(vec_part, d_gain_out, (3 * HEADS + D + rank * xw,))
    partial_sq = jnp.sum(shard_in * shard_in) + jnp.sum(shard_out * shard_out)
    total_sq, conv_tot, vec_tot = lax.psum((partial_sq, conv_part, vec_part), ALL)
    cw = conv_weight.shape[1]
    shard_conv = lax.dynamic_slice_in_dim(conv_tot, (lax.axis_index("dp") * n + rank) * cw, cw, 1)
    grad_norm = jnp.sqrt(total_sq + jnp.sum(conv_tot * conv_tot) + jnp.sum(vec_tot * vec_tot))
    clip = jnp.minimum(1.0, CLIP_NORM / (grad_norm + 1e-06))
    in_new = adamw(in_weight, shard_in, in_m, in_v, clip, WEIGHT_DECAY)
    conv_new = adamw(conv_weight, shard_conv, conv_m, conv_v, clip, WEIGHT_DECAY)
    out_new = adamw(out_weight, shard_out, out_m, out_v, clip, WEIGHT_DECAY)
    vec_new = adamw(packed, vec_tot, packed_m, packed_v, clip, 0.0)
    return (
        output, input_grad, grad_norm,
        in_weight + in_new[0], in_new[1], in_new[2],
        conv_new[0], conv_new[1], conv_new[2],
        out_weight + out_new[0], out_new[1], out_new[2],
        vec_new[0], vec_new[1], vec_new[2],
    )


def solution(mesh):
    tok, col, row = P(None, ALL, None), P(None, ALL), P(ALL, None)
    return jax.shard_map(
        per_device,
        mesh=mesh,
        in_specs=(tok, tok, P(None, "dp"), row, row, row, col, col, col, col, col, col, P(), P(), P()),
        out_specs=(tok, tok, P(), row, row, row, col, col, col, col, col, col, P(), P(), P()),
        check_vma=False,
    )
```

time: 3210 us -> 1400 us (0.44)
  waiting for transfers between devices: 2370 us -> 330 us
  local copies, waits for them, and re-layouts: 96.8 us -> 285 us
    reduce_scatter x2 -> x5, waiting for transfers between devices: 2050 us -> 91 us  [the longest x1 49.7 us: per_device(): lax.psum_scatter(d_hid, 'seq', scatter_dimension=1, tiled=True).astype(F32)]
    all_gather x6 -> x5, waiting for transfers between devices: 317 us -> 81.2 us  [the longest x1 68.3 us: per_device(): lax.all_gather(hidden_own, 'seq', axis=1, tiled=True)]
    psum x0 -> x1, waiting for transfers between devices: none -> 124 us  [per_device(): lax.psum((partial_sq, conv_part, vec_part), ALL)]
    reduce_sum x23 -> x17, other arithmetic: 103 us -> 51.5 us  [the longest x1 24.3 us: causal_conv(): conv_w[tap][None, :] * padded[tap:tap + length] * valid[:, None]]
    another operation x20 -> x49, local copies, waits for them, and re-layouts: 4.36 us -> 48.2 us
    squeeze x0 -> x36, local copies, waits for them, and re-layouts: none -> 37.3 us  [the longest x32 37.2 us: mixer(): lax.scan(jax.checkpoint(step), start, (xh, bm, cm, dt, segb, seg_prev))]
    transpose x2 -> x13, local copies, waits for them, and re-layouts: 1.08 us -> 36.9 us  [the longest x3 32.6 us: mixer(): return grad_lower(y.reshape(length, xw))]
    another operation x20 -> x47, other arithmetic: 40.6 us -> 75.5 us
  transfers between devices with their start and end apart: 13 -> 12, of which waited for: 9 -> 7; matrix products, arithmetic and copies ran while one was open for 16% -> 58% of each run, Pallas kernels for 0% -> 0%
where the time goes in v1:
time: 1400 us; the launch traced here: 1380 us
  waiting for transfers between devices  330 us (24%)
  matrix products  320 us (23%)
  local copies, waits for them, and re-layouts  285 us (20%)
  other arithmetic  265 us (19%)
  blocking collectives  155 us (11%)
  between operations  19.5 us (1%)
    dot_general x9, matrix products, dot(): return lax.dot_general(a, b, (dims, ((), ())), preferred_element_type=out)  155 us
    psum x1, waiting for transfers between devices, per_device(): lax.psum((partial_sq, conv_part, vec_part), ALL)  124 us
    dot_general x12, matrix products, block_parts(): y_intra = jnp.einsum('hts,shp->thp', mix, xh)  74.1 us
    another operation x42, other arithmetic  71.6 us
    all_gather x1, waiting for transfers between devices, per_device(): lax.all_gather(hidden_own, 'seq', axis=1, tiled=True)  68.3 us
    all_gather x1, blocking collectives, per_device(): conv_full = lax.all_gather(conv_weight.astype(BF), ALL, axis=1, tiled=True)  68.1 us
    reduce_scatter x1, waiting for transfers between devices, per_device(): lax.psum_scatter(d_hid, 'seq', scatter_dimension=1, tiled=True).astype(F32)  49.7 us
    another operation x45, local copies, waits for them, and re-layouts  44.2 us
  transfers between devices with their start and end apart: 12, of which 7 were waited for; matrix products, arithmetic and copies ran while one was open for 58% of the time, Pallas kernels for 0%

profile of v1, /device:TPU:0, one launch (start us, length us, event | category | flops | bytes accessed | tf_op | source)
XLA Modules:
  0.0 1381.3 jit_solution(7220957539344625673)
XLA Ops:
  20.8 27.0 %all_to_all.10 = bf16[4,64,3456]{2,1,0:T(8,128)(2,1)S(1)} all-to-all(bf16[4,64,3456]{2,1,0:T(8,128)(2,1)S(1)} %copy.386), channel_id=1, replica_groups=mesh['dp'=8,'seq'=4] {'seq'}, dimensions={0} | all-to-all | bytes 3538944 | tf_op jit(solution)/shard_map/all_to_all | solution.py:154
  58.1 68.1 %all-gather = bf16[32,136,5]{1,2,0:T(8,128)(2,1)S(1)} all-gather(bf16[1,136,5]{1,2,0:T(8,128)(2,1)S(1)} %convert_bitcast_fusion.4), channel_id=1, replica_groups=mesh['dp'=8,'seq'=4] {'dp','seq'}, dimensions={0}, use_global_device_ids=true | all-gather | bytes 44880 | tf_op jit(solution)/shard_map/all_gather | solution.py:159
  131.1 68.3 %all-gather.7.cloned.1.call-done = bf16[2,1024,2048]{2,1,0:T(8,128)(2,1)} async-done(((bf16[2,256,2048]{2,1,0:T(8,128)(2,1)}), bf16[2,1024,2048]{2,1,0:T(8,128)(2,1)}) %all-gather.7.cloned.1.call-update) | async-done | bytes 8388624 | tf_op jit(solution)/shard_map/all_gather | solution.py:171
  199.4 17.0 %convolution_convert_fusion.3 = bf16[2048,1408]{1,0:T(8,128)(2,1)S(1)} fusion(bf16[2048,2048]{1,0:T(8,128)(2,1)} %bitcast.521, bf16[2048,1408]{1,0:T(8,128)(2,1)} %all-gather.9.cloned.1.call-done), kind=kOutput, calls=%fused_computation.222 | convolution fusion | flops 11814043648 | bytes 19922944 | tf_op jit(solution)/shard_map/dot_general | solution.py:126
  218.9 11.7 fusion.117
  232.3 8.3 slice.258
  245.4 8.7 copy.391
  254.1 10.9 reshape.595
  265.1 8.2 copy.395
  279.2 55.6 %while.43 = (s32[]{:T(128)}, f32[2,16,64,128]{3,2,1,0:T(8,128)S(1)}, f32[4,2,256,16,64]{2,4,3,1,0:T(8,128)}, f32[4,2,16,64,128]{4,3,2,1,0:T(8,128)}, f32[4,2,256...) while((s32[]{:T(128)}, ...), condition=%wide.region_4.5_spmd.clone, body=%wide.region_1.4_spmd.clone.sunk | while | flops 589023360 | bytes 45310616 | solution.py:113
  283.3 4.6 fusion.263
  334.9 12.4 copy.398
  347.3 10.8 reshape.598
  358.1 15.0 %fusion.181 = f32[1024,2048]{1,0:T(8,128)} fusion(bf16[2048,1024]{1,0:T(8,128)(2,1)} %all-gather.13.cloned.1.call-done, bf16[2048,2048]{1,0:T(8,128)(2,1)} %bitcast.525), kind=kOutput, calls=%fused_computation.342 | convolution fusion | flops 8589934592 | bytes 20971520 | tf_op jit(solution)/shard_map/dot_general | solution.py:126
  373.1 12.9 all-gather.11.cloned.1.call-done
  386.0 20.2 %multiply_reduce_fusion.8 = (f32[2048]{0:T(1024)S(1)}, f32[2048]{0:T(1024)S(1)}, bf16[2048,1024]{0,1:T(8,128)(2,1)}) fusion(f32[2048,1024]{0,1:T(8,128)} %reshape.598, f32[1024]{0:T(1024)S(1)} %dynamic_slice.118, f32[1024,2048]{1,0:T(8,128)} %fusion.181, bf16[2048,2048]{1,0:T(8,128)(2,1)} %bitcast.522, bf16[2048,1024]{1,0:T(8,128)(2,1)} %all-gather.11.cloned.1.call-done), kind=kOutput, calls=%fused_computation.220 | convolution fusion | flops 8615096320 | bytes 33574912 | tf_op jit(solution)/shard_map/dot_general | solution.py:126
  406.2 16.2 %psum.28 = f32[2,2048]{1,0:T(2,128)S(1)} all-reduce(f32[2,2048]{1,0:T(2,128)S(1)} %pad_maximum_fusion.2), channel_id=1, replica_groups=mesh['dp'=8,'seq'=4] {'seq'}, use_global_device_ids=true, to_apply=%region_7.8 | all-reduce | flops 4096 | bytes 32768 | tf_op jit(solution)/shard_map/psum | solution.py:186
  422.5 16.9 %convert_bitcast_fusion = bf16[2048,1024]{1,0:T(8,128)(2,1)} fusion(bf16[2048,2048]{1,0:T(8,128)(2,1)} %bitcast.526, f32[2048]{0:T(1024)S(1)} %bitcast.509, f32[1024]{0:T(1024)S(1)} %dynamic_slice.118, f32[2048,1024]{0,1:T(8,128)} %reshape.598, bf16[2048,1024]{0,1:T(8,128)(2,1)} %get-tuple-element.965), kind=kOutput, calls=%fused_computation.240 | convolution fusion | flops 8610906112 | bytes 25178112 | tf_op jit(solution)/shard_map/dot_general | solution.py:126
  439.5 14.9 %fusion.130 = (f32[2048,1024]{0,1:T(8,128)}, bf16[2048,1024]{0,1:T(8,128)(2,1)}, f32[1024]{0:T(1024)}) fusion(bf16[2048,1024]{0,1:T(8,128)(2,1)} %get-tuple-element.965, f32[2048]{0:T(1024)S(1)} %fusion.148, f32[1024]{0:T(1024)S(1)} %dynamic_slice.118, f32[1024,2048]{1,0:T(8,128)} %fusion.181, f32[2048]{0:T(1024)S(1)} %bitcast.511, f32[2048,1024]{0,1:T(8,128)} %reshape.598), kind=kLoop, calls=%fused_computation.241 | loop fusion | flops 50330624 | bytes 33579008 | tf_op jit(solution)/shard_map/transpose(jvp(vmap()))/transpose | solution.py:114
  454.4 10.9 reshape.615
  465.3 9.4 copy.492
  482.3 377.1 %while.44 = (s32[]{:T(128)}, f32[16]{0:T(128)}, f32[16]{0:T(128)}, f32[2,16,64,128]{3,2,1,0:T(8,128)}, f32[4,2,256,16,64]{2,4,3,1,0:T(8,128)}, /*index=5*/f32[4,...) while((s32[]{:T(128)}, f32[16]{0:T(128)}, f32[16]{0:T(128)}, ...), condition=%wide.region_24.25_spmd.clone, body=%wide.region_9.24_spmd.clone.sunk | while | flops 1376102656 | bytes 74723408 | solution.py:113
  517.4 9.4 fusion.284
  543.8 6.3 reduce-window.70
  610.9 9.4 fusion.284
  638.0 6.3 reduce-window.70
  705.8 9.4 fusion.284
  732.8 6.3 reduce-window.70
  800.6 9.4 fusion.284
  827.6 6.3 reduce-window.70
  860.7 14.5 %copy.425 = f32[2,4,256,16,64]{4,3,2,1,0:T(8,128)} copy(f32[2,4,256,16,64]{2,4,3,0,1:T(8,128)} %bitcast.477) | data formatting | bytes 16777216 | tf_op jit(solution)/shard_map/transpose(jvp(vmap()))/reshape | solution.py:97
  875.3 14.6 %reshape.632 = f32[2,1024,1024]{2,1,0:T(8,128)} reshape(f32[2,4,256,16,64]{4,3,2,1,0:T(8,128)} %copy.425) | data formatting | bytes 16777216 | tf_op jit(solution)/shard_map/transpose(jvp(vmap()))/reshape | solution.py:97
  892.1 14.0 %convolution_convert_fusion.6 = bf16[2048,1024]{1,0:T(8,128)(2,1)} fusion(bf16[2048,2048]{1,0:T(8,128)(2,1)} %bitcast.523, bf16[2048,1024]{0,1:T(8,128)(2,1)} %get-tuple-element.939), kind=kOutput, calls=%fused_computation.246 | convolution fusion | flops 8592031744 | bytes 16777216 | tf_op jit(solution)/shard_map/dot_general | solution.py:126
  906.2 24.3 %multiply_reduce_fusion.5 = (f32[1280]{0:T(1024)S(1)}, f32[1280]{0:T(1024)S(1)}, f32[1280]{0:T(1024)S(1)}, f32[1280]{0:T(1024)S(1)}, f32[1280]{0:T(1024)S(1)}, /*index=5*/f32[2,1024,1280]{2,1,0:T(8,128)S(1)}) fusion(f32[2,1024,1280]{2,1,0:T(8,128)} %copy-done.1, f32[2,1024]{1,0:T(2,128)S(1)} %copy-done.35, f32[2,1024]{1,0:T(2,128)S(1)} %copy-done.37, ...), kind=kLoop, calls=%fused_computation.185 | loop fusion | flops 68151040 | bytes 47236096 | tf_op jit(solution)/shard_map/transpose(jvp(vmap()))/reduce_sum | solution.py:67
  930.5 14.6 %broadcast_multiply_fusion.2 = (f32[2,1024,1280]{2,1,0:T(8,128)}, f32[2,1024,1280]{2,1,0:T(8,128)}, f32[2,1024,1280]{2,1,0:T(8,128)}, f32[2,1024,1280]{2,1,0:T(8,128)}) fusion(f32[2,1024,1280]{2,1,0:T(8,128)S(1)} %get-tuple-element.916, f32[1280]{0:T(1024)S(1)} %copy-done.47, f32[2,1024]{1,0:T(2,128)S(1)} %copy-done.33, f32[1280]{0:T(1024)S(1)} %copy-done.45, ...), kind=kLoop, calls=%fused_computation.227 | loop fusion | flops 18350080 | bytes 52473856 | tf_op jit(solution)/shard_map/transpose(jvp(vmap()))/mul | solution.py:67
  945.2 14.7 %fusion.103 = bf16[2,1024,1280]{2,1,0:T(8,128)(2,1)S(1)} fusion(f32[2,1024,1280]{2,1,0:T(8,128)} %get-tuple-element.942, f32[2,1024,1280]{2,1,0:T(8,128)} %get-tuple-element.943, f32[2,1024,1280]{2,1,0:T(8,128)} %get-tuple-element.944, f32[2,1024,1280]{2,1,0:T(8,128)} %get-tuple-element.941), kind=kLoop, calls=%fused_computation.180 | loop fusion | flops 10485760 | bytes 47185920 | tf_op jit(solution)/shard_map/convert.15
  962.2 17.8 %convolution_convert_fusion.4 = bf16[2048,1408]{1,0:T(8,128)(2,1)} fusion(bf16[2048,2048]{1,0:T(8,128)(2,1)} %bitcast.524, bf16[2048,16]{1,0:T(8,128)(2,1)S(1)} %fusion.140, bf16[2048,1280]{1,0:T(8,128)(2,1)S(1)} %bitcast.494), kind=kOutput, calls=%fused_computation.223 | convolution fusion | flops 11831345152 | bytes 19464192 | tf_op jit(solution)/shard_map/dot_general | solution.py:126
  980.0 15.8 %fusion.182 = f32[2048,2048]{1,0:T(8,128)} fusion(bf16[2048,1024]{0,1:T(8,128)(2,1)} %get-tuple-element.939, bf16[2048,1024]{1,0:T(8,128)(2,1)} %all-gather.11.cloned.1.call-done), kind=kOutput, calls=%fused_computation.343 | convolution fusion | flops 8589934592 | bytes 25165824 | tf_op jit(solution)/shard_map/dot_general | solution.py:126
  995.8 21.3 %add_convert_fusion = bf16[2048,2048]{1,0:T(8,128)(2,1)} fusion(f32[2048,2048]{1,0:T(8,128)} %fusion.182, bf16[2048,1408]{1,0:T(8,128)(2,1)} %all-gather.9.cloned.1.call-done, bf16[2048,16]{1,0:T(8,128)(2,1)S(1)} %fusion.140, bf16[2048,1280]{1,0:T(8,128)(2,1)} %bitcast.495), kind=kOutput, calls=%fused_computation.167 | convolution fusion | flops 11836850176 | bytes 36241408 | tf_op jit(solution)/shard_map/dot_general | solution.py:126
  1018.1 17.2 %convolution_convert_fusion.2 = bf16[2048,2048]{1,0:T(8,128)(2,1)} fusion(bf16[2048,1024]{1,0:T(8,128)(2,1)} %all-gather.13.cloned.1.call-done, f32[2048]{0:T(1024)S(1)} %bitcast.512, f32[1024]{0:T(1024)S(1)} %copy-done.60, f32[2048,1024]{0,1:T(8,128)} %reshape.598, bf16[2048,1024]{0,1:T(8,128)(2,1)} %get-tuple-element.965), kind=kOutput, calls=%fused_computation.221 | convolution fusion | flops 8613003264 | bytes 25178112 | tf_op jit(solution)/shard_map/dot_general | solution.py:126
  1035.4 6.5 reduce-scatter.10.cloned.1.call-done
  1049.8 5.1 fusion.145
  1055.2 32.9 %all-to-all-done.1 = bf16[4,64,3456]{2,1,0:T(8,128)(2,1)} async-done(((bf16[4,64,3456]{2,1,0:T(8,128)(2,1)}), bf16[4,64,3456]{2,1,0:T(8,128)(2,1)}, u32[]{:S(2)}, u32[]{:S(2)}) %all-to-all-start.1) | async-done | bytes 1769504 | tf_op jit(solution)/shard_map/all_to_all | solution.py:207
  1096.5 49.7 %reduce-scatter.8.cloned.1.call-done = bf16[2,256,2048]{2,1,0:T(8,128)(2,1)} async-done(((bf16[2,1024,2048]{2,1,0:T(8,128)(2,1)}), bf16[2,256,2048]{2,1,0:T(8,128)(2,1)}) %reduce-scatter.8.cloned.1.call-update) | async-done | bytes 2097168 | tf_op jit(solution)/shard_map/reduce_scatter | solution.py:203
  1149.6 123.7 %all-reduce.22.cloned.1.call-done = f32[5,4352]{1,0:T(8,128)} async-done(((f32[5,4352]{1,0:T(8,128)}), f32[5,4352]{1,0:T(8,128)}) %all-reduce.22.cloned.1.call-update) | async-done | bytes 87056 | tf_op jit(solution)/shard_map/psum | solution.py:231
  1274.9 44.0 %all-reduce.19 = (f32[]{:T(128)}, f32[6336]{0:T(1024)S(1)}) all-reduce(f32[]{:T(128)S(6)} %add.331, f32[6336]{0:T(1024)S(1)} %dynamic_update_slice.69), channel_id=1, replica_groups=mesh['dp'=8,'seq'=4] {'dp','seq'}, use_global_device_ids=true, to_apply=%region_33.34 | all-reduce | flops 6337 | bytes 50696 | tf_op jit(solution)/shard_map/psum | solution.py:231
  1331.7 34.7 %reduce-scatter.6.cloned.1.call-done = bf16[2,256,2048]{2,1,0:T(8,128)(2,1)} async-done(((bf16[2,1024,2048]{2,1,0:T(8,128)(2,1)}), bf16[2,256,2048]{2,1,0:T(8,128)(2,1)}) %reduce-scatter.6.cloned.1.call-update) | async-done | bytes 2097168 | tf_op jit(solution)/shard_map/reduce_scatter | solution.py:195
  1366.4 5.6 fusion.121
  (698 shorter events, 453.7 us)
Async XLA Ops:
  7.2 123.9 %all-gather.9.cloned.1.call-start = ((), (), s32[]{:S(2)}) async-start(), calls=%async_computation.8 | async-start | bytes 6488064 | tf_op jit(solution)/shard_map/all_gather | solution.py:156
  13.0 37.8 %copy-start.3 = (bf16[2,256,2048]{2,1,0:T(8,128)(2,1)S(1)}, bf16[2,256,2048]{2,1,0:T(8,128)(2,1)}, u32[]{:S(2)}) copy-start(bf16[2,256,2048]{2,1,0:T(8,128)(2,1)} %param.21) | copy-start | bytes 6291460
  47.8 78.6 %copy-start.49 = (s32[2,1024]{1,0:T(2,128)S(1)}, s32[2,1024]{1,0:T(2,128)}, u32[]{:S(2)}) copy-start(s32[2,1024]{1,0:T(2,128)} %param.23) | copy-start | bytes 24580
  50.0 149.4 %all-gather.7.cloned.1.call-start = ((), (), s32[]{:S(2)}) async-start(), calls=%async_computation.7 | async-start | bytes 10485760 | tf_op jit(solution)/shard_map/all_gather | solution.py:171
  54.3 303.8 %all-gather.13.cloned.1.call-start = ((), (), s32[]{:S(2)}) async-start(), calls=%async_computation.10 | async-start | bytes 4718592 | tf_op jit(solution)/shard_map/all_gather | solution.py:158
  56.6 301.5 %all-gather.15.cloned.1.call-start = ((), (), s32[]{:S(2)}) async-start(), calls=%async_computation.11 | async-start | bytes 10485760 | tf_op jit(solution)/shard_map/all_gather | solution.py:172
  57.2 328.8 %all-gather.11.cloned.1.call-start = ((), (), s32[]{:S(2)}) async-start(), calls=%async_computation.9 | async-start | bytes 4718592 | tf_op jit(solution)/shard_map/all_gather | solution.py:157
  58.1 381.4 %copy-start.59 = (f32[1024]{0:T(1024)}, f32[1024]{0:T(1024)S(1)}, u32[]{:S(2)}) copy-start(f32[1024]{0:T(1024)S(1)} %dynamic_slice.118) | copy-start | bytes 12292
  129.7 89.1 %copy-start.40 = (f32[1280]{0:T(1024)}, f32[1280]{0:T(1024)S(1)}, u32[]{:S(2)}) copy-start(f32[1280]{0:T(1024)S(1)} %get-tuple-element.834) | copy-start | bytes 15364
  129.7 89.1 %copy-start.42 = (f32[1280]{0:T(1024)}, f32[1280]{0:T(1024)S(1)}, u32[]{:S(2)}) copy-start(f32[1280]{0:T(1024)S(1)} %get-tuple-element.835) | copy-start | bytes 15364
  129.7 89.1 %copy-start.44 = (f32[1280]{0:T(1024)}, f32[1280]{0:T(1024)S(1)}, u32[]{:S(2)}) copy-start(f32[1280]{0:T(1024)S(1)} %get-tuple-element.836) | copy-start | bytes 15364
  129.8 89.1 %copy-start.46 = (f32[1280]{0:T(1024)}, f32[1280]{0:T(1024)S(1)}, u32[]{:S(2)}) copy-start(f32[1280]{0:T(1024)S(1)} %get-tuple-element.837) | copy-start | bytes 15364
  130.7 110.0 %copy-start.67 = (f32[16]{0:T(128)}, f32[16]{0:T(128)S(1)}, u32[]{:S(2)}) copy-start(f32[16]{0:T(128)S(1)} %get-tuple-element.957) | copy-start | bytes 196
  130.8 88.1 %copy-start.32 = (f32[2,1024]{1,0:T(2,128)}, f32[2,1024]{1,0:T(2,128)S(1)}, u32[]{:S(2)}) copy-start(f32[2,1024]{1,0:T(2,128)S(1)} %get-tuple-element.960) | copy-start | bytes 24580
  130.8 88.1 %copy-start.34 = (f32[2,1024]{1,0:T(2,128)}, f32[2,1024]{1,0:T(2,128)S(1)}, u32[]{:S(2)}) copy-start(f32[2,1024]{1,0:T(2,128)S(1)} %get-tuple-element.961) | copy-start | bytes 24580
  130.8 88.1 %copy-start.36 = (f32[2,1024]{1,0:T(2,128)}, f32[2,1024]{1,0:T(2,128)S(1)}, u32[]{:S(2)}) copy-start(f32[2,1024]{1,0:T(2,128)S(1)} %get-tuple-element.962) | copy-start | bytes 24580
  130.8 904.6 %reduce-scatter.14.cloned.1.call-start = ((), (), s32[]{:S(2)}) async-start(), calls=%async_computation.16 | async-start | bytes 4718592 | tf_op jit(solution)/shard_map/reduce_scatter | solution.py:197
  216.4 24.2 %copy-start.14 = (f32[2048,16]{1,0:T(8,128)}, f32[2048,16]{1,0:T(8,128)S(1)}, u32[]{:S(2)}) copy-start(f32[2048,16]{1,0:T(8,128)S(1)} %slice_convert_fusion) | copy-start | bytes 393220
  422.5 17.0 %copy-start.38 = (f32[1,2048]{1,0:T(1,128)}, f32[1,2048]{1,0:T(1,128)S(1)}, u32[]{:S(2)}) copy-start(f32[1,2048]{1,0:T(1,128)S(1)} %get-tuple-element.959) | copy-start | bytes 24580
  439.5 596.0 %reduce-scatter.12.cloned.1.call-start = ((), (), s32[]{:S(2)}) async-start(), calls=%async_computation.15 | async-start | bytes 4718592 | tf_op jit(solution)/shard_map/reduce_scatter | solution.py:198
  875.3 14.6 %copy-start.68 = (f32[16]{0:T(128)S(1)}, f32[16]{0:T(128)}, u32[]{:S(2)}) copy-start(f32[16]{0:T(128)} %copy-done.67) | copy-start | bytes 196
  892.0 14.1 %copy-start.22 = (f32[4,2,256,128]{3,2,0,1:T(8,128)S(1)}, f32[4,2,256,128]{3,2,0,1:T(8,128)}, u32[]{:S(2)}) copy-start(f32[4,2,256,128]{3,2,0,1:T(8,128)} %get-tuple-element.463) | copy-start | bytes 3145732
  892.0 14.1 %copy-start.23 = (f32[4,2,256,128]{3,2,0,1:T(8,128)S(1)}, f32[4,2,256,128]{3,2,0,1:T(8,128)}, u32[]{:S(2)}) copy-start(f32[4,2,256,128]{3,2,0,1:T(8,128)} %get-tuple-element.464) | copy-start | bytes 3145732
  892.0 14.1 %copy-start.33 = (f32[2,1024]{1,0:T(2,128)S(1)}, f32[2,1024]{1,0:T(2,128)}, u32[]{:S(2)}) copy-start(f32[2,1024]{1,0:T(2,128)} %copy-done.32) | copy-start | bytes 24580
  892.0 14.1 %copy-start.35 = (f32[2,1024]{1,0:T(2,128)S(1)}, f32[2,1024]{1,0:T(2,128)}, u32[]{:S(2)}) copy-start(f32[2,1024]{1,0:T(2,128)} %copy-done.34) | copy-start | bytes 24580
  892.0 14.1 %copy-start.37 = (f32[2,1024]{1,0:T(2,128)S(1)}, f32[2,1024]{1,0:T(2,128)}, u32[]{:S(2)}) copy-start(f32[2,1024]{1,0:T(2,128)} %copy-done.36) | copy-start | bytes 24580
  906.1 135.9 %reduce-scatter.10.cloned.1.call-start = ((), (), s32[]{:S(2)}) async-start(), calls=%async_computation.14 | async-start | bytes 6488064 | tf_op jit(solution)/shard_map/reduce_scatter | solution.py:204
  906.2 24.3 %copy-start.41 = (f32[1280]{0:T(1024)S(1)}, f32[1280]{0:T(1024)}, u32[]{:S(2)}) copy-start(f32[1280]{0:T(1024)} %copy-done.40) | copy-start | bytes 15364
  906.2 24.3 %copy-start.43 = (f32[1280]{0:T(1024)S(1)}, f32[1280]{0:T(1024)}, u32[]{:S(2)}) copy-start(f32[1280]{0:T(1024)} %copy-done.42) | copy-start | bytes 15364
  906.2 24.3 %copy-start.45 = (f32[1280]{0:T(1024)S(1)}, f32[1280]{0:T(1024)}, u32[]{:S(2)}) copy-start(f32[1280]{0:T(1024)} %copy-done.44) | copy-start | bytes 15364
  906.2 24.3 %copy-start.47 = (f32[1280]{0:T(1024)S(1)}, f32[1280]{0:T(1024)}, u32[]{:S(2)}) copy-start(f32[1280]{0:T(1024)} %copy-done.46) | copy-start | bytes 15364
  979.9 166.2 %reduce-scatter.8.cloned.1.call-start = ((), (), s32[]{:S(2)}) async-start(), calls=%async_computation.13 | async-start | bytes 10485760 | tf_op jit(solution)/shard_map/reduce_scatter | solution.py:203
  1017.1 256.2 %all-reduce.22.cloned.1.call-start = ((), (), s32[]{:S(2)}) async-start(), calls=%async_computation.17 | async-start | bytes 278528 | tf_op jit(solution)/shard_map/psum | solution.py:231
  1018.0 348.4 %reduce-scatter.6.cloned.1.call-start = ((), (), s32[]{:S(2)}) async-start(), calls=%async_computation.12 | async-start | bytes 10485760 | tf_op jit(solution)/shard_map/reduce_scatter | solution.py:195
  1035.3 14.2 %copy-start.62 = (f32[16]{0:T(128)S(1)}, f32[16]{0:T(128)}, u32[]{:S(2)}) copy-start(f32[16]{0:T(128)} %get-tuple-element.468) | copy-start | bytes 196
  1035.3 14.5 %copy-start.15 = (f32[2048,16]{1,0:T(8,128)S(1)}, f32[2048,16]{1,0:T(8,128)}, u32[]{:S(2)}) copy-start(f32[2048,16]{1,0:T(8,128)} %copy-done.14) | copy-start | bytes 393220
  1035.3 14.4 %copy-start.69 = (f32[16]{0:T(128)S(1)}, f32[16]{0:T(128)}, u32[]{:S(2)}) copy-start(f32[16]{0:T(128)} %copy-done.67) | copy-start | bytes 196
  1044.8 101.4 %copy-start.4 = (bf16[2,256,2048]{2,1,0:T(8,128)(2,1)S(1)}, bf16[2,256,2048]{2,1,0:T(8,128)(2,1)}, u32[]{:S(2)}) copy-start(bf16[2,256,2048]{2,1,0:T(8,128)(2,1)} %param.21) | copy-start | bytes 6291460
  1044.8 101.4 %copy-start.31 = (f32[2048]{0:T(1024)S(1)}, f32[2048]{0:T(1024)}, u32[]{:S(2)}) copy-start(f32[2048]{0:T(1024)} %copy-done.30) | copy-start | bytes 24580
  1044.8 101.4 %copy-start.53 = (f32[2,256]{1,0:T(2,128)S(1)}, f32[2,256]{1,0:T(2,128)}, u32[]{:S(2)}) copy-start(f32[2,256]{1,0:T(2,128)} %copy-done.52) | copy-start | bytes 6148
  1044.8 43.4 %all-to-all-start.1 = ((bf16[4,64,3456]{2,1,0:T(8,128)(2,1)}), bf16[4,64,3456]{2,1,0:T(8,128)(2,1)}, u32[]{:S(2)}, u32[]{:S(2)}) async-start(bf16[4,64,3456]{2,1,0:T(8,128)(2,1)} %bitcast.491), calls=%async_computation.6 | async-start | bytes 3538944 | tf_op jit(solution)/shard_map/all_to_all | solution.py:207
  1049.8 99.6 %copy-start.61 = (f32[1024]{0:T(1024)S(1)}, f32[1024]{0:T(1024)}, u32[]{:S(2)}) copy-start(f32[1024]{0:T(1024)} %get-tuple-element.940) | copy-start | bytes 12292
  1090.8 232.3 %copy-start.54 = (f32[6336]{0:T(1024)S(1)}, f32[6336]{0:T(1024)}, u32[]{:S(2)}) copy-start(f32[6336]{0:T(1024)} %param.34) | copy-start | bytes 76036
  1090.8 232.3 %copy-start.55 = (f32[6336]{0:T(1024)S(1)}, f32[6336]{0:T(1024)}, u32[]{:S(2)}) copy-start(f32[6336]{0:T(1024)} %param.35) | copy-start | bytes 76036
  1328.3 38.1 %copy-start.70 = (f32[2,256]{1,0:T(2,128)S(1)}, f32[2,256]{1,0:T(2,128)}, u32[]{:S(2)}) copy-start(f32[2,256]{1,0:T(2,128)} %get-tuple-element.963) | copy-start | bytes 6148
  1331.7 40.3 %copy-start.51 = (f32[5,136]{1,0:T(8,128)S(1)}, f32[5,136]{1,0:T(8,128)}, u32[]{:S(2)}) copy-start(f32[5,136]{1,0:T(8,128)} %param.27) | copy-start | bytes 8164
  1331.7 40.3 %copy-start.65 = (f32[5,136]{1,0:T(8,128)S(1)}, f32[5,136]{1,0:T(8,128)}, u32[]{:S(2)}) copy-start(f32[5,136]{1,0:T(8,128)} %param.28) | copy-start | bytes 8164
  1331.7 40.3 %copy-start.66 = (f32[5,136]{1,0:T(8,128)S(1)}, f32[5,136]{1,0:T(8,128)}, u32[]{:S(2)}) copy-start(f32[5,136]{1,0:T(8,128)} %param.29) | copy-start | bytes 8164
  (94 other events, 679.6 us)
Sparse Core Ops, SparseCore 0:
  50.1 60.5 all-gather.8
  113.1 86.1 all-gather.6
  201.6 47.1 all-gather.12
  250.4 86.3 all-gather.14
  338.8 47.1 all-gather.10
  439.6 46.8 reduce-scatter.13
  906.2 47.0 reduce-scatter.11
  980.1 61.8 reduce-scatter.9
  1045.1 101.0 reduce-scatter.7
  1153.1 120.2 all-reduce.21
  1276.7 89.6 reduce-scatter.5

commit v2 on v1

v2 whole, which is shorter than its diff:
```python
import functools

import jax
import jax.numpy as jnp
from jax import lax
from jax.experimental import pallas as pl
from jax.experimental.pallas import tpu as pltpu
from jax.sharding import PartitionSpec as P

D = 2048
HEADS = 64
HEADDIM = 64
STATE = 128
CONV = 4
BLOCK = 256
MICRO = 2
INNER = 4096
CH = 4352
NORM_EPS = 1e-05
LEARN_RATE = 0.004
BETA_ONE = 0.9
BETA_TWO = 0.95
FIX_ONE = 1.0 - 0.9**10
FIX_TWO = 1.0 - 0.95**10
ADAM_EPS = 1e-08
WEIGHT_DECAY = 0.1
CLIP_NORM = 1.0
BF = jnp.bfloat16
F32 = jnp.float32
ALL = ("dp", "seq")


def dot(a, b, dims, out=F32):
    return lax.dot_general(a, b, (dims, ((), ())), preferred_element_type=out)


NN = ((1,), (0,))
NT = ((1,), (1,))
TN = ((0,), (0,))
LANES = 128
PAIR = 2 * HEADDIM
VMEM = 56 * 1024 * 1024


def iota2(shape, dim):
    return lax.broadcasted_iota(jnp.int32, shape, dim)


def running_sum(values, reverse):
    row, col = iota2((BLOCK, BLOCK), 0), iota2((BLOCK, BLOCK), 1)
    ones = jnp.where(row <= col if reverse else row >= col, 1.0, 0.0).astype(BF)
    high = values.astype(BF)
    rest = values - high.astype(F32)
    mid = rest.astype(BF)
    low = (rest - mid.astype(F32)).astype(BF)
    return dot(ones, high, NN) + dot(ones, mid, NN) + dot(ones, low, NN)


def step_sizes(raw, bias, a_neg):
    lifted = raw + bias
    dt = jnp.maximum(lifted, 0.0) + jnp.log1p(jnp.exp(-jnp.abs(lifted)))
    cum = running_sum(dt * a_neg, False)
    return lifted, dt, cum


def pick(left, columns, first):
    return jnp.where(left, columns[:, first : first + 1], columns[:, first + 1 : first + 2])


def conv_chunk(window, conv_w, aux, lo, hi):
    out = conv_w[CONV : CONV + 1, lo:hi] + conv_w[CONV - 1 : CONV, lo:hi] * window[8 : 8 + BLOCK, lo:hi]
    for tap in range(CONV - 1):
        out += conv_w[tap : tap + 1, lo:hi] * (window[5 + tap : 5 + tap + BLOCK, lo:hi] * aux[:, tap : tap + 1])
    return out


def forward_kernel(place, proj, conv_w, rows, aux, seg_row, y_out, s_out, window, act, state, *, hl):
    width = hl * HEADDIM
    conv_width = width + 2 * STATE
    step = pl.program_id(1)

    @pl.when(step == 0)
    def _():
        window[0:8, :] = jnp.zeros((8, conv_width), F32)
        state[...] = jnp.zeros(state.shape, F32)

    aux_v = aux[...]
    for lo in range(0, conv_width, LANES):
        hi = lo + LANES
        window[8 : 8 + BLOCK, lo:hi] = proj[:, lo:hi].astype(F32)
        out = conv_chunk(window, conv_w, aux_v, lo, hi)
        act[:, lo:hi] = (out * jax.nn.sigmoid(out)).astype(BF)
    window[0:8, :] = window[BLOCK : BLOCK + 8, :]

    _, dt, cum = step_sizes(proj[:, conv_width : conv_width + LANES].astype(F32), rows[0:1, :LANES], rows[1:2, :LANES])
    entry = jnp.exp(cum) * aux_v[:, 3:4]
    dt_end = dt * jnp.exp(cum[BLOCK - 1 : BLOCK, :] - cum) * aux_v[:, 4:5]
    cum_t, dt_t = cum.T, dt.T
    bm, cm = act[:, width : width + STATE], act[:, width + STATE :]
    same = (aux_v[:, 8:9] == seg_row[0:1, :]) & (iota2((BLOCK, BLOCK), 0) >= iota2((BLOCK, BLOCK), 1))
    inner = jnp.where(same, dot(cm, bm, NT), 0.0)
    left = iota2((BLOCK, PAIR), 1) < HEADDIM
    top = iota2((PAIR, STATE), 0) < HEADDIM
    for pair in range(hl // 2):
        first = 2 * pair
        lo, hi = pair * PAIR, (pair + 1) * PAIR
        xp = act[:, lo:hi]
        halves = []
        for h in (first, first + 1):
            decay = jnp.exp(jnp.minimum(cum[:, h : h + 1] - cum_t[h : h + 1, :], 0.0))
            mix = (inner * (decay * dt_t[h : h + 1, :])).astype(BF)
            halves.append(dot(mix, xp, NN))
        entering = state[lo:hi, :]
        low = entering.astype(BF)
        s_out[0, lo:hi, :] = low
        xf = xp.astype(F32)
        y = jnp.where(left, halves[0], halves[1]) + pick(left, entry, first) * dot(cm, low, NT) + rows[2:3, lo:hi] * xf
        y_out[:, lo:hi] = y.astype(BF)
        weighted = (xf * pick(left, dt_end, first)).astype(BF)
        last = entry[BLOCK - 1 : BLOCK, :]
        keep = jnp.where(top, last[:, first : first + 1], last[:, first + 1 : first + 2])
        state[lo:hi, :] = keep * entering + dot(weighted, bm, TN)


def backward_kernel(place, proj, before, conv_w, rows, aux, seg_row, dy, s_in, dproj, dconv, dvec,
                    window, act, dwin, grad_s, dcb, colsum, *, hl):
    width = hl * HEADDIM
    conv_width = width + 2 * STATE
    step = pl.program_id(1)

    @pl.when((step == 0) & (pl.program_id(0) == 0))
    def _():
        dconv[...] = jnp.zeros(dconv.shape, F32)
        dvec[...] = jnp.zeros(dvec.shape, F32)

    @pl.when(step == 0)
    def _():
        dwin[BLOCK : BLOCK + 8, :] = jnp.zeros((8, conv_width), F32)
        grad_s[...] = jnp.zeros(grad_s.shape, F32)
        colsum[...] = jnp.zeros(colsum.shape, F32)

    aux_v = aux[...]
    window[0:8, :] = before[8:16, :conv_width].astype(F32)
    for lo in range(0, conv_width, LANES):
        hi = lo + LANES
        window[8 : 8 + BLOCK, lo:hi] = proj[:, lo:hi].astype(F32)
        out = conv_chunk(window, conv_w, aux_v, lo, hi)
        sig = jax.nn.sigmoid(out)
        act[:, lo:hi] = (out * sig).astype(BF)
        dwin[0:BLOCK, lo:hi] = sig * (1.0 + out * (1.0 - sig))

    lifted, dt, cum = step_sizes(proj[:, conv_width : conv_width + LANES].astype(F32), rows[0:1, :LANES], rows[1:2, :LANES])
    a_neg = rows[1:2, :LANES]
    entry = jnp.exp(cum) * aux_v[:, 3:4]
    end = jnp.exp(cum[BLOCK - 1 : BLOCK, :] - cum) * aux_v[:, 4:5]
    dt_end = dt * end
    cum_t = cum.T
    bm, cm = act[:, width : width + STATE], act[:, width + STATE :]
    same = (aux_v[:, 8:9] == seg_row[0:1, :]) & (iota2((BLOCK, BLOCK), 0) <= iota2((BLOCK, BLOCK), 1))
    inner = jnp.where(same, dot(bm, cm, NT), 0.0)
    left = iota2((BLOCK, PAIR), 1) < HEADDIM
    top = iota2((PAIR, STATE), 0) < HEADDIM
    lane = iota2((BLOCK, LANES), 1)
    lane_one = iota2((1, LANES), 1)
    last = entry[BLOCK - 1 : BLOCK, :]
    d_dt = jnp.zeros((BLOCK, LANES), F32)
    d_cum = jnp.zeros((BLOCK, LANES), F32)
    d_last = jnp.zeros((1, LANES), F32)
    d_skip = jnp.zeros((1, LANES), F32)
    d_b = jnp.zeros((BLOCK, STATE), F32)
    d_c = jnp.zeros((BLOCK, STATE), F32)

    def through_silu(grad, lo, hi):
        dwin[0:BLOCK, lo:hi] = dwin[0:BLOCK, lo:hi] * grad.astype(BF).astype(F32)

    for pair in range(hl // 2):
        first = 2 * pair
        lo, hi = pair * PAIR, (pair + 1) * PAIR
        xp, dyp = act[:, lo:hi], dy[:, lo:hi]
        xf, dyf = xp.astype(F32), dyp.astype(F32)
        zero = jnp.zeros_like(xp)
        halves = []
        for h in (first, first + 1):
            mine = left if h == first else ~left
            decay = jnp.exp(jnp.minimum(cum_t[h : h + 1, :] - cum[:, h : h + 1], 0.0))
            d_mix = dot(jnp.where(mine, xp, zero), dyp, NT).astype(BF).astype(F32)
            dt_col = dt[:, h : h + 1]
            part = d_mix * decay
            scaled = inner * decay
            mix = (scaled * dt_col).astype(BF)
            weighted_part = part * dt_col
            if h == 0:
                dcb[...] = weighted_part
            else:
                dcb[...] += weighted_part
            pairwise = part * inner
            row_sum = jnp.sum(pairwise, axis=1, keepdims=True)
            d_dt += jnp.where(lane == h, row_sum, 0.0)
            colsum[h : h + 1, :] = jnp.sum(pairwise * dt_col, axis=0, keepdims=True)
            halves.append(dot(mix, dyp, NN))
        later = grad_s[lo:hi, :]
        later_b = later.astype(BF)
        low = s_in[0, lo:hi, :]
        entry_p = pick(left, entry, first)
        d_w = dot(bm, later_b, NT).astype(BF).astype(F32)
        skip_row = rows[2:3, lo:hi]
        dx = jnp.where(left, halves[0], halves[1]) + d_w * pick(left, dt_end, first) + skip_row * dyf
        through_silu(dx, lo, hi)
        used = d_w * xf
        into = dyf * dot(cm, low, NT)
        for h in (first, first + 1):
            mine = left if h == first else ~left
            u = jnp.sum(jnp.where(mine, used, 0.0), axis=1, keepdims=True) * end[:, h : h + 1]
            d_dt += jnp.where(lane == h, u, 0.0)
            d_last += jnp.where(lane_one == h, jnp.sum(u * dt[:, h : h + 1], axis=0, keepdims=True), 0.0)
            d_e = jnp.sum(jnp.where(mine, into, 0.0), axis=1, keepdims=True) * entry[:, h : h + 1]
            d_cum += jnp.where(lane == h, d_e, 0.0)
            rows_mine = top if h == first else ~top
            d_a = jnp.sum(jnp.where(rows_mine, later * low.astype(F32), 0.0), axis=0, keepdims=True)
            d_a = jnp.sum(d_a, axis=1, keepdims=True) * last[:, h : h + 1]
            d_last += jnp.where(lane_one == h, d_a, 0.0)
            ds = jnp.sum(jnp.where(mine, xf * dyf, 0.0), axis=0, keepdims=True)
            d_skip += jnp.where(lane_one == h, jnp.sum(ds, axis=1, keepdims=True), 0.0)
        weighted = (xf * pick(left, dt_end, first)).astype(BF)
        d_b += dot(weighted, later_b, NN)
        entering = (entry_p * dyf).astype(BF)
        d_c += dot(entering, low, NN)
        keep = jnp.where(top, last[:, first : first + 1], last[:, first + 1 : first + 2])
        grad_s[lo:hi, :] = dot(entering, cm, TN) + keep * later

    d_inner = jnp.where(same, dcb[...], 0.0).astype(BF)
    d_b += dot(d_inner, cm, NN)
    d_c += dot(d_inner, bm, TN)
    through_silu(d_b, width, width + STATE)
    through_silu(d_c, width + STATE, conv_width)

    d_cum += colsum[...].T - d_dt * dt
    d_cum += jnp.where(iota2((BLOCK, LANES), 0) == BLOCK - 1, d_last, 0.0)
    d_a = running_sum(d_cum, True)
    d_raw = (d_dt + d_a * a_neg) * jax.nn.sigmoid(lifted)
    d_raw = jnp.where(lane < hl, d_raw, 0.0)
    dproj[:, conv_width : conv_width + LANES] = d_raw.astype(BF)
    dvec[0:1, :] += jnp.sum(d_a * dt, axis=0, keepdims=True) * a_neg
    dvec[1:2, :] += d_skip
    dvec[2:3, :] += jnp.sum(d_raw, axis=0, keepdims=True)

    for lo in range(0, conv_width, LANES):
        hi = lo + LANES
        grad = conv_w[CONV - 1 : CONV, lo:hi] * dwin[0:BLOCK, lo:hi]
        for tap in range(CONV - 1):
            ahead = CONV - 1 - tap
            grad += conv_w[tap : tap + 1, lo:hi] * (dwin[ahead : ahead + BLOCK, lo:hi] * aux_v[:, 5 + tap : 6 + tap])
        dproj[:, lo:hi] = grad.astype(BF)
        own = dwin[0:BLOCK, lo:hi]
        fold = lambda a: jnp.sum(a.reshape(BLOCK // 8, 8, LANES), axis=0)
        dconv[CONV * 8 : CONV * 8 + 8, lo:hi] += fold(own)
        dconv[(CONV - 1) * 8 : CONV * 8, lo:hi] += fold(own * window[8 : 8 + BLOCK, lo:hi])
        for tap in range(CONV - 1):
            moved = window[5 + tap : 5 + tap + BLOCK, lo:hi] * aux_v[:, tap : tap + 1]
            dconv[tap * 8 : tap * 8 + 8, lo:hi] += fold(own * moved)
    dwin[BLOCK : BLOCK + 8, :] = dwin[0:8, :]


def segment_aux(segments):
    micro, length = segments.shape
    nb = length // BLOCK
    seg = segments.astype(F32)
    blocks = seg.reshape(micro, nb, BLOCK)
    prev = jnp.concatenate([jnp.full((micro, 1), -1.0, F32), blocks[:, :-1, -1]], axis=1)
    entry = (blocks == prev[:, :, None]).reshape(micro, length)
    end = (blocks == blocks[:, :, -1:]).reshape(micro, length)
    cols = []
    for tap in range(CONV - 1):
        back = CONV - 1 - tap
        cols.append(jnp.pad(seg, ((0, 0), (back, 0)), constant_values=-1.0)[:, :length] == seg)
    cols += [entry, end]
    for tap in range(CONV - 1):
        ahead = CONV - 1 - tap
        cols.append(jnp.pad(seg, ((0, 0), (0, ahead)), constant_values=-1.0)[:, ahead:] == seg)
    cols.append(seg)
    cols = [c.astype(F32) for c in cols] + [jnp.zeros_like(seg)] * 7
    aux = jnp.stack(cols, axis=-1).reshape(micro * length, 16)
    seg_row = jnp.broadcast_to(blocks.reshape(micro * nb, 1, BLOCK), (micro * nb, 8, BLOCK)).reshape(micro * nb * 8, BLOCK)
    return aux, seg_row


def scan_forward(place, proj, conv_w, rows, aux, seg_row, hl):
    tokens = proj.shape[0]
    nb = tokens // MICRO // BLOCK
    width = hl * HEADDIM
    conv_width = width + 2 * STATE
    held = lambda m, j, place: (m * nb + (j ^ place[0]), 0)
    at = lambda m, j, place: (m * nb + j, 0)
    whole = lambda m, j, place: (0, 0)
    grid_spec = pltpu.PrefetchScalarGridSpec(
        num_scalar_prefetch=1,
        grid=(MICRO, nb),
        in_specs=[
            pl.BlockSpec((BLOCK, conv_width + LANES), held),
            pl.BlockSpec((8, conv_width), whole),
            pl.BlockSpec(rows.shape, whole),
            pl.BlockSpec((BLOCK, 16), at),
            pl.BlockSpec((8, BLOCK), at),
        ],
        out_specs=[
            pl.BlockSpec((BLOCK, width), held),
            pl.BlockSpec((1, width, STATE), lambda m, j, place: (m * nb + j, 0, 0)),
        ],
        scratch_shapes=[
            pltpu.VMEM((BLOCK + 8, conv_width), F32),
            pltpu.VMEM((BLOCK, conv_width), BF),
            pltpu.VMEM((width, STATE), F32),
        ],
    )
    return pl.pallas_call(
        functools.partial(forward_kernel, hl=hl),
        grid_spec=grid_spec,
        out_shape=[
            jax.ShapeDtypeStruct((tokens, width), BF),
            jax.ShapeDtypeStruct((MICRO * nb, width, STATE), BF),
        ],
        compiler_params=pltpu.CompilerParams(vmem_limit_bytes=VMEM, dimension_semantics=("arbitrary", "arbitrary")),
        name="scan_forward",
    )(place, proj, conv_w, rows, aux, seg_row)


def scan_backward(place, proj, conv_w, rows, aux, seg_row, dy, states, hl):
    tokens = proj.shape[0]
    nb = tokens // MICRO // BLOCK
    width = hl * HEADDIM
    conv_width = width + 2 * STATE
    full = conv_width + LANES
    held = lambda m, j, place: (m * nb + ((nb - 1 - j) ^ place[0]), 0)
    ahead_of = lambda m, j, place: ((m * nb + (jnp.maximum(nb - 2 - j, 0) ^ place[0])) * (BLOCK // 16) + BLOCK // 16 - 1, 0)
    at = lambda m, j, place: (m * nb + nb - 1 - j, 0)
    whole = lambda m, j, place: (0, 0)
    grid_spec = pltpu.PrefetchScalarGridSpec(
        num_scalar_prefetch=1,
        grid=(MICRO, nb),
        in_specs=[
            pl.BlockSpec((BLOCK, full), held),
            pl.BlockSpec((16, full), ahead_of),
            pl.BlockSpec((8, conv_width), whole),
            pl.BlockSpec(rows.shape, whole),
            pl.BlockSpec((BLOCK, 16), at),
            pl.BlockSpec((8, BLOCK), at),
            pl.BlockSpec((BLOCK, width), held),
            pl.BlockSpec((1, width, STATE), lambda m, j, place: (m * nb + nb - 1 - j, 0, 0)),
        ],
        out_specs=[
            pl.BlockSpec((BLOCK, full), held),
            pl.BlockSpec((8 * (CONV + 1), conv_width), whole),
            pl.BlockSpec((8, LANES), whole),
        ],
        scratch_shapes=[
            pltpu.VMEM((BLOCK + 8, conv_width), F32),
            pltpu.VMEM((BLOCK, conv_width), BF),
            pltpu.VMEM((BLOCK + 8, conv_width), F32),
            pltpu.VMEM((width, STATE), F32),
            pltpu.VMEM((BLOCK, BLOCK), F32),
            pltpu.VMEM((LANES, BLOCK), F32),
        ],
    )
    return pl.pallas_call(
        functools.partial(backward_kernel, hl=hl),
        grid_spec=grid_spec,
        out_shape=[
            jax.ShapeDtypeStruct((tokens, full), BF),
            jax.ShapeDtypeStruct((8 * (CONV + 1), conv_width), F32),
            jax.ShapeDtypeStruct((8, LANES), F32),
        ],
        compiler_params=pltpu.CompilerParams(vmem_limit_bytes=VMEM, dimension_semantics=("arbitrary", "arbitrary")),
        name="scan_backward",
    )(place, proj, proj, conv_w, rows, aux, seg_row, dy, states)


def scan_rows(a_log, skip, dt_bias, hl):
    width = max(hl * HEADDIM, LANES)
    pad = lambda v: jnp.pad(v, (0, width - v.shape[0]))
    return jnp.pad(jnp.stack([pad(dt_bias), pad(-jnp.exp(a_log)), pad(jnp.repeat(skip, HEADDIM))]), ((0, 5), (0, 0)))


def swapped(value, axis, mask):
    return lax.ppermute(value, axis, [(i, i ^ mask) for i in range(lax.axis_size(axis))])


def axis_bits(axis):
    return [1 << i for i in range(lax.axis_size(axis).bit_length() - 1)]


def micro_order(micro, axis):
    bits = axis_bits(axis)
    return bits if micro % 2 == 0 else bits[::-1]


def gather_pieces(own):
    out = []
    for micro in range(MICRO):
        pieces = {0: own[micro]}
        for bit in micro_order(micro, "seq"):
            for at in list(pieces):
                pieces[at ^ bit] = swapped(pieces[at], "seq", bit)
        out += [pieces[at] for at in range(len(pieces))]
    return jnp.concatenate(out, axis=0)


def scatter_pieces(parts):
    out = []
    for micro in range(MICRO):
        pieces = {at: parts[micro, at] for at in range(parts.shape[1])}
        for bit in micro_order(micro, "seq"):
            pieces = {
                at: (pieces[at].astype(F32) + swapped(pieces[at | bit], "seq", bit).astype(F32)).astype(BF)
                for at in pieces
                if not at & bit
            }
        out.append(pieces[0])
    return jnp.stack(out)


def exchange(table, rank):
    n = table.shape[0]
    out = jnp.zeros_like(table)
    for mask in range(n):
        entry = lax.dynamic_index_in_dim(table, rank ^ mask, 0, True)
        if mask:
            entry = swapped(entry, "seq", mask)
        out = lax.dynamic_update_slice_in_dim(out, entry, rank ^ mask, 0)
    return out


def sum_all(value):
    for axis in ("dp", "seq"):
        for bit in axis_bits(axis):
            value = value + swapped(value, axis, bit)
    return value


def sum_pieces(value):
    n = value.shape[-2]
    total = value
    for mask in range(1, n):
        got = swapped(value, "seq", mask)
        total = total + jnp.concatenate([got[..., at ^ mask : (at ^ mask) + 1, :] for at in range(n)], axis=-2)
    return total


def adamw(master, gradient, first, second, clip, decay):
    clipped = gradient * clip
    first_new = BETA_ONE * first + (1.0 - BETA_ONE) * clipped
    second_new = BETA_TWO * second + (1.0 - BETA_TWO) * clipped * clipped
    update = first_new / FIX_ONE / (jnp.sqrt(second_new / FIX_TWO) + ADAM_EPS) + decay * master
    return (-LEARN_RATE * update, first_new, second_new)


def per_device(tokens, cotangent, segments, in_weight, in_m, in_v, conv_weight, conv_m, conv_v,
               out_weight, out_m, out_v, packed, packed_m, packed_v):
    n = lax.axis_size("seq")
    rank = lax.axis_index("seq")
    place = rank.astype(jnp.int32).reshape(1)
    ndev = n * lax.axis_size("dp")
    hl = HEADS // n
    xw = hl * HEADDIM
    rows = D // ndev
    piece = tokens.shape[1]
    count = MICRO * n * piece
    xs = INNER + INNER
    bc = 2 * STATE
    xc = xw + bc + LANES
    cw = conv_weight.shape[1]
    conv_cols = -(-(CONV + 1) * cw // rows)

    in_low = in_weight.astype(BF)
    out_low = out_weight.astype(BF).T
    conv_flat = conv_weight.astype(BF).reshape(-1)
    conv_flat = jnp.pad(conv_flat, (0, conv_cols * rows - conv_flat.shape[0])).reshape(rows, conv_cols)
    by_rank = lambda a: a.reshape(rows, n, -1).transpose(1, 0, 2)
    to_all = lambda a: jnp.broadcast_to(a[None], (n,) + a.shape)
    steps = jnp.concatenate([by_rank(in_low[:, xs + bc :]), to_all(conv_flat), jnp.zeros((n, rows, LANES - hl - conv_cols), BF)], axis=2)
    send_x = jnp.concatenate([by_rank(in_low[:, INNER:xs]), to_all(in_low[:, xs : xs + bc]), steps], axis=2)
    send_z = by_rank(in_low[:, :INNER])
    send_o = by_rank(out_low)
    w_x = lax.all_gather(exchange(send_x, rank).reshape(n * rows, -1), "dp", axis=0, tiled=True)
    w_z = lax.all_gather(exchange(send_z, rank).reshape(n * rows, -1), "dp", axis=0, tiled=True)
    w_o = lax.all_gather(exchange(send_o, rank).reshape(n * rows, -1), "dp", axis=0, tiled=True)
    conv_full = w_x[:, xw + bc + hl : xw + bc + hl + conv_cols].reshape(ndev, rows * conv_cols)[:, : (CONV + 1) * cw]
    conv_full = conv_full.reshape(ndev, CONV + 1, cw).transpose(1, 0, 2).reshape(CONV + 1, CH)
    conv_loc = jnp.concatenate([lax.dynamic_slice_in_dim(conv_full, rank * xw, xw, 1), conv_full[:, INNER:]], axis=1).astype(F32)
    conv_loc = jnp.pad(conv_loc, ((0, 8 - CONV - 1), (0, 0)))

    a_log = lax.dynamic_slice_in_dim(packed, rank * hl, hl)
    skip = lax.dynamic_slice_in_dim(packed, HEADS + rank * hl, hl)
    dt_bias = lax.dynamic_slice_in_dim(packed, 2 * HEADS + rank * hl, hl)
    gain_in = packed[3 * HEADS : 3 * HEADS + D]
    gain_out = lax.dynamic_slice_in_dim(packed, 3 * HEADS + D + rank * xw, xw)
    aux, seg_row = segment_aux(segments)
    scan_row = scan_rows(a_log, skip, dt_bias, hl)

    tok = tokens.astype(F32)
    r_in = lax.rsqrt(jnp.mean(tok * tok, axis=-1, keepdims=True) + NORM_EPS)
    hidden = gather_pieces((tok * r_in * gain_in).astype(BF))
    cot = gather_pieces(cotangent)

    proj_x = dot(hidden, w_x, NN).astype(BF)
    y, states = scan_forward(place, proj_x, conv_loc, scan_row, aux, seg_row, hl)
    z = dot(hidden, w_z, NN).astype(BF).astype(F32)
    y = y.astype(F32)
    sig = jax.nn.sigmoid(z)
    gz = y * z * sig
    dnr = dot(cot, w_o, NN)
    dng = dnr * gain_out
    sums = jnp.stack([jnp.sum(gz * gz, axis=1), jnp.sum(dng * gz, axis=1)])
    sums = sum_pieces(sums.reshape(2, MICRO, n, piece)).reshape(2, count)
    r = lax.rsqrt(sums[0] / INNER + NORM_EPS)
    normed = (gz * r[:, None] * gain_out).astype(BF)
    d_gz = r[:, None] * dng - gz * (r * r * r * sums[1] / INNER)[:, None]
    d_gain_out = jnp.sum(dnr * gz * r[:, None], axis=0)
    dy = (d_gz * z * sig).astype(BF)
    dz = (d_gz * y * (sig * (1.0 + z * (1.0 - sig)))).astype(BF)

    scatter = lambda a: lax.psum_scatter(a, "dp", scatter_dimension=0, tiled=True).reshape(n, rows, -1)
    out_part = dot(normed, w_o, NT).astype(BF).reshape(MICRO, n, piece, D)
    output = (tok + scatter_pieces(out_part).astype(F32)).astype(BF)
    got_o = exchange(scatter(dot(cot, normed, TN).astype(BF)), rank)
    got_z = exchange(scatter(dot(hidden, dz, TN).astype(BF)), rank)

    d_px, d_conv, d_vec = scan_backward(place, proj_x, conv_loc, scan_row, aux, seg_row, dy, states, hl)
    d_hid = (dot(dz, w_z, NT) + dot(d_px, w_x, NT)).astype(BF).reshape(MICRO, n, piece, D)
    d_hidden = scatter_pieces(d_hid).astype(F32)
    got_x = exchange(scatter(dot(hidden, d_px, TN).astype(BF)), rank)

    flat = lambda a: a.transpose(1, 0, 2).reshape(rows, -1)
    g_bc = jnp.sum(got_x[:, :, xw : xw + bc].astype(F32), axis=0)
    shard_in = jnp.concatenate(
        [flat(got_z).astype(F32), flat(got_x[:, :, :xw]).astype(F32), g_bc, flat(got_x[:, :, xw + bc : xw + bc + hl]).astype(F32)], axis=1
    )
    shard_out = flat(got_o).astype(F32).T

    dh = d_hidden * gain_in
    d_tok = r_in * (dh - tok * (r_in * r_in) * jnp.mean(dh * tok, axis=-1, keepdims=True))
    input_grad = (cotangent.astype(F32) + d_tok).astype(BF)

    d_conv = d_conv.reshape(CONV + 1, 8, -1).sum(axis=1)
    conv_part = lax.dynamic_update_slice(jnp.zeros((CONV + 1, CH), F32), d_conv[:, :xw], (0, rank * xw))
    conv_part = lax.dynamic_update_slice(conv_part, d_conv[:, xw:], (0, INNER))
    vec_part = jnp.zeros((3 * HEADS + INNER,), F32)
    for at in range(3):
        vec_part = lax.dynamic_update_slice(vec_part, d_vec[at, :hl], (at * HEADS + rank * hl,))
    vec_part = lax.dynamic_update_slice(vec_part, d_gain_out, (3 * HEADS + rank * xw,))
    small = jnp.concatenate([conv_part.reshape(-1), vec_part])
    small = jnp.pad(small, (0, -small.shape[0] % 1024)).reshape(-1, LANES)
    small = sum_all(small).reshape(-1)
    conv_tot = small[: (CONV + 1) * CH].reshape(CONV + 1, CH)
    vec_tot = small[(CONV + 1) * CH : (CONV + 1) * CH + 3 * HEADS + INNER]

    own = lax.axis_index("dp") * n + rank
    own_gain = lax.dynamic_slice_in_dim(gain_in, own * rows, rows)
    d_gain_in = jnp.sum(in_low.astype(F32) * shard_in, axis=1) / own_gain
    partial_sq = jnp.sum(shard_in * shard_in) + jnp.sum(shard_out * shard_out)
    last = lax.dynamic_update_slice(jnp.zeros((D + 1024,), F32), d_gain_in, (own * rows,))
    last = lax.dynamic_update_slice(last, partial_sq[None], (D,))
    last = sum_all(last.reshape(-1, LANES)).reshape(-1)
    vec_tot = jnp.concatenate([vec_tot[: 3 * HEADS], last[:D], vec_tot[3 * HEADS :]])
    shard_conv = lax.dynamic_slice_in_dim(conv_tot, own * cw, cw, 1)
    grad_norm = jnp.sqrt(last[D] + jnp.sum(conv_tot * conv_tot) + jnp.sum(vec_tot * vec_tot))
    clip = jnp.minimum(1.0, CLIP_NORM / (grad_norm + 1e-06))
    in_new = adamw(in_weight, shard_in, in_m, in_v, clip, WEIGHT_DECAY)
    conv_new = adamw(conv_weight, shard_conv, conv_m, conv_v, clip, WEIGHT_DECAY)
    out_new = adamw(out_weight, shard_out, out_m, out_v, clip, WEIGHT_DECAY)
    vec_new = adamw(packed, vec_tot, packed_m, packed_v, clip, 0.0)
    return (
        output, input_grad, grad_norm,
        in_weight + in_new[0], in_new[1], in_new[2],
        conv_new[0], conv_new[1], conv_new[2],
        out_weight + out_new[0], out_new[1], out_new[2],
        vec_new[0], vec_new[1], vec_new[2],
    )


def solution(mesh):
    tok, col, row = P(None, ALL, None), P(None, ALL), P(ALL, None)
    return jax.shard_map(
        per_device,
        mesh=mesh,
        in_specs=(tok, tok, P(None, "dp"), row, row, row, col, col, col, col, col, col, P(), P(), P()),
        out_specs=(tok, tok, P(), row, row, row, col, col, col, col, col, col, P(), P(), P()),
        check_vma=False,
    )
```

time: 1400 us -> 789 us (0.56)
  local copies, waits for them, and re-layouts: 285 us -> 77.5 us
  other arithmetic: 265 us -> 61.2 us
  matrix products: 320 us -> 159 us
  blocking collectives: 155 us -> 0 us
  Pallas kernels: 0 us -> 136 us
  waiting for transfers between devices: 330 us -> 259 us
  starting transfers between devices: 5.15 us -> 67.9 us
    ppermute x0 -> x55, waiting for transfers between devices: none -> 259 us  [swapped(): lax.ppermute(value, axis, [(i, i ^ mask) for i in range(lax.axis_size(axi...]
    dot_general x56 -> x0, matrix products: 164 us -> none  [the longest x12 74.1 us: block_parts(): y_intra = jnp.einsum('hts,shp->thp', mix, xh)]
    pallas_call x0 -> x2, Pallas kernels: none -> 136 us  [the longest x1 101 us: scan_backward(): pl.pallas_call(functools.partial(backward_kernel, hl=hl), grid_spec=grid_...]
    psum x1 -> x0, waiting for transfers between devices: 124 us -> none  [per_device(): lax.psum((partial_sq, conv_part, vec_part), ALL)]
    reduce_scatter x5 -> x3, waiting for transfers between devices: 91 us -> 0.01 us  [per_device(): lax.psum_scatter(a, 'dp', scatter_dimension=0, tiled=True)]
    all_gather x5 -> x3, waiting for transfers between devices: 81.2 us -> 0.01 us  [the longest x1 0.01 us: per_device(): lax.all_gather(exchange(send_z, rank).reshape(n * rows, -1), 'dp', axis=0...]
    all_gather x1 -> x0, blocking collectives: 68.1 us -> none  [per_device(): conv_full = lax.all_gather(conv_weight.astype(BF), ALL, axis=1, tiled=True)]
    ppermute x0 -> x55, starting transfers between devices: none -> 67.7 us  [swapped(): lax.ppermute(value, axis, [(i, i ^ mask) for i in range(lax.axis_size(axi...]
  transfers between devices with their start and end apart: 12 -> 61, of which waited for: 7 -> 29; matrix products, arithmetic and copies ran while one was open for 58% -> 29% of each run, Pallas kernels for 0% -> 17%
where the time goes in v2:
time: 789 us; the launch traced here: 781 us
  waiting for transfers between devices  259 us (33%)
  matrix products  159 us (20%)
  Pallas kernels  136 us (17%)
  local copies, waits for them, and re-layouts  77.5 us (10%)
  starting transfers between devices  67.9 us (9%)
  other arithmetic  61.2 us (8%)
  between operations  20.2 us (3%)
    ppermute x55, waiting for transfers between devices, swapped(): lax.ppermute(value, axis, [(i, i ^ mask) for i in range(lax.axis_size(axi...  259 us
    dot_general x9, matrix products, dot(): return lax.dot_general(a, b, (dims, ((), ())), preferred_element_type=out)  159 us
    pallas_call x1, Pallas kernels, scan_backward(): pl.pallas_call(functools.partial(backward_kernel, hl=hl), grid_spec=grid_...  101 us
    ppermute x55, starting transfers between devices, swapped(): lax.ppermute(value, axis, [(i, i ^ mask) for i in range(lax.axis_size(axi...  67.7 us
    pallas_call x1, Pallas kernels, scan_forward(): pl.pallas_call(functools.partial(forward_kernel, hl=hl), grid_spec=grid_s...  34.5 us
    unnamed x124, local copies, waits for them, and re-layouts  34.3 us
  transfers between devices with their start and end apart: 61, of which 29 were waited for; matrix products, arithmetic and copies ran while one was open for 29% of the time, Pallas kernels for 17%

profile of v2, /device:TPU:0, one launch (start us, length us, event | category | flops | bytes accessed | tf_op | source)
XLA Modules:
  0.0 780.7 jit_solution(9023059725587061784)
XLA Ops:
  11.4 3.0 collective-permute-start.9
  19.0 3.3 collective-permute-done.10
  29.7 2.5 collective-permute-start.8
  32.7 2.6 collective-permute-done.6
  35.4 4.3 collective-permute-done.7
  64.3 11.3 %collective-permute-done.18 = bf16[1,64,1024]{2,1,0:T(8,128)(2,1)S(1)} collective-permute-done((bf16[1,64,1024]{2,1,0:T(8,128)(2,1)S(1)}, bf16[1,64,1024]{2,1,0:T(8,128)(2,1)S(1)}, u32[]{:S(2)}, u32[]{:S(2)}) %collective-permute-start.18) | collective-permute-done | bytes 131104 | tf_op jit(solution)/shard_map/ppermute | solution.py:384
  79.6 16.9 %collective-permute-done.20 = bf16[1,64,1024]{2,1,0:T(8,128)(2,1)S(1)} collective-permute-done((bf16[1,64,1024]{2,1,0:T(8,128)(2,1)S(1)}, bf16[1,64,1024]{2,1,0:T(8,128)(2,1)S(1)}, u32[]{:S(2)}, u32[]{:S(2)}) %collective-permute-start.20) | collective-permute-done | bytes 131104 | tf_op jit(solution)/shard_map/ppermute | solution.py:384
  100.8 2.5 constant_dynamic-update-slice_fusion.6
  103.3 2.5 constant_dynamic-update-slice_fusion.14
  112.5 10.4 %collective-permute-done.4 = bf16[256,2048]{1,0:T(8,128)(2,1)} collective-permute-done((bf16[256,2048]{1,0:T(8,128)(2,1)}, bf16[256,2048]{1,0:T(8,128)(2,1)}, u32[]{:S(2)}, u32[]{:S(2)}) %collective-permute-start.4) | collective-permute-done | bytes 1048608 | tf_op jit(solution)/shard_map/ppermute | solution.py:384
  124.3 21.1 %collective-permute-done.16 = bf16[256,2048]{1,0:T(8,128)(2,1)} collective-permute-done((bf16[256,2048]{1,0:T(8,128)(2,1)}, bf16[256,2048]{1,0:T(8,128)(2,1)}, u32[]{:S(2)}, u32[]{:S(2)}) %collective-permute-start.16) | collective-permute-done | bytes 1048608 | tf_op jit(solution)/shard_map/ppermute | solution.py:384
  146.7 21.1 %collective-permute-done.2 = bf16[256,2048]{1,0:T(8,128)(2,1)} collective-permute-done((bf16[256,2048]{1,0:T(8,128)(2,1)}, bf16[256,2048]{1,0:T(8,128)(2,1)}, u32[]{:S(2)}, u32[]{:S(2)}) %collective-permute-start.2) | collective-permute-done | bytes 1048608 | tf_op jit(solution)/shard_map/ppermute | solution.py:384
  172.6 13.1 %collective-permute-done.14 = bf16[256,2048]{1,0:T(8,128)(2,1)S(1)} collective-permute-done((bf16[256,2048]{1,0:T(8,128)(2,1)}, bf16[256,2048]{1,0:T(8,128)(2,1)S(1)}, u32[]{:S(2)}, u32[]{:S(2)}) %collective-permute-start.14) | collective-permute-done | bytes 1048608 | tf_op jit(solution)/shard_map/ppermute | solution.py:384
  196.8 14.0 %convolution_convert_fusion.3 = bf16[2048,1024]{1,0:T(8,128)(2,1)} fusion(bf16[2048,2048]{1,0:T(8,128)(2,1)} %constant_dynamic-update-slice_fusion, bf16[2048,1024]{1,0:T(8,128)(2,1)} %all-gather.6.cloned.1.call-done), kind=kOutput, calls=%fused_computation.40 | convolution fusion | flops 8592031744 | bytes 16777216 | tf_op jit(solution)/shard_map/dot_general | solution.py:34
  213.8 18.4 %convolution_convert_fusion.1.proj.before = bf16[2048,1408]{1,0:T(8,128)(2,1)} fusion(bf16[2048,2048]{1,0:T(8,128)(2,1)} %constant_dynamic-update-slice_fusion, bf16[2048,1408]{1,0:T(8,128)(2,1)} %all-gather.4.cloned.1.call-done), kind=kOutput, calls=%fused_computation.27 | convolution fusion | flops 11814043648 | bytes 19922944 | tf_op jit(solution)/shard_map/dot_general | solution.py:34
  232.1 34.5 %scan_forward.1 = (bf16[2048,1024]{1,0:T(8,128)(2,1)}, bf16[8,1024,128]{2,1,0:T(8,128)(2,1)}) custom-call(s32[1]{0:T(128)} %bitcast.place, bf16[2048,1408]{1,0:T(8,128)(2,1)} %convolution_convert_fusion.1.proj.before, f32[8,1280]{1,0:T(8,128)} %fusion.44.conv_w, f32[8,1024]{1,0:T(8,128)} %select_maximum_fusion.1.rows, f32[2048,16]{1,0:T(8,128)} %copy.170.aux, ...), custom_call_target="tpu_custom_call" | custom-call | tf_op jit(solution)/shard_map/scan_forward/pallas_call | solution.py:315
  266.7 29.3 %multiply_reduce_fusion.1 = (f32[2048]{0:T(1024)S(1)}, f32[2048]{0:T(1024)S(1)}, f32[2048,1024]{1,0:T(8,128)}) fusion(f32[1024]{0:T(1024)S(1)} %copy-done.39, bf16[2048,1024]{1,0:T(8,128)(2,1)} %convolution_convert_fusion.3, bf16[2048,1024]{1,0:T(8,128)(2,1)} %get-tuple-element.20, bf16[2048,2048]{1,0:T(8,128)(2,1)} %constant_dynamic-update-slice_fusion.8, ...), kind=kOutput, calls=%fused_computation.19 | convolution fusion | flops 8615096320 | bytes 29380608 | tf_op jit(solution)/shard_map/dot_general | solution.py:34
  296.0 3.0 collective-permute-start.23
  303.2 16.7 %convolution_convert_fusion.4 = bf16[2048,1024]{1,0:T(8,128)(2,1)} fusion(bf16[2048,2048]{1,0:T(8,128)(2,1)} %constant_dynamic-update-slice_fusion.8, f32[2048]{0:T(1024)S(1)} %bitcast.286, f32[1024]{0:T(1024)S(1)} %copy-done.39, bf16[2048,1024]{1,0:T(8,128)(2,1)} %convolution_convert_fusion.3, bf16[2048,1024]{1,0:T(8,128)(2,1)} %get-tuple-element.20), kind=kOutput, calls=%fused_computation.41 | convolution fusion | flops 8613003264 | bytes 20983808 | tf_op jit(solution)/shard_map/dot_general | solution.py:34
  320.0 12.2 %fusion.1 = (bf16[2048,1024]{1,0:T(8,128)(2,1)S(1)}, bf16[2048,1024]{1,0:T(8,128)(2,1)}, f32[1024]{0:T(1024)S(1)}) fusion(bf16[2048,1024]{1,0:T(8,128)(2,1)} %get-tuple-element.20, bf16[2048,1024]{1,0:T(8,128)(2,1)} %convolution_convert_fusion.3, f32[2048]{0:T(1024)S(1)} %fusion.48, f32[2048,1024]{1,0:T(8,128)} %get-tuple-element.162, ...), kind=kLoop, calls=%fused_computation.7 | loop fusion | flops 50330624 | bytes 25190400 | tf_op jit(solution)/shard_map/convert_element_type | solution.py:519
  334.3 12.9 %convolution_convert_fusion.5 = bf16[2048,1024]{1,0:T(8,128)(2,1)} fusion(bf16[2048,2048]{1,0:T(8,128)(2,1)} %constant_dynamic-update-slice_fusion, bf16[2048,1024]{1,0:T(8,128)(2,1)S(1)} %get-tuple-element.86), kind=kOutput, calls=%fused_computation.42 | convolution fusion | flops 8592031744 | bytes 16777216 | tf_op jit(solution)/shard_map/dot_general | solution.py:34
  347.2 101.2 %scan_backward.1 = (bf16[2048,1408]{1,0:T(8,128)(2,1)}, f32[40,1280]{1,0:T(8,128)}, f32[8,128]{1,0:T(8,128)}) custom-call(s32[1]{0:T(128)} %bitcast.place, bf16[2048,1408]{1,0:T(8,128)(2,1)} %convolution_convert_fusion.1.proj.before, bf16[2048,1408]{1,0:T(8,128)(2,1)} %convolution_convert_fusion.1.proj.before, f32[8,1280]{1,0:T(8,128)} %fusion.44.conv_w, ...), custom_call_target="tpu_custom_call" | custom-call | tf_op jit(solution)/shard_map/scan_backward/pallas_call | solution.py:364
  452.4 19.1 %convolution_convert_fusion.2 = bf16[2048,1408]{1,0:T(8,128)(2,1)} fusion(bf16[2048,2048]{1,0:T(8,128)(2,1)} %constant_dynamic-update-slice_fusion, bf16[2048,1408]{1,0:T(8,128)(2,1)} %get-tuple-element.22), kind=kOutput, calls=%fused_computation.28 | convolution fusion | flops 11814043648 | bytes 19922944 | tf_op jit(solution)/shard_map/dot_general | solution.py:34
  471.5 14.3 %convolution_convert_fusion = bf16[2048,2048]{1,0:T(8,128)(2,1)S(1)} fusion(bf16[2048,1024]{1,0:T(8,128)(2,1)} %all-gather.8.cloned.1.call-done, f32[2048]{0:T(1024)S(1)} %bitcast.289, f32[1024]{0:T(1024)S(1)} %copy-done.39, bf16[2048,1024]{1,0:T(8,128)(2,1)} %convolution_convert_fusion.3, bf16[2048,1024]{1,0:T(8,128)(2,1)} %get-tuple-element.20), kind=kOutput, calls=%fused_computation.26 | convolution fusion | flops 8615100416 | bytes 20983808 | tf_op jit(solution)/shard_map/dot_general | solution.py:34
  485.8 2.5 slice_bitcast_fusion.14
  490.4 19.6 %fusion.76 = f32[2048,2048]{1,0:T(8,128)} fusion(bf16[2048,1408]{1,0:T(8,128)(2,1)} %get-tuple-element.22, bf16[2048,1408]{1,0:T(8,128)(2,1)} %all-gather.4.cloned.1.call-done), kind=kOutput, calls=%fused_computation.261 | convolution fusion | flops 11811160064 | bytes 28311552 | tf_op jit(solution)/shard_map/dot_general | solution.py:34
  510.0 14.8 %add_convert_fusion = bf16[2048,2048]{1,0:T(8,128)(2,1)S(1)} fusion(f32[2048,2048]{1,0:T(8,128)} %fusion.76, bf16[2048,1024]{1,0:T(8,128)(2,1)} %copy-done.12, bf16[2048,1024]{1,0:T(8,128)(2,1)} %all-gather.6.cloned.1.call-done), kind=kOutput, calls=%fused_computation | convolution fusion | flops 8598323200 | bytes 33554432 | tf_op jit(solution)/shard_map/dot_general | solution.py:34
  530.5 3.1 collective-permute-done.51
  539.2 2.9 collective-permute-done.52
  543.8 2.9 fusion.27
  548.3 30.1 %collective-permute-done.53 = f32[208,128]{1,0:T(8,128)S(1)} collective-permute-done((f32[208,128]{1,0:T(8,128)S(1)}, f32[208,128]{1,0:T(8,128)S(1)}, u32[]{:S(2)}, u32[]{:S(2)}) %collective-permute-start.53) | collective-permute-done | bytes 106528 | tf_op jit(solution)/shard_map/ppermute | solution.py:384
  580.1 6.4 collective-permute-done.54
  593.8 4.5 fusion.32
  601.0 9.1 %collective-permute-done.30 = bf16[256,2048]{1,0:T(8,128)(2,1)} collective-permute-done((bf16[256,2048]{1,0:T(8,128)(2,1)}, bf16[256,2048]{1,0:T(8,128)(2,1)}, u32[]{:S(2)}, u32[]{:S(2)}) %collective-permute-start.30) | collective-permute-done | bytes 1048608 | tf_op jit(solution)/shard_map/ppermute | solution.py:384
  610.8 2.6 collective-permute-done.34
  615.0 20.7 %collective-permute-done.32 = bf16[256,2048]{1,0:T(8,128)(2,1)S(1)} collective-permute-done((bf16[256,2048]{1,0:T(8,128)(2,1)}, bf16[256,2048]{1,0:T(8,128)(2,1)S(1)}, u32[]{:S(2)}, u32[]{:S(2)}) %collective-permute-start.32) | collective-permute-done | bytes 1048608 | tf_op jit(solution)/shard_map/ppermute | solution.py:384
  635.7 4.5 fusion.34
  645.5 35.1 %collective-permute-done.43 = bf16[1,64,1024]{2,1,0:T(8,128)(2,1)S(1)} collective-permute-done((bf16[1,64,1024]{2,1,0:T(8,128)(2,1)S(1)}, bf16[1,64,1024]{2,1,0:T(8,128)(2,1)S(1)}, u32[]{:S(2)}, u32[]{:S(2)}) %collective-permute-start.43) | collective-permute-done | bytes 131104 | tf_op jit(solution)/shard_map/ppermute | solution.py:384
  687.2 3.0 collective-permute-done.38
  694.1 19.9 %collective-permute-done.44 = bf16[1,64,1024]{2,1,0:T(8,128)(2,1)S(1)} collective-permute-done((bf16[1,64,1024]{2,1,0:T(8,128)(2,1)S(1)}, bf16[1,64,1024]{2,1,0:T(8,128)(2,1)S(1)}, u32[]{:S(2)}, u32[]{:S(2)}) %collective-permute-start.44) | collective-permute-done | bytes 131104 | tf_op jit(solution)/shard_map/ppermute | solution.py:384
  719.5 5.9 collective-permute-done.40
  727.2 4.6 collective-permute-done.41
  738.2 2.6 fusion.33
  742.8 2.5 fusion.35
  747.4 2.5 collective-permute-done.47
  751.2 2.5 collective-permute-done.48
  754.4 4.0 fusion.18
  764.6 4.7 multiply_add_fusion
  (371 shorter events, 159.2 us)
Async XLA Ops:
  7.2 189.6 %all-gather.6.cloned.1.call-start = ((), (), s32[]{:S(2)}) async-start(), calls=%async_computation.4 | async-start | bytes 4718592 | tf_op jit(solution)/shard_map/all_gather | solution.py:484
  11.4 6.9 collective-permute-start.9
  14.5 7.8 %collective-permute-start.10 = (bf16[1,64,1024]{2,1,0:T(8,128)(2,1)S(1)}, bf16[1,64,1024]{2,1,0:T(8,128)(2,1)S(1)}, u32[]{:S(2)}, u32[]{:S(2)}) collective-permute-start(bf16[1,64,1024]{2,1,0:T(8,128)(2,1)S(1)} %bitcast.282), channel_id=1, source_target_pairs={{0,2},{1,3},{2,0},{3,1},{4,6},{5,7},{6,4},{7,5},{8,10},{9,11},{10,... | collective-permute-start | bytes 393224 | tf_op jit(solution)/shard_map/ppermute | solution.py:384
  16.1 6.9 collective-permute-start.11
  23.7 187.1 %all-gather.4.cloned.1.call-start = ((), (), s32[]{:S(2)}) async-start(), calls=%async_computation.3 | async-start | bytes 6488064 | tf_op jit(solution)/shard_map/all_gather | solution.py:483
  29.7 10.0 %collective-permute-start.8 = (bf16[1,64,1408]{2,1,0:T(8,128)(2,1)S(1)}, bf16[1,64,1408]{2,1,0:T(8,128)(2,1)S(1)}, u32[]{:S(2)}, u32[]{:S(2)}) collective-permute-start(bf16[1,64,1408]{2,1,0:T(8,128)(2,1)S(1)} %get-tuple-element.113), channel_id=1, source_target_pairs={{0,3},{1,2},{2,1},{3,0},{4,7},{5,6},{6,5},{7,4},{8,11},{9,10},{10,... | collective-permute-start | bytes 540680 | tf_op jit(solution)/shard_map/ppermute | solution.py:384
  32.2 7.4 collective-permute-start.7
  40.6 226.1 %all-gather.8.cloned.1.call-start = ((), (), s32[]{:S(2)}) async-start(), calls=%async_computation.5 | async-start | bytes 4718592 | tf_op jit(solution)/shard_map/all_gather | solution.py:485
  45.8 59.9 %collective-permute-start.1 = (bf16[256,2048]{1,0:T(8,128)(2,1)}, bf16[256,2048]{1,0:T(8,128)(2,1)}, u32[]{:S(2)}, u32[]{:S(2)}) collective-permute-start(bf16[256,2048]{1,0:T(8,128)(2,1)} %get-tuple-element.104), channel_id=1, source_target_pairs={{0,2},{1,3},{2,0},{3,1},{4,6},{5,7},{6,4},{7,5},{8,10},{9,11},{10,... | collective-permute-start | bytes 3145736 | tf_op jit(solution)/shard_map/ppermute | solution.py:384
  46.4 51.4 %collective-permute-start = (bf16[256,2048]{1,0:T(8,128)(2,1)}, bf16[256,2048]{1,0:T(8,128)(2,1)}, u32[]{:S(2)}, u32[]{:S(2)}) collective-permute-start(bf16[256,2048]{1,0:T(8,128)(2,1)} %get-tuple-element.104), channel_id=1, source_target_pairs={{0,1},{1,0},{2,3},{3,2},{4,5},{5,4},{6,7},{7,6},{8,9},{9,8},{10,11... | collective-permute-start | bytes 3145736 | tf_op jit(solution)/shard_map/ppermute | solution.py:384
  49.7 25.8 %collective-permute-start.18 = (bf16[1,64,1024]{2,1,0:T(8,128)(2,1)S(1)}, bf16[1,64,1024]{2,1,0:T(8,128)(2,1)S(1)}, u32[]{:S(2)}, u32[]{:S(2)}) collective-permute-start(bf16[1,64,1024]{2,1,0:T(8,128)(2,1)S(1)} %bitcast.279), channel_id=1, source_target_pairs={{0,1},{1,0},{2,3},{3,2},{4,5},{5,4},{6,7},{7,6},{8,9},{9,8},{10,11... | collective-permute-start | bytes 393224 | tf_op jit(solution)/shard_map/ppermute | solution.py:384
  50.2 26.8 %collective-permute-start.19 = (bf16[1,64,1024]{2,1,0:T(8,128)(2,1)S(1)}, bf16[1,64,1024]{2,1,0:T(8,128)(2,1)}, u32[]{:S(2)}, u32[]{:S(2)}) collective-permute-start(bf16[1,64,1024]{2,1,0:T(8,128)(2,1)S(1)} %bitcast.278), channel_id=1, source_target_pairs={{0,2},{1,3},{2,0},{3,1},{4,6},{5,7},{6,4},{7,5},{8,10},{9,11},{10,... | collective-permute-start | bytes 393224 | tf_op jit(solution)/shard_map/ppermute | solution.py:384
  53.1 45.4 %collective-permute-start.12 = (bf16[256,2048]{1,0:T(8,128)(2,1)}, bf16[256,2048]{1,0:T(8,128)(2,1)}, u32[]{:S(2)}, u32[]{:S(2)}) collective-permute-start(bf16[256,2048]{1,0:T(8,128)(2,1)} %get-tuple-element.106), channel_id=1, source_target_pairs={{0,1},{1,0},{2,3},{3,2},{4,5},{5,4},{6,7},{7,6},{8,9},{9,8},{10,11... | collective-permute-start | bytes 3145736 | tf_op jit(solution)/shard_map/ppermute | solution.py:384
  75.5 33.2 %collective-permute-start.13 = (bf16[256,2048]{1,0:T(8,128)(2,1)}, bf16[256,2048]{1,0:T(8,128)(2,1)}, u32[]{:S(2)}, u32[]{:S(2)}) collective-permute-start(bf16[256,2048]{1,0:T(8,128)(2,1)} %get-tuple-element.106), channel_id=1, source_target_pairs={{0,2},{1,3},{2,0},{3,1},{4,6},{5,7},{6,4},{7,5},{8,10},{9,11},{10,... | collective-permute-start | bytes 3145736 | tf_op jit(solution)/shard_map/ppermute | solution.py:384
  77.0 19.5 %collective-permute-start.20 = (bf16[1,64,1024]{2,1,0:T(8,128)(2,1)S(1)}, bf16[1,64,1024]{2,1,0:T(8,128)(2,1)S(1)}, u32[]{:S(2)}, u32[]{:S(2)}) collective-permute-start(bf16[1,64,1024]{2,1,0:T(8,128)(2,1)S(1)} %bitcast.280), channel_id=1, source_target_pairs={{0,3},{1,2},{2,1},{3,0},{4,7},{5,6},{6,5},{7,4},{8,11},{9,10},{10,... | collective-permute-start | bytes 393224 | tf_op jit(solution)/shard_map/ppermute | solution.py:384
  96.5 26.4 %collective-permute-start.4 = (bf16[256,2048]{1,0:T(8,128)(2,1)}, bf16[256,2048]{1,0:T(8,128)(2,1)}, u32[]{:S(2)}, u32[]{:S(2)}) collective-permute-start(bf16[256,2048]{1,0:T(8,128)(2,1)} %get-tuple-element.103), channel_id=1, source_target_pairs={{0,2},{1,3},{2,0},{3,1},{4,6},{5,7},{6,4},{7,5},{8,10},{9,11},{10,... | collective-permute-start | bytes 3145736 | tf_op jit(solution)/shard_map/ppermute | solution.py:384
  97.8 47.6 %collective-permute-start.16 = (bf16[256,2048]{1,0:T(8,128)(2,1)}, bf16[256,2048]{1,0:T(8,128)(2,1)}, u32[]{:S(2)}, u32[]{:S(2)}) collective-permute-start(bf16[256,2048]{1,0:T(8,128)(2,1)} %get-tuple-element.105), channel_id=1, source_target_pairs={{0,2},{1,3},{2,0},{3,1},{4,6},{5,7},{6,4},{7,5},{8,10},{9,11},{10,... | collective-permute-start | bytes 3145736 | tf_op jit(solution)/shard_map/ppermute | solution.py:384
  98.5 69.3 %collective-permute-start.2 = (bf16[256,2048]{1,0:T(8,128)(2,1)}, bf16[256,2048]{1,0:T(8,128)(2,1)}, u32[]{:S(2)}, u32[]{:S(2)}) collective-permute-start(bf16[256,2048]{1,0:T(8,128)(2,1)} %collective-permute-done), channel_id=1, source_target_pairs={{0,2},{1,3},{2,0},{3,1},{4,6},{5,7},{6,4},{7,5},{8,10},{9,11},{10,... | collective-permute-start | bytes 3145736 | tf_op jit(solution)/shard_map/ppermute | solution.py:384
  100.7 497.6 %reduce-scatter.8.cloned.1.call-start = ((), (), s32[]{:S(2)}) async-start(), calls=%async_computation.8 | async-start | bytes 4718592 | tf_op jit(solution)/shard_map/reduce_scatter | solution.py:521
  105.7 80.0 %collective-permute-start.14 = (bf16[256,2048]{1,0:T(8,128)(2,1)}, bf16[256,2048]{1,0:T(8,128)(2,1)S(1)}, u32[]{:S(2)}, u32[]{:S(2)}) collective-permute-start(bf16[256,2048]{1,0:T(8,128)(2,1)} %collective-permute-done.12), channel_id=1, source_target_pairs={{0,2},{1,3},{2,0},{3,1},{4,6},{5,7},{6,4},{7,5},{8,10},{9,11},{10,... | collective-permute-start | bytes 3145736 | tf_op jit(solution)/shard_map/ppermute | solution.py:384
  108.8 79.0 %collective-permute-start.3 = (bf16[256,2048]{1,0:T(8,128)(2,1)S(1)}, bf16[256,2048]{1,0:T(8,128)(2,1)S(1)}, u32[]{:S(2)}, u32[]{:S(2)}) collective-permute-start(bf16[256,2048]{1,0:T(8,128)(2,1)S(1)} %copy-done.22), channel_id=1, source_target_pairs={{0,1},{1,0},{2,3},{3,2},{4,5},{5,4},{6,7},{7,6},{8,9},{9,8},{10,11... | collective-permute-start | bytes 3145736 | tf_op jit(solution)/shard_map/ppermute | solution.py:384
  122.9 68.3 %collective-permute-start.15 = (bf16[256,2048]{1,0:T(8,128)(2,1)S(1)}, bf16[256,2048]{1,0:T(8,128)(2,1)S(1)}, u32[]{:S(2)}, u32[]{:S(2)}) collective-permute-start(bf16[256,2048]{1,0:T(8,128)(2,1)S(1)} %copy-done.23), channel_id=1, source_target_pairs={{0,1},{1,0},{2,3},{3,2},{4,5},{5,4},{6,7},{7,6},{8,9},{9,8},{10,11... | collective-permute-start | bytes 3145736 | tf_op jit(solution)/shard_map/ppermute | solution.py:384
  145.4 49.3 %collective-permute-start.5 = (bf16[256,2048]{1,0:T(8,128)(2,1)}, bf16[256,2048]{1,0:T(8,128)(2,1)S(1)}, u32[]{:S(2)}, u32[]{:S(2)}) collective-permute-start(bf16[256,2048]{1,0:T(8,128)(2,1)} %collective-permute-done.4), channel_id=1, source_target_pairs={{0,1},{1,0},{2,3},{3,2},{4,5},{5,4},{6,7},{7,6},{8,9},{9,8},{10,11... | collective-permute-start | bytes 3145736 | tf_op jit(solution)/shard_map/ppermute | solution.py:384
  167.8 27.9 %collective-permute-start.17 = (bf16[256,2048]{1,0:T(8,128)(2,1)}, bf16[256,2048]{1,0:T(8,128)(2,1)S(1)}, u32[]{:S(2)}, u32[]{:S(2)}) collective-permute-start(bf16[256,2048]{1,0:T(8,128)(2,1)} %collective-permute-done.16), channel_id=1, source_target_pairs={{0,1},{1,0},{2,3},{3,2},{4,5},{5,4},{6,7},{7,6},{8,9},{9,8},{10,11... | collective-permute-start | bytes 3145736 | tf_op jit(solution)/shard_map/ppermute | solution.py:384
  319.9 322.0 %reduce-scatter.4.cloned.1.call-start = ((), (), s32[]{:S(2)}) async-start(), calls=%async_computation.6 | async-start | bytes 4718592 | tf_op jit(solution)/shard_map/reduce_scatter | solution.py:521
  347.1 345.6 %reduce-scatter.6.cloned.1.call-start = ((), (), s32[]{:S(2)}) async-start(), calls=%async_computation.7 | async-start | bytes 6488064 | tf_op jit(solution)/shard_map/reduce_scatter | solution.py:521
  452.3 72.5 %collective-permute-start.50 = (f32[208,128]{1,0:T(8,128)S(1)}, f32[208,128]{1,0:T(8,128)S(1)}, u32[]{:S(2)}, u32[]{:S(2)}) collective-permute-start(f32[208,128]{1,0:T(8,128)S(1)} %fusion.39), channel_id=1, source_target_pairs={{0,4},{4,0},{8,12},{12,8},{16,20},{20,16},{24,28},{28,24},{1,5},{5... | collective-permute-start | bytes 319496 | tf_op jit(solution)/shard_map/ppermute | solution.py:384
  490.4 53.4 %collective-permute-start.25 = (bf16[256,2048]{1,0:T(8,128)(2,1)}, bf16[256,2048]{1,0:T(8,128)(2,1)}, u32[]{:S(2)}, u32[]{:S(2)}) collective-permute-start(bf16[256,2048]{1,0:T(8,128)(2,1)} %get-tuple-element.100), channel_id=1, source_target_pairs={{0,1},{1,0},{2,3},{3,2},{4,5},{5,4},{6,7},{7,6},{8,9},{9,8},{10,11... | collective-permute-start | bytes 3145736 | tf_op jit(solution)/shard_map/ppermute | solution.py:384
  524.8 8.7 %collective-permute-start.51 = (f32[208,128]{1,0:T(8,128)S(1)}, f32[208,128]{1,0:T(8,128)S(1)}, u32[]{:S(2)}, u32[]{:S(2)}) collective-permute-start(f32[208,128]{1,0:T(8,128)S(1)} %fusion.93), channel_id=1, source_target_pairs={{0,8},{4,12},{8,0},{12,4},{16,24},{20,28},{24,16},{28,20},{1,9},{5... | collective-permute-start | bytes 319496 | tf_op jit(solution)/shard_map/ppermute | solution.py:384
  528.5 58.4 %collective-permute-start.31 = (bf16[256,2048]{1,0:T(8,128)(2,1)S(1)}, bf16[256,2048]{1,0:T(8,128)(2,1)S(1)}, u32[]{:S(2)}, u32[]{:S(2)}) collective-permute-start(bf16[256,2048]{1,0:T(8,128)(2,1)S(1)} %get-tuple-element.94), channel_id=1, source_target_pairs={{0,1},{1,0},{2,3},{3,2},{4,5},{5,4},{6,7},{7,6},{8,9},{9,8},{10,11... | collective-permute-start | bytes 3145736 | tf_op jit(solution)/shard_map/ppermute | solution.py:384
  533.6 8.6 %collective-permute-start.52 = (f32[208,128]{1,0:T(8,128)S(1)}, f32[208,128]{1,0:T(8,128)S(1)}, u32[]{:S(2)}, u32[]{:S(2)}) collective-permute-start(f32[208,128]{1,0:T(8,128)S(1)} %fusion.95), channel_id=1, source_target_pairs={{0,16},{4,20},{8,24},{12,28},{16,0},{20,4},{24,8},{28,12},{1,17},{... | collective-permute-start | bytes 319496 | tf_op jit(solution)/shard_map/ppermute | solution.py:384
  535.6 54.4 %collective-permute-start.24 = (bf16[256,2048]{1,0:T(8,128)(2,1)S(1)}, bf16[256,2048]{1,0:T(8,128)(2,1)S(1)}, u32[]{:S(2)}, u32[]{:S(2)}) collective-permute-start(bf16[256,2048]{1,0:T(8,128)(2,1)S(1)} %copy-done.24), channel_id=1, source_target_pairs={{0,1},{1,0},{2,3},{3,2},{4,5},{5,4},{6,7},{7,6},{8,9},{9,8},{10,11... | collective-permute-start | bytes 3145736 | tf_op jit(solution)/shard_map/ppermute | solution.py:384
  537.5 54.2 %collective-permute-start.28 = (bf16[256,2048]{1,0:T(8,128)(2,1)}, bf16[256,2048]{1,0:T(8,128)(2,1)}, u32[]{:S(2)}, u32[]{:S(2)}) collective-permute-start(bf16[256,2048]{1,0:T(8,128)(2,1)} %get-tuple-element.98), channel_id=1, source_target_pairs={{0,2},{1,3},{2,0},{3,1},{4,6},{5,7},{6,4},{7,5},{8,10},{9,11},{10,... | collective-permute-start | bytes 3145736 | tf_op jit(solution)/shard_map/ppermute | solution.py:384
  542.1 36.3 %collective-permute-start.53 = (f32[208,128]{1,0:T(8,128)S(1)}, f32[208,128]{1,0:T(8,128)S(1)}, u32[]{:S(2)}, u32[]{:S(2)}) collective-permute-start(f32[208,128]{1,0:T(8,128)S(1)} %add.396), channel_id=1, source_target_pairs={{0,1},{1,0},{2,3},{3,2},{4,5},{5,4},{6,7},{7,6},{8,9},{9,8},{10,11... | collective-permute-start | bytes 319496 | tf_op jit(solution)/shard_map/ppermute | solution.py:384
  546.7 46.7 %collective-permute-start.26 = (bf16[256,2048]{1,0:T(8,128)(2,1)}, bf16[256,2048]{1,0:T(8,128)(2,1)}, u32[]{:S(2)}, u32[]{:S(2)}) collective-permute-start(bf16[256,2048]{1,0:T(8,128)(2,1)} %fusion.27), channel_id=1, source_target_pairs={{0,2},{1,3},{2,0},{3,1},{4,6},{5,7},{6,4},{7,5},{8,10},{9,11},{10,... | collective-permute-start | bytes 3145736 | tf_op jit(solution)/shard_map/ppermute | solution.py:384
  578.5 8.0 %collective-permute-start.54 = (f32[208,128]{1,0:T(8,128)S(1)}, f32[208,128]{1,0:T(8,128)S(1)}, u32[]{:S(2)}, u32[]{:S(2)}) collective-permute-start(f32[208,128]{1,0:T(8,128)S(1)} %add.397), channel_id=1, source_target_pairs={{0,2},{1,3},{2,0},{3,1},{4,6},{5,7},{6,4},{7,5},{8,10},{9,11},{10,... | collective-permute-start | bytes 319496 | tf_op jit(solution)/shard_map/ppermute | solution.py:384
  586.5 23.5 %collective-permute-start.30 = (bf16[256,2048]{1,0:T(8,128)(2,1)}, bf16[256,2048]{1,0:T(8,128)(2,1)}, u32[]{:S(2)}, u32[]{:S(2)}) collective-permute-start(bf16[256,2048]{1,0:T(8,128)(2,1)} %get-tuple-element.91), channel_id=1, source_target_pairs={{0,1},{1,0},{2,3},{3,2},{4,5},{5,4},{6,7},{7,6},{8,9},{9,8},{10,11... | collective-permute-start | bytes 3145736 | tf_op jit(solution)/shard_map/ppermute | solution.py:384
  586.9 26.4 %collective-permute-start.34 = (bf16[256,2048]{1,0:T(8,128)(2,1)}, bf16[256,2048]{1,0:T(8,128)(2,1)}, u32[]{:S(2)}, u32[]{:S(2)}) collective-permute-start(bf16[256,2048]{1,0:T(8,128)(2,1)} %get-tuple-element.92), channel_id=1, source_target_pairs={{0,2},{1,3},{2,0},{3,1},{4,6},{5,7},{6,4},{7,5},{8,10},{9,11},{10,... | collective-permute-start | bytes 3145736 | tf_op jit(solution)/shard_map/ppermute | solution.py:384
  590.0 45.7 %collective-permute-start.32 = (bf16[256,2048]{1,0:T(8,128)(2,1)}, bf16[256,2048]{1,0:T(8,128)(2,1)S(1)}, u32[]{:S(2)}, u32[]{:S(2)}) collective-permute-start(bf16[256,2048]{1,0:T(8,128)(2,1)} %fusion.23), channel_id=1, source_target_pairs={{0,2},{1,3},{2,0},{3,1},{4,6},{5,7},{6,4},{7,5},{8,10},{9,11},{10,... | collective-permute-start | bytes 3145736 | tf_op jit(solution)/shard_map/ppermute | solution.py:384
  591.7 146.5 %collective-permute-start.27 = (bf16[256,2048]{1,0:T(8,128)(2,1)}, bf16[256,2048]{1,0:T(8,128)(2,1)}, u32[]{:S(2)}, u32[]{:S(2)}) collective-permute-start(bf16[256,2048]{1,0:T(8,128)(2,1)} %get-tuple-element.99), channel_id=1, source_target_pairs={{0,2},{1,3},{2,0},{3,1},{4,6},{5,7},{6,4},{7,5},{8,10},{9,11},{10,... | collective-permute-start | bytes 3145736 | tf_op jit(solution)/shard_map/ppermute | solution.py:384
  593.4 149.4 %collective-permute-start.33 = (bf16[256,2048]{1,0:T(8,128)(2,1)}, bf16[256,2048]{1,0:T(8,128)(2,1)}, u32[]{:S(2)}, u32[]{:S(2)}) collective-permute-start(bf16[256,2048]{1,0:T(8,128)(2,1)} %get-tuple-element.93), channel_id=1, source_target_pairs={{0,2},{1,3},{2,0},{3,1},{4,6},{5,7},{6,4},{7,5},{8,10},{9,11},{10,... | collective-permute-start | bytes 3145736 | tf_op jit(solution)/shard_map/ppermute | solution.py:384
  610.1 128.2 %collective-permute-start.29 = (bf16[256,2048]{1,0:T(8,128)(2,1)}, bf16[256,2048]{1,0:T(8,128)(2,1)}, u32[]{:S(2)}, u32[]{:S(2)}) collective-permute-start(bf16[256,2048]{1,0:T(8,128)(2,1)} %get-tuple-element.96), channel_id=1, source_target_pairs={{0,1},{1,0},{2,3},{3,2},{4,5},{5,4},{6,7},{7,6},{8,9},{9,8},{10,11... | collective-permute-start | bytes 3145736 | tf_op jit(solution)/shard_map/ppermute | solution.py:384
  613.3 29.8 %collective-permute-start.42 = (bf16[1,64,1024]{2,1,0:T(8,128)(2,1)S(1)}, bf16[1,64,1024]{2,1,0:T(8,128)(2,1)S(1)}, u32[]{:S(2)}, u32[]{:S(2)}) collective-permute-start(bf16[1,64,1024]{2,1,0:T(8,128)(2,1)S(1)} %get-tuple-element.119), channel_id=1, source_target_pairs={{0,1},{1,0},{2,3},{3,2},{4,5},{5,4},{6,7},{7,6},{8,9},{9,8},{10,11... | collective-permute-start | bytes 393224 | tf_op jit(solution)/shard_map/ppermute | solution.py:384
  640.2 40.4 %collective-permute-start.43 = (bf16[1,64,1024]{2,1,0:T(8,128)(2,1)S(1)}, bf16[1,64,1024]{2,1,0:T(8,128)(2,1)S(1)}, u32[]{:S(2)}, u32[]{:S(2)}) collective-permute-start(bf16[1,64,1024]{2,1,0:T(8,128)(2,1)S(1)} %get-tuple-element.118), channel_id=1, source_target_pairs={{0,2},{1,3},{2,0},{3,1},{4,6},{5,7},{6,4},{7,5},{8,10},{9,11},{10,... | collective-permute-start | bytes 393224 | tf_op jit(solution)/shard_map/ppermute | solution.py:384
  643.1 39.8 %collective-permute-start.36 = (bf16[1,64,1024]{2,1,0:T(8,128)(2,1)S(1)}, bf16[1,64,1024]{2,1,0:T(8,128)(2,1)S(1)}, u32[]{:S(2)}, u32[]{:S(2)}) collective-permute-start(bf16[1,64,1024]{2,1,0:T(8,128)(2,1)S(1)} %get-tuple-element.123), channel_id=1, source_target_pairs={{0,1},{1,0},{2,3},{3,2},{4,5},{5,4},{6,7},{7,6},{8,9},{9,8},{10,11... | collective-permute-start | bytes 393224 | tf_op jit(solution)/shard_map/ppermute | solution.py:384
  682.9 7.3 collective-permute-start.38
  686.2 56.6 %collective-permute-start.35 = (bf16[256,2048]{1,0:T(8,128)(2,1)}, bf16[256,2048]{1,0:T(8,128)(2,1)}, u32[]{:S(2)}, u32[]{:S(2)}) collective-permute-start(bf16[256,2048]{1,0:T(8,128)(2,1)} %get-tuple-element.90), channel_id=1, source_target_pairs={{0,1},{1,0},{2,3},{3,2},{4,5},{5,4},{6,7},{7,6},{8,9},{9,8},{10,11... | collective-permute-start | bytes 3145736 | tf_op jit(solution)/shard_map/ppermute | solution.py:384
  690.2 23.8 %collective-permute-start.44 = (bf16[1,64,1024]{2,1,0:T(8,128)(2,1)S(1)}, bf16[1,64,1024]{2,1,0:T(8,128)(2,1)S(1)}, u32[]{:S(2)}, u32[]{:S(2)}) collective-permute-start(bf16[1,64,1024]{2,1,0:T(8,128)(2,1)S(1)} %get-tuple-element.117), channel_id=1, source_target_pairs={{0,3},{1,2},{2,1},{3,0},{4,7},{5,6},{6,5},{7,4},{8,11},{9,10},{10,... | collective-permute-start | bytes 393224 | tf_op jit(solution)/shard_map/ppermute | solution.py:384
  (56 other events, 529.0 us)
Sparse Core Ops, SparseCore 0:
  23.8 47.4 all-gather.5
  73.5 59.1 all-gather.3
  134.3 45.8 all-gather.7
  320.0 50.5 reduce-scatter.7
  372.8 48.1 reduce-scatter.3
  471.6 67.6 reduce-scatter.5

commit v3 on v2

v3 whole, which is shorter than its diff:
```python
import functools

import jax
import jax.numpy as jnp
from jax import lax
from jax.experimental import pallas as pl
from jax.experimental.pallas import tpu as pltpu
from jax.sharding import PartitionSpec as P

D = 2048
HEADS = 64
HEADDIM = 64
STATE = 128
CONV = 4
BLOCK = 256
MICRO = 2
INNER = 4096
CH = 4352
NORM_EPS = 1e-05
LEARN_RATE = 0.004
BETA_ONE = 0.9
BETA_TWO = 0.95
FIX_ONE = 1.0 - 0.9**10
FIX_TWO = 1.0 - 0.95**10
ADAM_EPS = 1e-08
WEIGHT_DECAY = 0.1
CLIP_NORM = 1.0
BF = jnp.bfloat16
F32 = jnp.float32
ALL = ("dp", "seq")


def dot(a, b, dims, out=F32):
    return lax.dot_general(a, b, (dims, ((), ())), preferred_element_type=out)


NN = ((1,), (0,))
NT = ((1,), (1,))
TN = ((0,), (0,))
LANES = 128
PAIR = 2 * HEADDIM
VMEM = 56 * 1024 * 1024
TINY = 1e-37
CAP = 85.0


def iota2(shape, dim):
    return lax.broadcasted_iota(jnp.int32, shape, dim)


def running_sum(values, reverse):
    row, col = iota2((BLOCK, BLOCK), 0), iota2((BLOCK, BLOCK), 1)
    ones = jnp.where(row <= col if reverse else row >= col, 1.0, 0.0).astype(BF)
    high = values.astype(BF)
    rest = values - high.astype(F32)
    mid = rest.astype(BF)
    low = (rest - mid.astype(F32)).astype(BF)
    return dot(ones, high, NN) + dot(ones, mid, NN) + dot(ones, low, NN)


def step_sizes(raw, bias, a_neg):
    lifted = raw + bias
    dt = jnp.maximum(lifted, 0.0) + jnp.log1p(jnp.exp(-jnp.abs(lifted)))
    cum = running_sum(dt * a_neg, False)
    return lifted, dt, cum


def pick(left, columns, first):
    return jnp.where(left, columns[:, first : first + 1], columns[:, first + 1 : first + 2])


def thirds(value):
    high = value.astype(BF).astype(F32)
    rest = value - high
    mid = rest.astype(BF).astype(F32)
    return high, mid, (rest - mid).astype(BF).astype(F32)


def gap_depth(hl):
    return -(-3 * hl // 16) * 16 + 16


def gap_left(values, hl):
    lane = iota2(values.shape, 1)
    base = gap_depth(hl) - 16
    out = jnp.where((lane >= base) & (lane < base + 3), 1.0, 0.0)
    for at, part in enumerate(thirds(values)):
        part = jnp.where(lane < hl, part, 0.0)
        out += pltpu.roll(part, at * hl, 1) if at else part
    return out[:, : base + 16].astype(BF)


def gap_right_init(right, hl):
    base = gap_depth(hl) - 16
    row, col = iota2((base, BLOCK), 0), iota2((base, BLOCK), 1)
    for h in range(hl):
        hit = (row == h) | (row == hl + h) | (row == 2 * hl + h)
        right[0:base, h * BLOCK : (h + 1) * BLOCK] = jnp.where(hit, 1.0, 0.0).astype(BF)


def gap_right_fill(right, values_t, hl):
    base = gap_depth(hl) - 16
    row = iota2((16, BLOCK), 0)
    high, mid, low = thirds(values_t)
    for h in range(hl):
        one = slice(h, h + 1)
        slab = jnp.where(row == 0, high[one], jnp.where(row == 1, mid[one], jnp.where(row == 2, low[one], 0.0)))
        right[base : base + 16, h * BLOCK : (h + 1) * BLOCK] = slab.astype(BF)


def head_spread_init(spreads, hl):
    row, col = iota2(spreads.shape, 0), iota2(spreads.shape, 1)
    spreads[...] = jnp.where((row & (LANES - 1)) == col // HEADDIM, 1.0, 0.0).astype(BF)


def head_spread(values, spreads):
    high = values.astype(BF)
    low = (values - high.astype(F32)).astype(BF)
    return dot(jnp.concatenate([high, low], axis=1), spreads[...], NN)


def head_sum(values, spreads):
    return dot(values, spreads[0:LANES, :], NT)


def stacked(left, pair_values):
    zero = jnp.zeros_like(pair_values)
    return jnp.concatenate([jnp.where(left, pair_values, zero), jnp.where(left, zero, pair_values)], axis=0)


def conv_chunk(window, conv_w, valid, lo, hi):
    out = conv_w[CONV : CONV + 1, lo:hi] + conv_w[CONV - 1 : CONV, lo:hi] * window[8 : 8 + BLOCK, lo:hi]
    for tap in range(CONV - 1):
        out += conv_w[tap : tap + 1, lo:hi] * (window[5 + tap : 5 + tap + BLOCK, lo:hi] * valid[tap])
    return out


def spread(aux_v, at):
    return jnp.broadcast_to(aux_v[:, at : at + 1], (BLOCK, LANES))


def forward_kernel(place, proj, conv_w, rows, aux, seg_row, y_out, s_out, window, act, state, right, carried, spreads, end_s, *, hl):
    width = hl * HEADDIM
    conv_width = width + 2 * STATE

    @pl.when(pl.program_id(1) == 0)
    def _():
        window[0:8, :] = jnp.zeros((8, conv_width), F32)
        state[...] = jnp.zeros(state.shape, F32)
        gap_right_init(right, hl)
        head_spread_init(spreads, hl)

    aux_v = aux[...]
    valid = [spread(aux_v, tap) for tap in range(CONV - 1)]
    for lo in range(0, conv_width, LANES):
        hi = lo + LANES
        window[8 : 8 + BLOCK, lo:hi] = proj[:, lo:hi].astype(F32)
        out = conv_chunk(window, conv_w, valid, lo, hi)
        act[:, lo:hi] = (out * jax.nn.sigmoid(out)).astype(BF)
    window[0:8, :] = window[BLOCK : BLOCK + 8, :]

    _, dt, cum = step_sizes(proj[:, conv_width : conv_width + LANES].astype(F32), rows[0:1, :LANES], rows[1:2, :LANES])
    entry = jnp.exp(cum) * aux_v[:, 3:4]
    dt_end = dt * jnp.exp(cum[BLOCK - 1 : BLOCK, :] - cum) * aux_v[:, 4:5]
    shifted = jnp.log(jnp.maximum(dt, TINY)) - cum
    gaps = gap_left(cum, hl)
    gap_right_fill(right, shifted.T, hl)
    bm, cm = act[:, width : width + STATE], act[:, width + STATE :]
    same = (aux_v[:, 8:9] == seg_row[0:1, :]) & (iota2((BLOCK, BLOCK), 0) >= iota2((BLOCK, BLOCK), 1))
    inner = jnp.where(same, dot(cm, bm, NT), 0.0)
    left = iota2((BLOCK, PAIR), 1) < HEADDIM
    top = iota2((PAIR, STATE), 0) < HEADDIM
    last = entry[BLOCK - 1 : BLOCK, :]
    s_out[0] = state[...].astype(BF)
    carried[...] = dot(cm, s_out[0], NT) * head_spread(entry, spreads)
    end_s[...] = head_spread(dt_end, spreads)
    for pair in range(hl // 2):
        first = 2 * pair
        lo, hi = pair * PAIR, (pair + 1) * PAIR
        xp = act[:, lo:hi]
        mix = []
        for h in (first, first + 1):
            decay = jnp.exp(jnp.minimum(dot(gaps, right[:, h * BLOCK : (h + 1) * BLOCK], NN), CAP))
            mix.append((inner * decay).astype(BF))
        xf = xp.astype(F32)
        y = dot(jnp.concatenate(mix, axis=1), stacked(left, xp), NN)
        y += carried[:, lo:hi] + rows[2:3, lo:hi] * xf
        y_out[:, lo:hi] = y.astype(BF)
        weighted = (xf * end_s[:, lo:hi]).astype(BF)
        keep = jnp.where(top, last[:, first : first + 1], last[:, first + 1 : first + 2])
        state[lo:hi, :] = keep * state[lo:hi, :] + dot(weighted, bm, TN)


def backward_kernel(place, proj, before, conv_w, rows, aux, seg_row, dy, s_in, *refs, hl):
    dproj, dconv, dvec, dskip, window, act, dwin, grad_s, dcb, colsum, dkeep, right, carried, later_w, spreads, picks, entry_s, end_s, used, into = refs[-20:]
    width = hl * HEADDIM
    conv_width = width + 2 * STATE

    @pl.when(pl.program_id(0) == 0)
    def _():
        dconv[...] = jnp.zeros(dconv.shape, F32)
        dvec[...] = jnp.zeros(dvec.shape, F32)
        dskip[...] = jnp.zeros(dskip.shape, F32)
        dwin[BLOCK : BLOCK + 8, :] = jnp.zeros((8, conv_width), F32)
        grad_s[...] = jnp.zeros(grad_s.shape, F32)
        colsum[...] = jnp.zeros(colsum.shape, F32)
        dkeep[...] = jnp.zeros(dkeep.shape, F32)
        gap_right_init(right, hl)
        head_spread_init(spreads, hl)
        picks[...] = jnp.where(iota2(picks.shape, 0) == iota2(picks.shape, 1) // BLOCK, 1.0, 0.0).astype(BF)

    aux_v = aux[...]
    window[0:8, :] = before[8:16, :conv_width].astype(F32)
    valid = [spread(aux_v, tap) for tap in range(CONV - 1)]
    for lo in range(0, conv_width, LANES):
        hi = lo + LANES
        window[8 : 8 + BLOCK, lo:hi] = proj[:, lo:hi].astype(F32)
        out = conv_chunk(window, conv_w, valid, lo, hi)
        sig = jax.nn.sigmoid(out)
        act[:, lo:hi] = (out * sig).astype(BF)
        dwin[0:BLOCK, lo:hi] = sig * (1.0 + out * (1.0 - sig))

    lifted, dt, cum = step_sizes(proj[:, conv_width : conv_width + LANES].astype(F32), rows[0:1, :LANES], rows[1:2, :LANES])
    a_neg = rows[1:2, :LANES]
    entry = jnp.exp(cum) * aux_v[:, 3:4]
    dt_end = dt * jnp.exp(cum[BLOCK - 1 : BLOCK, :] - cum) * aux_v[:, 4:5]
    gaps = gap_left(jnp.log(jnp.maximum(dt, TINY)) - cum, hl)
    gap_right_fill(right, cum.T, hl)
    bm, cm = act[:, width : width + STATE], act[:, width + STATE :]
    same = (aux_v[:, 8:9] == seg_row[0:1, :]) & (iota2((BLOCK, BLOCK), 0) <= iota2((BLOCK, BLOCK), 1))
    inner = jnp.where(same, dot(bm, cm, NT), 0.0)
    left = iota2((BLOCK, PAIR), 1) < HEADDIM
    top = iota2((PAIR, STATE), 0) < HEADDIM
    lane = iota2((BLOCK, LANES), 1)
    last = entry[BLOCK - 1 : BLOCK, :]
    d_row = jnp.zeros((BLOCK, LANES), F32)
    d_b = jnp.zeros((BLOCK, STATE), F32)
    d_c = jnp.zeros((BLOCK, STATE), F32)
    carried[...] = dot(cm, s_in[0], NT)
    end_s[...] = head_spread(dt_end, spreads)
    later_w[...] = dot(bm, grad_s[...].astype(BF), NT) * end_s[...]
    entry_s[...] = head_spread(entry, spreads)

    for pair in range(hl // 2):
        first = 2 * pair
        lo, hi = pair * PAIR, (pair + 1) * PAIR
        xp, dyp = act[:, lo:hi], dy[:, lo:hi]
        xf, dyf = xp.astype(F32), dyp.astype(F32)
        d_mix = dot(stacked(left, xp), dyp, NT)
        mix, pairwise = [], []
        d_inner = 0.0
        for at, h in enumerate((first, first + 1)):
            decay = jnp.exp(jnp.minimum(dot(gaps, right[:, h * BLOCK : (h + 1) * BLOCK], NN), CAP))
            mix.append((inner * decay).astype(BF))
            part = d_mix[at * BLOCK : (at + 1) * BLOCK] * decay
            d_inner += part
            part = (part * inner).astype(BF)
            pairwise.append(part)
            colsum[h : h + 1, :] = jnp.sum(part.astype(F32), axis=0, keepdims=True)
        d_row += dot(jnp.concatenate(pairwise, axis=1), picks[:, first * BLOCK : (first + 2) * BLOCK], NT)
        if pair == 0:
            dcb[...] = d_inner
        else:
            dcb[...] += d_inner
        later = grad_s[lo:hi, :]
        low = s_in[0, lo:hi, :]
        from_end = later_w[:, lo:hi]
        dx = dot(jnp.concatenate(mix, axis=1), stacked(left, dyp), NN) + from_end + rows[2:3, lo:hi] * dyf
        dwin[0:BLOCK, lo:hi] = dwin[0:BLOCK, lo:hi] * dx
        used[:, lo:hi] = (from_end * xf).astype(BF)
        entering = entry_s[:, lo:hi] * dyf
        into[:, lo:hi] = (entering * carried[:, lo:hi]).astype(BF)
        entering = entering.astype(BF)
        dskip[:, lo:hi] += jnp.sum((xf * dyf).reshape(BLOCK // 8, 8, PAIR), axis=0)
        kept = later * low.astype(F32)
        dkeep[first : first + 1, :] = jnp.sum(kept[:HEADDIM], axis=0, keepdims=True)
        dkeep[first + 1 : first + 2, :] = jnp.sum(kept[HEADDIM:], axis=0, keepdims=True)
        weighted = (xf * end_s[:, lo:hi]).astype(BF)
        d_b += dot(weighted, later.astype(BF), NN)
        d_c += dot(entering, low, NN)
        keep = jnp.where(top, last[:, first : first + 1], last[:, first + 1 : first + 2])
        grad_s[lo:hi, :] = dot(entering, cm, TN) + keep * later

    d_inner = jnp.where(same, dcb[...], 0.0).astype(BF)
    d_b += dot(d_inner, cm, NN)
    d_c += dot(d_inner, bm, TN)
    dwin[0:BLOCK, width : width + STATE] = dwin[0:BLOCK, width : width + STATE] * d_b
    dwin[0:BLOCK, width + STATE :] = dwin[0:BLOCK, width + STATE :] * d_c

    d_end = head_sum(used[...], spreads)
    d_cum = head_sum(into[...], spreads)
    through = d_row + d_end
    d_last = jnp.sum(d_end, axis=0, keepdims=True) + jnp.sum(dkeep[...].T, axis=0, keepdims=True) * last
    d_cum += colsum[...].T - through
    d_cum += jnp.where(iota2((BLOCK, LANES), 0) == BLOCK - 1, d_last, 0.0)
    d_a = running_sum(d_cum, True)
    sig = jax.nn.sigmoid(lifted)
    d_raw = through * jnp.where(dt > TINY, sig / jnp.maximum(dt, TINY), 1.0) + d_a * a_neg * sig
    d_raw = jnp.where(lane < hl, d_raw, 0.0)
    dproj[:, conv_width : conv_width + LANES] = d_raw.astype(BF)
    dvec[0:1, :] += jnp.sum(d_a * dt, axis=0, keepdims=True) * a_neg
    dvec[1:2, :] += jnp.sum(d_raw, axis=0, keepdims=True)

    valid = [spread(aux_v, 5 + tap) for tap in range(CONV - 1)]
    fold = lambda a: jnp.sum(a.reshape(BLOCK // 8, 8, LANES), axis=0)
    for lo in range(0, conv_width, LANES):
        hi = lo + LANES
        own = dwin[0:BLOCK, lo:hi]
        value = window[8 : 8 + BLOCK, lo:hi]
        grad = conv_w[CONV - 1 : CONV, lo:hi] * own
        dconv[CONV * 8 : CONV * 8 + 8, lo:hi] += fold(own)
        dconv[(CONV - 1) * 8 : CONV * 8, lo:hi] += fold(own * value)
        for tap in range(CONV - 1):
            ahead = CONV - 1 - tap
            moved = dwin[ahead : ahead + BLOCK, lo:hi] * valid[tap]
            grad += conv_w[tap : tap + 1, lo:hi] * moved
            dconv[tap * 8 : tap * 8 + 8, lo:hi] += fold(moved * value)
        dproj[:, lo:hi] = grad.astype(BF)
    dwin[BLOCK : BLOCK + 8, :] = dwin[0:8, :]


def segment_aux(segments):
    micro, length = segments.shape
    nb = length // BLOCK
    seg = segments.astype(F32)
    blocks = seg.reshape(micro, nb, BLOCK)
    prev = jnp.concatenate([jnp.full((micro, 1), -1.0, F32), blocks[:, :-1, -1]], axis=1)
    entry = (blocks == prev[:, :, None]).reshape(micro, length)
    end = (blocks == blocks[:, :, -1:]).reshape(micro, length)
    cols = []
    for tap in range(CONV - 1):
        back = CONV - 1 - tap
        cols.append(jnp.pad(seg, ((0, 0), (back, 0)), constant_values=-1.0)[:, :length] == seg)
    cols += [entry, end]
    for tap in range(CONV - 1):
        ahead = CONV - 1 - tap
        cols.append(jnp.pad(seg, ((0, 0), (0, ahead)), constant_values=-1.0)[:, ahead:] == seg)
    cols.append(seg)
    cols = [c.astype(F32) for c in cols] + [jnp.zeros_like(seg)] * 7
    aux = jnp.stack(cols, axis=-1).reshape(micro * length, 16)
    seg_row = jnp.broadcast_to(blocks.reshape(micro * nb, 1, BLOCK), (micro * nb, 8, BLOCK)).reshape(micro * nb * 8, BLOCK)
    return aux, seg_row


def scan_forward(place, proj, conv_w, rows, aux, seg_row, hl):
    tokens = proj.shape[0]
    nb = tokens // MICRO // BLOCK
    width = hl * HEADDIM
    conv_width = width + 2 * STATE
    held = lambda m, j, place: (m * nb + (j ^ place[0]), 0)
    at = lambda m, j, place: (m * nb + j, 0)
    whole = lambda m, j, place: (0, 0)
    grid_spec = pltpu.PrefetchScalarGridSpec(
        num_scalar_prefetch=1,
        grid=(MICRO, nb),
        in_specs=[
            pl.BlockSpec((BLOCK, conv_width + LANES), held),
            pl.BlockSpec((8, conv_width), whole),
            pl.BlockSpec(rows.shape, whole),
            pl.BlockSpec((BLOCK, 16), at),
            pl.BlockSpec((8, BLOCK), at),
        ],
        out_specs=[
            pl.BlockSpec((BLOCK, width), held),
            pl.BlockSpec((1, width, STATE), lambda m, j, place: (m * nb + j, 0, 0)),
        ],
        scratch_shapes=[
            pltpu.VMEM((BLOCK + 8, conv_width), F32),
            pltpu.VMEM((BLOCK, conv_width), BF),
            pltpu.VMEM((width, STATE), F32),
            pltpu.VMEM((gap_depth(hl), hl * BLOCK), BF),
            pltpu.VMEM((BLOCK, width), F32),
            pltpu.VMEM((2 * LANES, width), BF),
            pltpu.VMEM((BLOCK, width), F32),
        ],
    )
    return pl.pallas_call(
        functools.partial(forward_kernel, hl=hl),
        grid_spec=grid_spec,
        out_shape=[
            jax.ShapeDtypeStruct((tokens, width), BF),
            jax.ShapeDtypeStruct((MICRO * nb, width, STATE), BF),
        ],
        compiler_params=pltpu.CompilerParams(vmem_limit_bytes=VMEM, dimension_semantics=("arbitrary", "arbitrary")),
        name="scan_forward",
    )(place, proj, conv_w, rows, aux, seg_row)


def scan_backward(place, micro, proj, conv_w, rows, aux, seg_row, dy, states, hl, *done):
    tokens = proj.shape[0] // MICRO
    nb = tokens // BLOCK
    width = hl * HEADDIM
    conv_width = width + 2 * STATE
    full = conv_width + LANES
    first = micro * nb
    held = lambda j, place: (first + ((nb - 1 - j) ^ place[0]), 0)
    ahead_of = lambda j, place: ((first + (jnp.maximum(nb - 2 - j, 0) ^ place[0])) * (BLOCK // 16) + BLOCK // 16 - 1, 0)
    at = lambda j, place: (first + nb - 1 - j, 0)
    whole = lambda j, place: (0, 0)
    grid_spec = pltpu.PrefetchScalarGridSpec(
        num_scalar_prefetch=1,
        grid=(nb,),
        in_specs=[
            pl.BlockSpec((BLOCK, full), held),
            pl.BlockSpec((16, full), ahead_of),
            pl.BlockSpec((8, conv_width), whole),
            pl.BlockSpec(rows.shape, whole),
            pl.BlockSpec((BLOCK, 16), at),
            pl.BlockSpec((8, BLOCK), at),
            pl.BlockSpec((BLOCK, width), held),
            pl.BlockSpec((1, width, STATE), lambda j, place: (first + nb - 1 - j, 0, 0)),
        ]
        + [pl.BlockSpec(memory_space=pl.ANY)] * len(done),
        out_specs=[
            pl.BlockSpec((BLOCK, full), lambda j, place: ((nb - 1 - j) ^ place[0], 0)),
            pl.BlockSpec((8 * (CONV + 1), conv_width), whole),
            pl.BlockSpec((8, LANES), whole),
            pl.BlockSpec((8, width), whole),
        ],
        scratch_shapes=[
            pltpu.VMEM((BLOCK + 8, conv_width), F32),
            pltpu.VMEM((BLOCK, conv_width), BF),
            pltpu.VMEM((BLOCK + 8, conv_width), F32),
            pltpu.VMEM((width, STATE), F32),
            pltpu.VMEM((BLOCK, BLOCK), F32),
            pltpu.VMEM((LANES, BLOCK), F32),
            pltpu.VMEM((LANES, STATE), F32),
            pltpu.VMEM((gap_depth(hl), hl * BLOCK), BF),
            pltpu.VMEM((BLOCK, width), F32),
            pltpu.VMEM((BLOCK, width), F32),
            pltpu.VMEM((2 * LANES, width), BF),
            pltpu.VMEM((LANES, hl * BLOCK), BF),
            pltpu.VMEM((BLOCK, width), F32),
            pltpu.VMEM((BLOCK, width), F32),
            pltpu.VMEM((BLOCK, width), BF),
            pltpu.VMEM((BLOCK, width), BF),
        ],
    )
    return pl.pallas_call(
        functools.partial(backward_kernel, hl=hl),
        grid_spec=grid_spec,
        out_shape=[
            jax.ShapeDtypeStruct((tokens, full), BF),
            jax.ShapeDtypeStruct((8 * (CONV + 1), conv_width), F32),
            jax.ShapeDtypeStruct((8, LANES), F32),
            jax.ShapeDtypeStruct((8, width), F32),
        ],
        compiler_params=pltpu.CompilerParams(vmem_limit_bytes=VMEM, dimension_semantics=("arbitrary",)),
        name="scan_backward",
    )(place, proj, proj, conv_w, rows, aux, seg_row, dy, states, *done)


def scan_rows(a_log, skip, dt_bias, hl):
    width = max(hl * HEADDIM, LANES)
    pad = lambda v: jnp.pad(v, (0, width - v.shape[0]))
    return jnp.pad(jnp.stack([pad(dt_bias), pad(-jnp.exp(a_log)), pad(jnp.repeat(skip, HEADDIM))]), ((0, 5), (0, 0)))


def fetch(pieces, buffer, sems, step):
    @pl.when(step == 0)
    def _():
        pltpu.make_async_copy(pieces[0], buffer.at[0], sems.at[0]).start()

    for at in range(1, len(pieces)):

        @pl.when(step == at - 1)
        def _():
            pltpu.make_async_copy(pieces[at], buffer.at[at % 2], sems.at[at % 2]).start()

    slot = step % 2
    pltpu.make_async_copy(pieces[0], buffer.at[slot], sems.at[slot]).wait()
    return slot


def fixed(array):
    return pl.BlockSpec(array.shape, lambda i: (0, 0), pipeline_mode=pl.Buffered(1))


def by_rows(width):
    return pl.BlockSpec((BLOCK, width), lambda i: (i, 0))


def arbitrary(name):
    return dict(compiler_params=pltpu.CompilerParams(vmem_limit_bytes=VMEM, dimension_semantics=("arbitrary",)), name=name)


def in_kernel(*refs, count):
    pieces, w, (proj, hidden, buffer, sems) = refs[:count], refs[count], refs[-4:]
    slot = fetch(pieces, buffer, sems, pl.program_id(0))
    value = buffer[slot]
    hidden[...] = value
    proj[...] = dot(value, w[...], NN).astype(BF)


def in_project(pieces, w, *done):
    count = len(pieces)
    depth, width = w.shape
    return pl.pallas_call(
        functools.partial(in_kernel, count=count),
        grid=(count,),
        in_specs=[pl.BlockSpec(memory_space=pl.ANY)] * count + [fixed(w)] + [pl.BlockSpec(memory_space=pl.ANY)] * len(done),
        out_specs=[by_rows(width), by_rows(depth)],
        out_shape=[
            jax.ShapeDtypeStruct((count * BLOCK, width), BF),
            jax.ShapeDtypeStruct((count * BLOCK, depth), BF),
        ],
        scratch_shapes=[pltpu.VMEM((2, BLOCK, depth), BF), pltpu.SemaphoreType.DMA((2,))],
        **arbitrary("in_project"),
    )(*pieces, w, *done)


def gate_kernel(*refs, count):
    pieces, (hidden, w_z, w_o, y, gain, z_out, dn_out, cot_out, sums, buffer, sems) = refs[:count], refs[count:]
    slot = fetch(pieces, buffer, sems, pl.program_id(0))
    cot = buffer[slot]
    cot_out[...] = cot
    z = dot(hidden[...], w_z[...], NN).astype(BF)
    z_out[...] = z
    dn = dot(cot, w_o[...], NN)
    dn_out[...] = dn.astype(BF)
    z = z.astype(F32)
    gz = y[...].astype(F32) * (z * jax.nn.sigmoid(z))
    ones = jnp.ones((8, gz.shape[1]), BF)
    first = dot(ones, (gz * gz).astype(BF), NT)
    second = dot(ones, (dn * gain[0:1, :] * gz).astype(BF), NT)
    sums[...] = jnp.where(iota2((8, BLOCK), 0) == 0, first, second)


def gate_forward(pieces, hidden, w_z, w_o, y, gain):
    count = len(pieces)
    depth, width = w_z.shape
    return pl.pallas_call(
        functools.partial(gate_kernel, count=count),
        grid=(count,),
        in_specs=[pl.BlockSpec(memory_space=pl.ANY)] * count + [by_rows(depth), fixed(w_z), fixed(w_o), by_rows(width), fixed(gain)],
        out_specs=[by_rows(width), by_rows(width), by_rows(depth), pl.BlockSpec((8, BLOCK), lambda i: (i, 0))],
        out_shape=[
            jax.ShapeDtypeStruct((count * BLOCK, width), BF),
            jax.ShapeDtypeStruct((count * BLOCK, width), BF),
            jax.ShapeDtypeStruct((count * BLOCK, depth), BF),
            jax.ShapeDtypeStruct((count * 8, BLOCK), F32),
        ],
        scratch_shapes=[pltpu.VMEM((2, BLOCK, depth), BF), pltpu.SemaphoreType.DMA((2,))],
        **arbitrary("gate_forward"),
    )(*pieces, hidden, w_z, w_o, y, gain)


def out_kernel(z_in, dn_in, y_in, sums, gain, w_o, normed, dy, dz, out, dgain):
    @pl.when(pl.program_id(0) == 0)
    def _():
        dgain[...] = jnp.zeros(dgain.shape, F32)

    scale = lax.rsqrt(sums[0:1, :] / INNER + NORM_EPS)
    slope = scale * scale * scale * sums[1:2, :] / INNER
    row = iota2((LANES, BLOCK), 0)
    columns = jnp.where(row == 0, scale, jnp.where(row == 1, slope, 0.0)).T
    scale, slope = columns[:, 0:1], columns[:, 1:2]
    for lo in range(0, normed.shape[1], 2 * LANES):
        hi = lo + 2 * LANES
        z, y, dn = z_in[:, lo:hi].astype(F32), y_in[:, lo:hi].astype(F32), dn_in[:, lo:hi].astype(F32)
        sig = jax.nn.sigmoid(z)
        silu = z * sig
        gz = y * silu
        unit = gz * scale
        normed[:, lo:hi] = (unit * gain[0:1, lo:hi]).astype(BF)
        dgain[:, lo:hi] += jnp.sum((dn * unit).reshape(BLOCK // 8, 8, 2 * LANES), axis=0)
        d_gz = dn * gain[0:1, lo:hi] * scale - gz * slope
        dy[:, lo:hi] = (d_gz * silu).astype(BF)
        dz[:, lo:hi] = (d_gz * y * (sig + silu * (1.0 - sig))).astype(BF)
    out[...] = dot(normed[...], w_o[...], NT).astype(BF)


def out_project(z, dn, y, sums, gain, w_o):
    depth, width = w_o.shape
    tokens = z.shape[0]
    one = by_rows(width)
    return pl.pallas_call(
        out_kernel,
        grid=(tokens // BLOCK,),
        in_specs=[one, one, one, pl.BlockSpec((8, BLOCK), lambda i: (i, 0)), fixed(gain), fixed(w_o)],
        out_specs=[one, one, one, by_rows(depth), pl.BlockSpec((8, width), lambda i: (0, 0))],
        out_shape=[jax.ShapeDtypeStruct((tokens, width), BF)] * 3
        + [jax.ShapeDtypeStruct((tokens, depth), BF), jax.ShapeDtypeStruct((8, width), F32)],
        **arbitrary("out_project"),
    )(z, dn, y, sums, gain, w_o)


def back_kernel(dz, px, w_z, w_x, out):
    out[...] = (dot(dz[...], w_z[...], NT) + dot(px[...], w_x[...], NT)).astype(BF)


def back_project(micro, dz, px, w_z, w_x):
    tokens, width = px.shape
    depth = w_z.shape[0]
    first = micro * tokens // BLOCK
    return pl.pallas_call(
        back_kernel,
        grid=(tokens // BLOCK,),
        in_specs=[pl.BlockSpec((BLOCK, dz.shape[1]), lambda i: (first + i, 0)), by_rows(width), fixed(w_z), fixed(w_x)],
        out_specs=by_rows(depth),
        out_shape=jax.ShapeDtypeStruct((tokens, depth), BF),
        **arbitrary("back_project"),
    )(dz, px, w_z, w_x)

def swapped(value, axis, mask):
    return lax.ppermute(value, axis, [(i, i ^ mask) for i in range(lax.axis_size(axis))])


def axis_bits(axis):
    return [1 << i for i in range(lax.axis_size(axis).bit_length() - 1)]


def micro_order(micro, axis):
    bits = axis_bits(axis)
    return bits if micro % 2 == 0 else bits[::-1]


def nothing(*refs):
    pass


def after(values, *done):
    values = list(values)
    anywhere = pl.BlockSpec(memory_space=pl.ANY)
    held = pl.pallas_call(
        nothing,
        in_specs=[anywhere] * (len(values) + len(done)),
        out_specs=[anywhere] * len(values),
        out_shape=[jax.ShapeDtypeStruct(v.shape, v.dtype) for v in values],
        input_output_aliases={at: at for at in range(len(values))},
        name="after",
    )(*values, *done)
    return list(held)


def gather_stages(own):
    held = [{0: own[micro]} for micro in range(MICRO)]
    for turn in range(len(axis_bits("seq"))):
        got = []
        for micro in range(MICRO):
            bit = micro_order(micro, "seq")[turn]
            got.append({at ^ bit: swapped(held[micro][at], "seq", bit) for at in held[micro]})
        wait = yield [piece for one in got for piece in one.values()], [piece for one in held for piece in one.values()]
        for micro in range(MICRO):
            if wait is not None:
                got[micro] = dict(zip(got[micro], after(got[micro].values(), *wait)))
            held[micro].update(got[micro])
    yield [held[micro][at] for micro in range(MICRO) for at in range(len(held[micro]))]


def scatter_stages(parts):
    some, n, piece, width = parts.shape
    pick = lambda a, at: jnp.concatenate([a[:, k : k + 1] for k in at], axis=1)
    held = [parts[:, :, half * piece // 2 : (half + 1) * piece // 2] for half in range(2)]
    places = [list(range(n)) for half in range(2)]
    for turn in range(len(axis_bits("seq"))):
        sent = []
        for half in range(2):
            bit = micro_order(half, "seq")[turn]
            away = [at for at, place in enumerate(places[half]) if place & bit]
            stay = [at for at, place in enumerate(places[half]) if not place & bit]
            sent.append((pick(held[half], away), bit))
            held[half] = pick(held[half], stay)
            places[half] = [places[half][at] for at in stay]
        got = [swapped(one, "seq", bit) for one, bit in sent]
        wait = yield got, [one for one, _ in sent]
        if wait is not None:
            got = after(got, *wait)
        held = [(one.astype(F32) + more.astype(F32)).astype(BF) for one, more in zip(held, got)]
    yield jnp.concatenate([one[:, 0] for one in held], axis=1), None


def finish(stages, wait=None):
    last = None
    try:
        while True:
            last = stages.send(wait)
    except StopIteration:
        return last[0]


def turned(entries, rank):
    entries = list(entries)
    for bit in axis_bits("seq"):
        flip = (rank & bit) != 0
        entries = [jnp.where(flip, entries[at ^ bit], entries[at]) for at in range(len(entries))]
    return entries


def exchange(entries, rank):
    entries = turned(entries, rank)
    return entries, [swapped(one, "seq", mask) for mask, one in enumerate(entries) if mask]


def sum_all(value):
    for axis in ("dp", "seq"):
        for bit in axis_bits(axis):
            value = value + swapped(value, axis, bit)
    return value


def sum_pieces(value):
    n = value.shape[-2]
    total = value
    for mask in range(1, n):
        got = swapped(value, "seq", mask)
        total = total + jnp.concatenate([got[..., at ^ mask : (at ^ mask) + 1, :] for at in range(n)], axis=-2)
    return total


def adamw(master, gradient, first, second, clip, decay):
    clipped = gradient * clip
    first_new = BETA_ONE * first + (1.0 - BETA_ONE) * clipped
    second_new = BETA_TWO * second + (1.0 - BETA_TWO) * clipped * clipped
    update = first_new / FIX_ONE / (jnp.sqrt(second_new / FIX_TWO) + ADAM_EPS) + decay * master
    return (-LEARN_RATE * update, first_new, second_new)


def per_device(tokens, cotangent, segments, in_weight, in_m, in_v, conv_weight, conv_m, conv_v,
               out_weight, out_m, out_v, packed, packed_m, packed_v):
    n = lax.axis_size("seq")
    rank = lax.axis_index("seq")
    place = rank.astype(jnp.int32).reshape(1)
    ndev = n * lax.axis_size("dp")
    hl = HEADS // n
    xw = hl * HEADDIM
    rows = D // ndev
    piece = tokens.shape[1]
    count = MICRO * n * piece
    xs = INNER + INNER
    bc = 2 * STATE
    xc = xw + bc + LANES
    cw = conv_weight.shape[1]
    conv_cols = -(-(CONV + 1) * cw // rows)

    in_low = in_weight.astype(BF)
    out_low = out_weight.astype(BF).T
    conv_flat = conv_weight.astype(BF).reshape(-1)
    conv_flat = jnp.pad(conv_flat, (0, conv_cols * rows - conv_flat.shape[0])).reshape(rows, conv_cols)
    column = lambda a, q, width: a[:, q * width : (q + 1) * width]
    pad = jnp.zeros((rows, LANES - hl - conv_cols), BF)
    send_x = [
        jnp.concatenate(
            [column(in_low[:, INNER:xs], q, xw), in_low[:, xs : xs + bc], column(in_low[:, xs + bc :], q, hl), conv_flat, pad], axis=1
        )
        for q in range(n)
    ]
    gain_in = packed[3 * HEADS : 3 * HEADS + D]
    send_x = turned(send_x, rank)
    got_wx = [one if not mask else swapped(one, "seq", mask) for mask, one in enumerate(send_x)]
    tok = tokens.astype(F32)
    r_in = lax.rsqrt(jnp.mean(tok * tok, axis=-1, keepdims=True) + NORM_EPS)
    hidden_stages = gather_stages((tok * r_in * gain_in).astype(BF))
    arrived, sent = next(hidden_stages)
    got_wx = jnp.concatenate(turned(got_wx[:1] + after(got_wx[1:], *sent), rank), axis=0)
    w_x = lax.all_gather(got_wx, "dp", axis=0, tiled=True)
    send_zo = jnp.stack(turned([jnp.concatenate([column(in_low, q, xw), column(out_low, q, xw)], axis=1) for q in range(n)], rank))
    [send_zo] = after([send_zo], got_wx, *arrived)
    got_wzo = [send_zo[mask] if not mask else swapped(send_zo[mask], "seq", mask) for mask in range(n)]
    got_wzo = jnp.concatenate(turned(got_wzo, rank), axis=0)
    w_z = lax.all_gather(got_wzo[:, :xw], "dp", axis=0, tiled=True)
    w_o = lax.all_gather(got_wzo[:, xw:], "dp", axis=0, tiled=True)
    conv_full = w_x[:, xw + bc + hl : xw + bc + hl + conv_cols].reshape(ndev, rows * conv_cols)[:, : (CONV + 1) * cw]
    conv_full = conv_full.reshape(ndev, CONV + 1, cw).transpose(1, 0, 2).reshape(CONV + 1, CH)
    conv_loc = jnp.concatenate([lax.dynamic_slice_in_dim(conv_full, rank * xw, xw, 1), conv_full[:, INNER:]], axis=1).astype(F32)
    conv_loc = jnp.pad(conv_loc, ((0, 8 - CONV - 1), (0, 0)))

    a_log = lax.dynamic_slice_in_dim(packed, rank * hl, hl)
    skip = lax.dynamic_slice_in_dim(packed, HEADS + rank * hl, hl)
    dt_bias = lax.dynamic_slice_in_dim(packed, 2 * HEADS + rank * hl, hl)
    gain_out = lax.dynamic_slice_in_dim(packed, 3 * HEADS + D + rank * xw, xw)
    aux, seg_row = segment_aux(segments)
    scan_row = scan_rows(a_log, skip, dt_bias, hl)

    for _ in axis_bits("seq")[1:]:
        arrived, _ = hidden_stages.send(None)
    proj_x, hidden = in_project(hidden_stages.send(None), w_x, conv_loc)

    [cot] = after([cotangent], *arrived)
    cot_stages = gather_stages(cot)
    next(cot_stages)
    y, states = scan_forward(place, proj_x, conv_loc, scan_row, aux, seg_row, hl)
    for bit in axis_bits("seq"):
        cot = cot_stages.send([proj_x] if bit == 1 else [y])
    gain = jnp.broadcast_to(gain_out[None], (8, xw))
    z, dn, cot, sums = gate_forward(cot, hidden, w_z, w_o, y, gain)
    sums = sum_pieces(sums.reshape(MICRO, n, 8 * BLOCK)).reshape(-1, BLOCK)
    normed, dy, dz, out_part, d_gain_out = out_project(z, dn, y, sums, gain, w_o)
    d_gain_out = jnp.sum(d_gain_out, axis=0)

    scatter = lambda a: lax.psum_scatter(a, "dp", scatter_dimension=0, tiled=True)
    split = lambda a: [a[q * rows : (q + 1) * rows] for q in range(n)]
    out_stages = scatter_stages(out_part.reshape(MICRO, n, piece, D))
    _, sent = next(out_stages)
    [normed] = after([normed], *sent)
    part_o = dot(cot, normed, TN).astype(BF)
    part_z = dot(hidden, dz, TN).astype(BF)
    got_o, got_z = scatter(part_o), scatter(part_z)

    through_in = lambda micro, one: back_project(micro, dz, one, w_z, w_x).reshape(1, n, piece, D)
    scan_back = lambda micro, *done: scan_backward(place, micro, proj_x, conv_loc, scan_row, aux, seg_row, dy, states, hl, *done)

    px_0, conv_0, vec_0, skip_0 = scan_back(0, part_o, part_z)
    hid_0 = through_in(0, px_0)
    out_got, out_sent = out_stages.send([hid_0])
    stages_0 = scatter_stages(hid_0)
    hid_got, sent = next(stages_0)
    px_1, conv_1, vec_1, skip_1 = scan_back(1, *sent, *out_sent)
    [px_1] = after([px_1], *hid_got)
    part_x = dot(hidden, jnp.concatenate([px_0, px_1], axis=0), TN).astype(BF)
    got_x = scatter(part_x)
    hid_got, sent = stages_0.send([part_x])
    [px_1] = after([px_1], part_x, *sent, *out_got)
    hid_1 = through_in(1, px_1)
    [got_o, got_z] = after([got_o, got_z], part_x)
    sent_oz, got_oz = exchange(split(jnp.concatenate([got_o, got_z], axis=1)), rank)
    [hid_1] = after([hid_1], *got_oz, *hid_got)
    stages_1 = scatter_stages(hid_1)
    hid_got, hid_sent = next(stages_1)
    output = (tok + finish(out_stages, [part_x]).astype(F32)).astype(BF)

    d_conv = (conv_0 + conv_1).reshape(CONV + 1, 8, -1).sum(axis=1)
    d_skip = jnp.sum((skip_0 + skip_1).reshape(8, hl, HEADDIM), axis=(0, 2))
    d_vec = vec_0 + vec_1
    head_rows = jnp.concatenate([d_vec[0, :hl], d_skip, d_vec[1, :hl]])
    small = jnp.concatenate([d_conv.reshape(-1), d_gain_out, head_rows])
    small_size = small.shape[0]
    small = jnp.pad(small, (0, -small_size % 1024)).reshape(-1, LANES)
    [small] = after([small], *hid_sent)
    for bit in axis_bits("dp"):
        small = small + swapped(small, "dp", bit)
    small = jnp.stack(turned([small] + [swapped(small, "seq", mask) for mask in range(1, n)], rank)).reshape(n, -1)[:, :small_size]
    conv_all = small[:, : (CONV + 1) * (xw + bc)].reshape(n, CONV + 1, xw + bc)
    conv_tot = jnp.concatenate(
        [conv_all[:, :, :xw].transpose(1, 0, 2).reshape(CONV + 1, INNER), jnp.sum(conv_all[:, :, xw:], axis=0)], axis=1
    )
    gain_out_tot = small[:, (CONV + 1) * (xw + bc) : small_size - 3 * hl].reshape(-1)
    heads_tot = small[:, small_size - 3 * hl :].reshape(n, 3, hl).transpose(1, 0, 2).reshape(-1)

    [got_x] = after([got_x], conv_tot, *hid_got)
    sent_x, got_x = exchange(split(got_x), rank)
    d_hidden = jnp.concatenate([finish(stages_0, [hid_1]), finish(stages_1)], axis=0).astype(F32)
    got_oz, got_x = (turned(sent[:1] + got, rank) for sent, got in ((sent_oz, got_oz), (sent_x, got_x)))

    together = lambda parts, lo, hi: jnp.concatenate([one[:, lo:hi] for one in parts], axis=1).astype(F32)
    g_bc = sum(one[:, xw : xw + bc].astype(F32) for one in got_x)
    shard_in = jnp.concatenate(
        [together(got_oz, xw, 2 * xw), together(got_x, 0, xw), g_bc, together(got_x, xw + bc, xw + bc + hl)], axis=1
    )
    shard_out = together(got_oz, 0, xw).T

    dh = d_hidden * gain_in
    d_tok = r_in * (dh - tok * (r_in * r_in) * jnp.mean(dh * tok, axis=-1, keepdims=True))
    input_grad = (cotangent.astype(F32) + d_tok).astype(BF)

    own = lax.axis_index("dp") * n + rank
    own_gain = lax.dynamic_slice_in_dim(gain_in, own * rows, rows)
    d_gain_in = jnp.sum(in_low.astype(F32) * shard_in, axis=1) / own_gain
    partial_sq = jnp.sum(shard_in * shard_in) + jnp.sum(shard_out * shard_out)
    last = lax.dynamic_update_slice(jnp.zeros((D + 1024,), F32), d_gain_in, (own * rows,))
    last = lax.dynamic_update_slice(last, partial_sq[None], (D,))
    last = sum_all(last.reshape(-1, LANES)).reshape(-1)
    vec_tot = jnp.concatenate([heads_tot, last[:D], gain_out_tot])
    shard_conv = lax.dynamic_slice_in_dim(conv_tot, own * cw, cw, 1)
    grad_norm = jnp.sqrt(last[D] + jnp.sum(conv_tot * conv_tot) + jnp.sum(vec_tot * vec_tot))
    clip = jnp.minimum(1.0, CLIP_NORM / (grad_norm + 1e-06))
    in_new = adamw(in_weight, shard_in, in_m, in_v, clip, WEIGHT_DECAY)
    conv_new = adamw(conv_weight, shard_conv, conv_m, conv_v, clip, WEIGHT_DECAY)
    out_new = adamw(out_weight, shard_out, out_m, out_v, clip, WEIGHT_DECAY)
    vec_new = adamw(packed, vec_tot, packed_m, packed_v, clip, 0.0)
    return (
        output, input_grad, grad_norm,
        in_weight + in_new[0], in_new[1], in_new[2],
        conv_new[0], conv_new[1], conv_new[2],
        out_weight + out_new[0], out_new[1], out_new[2],
        vec_new[0], vec_new[1], vec_new[2],
    )


def solution(mesh):
    tok, col, row = P(None, ALL, None), P(None, ALL), P(ALL, None)
    return jax.shard_map(
        per_device,
        mesh=mesh,
        in_specs=(tok, tok, P(None, "dp"), row, row, row, col, col, col, col, col, col, P(), P(), P()),
        out_specs=(tok, tok, P(), row, row, row, col, col, col, col, col, col, P(), P(), P()),
        check_vma=False,
    )
```

time: 789 us -> 595 us (0.75)
  waiting for transfers between devices: 259 us -> 107 us
  matrix products: 159 us -> 47.6 us
  Pallas kernels: 136 us -> 209 us
  starting transfers between devices: 67.9 us -> 56.4 us
  other arithmetic: 61.2 us -> 72.3 us
    ppermute x55 -> x50, waiting for transfers between devices: 259 us -> 106 us  [swapped(): lax.ppermute(value, axis, [(i, i ^ mask) for i in range(lax.axis_size(axi...]
    dot_general x9 -> x3, matrix products: 159 us -> 47.6 us  [dot(): return lax.dot_general(a, b, (dims, ((), ())), preferred_element_type=out)]
    pallas_call x0 -> x23, Pallas kernels: none -> 104 us  [the longest x2 34.6 us: back_project(): pl.pallas_call(back_kernel, grid=(tokens // BLOCK,), in_specs=[pl.BlockSp...]
    pallas_call x1 -> x2, Pallas kernels: 101 us -> 73 us  [scan_backward(): pl.pallas_call(functools.partial(backward_kernel, hl=hl), grid_spec=grid_...]
    slice x6 -> x25, local copies, waits for them, and re-layouts: 1.68 us -> 16.6 us  [the longest x7 12.8 us: scatter_stages(): pick = lambda a, at: jnp.concatenate([a[:, k:k + 1] for k in at], axis=1)]
    another operation x4 -> x2, other arithmetic: 14.2 us -> 1.89 us  [the longest x1 1.1 us: per_device(): jnp.stack(turned([jnp.concatenate([column(in_low, q, xw), column(out_low,...]
    ppermute x55 -> x50, starting transfers between devices: 67.7 us -> 56.1 us  [swapped(): lax.ppermute(value, axis, [(i, i ^ mask) for i in range(lax.axis_size(axi...]
    concatenate x4 -> x15, local copies, waits for them, and re-layouts: 3.22 us -> 11.9 us  [the longest x3 8.55 us: scatter_stages(): pick = lambda a, at: jnp.concatenate([a[:, k:k + 1] for k in at], axis=1)]
  transfers between devices with their start and end apart: 61 -> 56, of which waited for: 29 -> 23; matrix products, arithmetic and copies ran while one was open for 29% -> 24% of each run, Pallas kernels for 17% -> 27%
where the time goes in v3:
time: 595 us; the launch traced here: 588 us
  Pallas kernels  209 us (35%)
  waiting for transfers between devices  107 us (18%)
  local copies, waits for them, and re-layouts  75.3 us (13%)
  other arithmetic  72.3 us (12%)
  starting transfers between devices  56.4 us (9%)
  matrix products  47.6 us (8%)
  between operations  20.6 us (3%)
    ppermute x50, waiting for transfers between devices, swapped(): lax.ppermute(value, axis, [(i, i ^ mask) for i in range(lax.axis_size(axi...  106 us
    pallas_call x2, Pallas kernels, scan_backward(): pl.pallas_call(functools.partial(backward_kernel, hl=hl), grid_spec=grid_...  73 us
    ppermute x50, starting transfers between devices, swapped(): lax.ppermute(value, axis, [(i, i ^ mask) for i in range(lax.axis_size(axi...  56.1 us
    dot_general x3, matrix products, dot(): return lax.dot_general(a, b, (dims, ((), ())), preferred_element_type=out)  47.6 us
    pallas_call x2, Pallas kernels, back_project(): pl.pallas_call(back_kernel, grid=(tokens // BLOCK,), in_specs=[pl.BlockSp...  34.6 us
    pallas_call x1, Pallas kernels, scan_forward(): pl.pallas_call(functools.partial(forward_kernel, hl=hl), grid_spec=grid_s...  32.4 us
    pallas_call x1, Pallas kernels, gate_forward(): pl.pallas_call(functools.partial(gate_kernel, count=count), grid=(count,)...  27.5 us
    unnamed x195, local copies, waits for them, and re-layouts  25.8 us
  transfers between devices with their start and end apart: 56, of which 23 were waited for; matrix products, arithmetic and copies ran while one was open for 24% of the time, Pallas kernels for 27%

profile of v3, /device:TPU:0, one launch (start us, length us, event | category | flops | bytes accessed | tf_op | source)
XLA Modules:
  0.0 588.0 jit_solution(5089344033052441195)
XLA Ops:
  7.2 1.7 convert_element_type.215
  10.7 3.0 collective-permute-start.7
  19.2 4.4 collective-permute-done.8.refs_1_
  33.7 17.9 %collective-permute-done.1.refs_1_.refs_2_ = bf16[256,2048]{1,0:T(8,128)(2,1)S(1)} collective-permute-done((bf16[256,2048]{1,0:T(8,128)(2,1)S(1)}, bf16[256,2048]{1,0:T(8,128)(2,1)S(1)}, u32[]{:S(2)}, u32[]{:S(2)}) %collective-permute-start.1) | collective-permute-done | bytes 1048608 | tf_op jit(solution)/shard_map/ppermute | solution.py:606
  57.6 6.3 %collective-permute-done.15 = bf16[64,2048]{1,0:T(8,128)(2,1)S(1)} collective-permute-done((bf16[64,2048]{1,0:T(8,128)(2,1)S(1)}, bf16[64,2048]{1,0:T(8,128)(2,1)S(1)}, u32[]{:S(2)}, u32[]{:S(2)}) %collective-permute-start.15) | collective-permute-done | bytes 262176 | tf_op jit(solution)/shard_map/ppermute | solution.py:606
  63.9 2.7 collective-permute-done.16
  73.8 3.2 copy.189.refs_0_
  77.0 18.9 %collective-permute-done.refs_1_.refs_2_ = bf16[256,2048]{1,0:T(8,128)(2,1)S(1)} collective-permute-done((bf16[256,2048]{1,0:T(8,128)(2,1)S(1)}, bf16[256,2048]{1,0:T(8,128)(2,1)S(1)}, u32[]{:S(2)}, u32[]{:S(2)}) %collective-permute-start) | collective-permute-done | bytes 1048608 | tf_op jit(solution)/shard_map/ppermute | solution.py:606
  96.5 20.4 %collective-permute-done.2.refs_2_.refs_3_ = bf16[256,2048]{1,0:T(8,128)(2,1)S(1)} collective-permute-done((bf16[256,2048]{1,0:T(8,128)(2,1)S(1)}, bf16[256,2048]{1,0:T(8,128)(2,1)S(1)}, u32[]{:S(2)}, u32[]{:S(2)}) %collective-permute-start.2) | collective-permute-done | bytes 1048608 | tf_op jit(solution)/shard_map/ppermute | solution.py:606
  117.9 2.7 slice_bitcast_fusion.2
  125.0 2.0 slice.533
  129.8 19.6 %in_project.1 = (bf16[2048,1408]{1,0:T(8,128)(2,1)}, bf16[2048,2048]{1,0:T(8,128)(2,1)}) custom-call(bf16[256,2048]{1,0:T(8,128)(2,1)} %get-tuple-element.138.refs_3_.refs_0_, bf16[256,2048]{1,0:T(8,128)(2,1)} %copy-done.25, bf16[256,2048]{1,0:T(8,128)(2,1)} %copy-done.43, bf16[256,2048]{1,0:T(8,128)(2,1)} %copy-done.45, ...), custom_call_target="tpu_custom_call" | custom-call | tf_op jit(solution)/shard_map/in_project/pallas_call | solution.py:498
  158.0 32.4 %scan_forward.1 = (bf16[2048,1024]{1,0:T(8,128)(2,1)}, bf16[8,1024,128]{2,1,0:T(8,128)(2,1)}) custom-call(s32[1]{0:T(128)} %bitcast.4.place, bf16[2048,1408]{1,0:T(8,128)(2,1)} %get-tuple-element.56.refs_1_.proj.before, f32[8,1280]{1,0:T(8,128)} %fusion.29.refs_9_.conv_w, f32[8,1024]{1,0:T(8,128)} %select_maximum_fusion.rows, f32[2048,16]{1,0:T(8,128)} %copy.150.aux, ...), custom_call_target="tpu_custom_call" | custom-call | tf_op jit(solution)/shard_map/scan_forward/pallas_call | solution.py:377
  193.0 27.5 %gate_forward.1 = (bf16[2048,1024]{1,0:T(8,128)(2,1)}, bf16[2048,1024]{1,0:T(8,128)(2,1)}, bf16[2048,2048]{1,0:T(8,128)(2,1)}, f32[64,256]{1,0:T(8,128)}) custom-call(bf16[256,2048]{1,0:T(8,128)(2,1)} %get-tuple-element.136.refs_0_, bf16[256,2048]{1,0:T(8,128)(2,1)} %after.20.refs_1_, bf16[256,2048]{1,0:T(8,128)(2,1)} %get-tuple-element.58.refs_2_, ...), custom_call_target="tpu_custom_call" | custom-call | tf_op jit(solution)/shard_map/gate_forward/pallas_call | solution.py:532
  226.8 2.3 collective-permute-done.20
  230.8 21.8 %out_project.1 = (bf16[2048,1024]{1,0:T(8,128)(2,1)}, bf16[2048,1024]{1,0:T(8,128)(2,1)}, bf16[2048,1024]{1,0:T(8,128)(2,1)}, bf16[2048,2048]{1,0:T(8,128)(2,1)}, f32[8,1024]{1,0:T(8,128)}) custom-call(bf16[2048,1024]{1,0:T(8,128)(2,1)} %get-tuple-element.63.z_in, bf16[2048,1024]{1,0:T(8,128)(2,1)} %get-tuple-element.64.dn_in, ...), custom_call_target="tpu_custom_call" | custom-call | tf_op jit(solution)/shard_map/out_project/pallas_call | solution.py:577
  252.6 14.2 %convolution_convert_fusion.1.refs_1_ = bf16[2048,1024]{1,0:T(8,128)(2,1)} fusion(bf16[2048,2048]{1,0:T(8,128)(2,1)} %get-tuple-element.62.refs_8_, bf16[2048,1024]{1,0:T(8,128)(2,1)} %get-tuple-element.67.dz), kind=kOutput, calls=%fused_computation.22 | convolution fusion | flops 8592031744 | bytes 16777216 | tf_op jit(solution)/shard_map/dot_general | solution.py:34
  266.8 4.1 slice_bitcast_fusion.1
  272.4 4.9 fusion.48
  277.3 14.1 %convolution_convert_fusion.2.refs_0_ = bf16[2048,1024]{1,0:T(8,128)(2,1)} fusion(bf16[2048,2048]{1,0:T(8,128)(2,1)} %get-tuple-element.70, bf16[2048,1024]{1,0:T(8,128)(2,1)} %after.25), kind=kOutput, calls=%fused_computation.23 | convolution fusion | flops 8592031744 | bytes 16777216 | tf_op jit(solution)/shard_map/dot_general | solution.py:34
  293.2 36.7 %scan_backward.2 = (bf16[1024,1408]{1,0:T(8,128)(2,1)}, f32[40,1280]{1,0:T(8,128)}, f32[8,128]{1,0:T(8,128)}, f32[8,1024]{1,0:T(8,128)}) custom-call(s32[1]{0:T(128)} %bitcast.4.place, bf16[2048,1408]{1,0:T(8,128)(2,1)} %get-tuple-element.56.refs_1_.proj.before, bf16[2048,1408]{1,0:T(8,128)(2,1)} %get-tuple-element.56.refs_1_.proj.before, ...), custom_call_target="tpu_custom_call" | custom-call | tf_op jit(solution)/shard_map/scan_backward/pallas_call | solution.py:439
  329.9 17.3 %back_project.2 = bf16[1024,2048]{1,0:T(8,128)(2,1)} custom-call(bf16[2048,1024]{1,0:T(8,128)(2,1)} %get-tuple-element.67.dz, bf16[1024,1408]{1,0:T(8,128)(2,1)} %get-tuple-element.72.px, bf16[2048,1024]{1,0:T(8,128)(2,1)} %all-gather.6.cloned.1.call-done.refs_9_.w_z, bf16[2048,1408]{1,0:T(8,128)(2,1)} %all-gather.4.cloned.1.call-done.refs_8_.w_x), custom_call_target="tpu_custom_call" | custom-call | tf_op jit(solution)/shard_map/back_project/pallas_call | solution.py:596
  348.5 3.1 fusion.50
  352.7 1.7 collective-permute-start.25
  355.2 3.2 add_convert_fusion
  358.4 3.2 add_convert_fusion.1
  361.6 2.4 slice_bitcast_fusion.21
  364.3 36.3 %scan_backward.3 = (bf16[1024,1408]{1,0:T(8,128)(2,1)}, f32[40,1280]{1,0:T(8,128)}, f32[8,128]{1,0:T(8,128)}, f32[8,1024]{1,0:T(8,128)}) custom-call(s32[1]{0:T(128)} %bitcast.4.place, bf16[2048,1408]{1,0:T(8,128)(2,1)} %get-tuple-element.56.refs_1_.proj.before, bf16[2048,1408]{1,0:T(8,128)(2,1)} %get-tuple-element.56.refs_1_.proj.before, ...), custom_call_target="tpu_custom_call" | custom-call | tf_op jit(solution)/shard_map/scan_backward/pallas_call | solution.py:439
  401.9 19.3 %convolution_convert_fusion.refs_2_.refs_1_ = bf16[2048,1408]{1,0:T(8,128)(2,1)} fusion(bf16[2048,2048]{1,0:T(8,128)(2,1)} %get-tuple-element.62.refs_8_, bf16[1024,1408]{1,0:T(8,128)(2,1)} %after.27.refs_0_, bf16[1024,1408]{1,0:T(8,128)(2,1)} %get-tuple-element.72.px), kind=kOutput, calls=%fused_computation.5 | convolution fusion | flops 11825577984 | bytes 19922944 | tf_op jit(solution)/shard_map/dot_general | solution.py:34
  424.1 3.0 add_convert_fusion.4
  431.9 1.9 slice.577.refs_3_
  439.9 7.7 %collective-permute-done.23 = bf16[2,1,128,2048]{3,2,0,1:T(8,128)(2,1)S(1)} collective-permute-done((bf16[2,1,128,2048]{3,2,0,1:T(8,128)(2,1)}, bf16[2,1,128,2048]{3,2,0,1:T(8,128)(2,1)S(1)}, u32[]{:S(2)}, u32[]{:S(2)}) %collective-permute-start.23) | collective-permute-done | bytes 1048608 | tf_op jit(solution)/shard_map/ppermute | solution.py:606
  447.5 2.0 collective-permute-done.24
  452.1 2.6 fusion.19
  462.7 17.3 %back_project.3 = bf16[1024,2048]{1,0:T(8,128)(2,1)} custom-call(bf16[2048,1024]{1,0:T(8,128)(2,1)} %get-tuple-element.67.dz, bf16[1024,1408]{1,0:T(8,128)(2,1)} %after.30.px, bf16[2048,1024]{1,0:T(8,128)(2,1)} %all-gather.6.cloned.1.call-done.refs_9_.w_z, bf16[2048,1408]{1,0:T(8,128)(2,1)} %all-gather.4.cloned.1.call-done.refs_8_.w_x), custom_call_target="tpu_custom_call" | custom-call | tf_op jit(solution)/shard_map/back_project/pallas_call | solution.py:596
  481.3 2.3 concatenate.311.refs_2_
  483.6 2.7 fusion.49
  495.5 2.3 collective-permute-done.37
  497.8 2.9 collective-permute-start.38
  500.7 1.9 collective-permute-done.38
  517.6 2.0 add_convert_fusion.3
  531.7 7.4 %collective-permute-done.43 = bf16[64,1408]{1,0:T(8,128)(2,1)S(1)} collective-permute-done((bf16[64,1408]{1,0:T(8,128)(2,1)S(1)}, bf16[64,1408]{1,0:T(8,128)(2,1)S(1)}, u32[]{:S(2)}, u32[]{:S(2)}) %collective-permute-start.43) | collective-permute-done | bytes 180256 | tf_op jit(solution)/shard_map/ppermute | solution.py:606
  546.3 1.8 collective-permute-start.46
  550.1 2.7 collective-permute-start.47
  555.5 2.9 collective-permute-done.48
  559.3 5.1 fusion.11
  569.9 4.2 multiply_add_fusion.2
  574.2 4.6 multiply_add_fusion
  (461 shorter events, 142.8 us)
Async XLA Ops:
  7.2 117.8 %all-gather.4.cloned.1.call-start = ((), (), s32[]{:S(2)}) async-start(), calls=%async_computation.3 | async-start | bytes 6488064 | tf_op jit(solution)/shard_map/all_gather | solution.py:756
  10.7 8.4 %collective-permute-start.7 = (bf16[64,1408]{1,0:T(8,128)(2,1)S(1)}, bf16[64,1408]{1,0:T(8,128)(2,1)S(1)}, u32[]{:S(2)}, u32[]{:S(2)}) collective-permute-start(bf16[64,1408]{1,0:T(8,128)(2,1)S(1)} %get-tuple-element.184), channel_id=1, source_target_pairs={{0,1},{1,0},{2,3},{3,2},{4,5},{5,4},{6,7},{7,6},{8,9},{9,8},{10,11... | collective-permute-start | bytes 540680 | tf_op jit(solution)/shard_map/ppermute | solution.py:606
  13.8 9.9 %collective-permute-start.8 = (bf16[64,1408]{1,0:T(8,128)(2,1)S(1)}, bf16[64,1408]{1,0:T(8,128)(2,1)S(1)}, u32[]{:S(2)}, u32[]{:S(2)}) collective-permute-start(bf16[64,1408]{1,0:T(8,128)(2,1)S(1)} %get-tuple-element.183), channel_id=1, source_target_pairs={{0,2},{1,3},{2,0},{3,1},{4,6},{5,7},{6,4},{7,5},{8,10},{9,11},{10,... | collective-permute-start | bytes 540680 | tf_op jit(solution)/shard_map/ppermute | solution.py:606
  15.3 8.4 %collective-permute-start.9 = (bf16[64,1408]{1,0:T(8,128)(2,1)S(1)}, bf16[64,1408]{1,0:T(8,128)(2,1)S(1)}, u32[]{:S(2)}, u32[]{:S(2)}) collective-permute-start(bf16[64,1408]{1,0:T(8,128)(2,1)S(1)} %get-tuple-element.182), channel_id=1, source_target_pairs={{0,3},{1,2},{2,1},{3,0},{4,7},{5,6},{6,5},{7,4},{8,11},{9,10},{10,... | collective-permute-start | bytes 540680 | tf_op jit(solution)/shard_map/ppermute | solution.py:606
  27.7 164.7 %all-gather.6.cloned.1.call-start = ((), (), s32[]{:S(2)}) async-start(), calls=%async_computation.4 | async-start | bytes 4718592 | tf_op jit(solution)/shard_map/all_gather | solution.py:761
  27.8 23.8 %collective-permute-start.1 = (bf16[256,2048]{1,0:T(8,128)(2,1)S(1)}, bf16[256,2048]{1,0:T(8,128)(2,1)S(1)}, u32[]{:S(2)}, u32[]{:S(2)}) collective-permute-start(bf16[256,2048]{1,0:T(8,128)(2,1)S(1)} %copy-done.13), channel_id=1, source_target_pairs={{0,1},{1,0},{2,3},{3,2},{4,5},{5,4},{6,7},{7,6},{8,9},{9,8},{10,11... | collective-permute-start | bytes 3145736 | tf_op jit(solution)/shard_map/ppermute | solution.py:606
  29.0 23.9 %collective-permute-start.4 = (bf16[256,2048]{1,0:T(8,128)(2,1)S(1)}, bf16[256,2048]{1,0:T(8,128)(2,1)}, u32[]{:S(2)}, u32[]{:S(2)}) collective-permute-start(bf16[256,2048]{1,0:T(8,128)(2,1)S(1)} %copy-done.12), channel_id=1, source_target_pairs={{0,2},{1,3},{2,0},{3,1},{4,6},{5,7},{6,4},{7,5},{8,10},{9,11},{10,... | collective-permute-start | bytes 3145736 | tf_op jit(solution)/shard_map/ppermute | solution.py:606
  54.1 9.8 %collective-permute-start.15 = (bf16[64,2048]{1,0:T(8,128)(2,1)S(1)}, bf16[64,2048]{1,0:T(8,128)(2,1)S(1)}, u32[]{:S(2)}, u32[]{:S(2)}) collective-permute-start(bf16[64,2048]{1,0:T(8,128)(2,1)S(1)} %get-tuple-element.168), channel_id=1, source_target_pairs={{0,3},{1,2},{2,1},{3,0},{4,7},{5,6},{6,5},{7,4},{8,11},{9,10},{10,... | collective-permute-start | bytes 786440 | tf_op jit(solution)/shard_map/ppermute | solution.py:606
  55.3 11.4 %collective-permute-start.16 = (bf16[64,2048]{1,0:T(8,128)(2,1)S(1)}, bf16[64,2048]{1,0:T(8,128)(2,1)S(1)}, u32[]{:S(2)}, u32[]{:S(2)}) collective-permute-start(bf16[64,2048]{1,0:T(8,128)(2,1)S(1)} %get-tuple-element.167), channel_id=1, source_target_pairs={{0,2},{1,3},{2,0},{3,1},{4,6},{5,7},{6,4},{7,5},{8,10},{9,11},{10,... | collective-permute-start | bytes 786440 | tf_op jit(solution)/shard_map/ppermute | solution.py:606
  56.8 9.9 %collective-permute-start.17 = (bf16[64,2048]{1,0:T(8,128)(2,1)S(1)}, bf16[64,2048]{1,0:T(8,128)(2,1)S(1)}, u32[]{:S(2)}, u32[]{:S(2)}) collective-permute-start(bf16[64,2048]{1,0:T(8,128)(2,1)S(1)} %get-tuple-element.166), channel_id=1, source_target_pairs={{0,1},{1,0},{2,3},{3,2},{4,5},{5,4},{6,7},{7,6},{8,9},{9,8},{10,11... | collective-permute-start | bytes 786440 | tf_op jit(solution)/shard_map/ppermute | solution.py:606
  68.9 123.5 %all-gather.8.cloned.1.call-start = ((), (), s32[]{:S(2)}) async-start(), calls=%async_computation.5 | async-start | bytes 4718592 | tf_op jit(solution)/shard_map/all_gather | solution.py:762
  69.6 385.1 %reduce-scatter.6.cloned.1.call-start = ((), (), s32[]{:S(2)}) async-start(), calls=%async_computation.7 | async-start | bytes 4718592 | tf_op jit(solution)/shard_map/reduce_scatter | solution.py:791
  69.7 26.1 %collective-permute-start = (bf16[256,2048]{1,0:T(8,128)(2,1)S(1)}, bf16[256,2048]{1,0:T(8,128)(2,1)S(1)}, u32[]{:S(2)}, u32[]{:S(2)}) collective-permute-start(bf16[256,2048]{1,0:T(8,128)(2,1)S(1)} %copy-done.13), channel_id=1, source_target_pairs={{0,2},{1,3},{2,0},{3,1},{4,6},{5,7},{6,4},{7,5},{8,10},{9,11},{10,... | collective-permute-start | bytes 3145736 | tf_op jit(solution)/shard_map/ppermute | solution.py:606
  70.4 26.1 %collective-permute-start.3 = (bf16[256,2048]{1,0:T(8,128)(2,1)S(1)}, bf16[256,2048]{1,0:T(8,128)(2,1)S(1)}, u32[]{:S(2)}, u32[]{:S(2)}) collective-permute-start(bf16[256,2048]{1,0:T(8,128)(2,1)S(1)} %copy-done.12), channel_id=1, source_target_pairs={{0,1},{1,0},{2,3},{3,2},{4,5},{5,4},{6,7},{7,6},{8,9},{9,8},{10,11... | collective-permute-start | bytes 3145736 | tf_op jit(solution)/shard_map/ppermute | solution.py:606
  71.9 45.0 %collective-permute-start.2 = (bf16[256,2048]{1,0:T(8,128)(2,1)S(1)}, bf16[256,2048]{1,0:T(8,128)(2,1)S(1)}, u32[]{:S(2)}, u32[]{:S(2)}) collective-permute-start(bf16[256,2048]{1,0:T(8,128)(2,1)S(1)} %copy-done.26), channel_id=1, source_target_pairs={{0,2},{1,3},{2,0},{3,1},{4,6},{5,7},{6,4},{7,5},{8,10},{9,11},{10,... | collective-permute-start | bytes 3145736 | tf_op jit(solution)/shard_map/ppermute | solution.py:606
  72.5 45.4 %collective-permute-start.5 = (bf16[256,2048]{1,0:T(8,128)(2,1)}, bf16[256,2048]{1,0:T(8,128)(2,1)}, u32[]{:S(2)}, u32[]{:S(2)}) collective-permute-start(bf16[256,2048]{1,0:T(8,128)(2,1)} %collective-permute-done.4.refs_6_.refs_3_), channel_id=1, source_target_pairs={{0,1},{1,0},{2,3},{3,2},{4,5},{5,4},{6,7},{7,6},{8,9},{9,8},{10,11... | collective-permute-start | bytes 3145736 | tf_op jit(solution)/shard_map/ppermute | solution.py:606
  120.6 28.7 %collective-permute-start.13 = (bf16[256,2048]{1,0:T(8,128)(2,1)S(1)}, bf16[256,2048]{1,0:T(8,128)(2,1)S(1)}, u32[]{:S(2)}, u32[]{:S(2)}) collective-permute-start(bf16[256,2048]{1,0:T(8,128)(2,1)S(1)} %get-tuple-element.135.refs_4_), channel_id=1, source_target_pairs={{0,2},{1,3},{2,0},{3,1},{4,6},{5,7},{6,4},{7,5},{8,10},{9,11},{10,... | collective-permute-start | bytes 3145736 | tf_op jit(solution)/shard_map/ppermute | solution.py:606
  121.5 29.2 %collective-permute-start.6 = (bf16[256,2048]{1,0:T(8,128)(2,1)}, bf16[256,2048]{1,0:T(8,128)(2,1)S(1)}, u32[]{:S(2)}, u32[]{:S(2)}) collective-permute-start(bf16[256,2048]{1,0:T(8,128)(2,1)} %get-tuple-element.136.refs_0_), channel_id=1, source_target_pairs={{0,1},{1,0},{2,3},{3,2},{4,5},{5,4},{6,7},{7,6},{8,9},{9,8},{10,11... | collective-permute-start | bytes 3145736 | tf_op jit(solution)/shard_map/ppermute | solution.py:606
  122.5 67.9 %collective-permute-start.12 = (bf16[256,2048]{1,0:T(8,128)(2,1)S(1)}, bf16[256,2048]{1,0:T(8,128)(2,1)}, u32[]{:S(2)}, u32[]{:S(2)}) collective-permute-start(bf16[256,2048]{1,0:T(8,128)(2,1)S(1)} %get-tuple-element.135.refs_4_), channel_id=1, source_target_pairs={{0,1},{1,0},{2,3},{3,2},{4,5},{5,4},{6,7},{7,6},{8,9},{9,8},{10,11... | collective-permute-start | bytes 3145736 | tf_op jit(solution)/shard_map/ppermute | solution.py:606
  123.8 67.5 %collective-permute-start.10 = (bf16[256,2048]{1,0:T(8,128)(2,1)}, bf16[256,2048]{1,0:T(8,128)(2,1)}, u32[]{:S(2)}, u32[]{:S(2)}) collective-permute-start(bf16[256,2048]{1,0:T(8,128)(2,1)} %get-tuple-element.136.refs_0_), channel_id=1, source_target_pairs={{0,2},{1,3},{2,0},{3,1},{4,6},{5,7},{6,4},{7,5},{8,10},{9,11},{10,... | collective-permute-start | bytes 3145736 | tf_op jit(solution)/shard_map/ppermute | solution.py:606
  150.3 40.1 %collective-permute-start.14 = (bf16[256,2048]{1,0:T(8,128)(2,1)}, bf16[256,2048]{1,0:T(8,128)(2,1)S(1)}, u32[]{:S(2)}, u32[]{:S(2)}) collective-permute-start(bf16[256,2048]{1,0:T(8,128)(2,1)} %after.22.refs_6_), channel_id=1, source_target_pairs={{0,1},{1,0},{2,3},{3,2},{4,5},{5,4},{6,7},{7,6},{8,9},{9,8},{10,11... | collective-permute-start | bytes 3145736 | tf_op jit(solution)/shard_map/ppermute | solution.py:606
  151.7 39.7 %collective-permute-start.11 = (bf16[256,2048]{1,0:T(8,128)(2,1)}, bf16[256,2048]{1,0:T(8,128)(2,1)S(1)}, u32[]{:S(2)}, u32[]{:S(2)}) collective-permute-start(bf16[256,2048]{1,0:T(8,128)(2,1)} %after.20.refs_1_), channel_id=1, source_target_pairs={{0,2},{1,3},{2,0},{3,1},{4,6},{5,7},{6,4},{7,5},{8,10},{9,11},{10,... | collective-permute-start | bytes 3145736 | tf_op jit(solution)/shard_map/ppermute | solution.py:606
  221.4 4.3 collective-permute-start.19
  223.9 5.2 collective-permute-start.20
  266.8 187.9 %reduce-scatter.4.cloned.1.call-start = ((), (), s32[]{:S(2)}) async-start(), calls=%async_computation.6 | async-start | bytes 4718592 | tf_op jit(solution)/shard_map/reduce_scatter | solution.py:791
  291.5 230.0 %reduce-scatter.8.cloned.1.call-start = ((), (), s32[]{:S(2)}) async-start(), calls=%async_computation.8 | async-start | bytes 6488064 | tf_op jit(solution)/shard_map/reduce_scatter | solution.py:791
  291.5 63.7 %collective-permute-start.21 = (bf16[2,2,128,2048]{3,2,1,0:T(8,128)(2,1)}, bf16[2,2,128,2048]{3,2,1,0:T(8,128)(2,1)}, u32[]{:S(2)}, u32[]{:S(2)}) collective-permute-start(bf16[2,2,128,2048]{3,2,1,0:T(8,128)(2,1)} %pad_maximum_fusion.1.refs_1_), channel_id=1, source_target_pairs={{0,1},{1,0},{2,3},{3,2},{4,5},{5,4},{6,7},{7,6},{8,9},{9,8},{10,11... | collective-permute-start | bytes 6291464 | tf_op jit(solution)/shard_map/ppermute | solution.py:606
  292.3 62.9 %collective-permute-start.22 = (bf16[2,2,128,2048]{3,2,1,0:T(8,128)(2,1)}, bf16[2,2,128,2048]{3,2,1,0:T(8,128)(2,1)}, u32[]{:S(2)}, u32[]{:S(2)}) collective-permute-start(bf16[2,2,128,2048]{3,2,1,0:T(8,128)(2,1)} %get-tuple-element.119.refs_2_), channel_id=1, source_target_pairs={{0,2},{1,3},{2,0},{3,1},{4,6},{5,7},{6,4},{7,5},{8,10},{9,11},{10,... | collective-permute-start | bytes 6291464 | tf_op jit(solution)/shard_map/ppermute | solution.py:606
  352.7 47.9 %collective-permute-start.25 = (bf16[1,2,128,2048]{3,2,1,0:T(8,128)(2,1)}, bf16[1,2,128,2048]{3,2,1,0:T(8,128)(2,1)S(1)}, u32[]{:S(2)}, u32[]{:S(2)}) collective-permute-start(bf16[1,2,128,2048]{3,2,1,0:T(8,128)(2,1)} %pad_maximum_fusion.4.refs_0_), channel_id=1, source_target_pairs={{0,1},{1,0},{2,3},{3,2},{4,5},{5,4},{6,7},{7,6},{8,9},{9,8},{10,11... | collective-permute-start | bytes 3145736 | tf_op jit(solution)/shard_map/ppermute | solution.py:606
  354.4 46.2 %collective-permute-start.26 = (bf16[1,2,128,2048]{3,2,1,0:T(8,128)(2,1)S(1)}, bf16[1,2,128,2048]{3,2,1,0:T(8,128)(2,1)S(1)}, u32[]{:S(2)}, u32[]{:S(2)}) collective-permute-start(bf16[1,2,128,2048]{3,2,1,0:T(8,128)(2,1)S(1)} %concatenate.308.refs_1_), channel_id=1, source_target_pairs={{0,2},{1,3},{2,0},{3,1},{4,6},{5,7},{6,4},{7,5},{8,10},{9,11},{10,... | collective-permute-start | bytes 3145736 | tf_op jit(solution)/shard_map/ppermute | solution.py:606
  422.5 25.0 %collective-permute-start.23 = (bf16[2,1,128,2048]{3,2,0,1:T(8,128)(2,1)}, bf16[2,1,128,2048]{3,2,0,1:T(8,128)(2,1)S(1)}, u32[]{:S(2)}, u32[]{:S(2)}) collective-permute-start(bf16[2,1,128,2048]{3,2,0,1:T(8,128)(2,1)} %get-tuple-element.232), channel_id=1, source_target_pairs={{0,2},{1,3},{2,0},{3,1},{4,6},{5,7},{6,4},{7,5},{8,10},{9,11},{10,... | collective-permute-start | bytes 3145736 | tf_op jit(solution)/shard_map/ppermute | solution.py:606
  423.8 25.7 %collective-permute-start.24 = (bf16[2,1,128,2048]{3,2,0,1:T(8,128)(2,1)}, bf16[2,1,128,2048]{3,2,0,1:T(8,128)(2,1)S(1)}, u32[]{:S(2)}, u32[]{:S(2)}) collective-permute-start(bf16[2,1,128,2048]{3,2,0,1:T(8,128)(2,1)} %get-tuple-element.132), channel_id=1, source_target_pairs={{0,1},{1,0},{2,3},{3,2},{4,5},{5,4},{6,7},{7,6},{8,9},{9,8},{10,11... | collective-permute-start | bytes 3145736 | tf_op jit(solution)/shard_map/ppermute | solution.py:606
  436.6 43.4 %collective-permute-start.28 = (bf16[1,1,128,2048]{3,2,1,0:T(8,128)(2,1)}, bf16[1,1,128,2048]{3,2,1,0:T(8,128)(2,1)S(1)}, u32[]{:S(2)}, u32[]{:S(2)}) collective-permute-start(bf16[1,1,128,2048]{3,2,1,0:T(8,128)(2,1)} %slice.577.refs_3_), channel_id=1, source_target_pairs={{0,1},{1,0},{2,3},{3,2},{4,5},{5,4},{6,7},{7,6},{8,9},{9,8},{10,11... | collective-permute-start | bytes 1572872 | tf_op jit(solution)/shard_map/ppermute | solution.py:606
  438.3 41.8 %collective-permute-start.27 = (bf16[1,1,128,2048]{3,2,1,0:T(8,128)(2,1)}, bf16[1,1,128,2048]{3,2,1,0:T(8,128)(2,1)S(1)}, u32[]{:S(2)}, u32[]{:S(2)}) collective-permute-start(bf16[1,1,128,2048]{3,2,1,0:T(8,128)(2,1)} %slice.576.refs_2_), channel_id=1, source_target_pairs={{0,2},{1,3},{2,0},{3,1},{4,6},{5,7},{6,4},{7,5},{8,10},{9,11},{10,... | collective-permute-start | bytes 1572872 | tf_op jit(solution)/shard_map/ppermute | solution.py:606
  457.8 22.3 %collective-permute-start.29 = (bf16[64,2048]{1,0:T(8,128)(2,1)S(1)}, bf16[64,2048]{1,0:T(8,128)(2,1)S(1)}, u32[]{:S(2)}, u32[]{:S(2)}) collective-permute-start(bf16[64,2048]{1,0:T(8,128)(2,1)S(1)} %get-tuple-element.160), channel_id=1, source_target_pairs={{0,1},{1,0},{2,3},{3,2},{4,5},{5,4},{6,7},{7,6},{8,9},{9,8},{10,11... | collective-permute-start | bytes 786440 | tf_op jit(solution)/shard_map/ppermute | solution.py:606
  458.3 21.9 %collective-permute-start.30 = (bf16[64,2048]{1,0:T(8,128)(2,1)S(1)}, bf16[64,2048]{1,0:T(8,128)(2,1)S(1)}, u32[]{:S(2)}, u32[]{:S(2)}) collective-permute-start(bf16[64,2048]{1,0:T(8,128)(2,1)S(1)} %get-tuple-element.161), channel_id=1, source_target_pairs={{0,2},{1,3},{2,0},{3,1},{4,6},{5,7},{6,4},{7,5},{8,10},{9,11},{10,... | collective-permute-start | bytes 786440 | tf_op jit(solution)/shard_map/ppermute | solution.py:606
  459.9 20.3 %collective-permute-start.31 = (bf16[64,2048]{1,0:T(8,128)(2,1)S(1)}, bf16[64,2048]{1,0:T(8,128)(2,1)S(1)}, u32[]{:S(2)}, u32[]{:S(2)}) collective-permute-start(bf16[64,2048]{1,0:T(8,128)(2,1)S(1)} %get-tuple-element.159), channel_id=1, source_target_pairs={{0,3},{1,2},{2,1},{3,0},{4,7},{5,6},{6,5},{7,4},{8,11},{9,10},{10,... | collective-permute-start | bytes 786440 | tf_op jit(solution)/shard_map/ppermute | solution.py:606
  487.4 30.2 %collective-permute-start.32 = (bf16[1,2,128,2048]{3,2,1,0:T(8,128)(2,1)}, bf16[1,2,128,2048]{3,2,1,0:T(8,128)(2,1)S(1)}, u32[]{:S(2)}, u32[]{:S(2)}) collective-permute-start(bf16[1,2,128,2048]{3,2,1,0:T(8,128)(2,1)} %pad_maximum_fusion.5.refs_1_), channel_id=1, source_target_pairs={{0,1},{1,0},{2,3},{3,2},{4,5},{5,4},{6,7},{7,6},{8,9},{9,8},{10,11... | collective-permute-start | bytes 3145736 | tf_op jit(solution)/shard_map/ppermute | solution.py:606
  487.8 33.6 %collective-permute-start.34 = (bf16[1,2,128,2048]{3,2,1,0:T(8,128)(2,1)}, bf16[1,2,128,2048]{3,2,1,0:T(8,128)(2,1)S(1)}, u32[]{:S(2)}, u32[]{:S(2)}) collective-permute-start(bf16[1,2,128,2048]{3,2,1,0:T(8,128)(2,1)} %concatenate.311.refs_2_), channel_id=1, source_target_pairs={{0,2},{1,3},{2,0},{3,1},{4,6},{5,7},{6,4},{7,5},{8,10},{9,11},{10,... | collective-permute-start | bytes 3145736 | tf_op jit(solution)/shard_map/ppermute | solution.py:606
  497.8 4.8 collective-permute-start.38
  502.6 4.8 collective-permute-start.39
  520.7 24.2 %collective-permute-start.33 = (bf16[1,1,128,2048]{3,2,1,0:T(8,128)(2,1)}, bf16[1,1,128,2048]{3,2,1,0:T(8,128)(2,1)}, u32[]{:S(2)}, u32[]{:S(2)}) collective-permute-start(bf16[1,1,128,2048]{3,2,1,0:T(8,128)(2,1)} %slice.588), channel_id=1, source_target_pairs={{0,2},{1,3},{2,0},{3,1},{4,6},{5,7},{6,4},{7,5},{8,10},{9,11},{10,... | collective-permute-start | bytes 1572872 | tf_op jit(solution)/shard_map/ppermute | solution.py:606
  523.8 7.9 %collective-permute-start.42 = (bf16[64,1408]{1,0:T(8,128)(2,1)S(1)}, bf16[64,1408]{1,0:T(8,128)(2,1)S(1)}, u32[]{:S(2)}, u32[]{:S(2)}) collective-permute-start(bf16[64,1408]{1,0:T(8,128)(2,1)S(1)} %get-tuple-element.178), channel_id=1, source_target_pairs={{0,3},{1,2},{2,1},{3,0},{4,7},{5,6},{6,5},{7,4},{8,11},{9,10},{10,... | collective-permute-start | bytes 540680 | tf_op jit(solution)/shard_map/ppermute | solution.py:606
  525.3 13.8 %collective-permute-start.43 = (bf16[64,1408]{1,0:T(8,128)(2,1)S(1)}, bf16[64,1408]{1,0:T(8,128)(2,1)S(1)}, u32[]{:S(2)}, u32[]{:S(2)}) collective-permute-start(bf16[64,1408]{1,0:T(8,128)(2,1)S(1)} %get-tuple-element.179), channel_id=1, source_target_pairs={{0,2},{1,3},{2,0},{3,1},{4,6},{5,7},{6,4},{7,5},{8,10},{9,11},{10,... | collective-permute-start | bytes 540680 | tf_op jit(solution)/shard_map/ppermute | solution.py:606
  525.7 13.4 %collective-permute-start.44 = (bf16[64,1408]{1,0:T(8,128)(2,1)S(1)}, bf16[64,1408]{1,0:T(8,128)(2,1)S(1)}, u32[]{:S(2)}, u32[]{:S(2)}) collective-permute-start(bf16[64,1408]{1,0:T(8,128)(2,1)S(1)} %get-tuple-element.177), channel_id=1, source_target_pairs={{0,1},{1,0},{2,3},{3,2},{4,5},{5,4},{6,7},{7,6},{8,9},{9,8},{10,11... | collective-permute-start | bytes 540680 | tf_op jit(solution)/shard_map/ppermute | solution.py:606
  529.9 18.3 %collective-permute-start.35 = (bf16[1,1,128,2048]{3,2,1,0:T(8,128)(2,1)}, bf16[1,1,128,2048]{3,2,1,0:T(8,128)(2,1)}, u32[]{:S(2)}, u32[]{:S(2)}) collective-permute-start(bf16[1,1,128,2048]{3,2,1,0:T(8,128)(2,1)} %slice.590), channel_id=1, source_target_pairs={{0,1},{1,0},{2,3},{3,2},{4,5},{5,4},{6,7},{7,6},{8,9},{9,8},{10,11... | collective-permute-start | bytes 1572872 | tf_op jit(solution)/shard_map/ppermute | solution.py:606
  550.1 4.6 collective-permute-start.47
  558.4 6.1 %collective-permute-start.49 = (f32[24,128]{1,0:T(8,128)S(1)}, f32[24,128]{1,0:T(8,128)S(1)}, u32[]{:S(2)}, u32[]{:S(2)}) collective-permute-start(f32[24,128]{1,0:T(8,128)S(1)} %add.297), channel_id=1, source_target_pairs={{0,2},{1,3},{2,0},{3,1},{4,6},{5,7},{6,4},{7,5},{8,10},{9,11},{10,... | collective-permute-start | bytes 36872 | tf_op jit(solution)/shard_map/ppermute | solution.py:606
  (96 other events, 420.2 us)
Sparse Core Ops, SparseCore 0:
  27.8 60.7 all-gather.3
  90.2 45.8 all-gather.5
  137.7 45.8 all-gather.7
  266.9 49.7 reduce-scatter.5
  318.8 48.1 reduce-scatter.3
  421.3 64.8 reduce-scatter.7

commit v4 on v3

v4 whole, which is shorter than its diff:
```python
import functools

import jax
import jax.numpy as jnp
from jax import lax
from jax.experimental import pallas as pl
from jax.experimental.pallas import tpu as pltpu
from jax.sharding import PartitionSpec as P

D = 2048
HEADS = 64
HEADDIM = 64
STATE = 128
CONV = 4
BLOCK = 256
MICRO = 2
INNER = 4096
CH = 4352
NORM_EPS = 1e-05
LEARN_RATE = 0.004
BETA_ONE = 0.9
BETA_TWO = 0.95
FIX_ONE = 1.0 - 0.9**10
FIX_TWO = 1.0 - 0.95**10
ADAM_EPS = 1e-08
WEIGHT_DECAY = 0.1
CLIP_NORM = 1.0
BF = jnp.bfloat16
F32 = jnp.float32
ALL = ("dp", "seq")


def dot(a, b, dims, out=F32):
    return lax.dot_general(a, b, (dims, ((), ())), preferred_element_type=out)


NN = ((1,), (0,))
NT = ((1,), (1,))
TN = ((0,), (0,))
LANES = 128
PAIR = 2 * HEADDIM
VMEM = 56 * 1024 * 1024
SLOT = 16
TINY = 1e-37
CAP = 85.0


def iota2(shape, dim):
    return lax.broadcasted_iota(jnp.int32, shape, dim)


def tree(value, rows=8):
    while value.shape[0] > rows:
        half = value.shape[0] // 2
        value = value[:half] + value[half:]
    return value


def thirds(value):
    high = value.astype(BF).astype(F32)
    rest = value - high
    mid = rest.astype(BF).astype(F32)
    return high, mid, (rest - mid).astype(BF).astype(F32)


def running_sum(values, reverse):
    row, col = iota2((BLOCK, BLOCK), 0), iota2((BLOCK, BLOCK), 1)
    ones = jnp.where(row >= col if reverse else row <= col, 1.0, 0.0).astype(BF)
    sums = dot(jnp.concatenate(thirds(values), axis=0).astype(BF), ones, NN)
    return sums[:SLOT] + sums[SLOT : 2 * SLOT] + sums[2 * SLOT :]


def step_rows(raw, heads, masks):
    lifted = raw.astype(F32).T[:SLOT] + heads[:, 0:1]
    dt = jnp.maximum(lifted, 0.0) + jnp.log1p(jnp.exp(-jnp.abs(lifted)))
    cum = running_sum(dt * heads[:, 1:2], False)
    entry = jnp.exp(cum) * masks[1:2, :]
    dt_end = dt * jnp.exp(cum[:, BLOCK - 1 : BLOCK] - cum) * masks[2:3, :]
    return lifted, dt, cum, entry, dt_end


def two(value):
    high = value.astype(BF).astype(F32)
    return [high, value - high]


def as_columns(gap_rows, entry, dt_end):
    ones = jnp.where(iota2((SLOT, BLOCK), 0) < 3, 1.0, 0.0)
    return jnp.concatenate([*thirds(gap_rows), ones, *two(entry), *two(dt_end)], axis=0).T.astype(BF)


def gap_right_init(right, hl):
    row = iota2((3 * SLOT, BLOCK), 0)
    for h in range(hl):
        right[0 : 3 * SLOT, h * BLOCK : (h + 1) * BLOCK] = jnp.where((row & (SLOT - 1)) == h, 1.0, 0.0).astype(BF)


def gap_right_fill(right, values, hl):
    row = iota2((SLOT, BLOCK), 0)
    high, mid, low = thirds(values)
    for h in range(hl):
        one = slice(h, h + 1)
        slab = jnp.where(row == 0, high[one], jnp.where(row == 1, mid[one], jnp.where(row == 2, low[one], 0.0)))
        right[3 * SLOT :, h * BLOCK : (h + 1) * BLOCK] = slab.astype(BF)


def head_spread_init(spreads, hl):
    row, col = iota2(spreads.shape, 0), iota2(spreads.shape, 1)
    head = jnp.where(col < hl * HEADDIM, col, col - hl * HEADDIM) // HEADDIM
    slot = jnp.where(col < hl * HEADDIM, 2, 3)
    spreads[...] = jnp.where(((row & (SLOT - 1)) == head) & (row // (2 * SLOT) == slot), 1.0, 0.0).astype(BF)


def stacked(left, pair_values):
    zero = jnp.zeros_like(pair_values)
    return jnp.concatenate([jnp.where(left, pair_values, zero), jnp.where(left, zero, pair_values)], axis=0)


def conv_chunk(window, conv_w, valid, lo, hi):
    out = conv_w[CONV : CONV + 1, lo:hi] + conv_w[CONV - 1 : CONV, lo:hi] * window[8 : 8 + BLOCK, lo:hi]
    for tap in range(CONV - 1):
        out += conv_w[tap : tap + 1, lo:hi] * (window[5 + tap : 5 + tap + BLOCK, lo:hi] * valid[tap])
    return out


def spread(aux_v, at):
    return jnp.broadcast_to(aux_v[:, at : at + 1], (BLOCK, LANES))


def forward_kernel(place, proj, conv_w, skip, heads, aux, masks, y_out, s_out, act, slope, window, state, right, carried, spreads, *, hl):
    width = hl * HEADDIM
    conv_width = width + 2 * STATE

    @pl.when(pl.program_id(1) == 0)
    def _():
        window[0:8, :] = jnp.zeros((8, conv_width), F32)
        state[...] = jnp.zeros(state.shape, F32)
        gap_right_init(right, hl)
        head_spread_init(spreads, hl)

    aux_v = aux[...]
    valid = [spread(aux_v, tap) for tap in range(CONV - 1)]
    for lo in range(0, conv_width, LANES):
        hi = lo + LANES
        window[8 : 8 + BLOCK, lo:hi] = proj[:, lo:hi].astype(F32)
        out = conv_chunk(window, conv_w, valid, lo, hi)
        sig = jax.nn.sigmoid(out)
        silu = out * sig
        act[:, lo:hi] = silu.astype(BF)
        slope[:, lo:hi] = (sig + silu * (1.0 - sig)).astype(BF)
    window[0:8, :] = window[BLOCK : BLOCK + 8, :]

    _, dt, cum, entry, dt_end = step_rows(proj[:, conv_width : conv_width + LANES], heads[...], masks)
    columns = as_columns(cum, entry, dt_end)
    gaps = columns[:, : 4 * SLOT]
    gap_right_fill(right, jnp.log(jnp.maximum(dt, TINY)) - cum, hl)
    bm, cm = act[:, width : width + STATE], act[:, width + STATE :]
    same = (aux_v[:, 3:4] == masks[0:1, :]) & (iota2((BLOCK, BLOCK), 0) >= iota2((BLOCK, BLOCK), 1))
    inner = jnp.where(same, dot(cm, bm, NT), 0.0)
    left = iota2((BLOCK, PAIR), 1) < HEADDIM
    top = iota2((PAIR, STATE), 0) < HEADDIM
    last = entry[:, BLOCK - 1 : BLOCK]
    s_out[0] = state[...].astype(BF)
    carried[...] = dot(columns, spreads[...], NN)
    carried[:, :width] = carried[:, :width] * dot(cm, s_out[0], NT)
    for pair in range(hl // 2):
        first = 2 * pair
        lo, hi = pair * PAIR, (pair + 1) * PAIR
        xp = act[:, lo:hi]
        mix = []
        for h in (first, first + 1):
            decay = jnp.exp(jnp.minimum(dot(gaps, right[:, h * BLOCK : (h + 1) * BLOCK], NN), CAP))
            mix.append((inner * decay).astype(BF))
        xf = xp.astype(F32)
        y = dot(jnp.concatenate(mix, axis=1), stacked(left, xp), NN)
        y += carried[:, lo:hi] + skip[0:1, lo:hi] * xf
        y_out[:, lo:hi] = y.astype(BF)
        weighted = (xf * carried[:, width + lo : width + hi]).astype(BF)
        keep = jnp.where(top, last[first : first + 1], last[first + 1 : first + 2])
        state[lo:hi, :] = keep * state[lo:hi, :] + dot(weighted, bm, TN)


def backward_kernel(place, proj, conv_w, skip, heads, aux, masks, act, slope, dy, s_in, *refs, hl):
    dproj, dconv, dvec, dskip, dwin, grad_s, dcb, colsum, dkeep, right, carried, later_w, spreads, picks, sums, used, into = refs[-17:]
    width = hl * HEADDIM
    conv_width = width + 2 * STATE

    @pl.when(pl.program_id(0) == 0)
    def _():
        dconv[...] = jnp.zeros(dconv.shape, F32)
        dvec[...] = jnp.zeros(dvec.shape, F32)
        dskip[...] = jnp.zeros(dskip.shape, F32)
        dwin[BLOCK : BLOCK + 8, :] = jnp.zeros((8, conv_width), F32)
        grad_s[...] = jnp.zeros(grad_s.shape, F32)
        colsum[...] = jnp.zeros(colsum.shape, F32)
        dkeep[...] = jnp.zeros(dkeep.shape, F32)
        gap_right_init(right, hl)
        head_spread_init(spreads, hl)
        picks[...] = jnp.where(iota2(picks.shape, 0) == iota2(picks.shape, 1) // BLOCK, 1.0, 0.0).astype(BF)
        sums[...] = jnp.where(iota2(sums.shape, 0) == iota2(sums.shape, 1) // HEADDIM, 1.0, 0.0).astype(BF)

    aux_v = aux[...]
    lifted, dt, cum, entry, dt_end = step_rows(proj[:, conv_width : conv_width + LANES], heads[...], masks)
    a_neg = heads[:, 1:2]
    columns = as_columns(jnp.log(jnp.maximum(dt, TINY)) - cum, entry, dt_end)
    gaps = columns[:, : 4 * SLOT]
    gap_right_fill(right, cum, hl)
    bm, cm = act[:, width : width + STATE], act[:, width + STATE :]
    same = (aux_v[:, 3:4] == masks[0:1, :]) & (iota2((BLOCK, BLOCK), 0) <= iota2((BLOCK, BLOCK), 1))
    inner = jnp.where(same, dot(bm, cm, NT), 0.0)
    left = iota2((BLOCK, PAIR), 1) < HEADDIM
    top = iota2((PAIR, STATE), 0) < HEADDIM
    last = entry[:, BLOCK - 1 : BLOCK]
    d_row = jnp.zeros((SLOT, BLOCK), F32)
    d_b = jnp.zeros((BLOCK, STATE), F32)
    d_c = jnp.zeros((BLOCK, STATE), F32)
    spreaded = dot(columns, spreads[...], NN)
    carried[...] = spreaded
    later_w[:, :width] = dot(cm, s_in[0], NT)
    later_w[:, width:] = dot(bm, grad_s[...].astype(BF), NT)

    for pair in range(hl // 2):
        first = 2 * pair
        lo, hi = pair * PAIR, (pair + 1) * PAIR
        xp, dyp = act[:, lo:hi], dy[:, lo:hi]
        xf, dyf = xp.astype(F32), dyp.astype(F32)
        d_mix = dot(stacked(left, xp), dyp, NT)
        mix, pairwise = [], []
        d_inner = 0.0
        for at, h in enumerate((first, first + 1)):
            decay = jnp.exp(jnp.minimum(dot(gaps, right[:, h * BLOCK : (h + 1) * BLOCK], NN), CAP))
            mix.append((inner * decay).astype(BF))
            part = d_mix[at * BLOCK : (at + 1) * BLOCK] * decay
            d_inner += part
            part = (part * inner).astype(BF)
            pairwise.append(part)
            colsum[h : h + 1, :] = jnp.sum(tree(part.astype(F32)), axis=0, keepdims=True)
        d_row += dot(picks[:, first * BLOCK : (first + 2) * BLOCK], jnp.concatenate(pairwise, axis=1), NT)
        if pair == 0:
            dcb[...] = d_inner
        else:
            dcb[...] += d_inner
        later = grad_s[lo:hi, :]
        low = s_in[0, lo:hi, :]
        end_p = carried[:, width + lo : width + hi]
        from_end = later_w[:, width + lo : width + hi] * end_p
        dx = dot(jnp.concatenate(mix, axis=1), stacked(left, dyp), NN) + from_end + skip[0:1, lo:hi] * dyf
        dwin[0:BLOCK, lo:hi] = slope[:, lo:hi].astype(F32) * dx
        used[:, lo:hi] = (from_end * xf).astype(BF)
        entering = carried[:, lo:hi] * dyf
        into[:, lo:hi] = (entering * later_w[:, lo:hi]).astype(BF)
        entering = entering.astype(BF)
        dskip[:, lo:hi] += tree(xf * dyf)
        kept = later * low.astype(F32)
        dkeep[first : first + 1, :] = jnp.sum(tree(kept[:HEADDIM]), axis=0, keepdims=True)
        dkeep[first + 1 : first + 2, :] = jnp.sum(tree(kept[HEADDIM:]), axis=0, keepdims=True)
        weighted = (xf * end_p).astype(BF)
        d_b += dot(weighted, later.astype(BF), NN)
        d_c += dot(entering, low, NN)
        keep = jnp.where(top, last[first : first + 1], last[first + 1 : first + 2])
        grad_s[lo:hi, :] = dot(entering, cm, TN) + keep * later

    d_inner = jnp.where(same, dcb[...], 0.0).astype(BF)
    d_b += dot(d_inner, cm, NN)
    d_c += dot(d_inner, bm, TN)
    dwin[0:BLOCK, width : width + STATE] = slope[:, width : width + STATE].astype(F32) * d_b
    dwin[0:BLOCK, width + STATE :] = slope[:, width + STATE :].astype(F32) * d_c

    d_end = dot(sums[...], used[...], NT)
    through = d_row + d_end
    d_last = jnp.sum(d_end, axis=1, keepdims=True) + jnp.sum(dkeep[...], axis=1, keepdims=True) * last
    d_cum = dot(sums[...], into[...], NT) + colsum[...] - through
    d_cum += jnp.where(iota2((SLOT, BLOCK), 1) == BLOCK - 1, d_last, 0.0)
    d_a = running_sum(d_cum, True)
    sig = jax.nn.sigmoid(lifted)
    d_raw = through * jnp.where(dt > TINY, sig / jnp.maximum(dt, TINY), 1.0) + d_a * a_neg * sig
    d_raw = jnp.where(iota2((SLOT, BLOCK), 0) < hl, d_raw, 0.0)
    dproj[:, conv_width : conv_width + LANES] = jnp.concatenate([d_raw, jnp.zeros((LANES - SLOT, BLOCK), F32)], axis=0).T.astype(BF)
    lane = iota2((SLOT, LANES), 1)
    d_log = jnp.sum(d_a * dt, axis=1, keepdims=True) * a_neg
    dvec[...] += jnp.where(lane == 0, d_log, jnp.where(lane == 1, jnp.sum(d_raw, axis=1, keepdims=True), 0.0))

    valid = [spread(aux_v, 4 + tap) for tap in range(CONV - 1)]
    for lo in range(0, conv_width, LANES):
        hi = lo + LANES
        own = dwin[0:BLOCK, lo:hi]
        value = proj[:, lo:hi].astype(F32)
        grad = conv_w[CONV - 1 : CONV, lo:hi] * own
        dconv[CONV * 8 : CONV * 8 + 8, lo:hi] += tree(own)
        dconv[(CONV - 1) * 8 : CONV * 8, lo:hi] += tree(own * value)
        for tap in range(CONV - 1):
            ahead = CONV - 1 - tap
            moved = dwin[ahead : ahead + BLOCK, lo:hi] * valid[tap]
            grad += conv_w[tap : tap + 1, lo:hi] * moved
            dconv[tap * 8 : tap * 8 + 8, lo:hi] += tree(moved * value)
        dproj[:, lo:hi] = grad.astype(BF)
    dwin[BLOCK : BLOCK + 8, :] = dwin[0:8, :]


def segment_aux(segments):
    micro, length = segments.shape
    nb = length // BLOCK
    seg = segments.astype(F32)
    blocks = seg.reshape(micro, nb, BLOCK)
    prev = jnp.concatenate([jnp.full((micro, 1), -1.0, F32), blocks[:, :-1, -1]], axis=1)
    reach = range(CONV - 1, 0, -1)
    earlier = [jnp.pad(seg, ((0, 0), (by, 0)), constant_values=-1.0)[:, :length] == seg for by in reach]
    later = [jnp.pad(seg, ((0, 0), (0, by)), constant_values=-1.0)[:, by:] == seg for by in reach]
    columns = [c.astype(F32) for c in (*earlier, seg, *later, jnp.zeros_like(seg))]
    aux = jnp.stack(columns, axis=-1).reshape(micro * length, 8)
    zero = jnp.zeros_like(blocks)
    masks = [blocks, blocks == prev[:, :, None], blocks == blocks[:, :, -1:]] + [zero] * 5
    return aux, jnp.stack([m.astype(F32) for m in masks], axis=2).reshape(micro * nb * 8, BLOCK)


def head_columns(a_log, dt_bias):
    hl = a_log.shape[0]
    both = jnp.stack([dt_bias, -jnp.exp(a_log)], axis=1)
    return jnp.pad(both, ((0, SLOT - hl), (0, LANES - 2)))


def scan_forward(place, proj, conv_w, skip, heads, aux, masks, hl):
    tokens = proj.shape[0]
    nb = tokens // MICRO // BLOCK
    width = hl * HEADDIM
    conv_width = width + 2 * STATE
    held = lambda m, j, place: (m * nb + (j ^ place[0]), 0)
    at = lambda m, j, place: (m * nb + j, 0)
    whole = lambda m, j, place: (0, 0)
    grid_spec = pltpu.PrefetchScalarGridSpec(
        num_scalar_prefetch=1,
        grid=(MICRO, nb),
        in_specs=[
            pl.BlockSpec((BLOCK, conv_width + LANES), held),
            pl.BlockSpec((8, conv_width), whole),
            pl.BlockSpec(skip.shape, whole),
            pl.BlockSpec(heads.shape, whole),
            pl.BlockSpec((BLOCK, 8), at),
            pl.BlockSpec((8, BLOCK), at),
        ],
        out_specs=[
            pl.BlockSpec((BLOCK, width), held),
            pl.BlockSpec((1, width, STATE), lambda m, j, place: (m * nb + j, 0, 0)),
            pl.BlockSpec((BLOCK, conv_width), held),
            pl.BlockSpec((BLOCK, conv_width), held),
        ],
        scratch_shapes=[
            pltpu.VMEM((BLOCK + 8, conv_width), F32),
            pltpu.VMEM((width, STATE), F32),
            pltpu.VMEM((4 * SLOT, hl * BLOCK), BF),
            pltpu.VMEM((BLOCK, 2 * width), F32),
            pltpu.VMEM((LANES, 2 * width), BF),
        ],
    )
    return pl.pallas_call(
        functools.partial(forward_kernel, hl=hl),
        grid_spec=grid_spec,
        out_shape=[
            jax.ShapeDtypeStruct((tokens, width), BF),
            jax.ShapeDtypeStruct((MICRO * nb, width, STATE), BF),
            jax.ShapeDtypeStruct((tokens, conv_width), BF),
            jax.ShapeDtypeStruct((tokens, conv_width), BF),
        ],
        compiler_params=pltpu.CompilerParams(vmem_limit_bytes=VMEM, dimension_semantics=("arbitrary", "arbitrary")),
        name="scan_forward",
    )(place, proj, conv_w, skip, heads, aux, masks)


def scan_backward(place, micro, proj, conv_w, skip, heads, aux, masks, act, slope, dy, states, hl, *done):
    tokens = proj.shape[0] // MICRO
    nb = tokens // BLOCK
    width = hl * HEADDIM
    conv_width = width + 2 * STATE
    full = conv_width + LANES
    first = micro * nb
    held = lambda j, place: (first + ((nb - 1 - j) ^ place[0]), 0)
    at = lambda j, place: (first + nb - 1 - j, 0)
    whole = lambda j, place: (0, 0)
    grid_spec = pltpu.PrefetchScalarGridSpec(
        num_scalar_prefetch=1,
        grid=(nb,),
        in_specs=[
            pl.BlockSpec((BLOCK, full), held),
            pl.BlockSpec((8, conv_width), whole),
            pl.BlockSpec(skip.shape, whole),
            pl.BlockSpec(heads.shape, whole),
            pl.BlockSpec((BLOCK, 8), at),
            pl.BlockSpec((8, BLOCK), at),
            pl.BlockSpec((BLOCK, conv_width), held),
            pl.BlockSpec((BLOCK, conv_width), held),
            pl.BlockSpec((BLOCK, width), held),
            pl.BlockSpec((1, width, STATE), lambda j, place: (first + nb - 1 - j, 0, 0)),
        ]
        + [pl.BlockSpec(memory_space=pl.ANY)] * len(done),
        out_specs=[
            pl.BlockSpec((BLOCK, full), lambda j, place: ((nb - 1 - j) ^ place[0], 0)),
            pl.BlockSpec((8 * (CONV + 1), conv_width), whole),
            pl.BlockSpec((SLOT, LANES), whole),
            pl.BlockSpec((8, width), whole),
        ],
        scratch_shapes=[
            pltpu.VMEM((BLOCK + 8, conv_width), F32),
            pltpu.VMEM((width, STATE), F32),
            pltpu.VMEM((BLOCK, BLOCK), F32),
            pltpu.VMEM((SLOT, BLOCK), F32),
            pltpu.VMEM((SLOT, STATE), F32),
            pltpu.VMEM((4 * SLOT, hl * BLOCK), BF),
            pltpu.VMEM((BLOCK, 2 * width), F32),
            pltpu.VMEM((BLOCK, 2 * width), F32),
            pltpu.VMEM((LANES, 2 * width), BF),
            pltpu.VMEM((SLOT, hl * BLOCK), BF),
            pltpu.VMEM((SLOT, width), BF),
            pltpu.VMEM((BLOCK, width), BF),
            pltpu.VMEM((BLOCK, width), BF),
        ],
    )
    return pl.pallas_call(
        functools.partial(backward_kernel, hl=hl),
        grid_spec=grid_spec,
        out_shape=[
            jax.ShapeDtypeStruct((tokens, full), BF),
            jax.ShapeDtypeStruct((8 * (CONV + 1), conv_width), F32),
            jax.ShapeDtypeStruct((SLOT, LANES), F32),
            jax.ShapeDtypeStruct((8, width), F32),
        ],
        compiler_params=pltpu.CompilerParams(vmem_limit_bytes=VMEM, dimension_semantics=("arbitrary",)),
        name="scan_backward",
    )(place, proj, conv_w, skip, heads, aux, masks, act, slope, dy, states, *done)


def fetch(pieces, buffer, sems, step):
    @pl.when(step == 0)
    def _():
        pltpu.make_async_copy(pieces[0], buffer.at[0], sems.at[0]).start()

    for at in range(1, len(pieces)):

        @pl.when(step == at - 1)
        def _():
            pltpu.make_async_copy(pieces[at], buffer.at[at % 2], sems.at[at % 2]).start()

    slot = step % 2
    pltpu.make_async_copy(pieces[0], buffer.at[slot], sems.at[slot]).wait()
    return slot


def emit(value, targets, buffer, sems, micro, place, bits, step, steps):
    slot = step % 2
    rows = value.shape[0] // 2

    def waiting(at):
        for half in range(2):
            pltpu.make_async_copy(buffer.at[at, pl.ds(half * rows, rows)], targets[0].at[0, 0], sems.at[at, half]).wait()

    @pl.when(step >= 2)
    def _():
        waiting(slot)

    buffer[slot] = value
    for half, bit in enumerate(bits):
        index = place // (2 * bit) * bit + place % bit
        set_ = (place // bit) % 2
        for target, wanted in ((targets[2 * half], 1), (targets[2 * half + 1], 0)):

            @pl.when(set_ == wanted)
            def _():
                pltpu.make_async_copy(
                    buffer.at[slot, pl.ds(half * rows, rows)], target.at[micro, index], sems.at[slot, half]
                ).start()

    @pl.when(step == steps - 1)
    def _():
        waiting(0)
        waiting(1)


def emitted(some, n, depth):
    shapes = [jax.ShapeDtypeStruct((some, n // 2, BLOCK // 2, depth), BF)] * 4
    return shapes, [pl.BlockSpec(memory_space=pl.ANY)] * 4, [pltpu.VMEM((2, BLOCK, depth), BF), pltpu.SemaphoreType.DMA((2, 2))]


def fixed(array):
    return pl.BlockSpec(array.shape, lambda i: (0, 0), pipeline_mode=pl.Buffered(1))


def by_rows(width):
    return pl.BlockSpec((BLOCK, width), lambda i: (i, 0))


def arbitrary(name):
    return dict(compiler_params=pltpu.CompilerParams(vmem_limit_bytes=VMEM, dimension_semantics=("arbitrary",)), name=name)


def in_kernel(*refs, count):
    pieces, w, (proj, hidden, buffer, sems) = refs[1 : count + 1], refs[count + 1], refs[-4:]
    slot = fetch(pieces, buffer, sems, pl.program_id(0))
    value = buffer[slot]
    hidden[...] = value
    proj[...] = dot(value, w[...], NN).astype(BF)


def in_project(pieces, places, total, w, earlier=(), done=()):
    count = len(pieces)
    depth, width = w.shape
    anywhere = [pl.BlockSpec(memory_space=pl.ANY)]
    at = lambda i, table: (table[i], 0)
    return pl.pallas_call(
        functools.partial(in_kernel, count=count),
        grid_spec=pltpu.PrefetchScalarGridSpec(
            num_scalar_prefetch=1,
            grid=(count,),
            in_specs=anywhere * count
            + [pl.BlockSpec(w.shape, lambda i, table: (0, 0), pipeline_mode=pl.Buffered(1))]
            + anywhere * (len(earlier) + len(done)),
            out_specs=[pl.BlockSpec((BLOCK, width), at), pl.BlockSpec((BLOCK, depth), at)],
            scratch_shapes=[pltpu.VMEM((2, BLOCK, depth), BF), pltpu.SemaphoreType.DMA((2,))],
        ),
        out_shape=[
            jax.ShapeDtypeStruct((total * BLOCK, width), BF),
            jax.ShapeDtypeStruct((total * BLOCK, depth), BF),
        ],
        input_output_aliases={count + 2 + i: i for i in range(len(earlier))},
        **arbitrary("in_project"),
    )(jnp.array(places, jnp.int32), *pieces, w, *earlier, *done)


def gate_kernel(*refs, count):
    pieces, (z, w_o, y, gain, dn_out, cot_out, sums, buffer, sems) = refs[:count], refs[count:]
    slot = fetch(pieces, buffer, sems, pl.program_id(0))
    cot = buffer[slot]
    cot_out[...] = cot
    dn = dot(cot, w_o[...], NN)
    dn_out[...] = dn.astype(BF)
    zf = z[...].astype(F32)
    gz = y[...].astype(F32) * (zf * jax.nn.sigmoid(zf))
    ones = jnp.ones((8, gz.shape[1]), BF)
    first = dot(ones, (gz * gz).astype(BF), NT)
    second = dot(ones, (dn * gain[0:1, :] * gz).astype(BF), NT)
    sums[...] = jnp.where(iota2((8, BLOCK), 0) == 0, first, second)


def gate_forward(pieces, z, w_o, y, gain):
    count = len(pieces)
    depth, width = w_o.shape
    return pl.pallas_call(
        functools.partial(gate_kernel, count=count),
        grid=(count,),
        in_specs=[pl.BlockSpec(memory_space=pl.ANY)] * count + [by_rows(width), fixed(w_o), by_rows(width), fixed(gain)],
        out_specs=[by_rows(width), by_rows(depth), pl.BlockSpec((8, BLOCK), lambda i: (i, 0))],
        out_shape=[
            jax.ShapeDtypeStruct((count * BLOCK, width), BF),
            jax.ShapeDtypeStruct((count * BLOCK, depth), BF),
            jax.ShapeDtypeStruct((count * 8, BLOCK), F32),
        ],
        scratch_shapes=[pltpu.VMEM((2, BLOCK, depth), BF), pltpu.SemaphoreType.DMA((2,))],
        **arbitrary("gate_forward"),
    )(*pieces, z, w_o, y, gain)


def out_kernel(z_in, dn_in, y_in, sums, gain, w_o, normed, dy, dz, dgain, *refs, n, bits):
    step = pl.program_id(0)
    @pl.when(pl.program_id(0) == 0)
    def _():
        dgain[...] = jnp.zeros(dgain.shape, F32)

    scale = lax.rsqrt(sums[0:1, :] / INNER + NORM_EPS)
    slope = scale * scale * scale * sums[1:2, :] / INNER
    row = iota2((LANES, BLOCK), 0)
    columns = jnp.where(row == 0, scale, jnp.where(row == 1, slope, 0.0)).T
    scale, slope = columns[:, 0:1], columns[:, 1:2]
    for lo in range(0, normed.shape[1], 2 * LANES):
        hi = lo + 2 * LANES
        z, y, dn = z_in[:, lo:hi].astype(F32), y_in[:, lo:hi].astype(F32), dn_in[:, lo:hi].astype(F32)
        sig = jax.nn.sigmoid(z)
        silu = z * sig
        gz = y * silu
        unit = gz * scale
        normed[:, lo:hi] = (unit * gain[0:1, lo:hi]).astype(BF)
        dgain[:, lo:hi] += jnp.sum((dn * unit).reshape(BLOCK // 8, 8, 2 * LANES), axis=0)
        d_gz = dn * gain[0:1, lo:hi] * scale - gz * slope
        dy[:, lo:hi] = (d_gz * silu).astype(BF)
        dz[:, lo:hi] = (d_gz * y * (sig + silu * (1.0 - sig))).astype(BF)
    out = dot(normed[...], w_o[...], NT).astype(BF)
    emit(out, refs[:4], refs[4], refs[5], step // n, step % n, bits, step, MICRO * n)


def out_project(z, dn, y, sums, gain, w_o, bits):
    depth, width = w_o.shape
    tokens = z.shape[0]
    n = tokens // BLOCK // MICRO
    one = by_rows(width)
    shapes, places, scratch = emitted(MICRO, n, depth)
    return pl.pallas_call(
        functools.partial(out_kernel, n=n, bits=bits),
        grid=(tokens // BLOCK,),
        in_specs=[one, one, one, pl.BlockSpec((8, BLOCK), lambda i: (i, 0)), fixed(gain), fixed(w_o)],
        out_specs=[one, one, one, pl.BlockSpec((8, width), lambda i: (0, 0))] + places,
        out_shape=[jax.ShapeDtypeStruct((tokens, width), BF)] * 3 + [jax.ShapeDtypeStruct((8, width), F32)] + shapes,
        scratch_shapes=scratch,
        **arbitrary("out_project"),
    )(z, dn, y, sums, gain, w_o)


def back_kernel(dz, px, w_z, w_x, *refs, n, bits):
    step = pl.program_id(0)
    out = (dot(dz[...], w_z[...], NT) + dot(px[...], w_x[...], NT)).astype(BF)
    emit(out, refs[:4], refs[4], refs[5], 0, step, bits, step, n)


def back_project(micro, dz, px, w_z, w_x, bits):
    tokens, width = px.shape
    depth = w_z.shape[0]
    n = tokens // BLOCK
    shapes, places, scratch = emitted(1, n, depth)
    return pl.pallas_call(
        functools.partial(back_kernel, n=n, bits=bits),
        grid=(n,),
        in_specs=[pl.BlockSpec((BLOCK, dz.shape[1]), lambda i: (micro * n + i, 0)), by_rows(width), fixed(w_z), fixed(w_x)],
        out_specs=places,
        out_shape=shapes,
        scratch_shapes=scratch,
        **arbitrary("back_project"),
    )(dz, px, w_z, w_x)

def swapped(value, axis, mask):
    return lax.ppermute(value, axis, [(i, i ^ mask) for i in range(lax.axis_size(axis))])


def axis_bits(axis):
    return [1 << i for i in range(lax.axis_size(axis).bit_length() - 1)]


def micro_order(micro, axis):
    bits = axis_bits(axis)
    return bits if micro % 2 == 0 else bits[::-1]


def nothing(*refs):
    pass


def after(values, *done):
    values = list(values)
    anywhere = pl.BlockSpec(memory_space=pl.ANY)
    held = pl.pallas_call(
        nothing,
        in_specs=[anywhere] * (len(values) + len(done)),
        out_specs=[anywhere] * len(values),
        out_shape=[jax.ShapeDtypeStruct(v.shape, v.dtype) for v in values],
        input_output_aliases={at: at for at in range(len(values))},
        name="after",
    )(*values, *done)
    return list(held)


def gather_stages(own):
    held = [{0: own[micro]} for micro in range(MICRO)]
    for turn in range(len(axis_bits("seq"))):
        got = []
        for micro in range(MICRO):
            bit = micro_order(micro, "seq")[turn]
            got.append({at ^ bit: swapped(held[micro][at], "seq", bit) for at in held[micro]})
        wait = yield [piece for one in got for piece in one.values()], [piece for one in held for piece in one.values()]
        for micro in range(MICRO):
            if wait is not None:
                got[micro] = dict(zip(got[micro], after(got[micro].values(), *wait)))
            held[micro].update(got[micro])
    yield [held[micro][at] for micro in range(MICRO) for at in range(len(held[micro]))]


def scatter_stages(parts):
    n = 2 * parts[0].shape[1]
    away, stay = list(parts[0::2]), list(parts[1::2])
    places = [[at for at in range(n) if not at & micro_order(half, "seq")[0]] for half in range(2)]
    join = lambda one, more: (one.astype(F32) + more.astype(F32)).astype(BF)
    pick = lambda a, at: jnp.concatenate([a[:, k : k + 1] for k in at], axis=1)
    turns = len(axis_bits("seq"))
    for turn in range(turns):
        got = [swapped(away[half], "seq", micro_order(half, "seq")[turn]) for half in range(2)]
        wait = yield got, away
        if wait is not None:
            got = after(got, *wait)
        if turn == turns - 1:
            break
        held, away, stay = stay, [], []
        for half in range(2):
            bit = micro_order(half, "seq")[turn + 1]
            leave = [at for at, place in enumerate(places[half]) if place & bit]
            keep = [at for at, place in enumerate(places[half]) if not place & bit]
            away.append(join(pick(held[half], leave), pick(got[half], leave)))
            stay.append(join(pick(held[half], keep), pick(got[half], keep)))
            places[half] = [places[half][at] for at in keep]
    yield jnp.concatenate([join(one, more)[:, 0] for one, more in zip(stay, got)], axis=1), None


def finish(stages, wait=None):
    last = None
    try:
        while True:
            last = stages.send(wait)
    except StopIteration:
        return last[0]


def turned(entries, rank):
    entries = list(entries)
    for bit in axis_bits("seq"):
        flip = (rank & bit) != 0
        entries = [jnp.where(flip, entries[at ^ bit], entries[at]) for at in range(len(entries))]
    return entries


def exchange(entries, rank):
    entries = turned(entries, rank)
    return entries, [swapped(one, "seq", mask) for mask, one in enumerate(entries) if mask]


def sum_all(value):
    for axis in ("dp", "seq"):
        for bit in axis_bits(axis):
            value = value + swapped(value, axis, bit)
    return value


def sum_pieces(value):
    n = value.shape[-2]
    total = value
    for mask in range(1, n):
        got = swapped(value, "seq", mask)
        total = total + jnp.concatenate([got[..., at ^ mask : (at ^ mask) + 1, :] for at in range(n)], axis=-2)
    return total


def adamw(master, gradient, first, second, clip, decay):
    clipped = gradient * clip
    first_new = BETA_ONE * first + (1.0 - BETA_ONE) * clipped
    second_new = BETA_TWO * second + (1.0 - BETA_TWO) * clipped * clipped
    update = first_new / FIX_ONE / (jnp.sqrt(second_new / FIX_TWO) + ADAM_EPS) + decay * master
    return (-LEARN_RATE * update, first_new, second_new)


def per_device(tokens, cotangent, segments, in_weight, in_m, in_v, conv_weight, conv_m, conv_v,
               out_weight, out_m, out_v, packed, packed_m, packed_v):
    n = lax.axis_size("seq")
    rank = lax.axis_index("seq")
    place = rank.astype(jnp.int32).reshape(1)
    ndev = n * lax.axis_size("dp")
    hl = HEADS // n
    xw = hl * HEADDIM
    rows = D // ndev
    piece = tokens.shape[1]
    count = MICRO * n * piece
    xs = INNER + INNER
    bc = 2 * STATE
    xc = xw + bc + LANES
    cw = conv_weight.shape[1]
    conv_cols = -(-(CONV + 1) * cw // rows)

    in_low = in_weight.astype(BF)
    out_low = out_weight.astype(BF).T
    conv_flat = conv_weight.astype(BF).reshape(-1)
    conv_flat = jnp.pad(conv_flat, (0, conv_cols * rows - conv_flat.shape[0])).reshape(rows, conv_cols)
    column = lambda a, q, width: a[:, q * width : (q + 1) * width]
    pad = jnp.zeros((rows, LANES - hl - conv_cols), BF)
    send_x = [
        jnp.concatenate(
            [column(in_low[:, INNER:xs], q, xw), in_low[:, xs : xs + bc], column(in_low[:, xs + bc :], q, hl), conv_flat, pad], axis=1
        )
        for q in range(n)
    ]
    gain_in = packed[3 * HEADS : 3 * HEADS + D]
    send_x = turned(send_x, rank)
    got_wx = [one if not mask else swapped(one, "seq", mask) for mask, one in enumerate(send_x)]
    a_log = lax.dynamic_slice_in_dim(packed, rank * hl, hl)
    skip = lax.dynamic_slice_in_dim(packed, HEADS + rank * hl, hl)
    dt_bias = lax.dynamic_slice_in_dim(packed, 2 * HEADS + rank * hl, hl)
    gain_out = lax.dynamic_slice_in_dim(packed, 3 * HEADS + D + rank * xw, xw)
    aux, masks = segment_aux(segments)
    heads = head_columns(a_log, dt_bias)
    skip = jnp.broadcast_to(jnp.repeat(skip, HEADDIM)[None], (8, xw))

    tok = tokens.astype(F32)
    r_in = lax.rsqrt(jnp.mean(tok * tok, axis=-1, keepdims=True) + NORM_EPS)
    hidden_stages = gather_stages((tok * r_in * gain_in).astype(BF))
    arrived, sent = next(hidden_stages)
    more, _ = hidden_stages.send(None)
    got_wx = jnp.concatenate(turned(got_wx[:1] + after(got_wx[1:], *sent), rank), axis=0)
    w_x = lax.all_gather(got_wx, "dp", axis=0, tiled=True)
    send_zo = jnp.stack(turned([jnp.concatenate([column(in_low, q, xw), column(out_low, q, xw)], axis=1) for q in range(n)], rank))
    [send_zo] = after([send_zo], got_wx, more[0], more[2])
    got_wzo = [send_zo[mask] if not mask else swapped(send_zo[mask], "seq", mask) for mask in range(n)]
    got_wzo = jnp.concatenate(turned(got_wzo, rank), axis=0)
    w_z = lax.all_gather(got_wzo[:, :xw], "dp", axis=0, tiled=True)
    w_o = lax.all_gather(got_wzo[:, xw:], "dp", axis=0, tiled=True)
    conv_full = w_x[:, xw + bc + hl : xw + bc + hl + conv_cols].reshape(ndev, rows * conv_cols)[:, : (CONV + 1) * cw]
    conv_full = conv_full.reshape(ndev, CONV + 1, cw).transpose(1, 0, 2).reshape(CONV + 1, CH)
    conv_loc = jnp.concatenate([lax.dynamic_slice_in_dim(conv_full, rank * xw, xw, 1), conv_full[:, INNER:]], axis=1).astype(F32)
    conv_loc = jnp.pad(conv_loc, ((0, 8 - CONV - 1), (0, 0)))

    for _ in axis_bits("seq")[1:]:
        arrived, more = more, hidden_stages.send(None)
        more = more[0] if isinstance(more, tuple) else more
    late = [micro * n + at for micro in range(MICRO) for at in range(n) if at & (last := micro_order(micro, "seq")[-1]) and at != last]
    soon = [at for at in range(MICRO * n) if at not in late]
    soon.sort(key=lambda at: (at % n).bit_count())
    earlier = in_project([more[at] for at in soon], soon, MICRO * n, w_x, done=(aux, masks))
    late_pieces = after([more[at] for at in late], earlier[0])
    proj_x, hidden = in_project(late_pieces, late, MICRO * n, w_x, earlier)

    cot_stages = gather_stages(after([cotangent[micro] for micro in range(MICRO)], *late_pieces))
    next(cot_stages)
    y, states, act, slope = scan_forward(place, proj_x, conv_loc, skip, heads, aux, masks, hl)
    for bit in axis_bits("seq"):
        cot = cot_stages.send([proj_x] if bit == 1 else [y])
    gain = jnp.broadcast_to(gain_out[None], (8, xw))
    [w_z] = after([w_z], y)
    z = dot(hidden, w_z, NN).astype(BF)
    dn, cot, sums = gate_forward(cot, z, w_o, y, gain)
    sums = sum_pieces(sums.reshape(MICRO, n, 8 * BLOCK)).reshape(-1, BLOCK)
    first_bits = tuple(micro_order(half, "seq")[0] for half in range(2))
    normed, dy, dz, d_gain_out, *out_part = out_project(z, dn, y, sums, gain, w_o, first_bits)
    d_gain_out = jnp.sum(d_gain_out, axis=0)

    scatter = lambda a: lax.psum_scatter(a, "dp", scatter_dimension=0, tiled=True)
    split = lambda a: [a[q * rows : (q + 1) * rows] for q in range(n)]
    out_stages = scatter_stages(out_part)
    next(out_stages)
    part_o = dot(cot, normed, TN).astype(BF)
    part_z = dot(hidden, dz, TN).astype(BF)
    got_o, got_z = scatter(part_o), scatter(part_z)

    through_in = lambda micro, one: back_project(micro, dz, one, w_z, w_x, first_bits)
    scan_back = lambda micro, *done: scan_backward(
        place, micro, proj_x, conv_loc, skip, heads, aux, masks, act, slope, dy, states, hl, *done
    )

    px_0, conv_0, vec_0, skip_0 = scan_back(0, part_o, part_z)
    hid_0 = through_in(0, px_0)
    out_got, out_sent = out_stages.send([hid_0[0]])
    stages_0 = scatter_stages(hid_0)
    hid_got, sent = next(stages_0)
    px_1, conv_1, vec_1, skip_1 = scan_back(1, *sent, *out_sent)
    [px_1] = after([px_1], *hid_got, *out_got)
    part_x = dot(hidden, jnp.concatenate([px_0, px_1], axis=0), TN).astype(BF)
    got_x = scatter(part_x)
    hid_got, sent = stages_0.send([part_x])
    [got_o, got_z] = after([got_o, got_z], px_1)
    sent_oz, got_oz = exchange(split(jnp.concatenate([got_o, got_z], axis=1)), rank)
    [px_1] = after([px_1], part_x, *sent, *got_oz)
    hid_1 = after(through_in(1, px_1), *hid_got)
    stages_1 = scatter_stages(hid_1)
    hid_got, hid_sent = next(stages_1)
    output = (tok + finish(out_stages, [hid_1[0]]).astype(F32)).astype(BF)

    d_conv = (conv_0 + conv_1).reshape(CONV + 1, 8, -1).sum(axis=1)
    d_skip = jnp.sum((skip_0 + skip_1).reshape(8, hl, HEADDIM), axis=(0, 2))
    d_vec = vec_0 + vec_1
    head_rows = jnp.concatenate([d_vec[:hl, 0], d_skip, d_vec[:hl, 1]])
    small = jnp.concatenate([d_conv.reshape(-1), d_gain_out, head_rows])
    small_size = small.shape[0]
    small = jnp.pad(small, (0, -small_size % 1024)).reshape(-1, LANES)
    [small] = after([small], hid_1[0])
    for bit in axis_bits("dp"):
        small = small + swapped(small, "dp", bit)
    small = [small] + after([swapped(small, "seq", mask) for mask in range(1, n)], *hid_got)
    small = jnp.stack(turned(small, rank)).reshape(n, -1)[:, :small_size]
    conv_all = small[:, : (CONV + 1) * (xw + bc)].reshape(n, CONV + 1, xw + bc)
    conv_tot = jnp.concatenate(
        [conv_all[:, :, :xw].transpose(1, 0, 2).reshape(CONV + 1, INNER), jnp.sum(conv_all[:, :, xw:], axis=0)], axis=1
    )
    gain_out_tot = small[:, (CONV + 1) * (xw + bc) : small_size - 3 * hl].reshape(-1)
    heads_tot = small[:, small_size - 3 * hl :].reshape(n, 3, hl).transpose(1, 0, 2).reshape(-1)

    [got_x] = after([got_x], conv_tot, output)
    sent_x, got_x = exchange(split(got_x), rank)
    d_hidden = jnp.concatenate([finish(stages_0, [hid_1[0]]), finish(stages_1, sent_x)], axis=0).astype(F32)
    dh = d_hidden * gain_in
    d_tok = r_in * (dh - tok * (r_in * r_in) * jnp.mean(dh * tok, axis=-1, keepdims=True))
    input_grad = (cotangent.astype(F32) + d_tok).astype(BF)
    got_x = after(got_x, input_grad)
    got_oz, got_x = (turned(sent[:1] + got, rank) for sent, got in ((sent_oz, got_oz), (sent_x, got_x)))

    together = lambda parts, lo, hi: jnp.concatenate([one[:, lo:hi] for one in parts], axis=1).astype(F32)
    g_bc = sum(one[:, xw : xw + bc].astype(F32) for one in got_x)
    shard_in = jnp.concatenate(
        [together(got_oz, xw, 2 * xw), together(got_x, 0, xw), g_bc, together(got_x, xw + bc, xw + bc + hl)], axis=1
    )
    shard_out = together(got_oz, 0, xw).T

    own = lax.axis_index("dp") * n + rank
    own_gain = lax.dynamic_slice_in_dim(gain_in, own * rows, rows)
    d_gain_in = jnp.sum(in_low.astype(F32) * shard_in, axis=1) / own_gain
    partial_sq = jnp.sum(shard_in * shard_in) + jnp.sum(shard_out * shard_out)
    last = lax.dynamic_update_slice(jnp.zeros((D + 1024,), F32), d_gain_in, (own * rows,))
    last = lax.dynamic_update_slice(last, partial_sq[None], (D,))
    last = sum_all(last.reshape(-1, LANES)).reshape(-1)
    vec_tot = jnp.concatenate([heads_tot, last[:D], gain_out_tot])
    shard_conv = lax.dynamic_slice_in_dim(conv_tot, own * cw, cw, 1)
    grad_norm = jnp.sqrt(last[D] + jnp.sum(conv_tot * conv_tot) + jnp.sum(vec_tot * vec_tot))
    clip = jnp.minimum(1.0, CLIP_NORM / (grad_norm + 1e-06))
    in_new = adamw(in_weight, shard_in, in_m, in_v, clip, WEIGHT_DECAY)
    conv_new = adamw(conv_weight, shard_conv, conv_m, conv_v, clip, WEIGHT_DECAY)
    out_new = adamw(out_weight, shard_out, out_m, out_v, clip, WEIGHT_DECAY)
    vec_new = adamw(packed, vec_tot, packed_m, packed_v, clip, 0.0)
    return (
        output, input_grad, grad_norm,
        in_weight + in_new[0], in_new[1], in_new[2],
        conv_new[0], conv_new[1], conv_new[2],
        out_weight + out_new[0], out_new[1], out_new[2],
        vec_new[0], vec_new[1], vec_new[2],
    )


def solution(mesh):
    tok, col, row = P(None, ALL, None), P(None, ALL), P(ALL, None)
    return jax.shard_map(
        per_device,
        mesh=mesh,
        in_specs=(tok, tok, P(None, "dp"), row, row, row, col, col, col, col, col, col, P(), P(), P()),
        out_specs=(tok, tok, P(), row, row, row, col, col, col, col, col, col, P(), P(), P()),
        check_vma=False,
    )
```

time: 595 us -> 549 us (0.923)
  local copies, waits for them, and re-layouts: 75.3 us -> 47.5 us
  matrix products: 47.6 us -> 61.2 us
  waiting for transfers between devices: 107 us -> 94.3 us
  Pallas kernels: 209 us -> 197 us
    dot_general x3 -> x4, matrix products: 47.6 us -> 61.2 us  [dot(): return lax.dot_general(a, b, (dims, ((), ())), preferred_element_type=out)]
    pallas_call x2, Pallas kernels: 73 us -> 60.1 us  [scan_backward(): pl.pallas_call(functools.partial(backward_kernel, hl=hl), grid_spec=grid_...]
    slice x8 -> x2, local copies, waits for them, and re-layouts: 12.9 us -> 0.24 us  [the longest x1 0.17 us: per_device(): head_rows = jnp.concatenate([d_vec[:hl, 0], d_skip, d_vec[:hl, 1]])]
    ppermute x50, waiting for transfers between devices: 106 us -> 93.5 us  [swapped(): lax.ppermute(value, axis, [(i, i ^ mask) for i in range(lax.axis_size(axi...]
    pallas_call x4 -> x5, Pallas kernels: 76 us -> 84.9 us  [the longest x2 35 us: back_project(): pl.pallas_call(functools.partial(back_kernel, n=n, bits=bits), grid=(n,),...]
    concatenate x3 -> x0, local copies, waits for them, and re-layouts: 8.55 us -> none  [scatter_stages(): pick = lambda a, at: jnp.concatenate([a[:, k:k + 1] for k in at], axis=1)]
    pallas_call x1, Pallas kernels: 27.5 us -> 19.2 us  [gate_forward(): pl.pallas_call(functools.partial(gate_kernel, count=count), grid=(count,)...]
    convert_element_type x6 -> x8, other arithmetic: 14.6 us -> 11.1 us  [the longest x6 8.86 us: scatter_stages(): join = lambda one, more: (one.astype(F32) + more.astype(F32)).astype(BF)]
  transfers between devices with their start and end apart: 56 -> 56, of which waited for: 23 -> 24; matrix products, arithmetic and copies ran while one was open for 24% -> 20% of each run, Pallas kernels for 27% -> 28%
where the time goes in v4:
time: 549 us; the launch traced here: 542 us
  Pallas kernels  197 us (36%)
  waiting for transfers between devices  94.3 us (17%)
  other arithmetic  67.4 us (12%)
  matrix products  61.2 us (11%)
  starting transfers between devices  54.3 us (10%)
  local copies, waits for them, and re-layouts  47.5 us (9%)
  between operations  20.3 us (4%)
    ppermute x50, waiting for transfers between devices, swapped(): lax.ppermute(value, axis, [(i, i ^ mask) for i in range(lax.axis_size(axi...  93.5 us
    dot_general x4, matrix products, dot(): return lax.dot_general(a, b, (dims, ((), ())), preferred_element_type=out)  61.2 us
    pallas_call x2, Pallas kernels, scan_backward(): pl.pallas_call(functools.partial(backward_kernel, hl=hl), grid_spec=grid_...  60.1 us
    ppermute x50, starting transfers between devices, swapped(): lax.ppermute(value, axis, [(i, i ^ mask) for i in range(lax.axis_size(axi...  54 us
    pallas_call x2, Pallas kernels, back_project(): pl.pallas_call(functools.partial(back_kernel, n=n, bits=bits), grid=(n,),...  35 us
    pallas_call x1, Pallas kernels, scan_forward(): pl.pallas_call(functools.partial(forward_kernel, hl=hl), grid_spec=grid_s...  32.8 us
    pallas_call x2, Pallas kernels, in_project(): pl.pallas_call(functools.partial(in_kernel, count=count), grid_spec=pltpu...  26.1 us
    pallas_call x1, Pallas kernels, out_project(): pl.pallas_call(functools.partial(out_kernel, n=n, bits=bits), grid=(token...  23.8 us
  transfers between devices with their start and end apart: 56, of which 24 were waited for; matrix products, arithmetic and copies ran while one was open for 20% of the time, Pallas kernels for 28%

profile of v4, /device:TPU:0, one launch (start us, length us, event | category | flops | bytes accessed | tf_op | source)
XLA Modules:
  0.0 542.0 jit_solution(14434958004289523313)
XLA Ops:
  7.2 1.7 convert_element_type.271
  10.7 3.0 collective-permute-start.6
  19.2 4.4 collective-permute-done.7.refs_1_
  33.7 17.9 %collective-permute-done.4.refs_4_.refs_2_ = bf16[256,2048]{1,0:T(8,128)(2,1)S(1)} collective-permute-done((bf16[256,2048]{1,0:T(8,128)(2,1)S(1)}, bf16[256,2048]{1,0:T(8,128)(2,1)S(1)}, u32[]{:S(2)}, u32[]{:S(2)}) %collective-permute-start.4) | collective-permute-done | bytes 1048608 | tf_op jit(solution)/shard_map/ppermute | solution.py:626
  57.4 5.5 %collective-permute-done.10 = bf16[64,2048]{1,0:T(8,128)(2,1)S(1)} collective-permute-done((bf16[64,2048]{1,0:T(8,128)(2,1)S(1)}, bf16[64,2048]{1,0:T(8,128)(2,1)S(1)}, u32[]{:S(2)}, u32[]{:S(2)}) %collective-permute-start.10) | collective-permute-done | bytes 262176 | tf_op jit(solution)/shard_map/ppermute | solution.py:626
  63.0 3.7 collective-permute-done.9
  69.8 1.8 collective-permute-start
  72.0 19.9 %collective-permute-done.refs_3_ = bf16[256,2048]{1,0:T(8,128)(2,1)S(1)} collective-permute-done((bf16[256,2048]{1,0:T(8,128)(2,1)S(1)}, bf16[256,2048]{1,0:T(8,128)(2,1)S(1)}, u32[]{:S(2)}, u32[]{:S(2)}) %collective-permute-start) | collective-permute-done | bytes 1048608 | tf_op jit(solution)/shard_map/ppermute | solution.py:626
  92.0 4.0 collective-permute-done.2.refs_6_
  99.1 3.1 slice_bitcast_fusion.2
  102.2 16.9 %in_project.2 = (bf16[2048,1408]{1,0:T(8,128)(2,1)}, bf16[2048,2048]{1,0:T(8,128)(2,1)}) custom-call(s32[6]{0:T(128)} %constant.29.clone.refs_0_, bf16[256,2048]{1,0:T(8,128)(2,1)} %get-tuple-element.181.refs_3_.refs_1_, bf16[256,2048]{1,0:T(8,128)(2,1)} %get-tuple-element.180.refs_4_.refs_2_, bf16[256,2048]{1,0:T(8,128)(2,1)} %copy-done.46, ...), custom_call_target="tpu_custom_call" | custom-call | tf_op jit(solution)/shard_map/in_project/pallas_call | solution.py:507
  121.0 1.8 collective-permute-start.12
  127.0 2.0 slice.499
  129.1 1.6 reshape.472
  131.1 9.1 %in_project.3 = (bf16[2048,1408]{1,0:T(8,128)(2,1)}, bf16[2048,2048]{1,0:T(8,128)(2,1)}) custom-call(s32[2]{0:T(128)} %constant.30.clone.refs_0_, bf16[256,2048]{1,0:T(8,128)(2,1)} %get-tuple-element.89.refs_1_.refs_2_, bf16[256,2048]{1,0:T(8,128)(2,1)} %get-tuple-element.90.refs_2_.refs_3_, ...), custom_call_target="tpu_custom_call", output_to_operand_aliasing={{0}: (4, {}), {1}: (5, {})} | custom-call | tf_op jit(solution)/shard_map/in_project/pallas_call | solution.py:507
  141.5 32.8 %scan_forward.1 = (bf16[2048,1024]{1,0:T(8,128)(2,1)}, bf16[8,1024,128]{2,1,0:T(8,128)(2,1)}, bf16[2048,1280]{1,0:T(8,128)(2,1)}, bf16[2048,1280]{1,0:T(8,128)(2,1)}) custom-call(s32[1]{0:T(128)} %bitcast.18.place, bf16[2048,1408]{1,0:T(8,128)(2,1)} %get-tuple-element.93.proj.refs_1_, f32[8,1280]{1,0:T(8,128)} %fusion.29.conv_w, ...), custom_call_target="tpu_custom_call" | custom-call | tf_op jit(solution)/shard_map/scan_forward/pallas_call | solution.py:355
  175.3 2.0 collective-permute-start.17
  178.5 13.8 %convolution_convert_fusion.1.refs_8_.z_in = bf16[2048,1024]{1,0:T(8,128)(2,1)} fusion(bf16[2048,2048]{1,0:T(8,128)(2,1)} %get-tuple-element.92, bf16[2048,1024]{1,0:T(8,128)(2,1)} %after.26.w_z), kind=kOutput, calls=%fused_computation.20 | convolution fusion | flops 8592031744 | bytes 16777216 | tf_op jit(solution)/shard_map/dot_general | solution.py:34
  197.2 19.2 %gate_forward.1 = (bf16[2048,1024]{1,0:T(8,128)(2,1)}, bf16[2048,2048]{1,0:T(8,128)(2,1)}, f32[64,256]{1,0:T(8,128)}) custom-call(bf16[256,2048]{1,0:T(8,128)(2,1)} %get-tuple-element.95.refs_0_, bf16[256,2048]{1,0:T(8,128)(2,1)} %after.28.refs_1_, bf16[256,2048]{1,0:T(8,128)(2,1)} %get-tuple-element.96.refs_2_, ...), custom_call_target="tpu_custom_call" | custom-call | tf_op jit(solution)/shard_map/gate_forward/pallas_call | solution.py:545
  226.3 23.8 %out_project.1 = (bf16[2048,1024]{1,0:T(8,128)(2,1)}, bf16[2048,1024]{1,0:T(8,128)(2,1)}, bf16[2048,1024]{1,0:T(8,128)(2,1)}, f32[8,1024]{1,0:T(8,128)}, bf16[2,...) custom-call(bf16[2048,1024]{1,0:T(8,128)(2,1)} %convolution_convert_, ...), custom_call_target="tpu_custom_call" | custom-call | tf_op jit(solution)/shard_map/out_project/pallas_call | solution.py:593
  250.1 14.0 %convolution_convert_fusion.2.refs_1_ = bf16[2048,1024]{1,0:T(8,128)(2,1)} fusion(bf16[2048,2048]{1,0:T(8,128)(2,1)} %get-tuple-element.92, bf16[2048,1024]{1,0:T(8,128)(2,1)} %get-tuple-element.106.dz), kind=kOutput, calls=%fused_computation.21 | convolution fusion | flops 8592031744 | bytes 16777216 | tf_op jit(solution)/shard_map/dot_general | solution.py:34
  264.2 14.0 %convolution_convert_fusion.3.refs_0_ = bf16[2048,1024]{1,0:T(8,128)(2,1)} fusion(bf16[2048,2048]{1,0:T(8,128)(2,1)} %get-tuple-element.111, bf16[2048,1024]{1,0:T(8,128)(2,1)} %get-tuple-element.112), kind=kOutput, calls=%fused_computation.22 | convolution fusion | flops 8592031744 | bytes 16777216 | tf_op jit(solution)/shard_map/dot_general | solution.py:34
  280.2 30.0 %scan_backward.2 = (bf16[1024,1408]{1,0:T(8,128)(2,1)}, f32[40,1280]{1,0:T(8,128)}, f32[16,128]{1,0:T(8,128)}, f32[8,1024]{1,0:T(8,128)}) custom-call(s32[1]{0:T(128)} %bitcast.18.place, bf16[2048,1408]{1,0:T(8,128)(2,1)} %get-tuple-element.93.proj.refs_1_, f32[8,1280]{1,0:T(8,128)} %fusion.29.conv_w, f32[8,1024]{1,0:T(8,128)} %broadcast_in_dim.33.skip, ...), custom_call_target="tpu_custom_call" | custom-call | tf_op jit(solution)/shard_map/scan_backward/pallas_call | solution.py:417
  310.2 17.5 %back_project.2 = (bf16[1,2,128,2048]{3,2,1,0:T(8,128)(2,1)}, bf16[1,2,128,2048]{3,2,1,0:T(8,128)(2,1)}, bf16[1,2,128,2048]{3,2,1,0:T(8,128)(2,1)}, bf16[1,2,128,2048]{3,2,1,0:T(8,128)(2,1)}) custom-call(bf16[2048,1024]{1,0:T(8,128)(2,1)} %get-tuple-element.106.dz, bf16[1024,1408]{1,0:T(8,128)(2,1)} %get-tuple-element.113.px, bf16[2048,1024]{1,0:T(8,128)(2,1)} %after.26.w_z, ...), custom_call_target="tpu_custom_call" | custom-call | tf_op jit(solution)/shard_map/back_project/pallas_call | solution.py:615
  331.3 2.1 add_convert_fusion.3.refs_3_
  337.3 30.1 %scan_backward.3 = (bf16[1024,1408]{1,0:T(8,128)(2,1)}, f32[40,1280]{1,0:T(8,128)}, f32[16,128]{1,0:T(8,128)}, f32[8,1024]{1,0:T(8,128)}) custom-call(s32[1]{0:T(128)} %bitcast.18.place, bf16[2048,1408]{1,0:T(8,128)(2,1)} %get-tuple-element.93.proj.refs_1_, f32[8,1280]{1,0:T(8,128)} %fusion.29.conv_w, f32[8,1024]{1,0:T(8,128)} %broadcast_in_dim.33.skip, ...), custom_call_target="tpu_custom_call" | custom-call | tf_op jit(solution)/shard_map/scan_backward/pallas_call | solution.py:417
  369.0 19.4 %convolution_convert_fusion.refs_2_.refs_1_ = bf16[2048,1408]{1,0:T(8,128)(2,1)} fusion(bf16[2048,2048]{1,0:T(8,128)(2,1)} %get-tuple-element.92, bf16[1024,1408]{1,0:T(8,128)(2,1)} %after.33.refs_2_.refs_0_, bf16[1024,1408]{1,0:T(8,128)(2,1)} %get-tuple-element.113.px), kind=kOutput, calls=%fused_computation.5 | convolution fusion | flops 11825577984 | bytes 19922944 | tf_op jit(solution)/shard_map/dot_general | solution.py:34
  403.1 2.0 collective-permute-done.27.refs_4_
  405.1 4.1 collective-permute-done.28.refs_5_
  410.6 17.5 %back_project.3 = (bf16[1,2,128,2048]{3,2,1,0:T(8,128)(2,1)}, bf16[1,2,128,2048]{3,2,1,0:T(8,128)(2,1)}, bf16[1,2,128,2048]{3,2,1,0:T(8,128)(2,1)}, bf16[1,2,128,2048]{3,2,1,0:T(8,128)(2,1)}) custom-call(bf16[2048,1024]{1,0:T(8,128)(2,1)} %get-tuple-element.106.dz, bf16[1024,1408]{1,0:T(8,128)(2,1)} %after.36.px, bf16[2048,1024]{1,0:T(8,128)(2,1)} %after.26.w_z, ...), custom_call_target="tpu_custom_call" | custom-call | tf_op jit(solution)/shard_map/back_project/pallas_call | solution.py:615
  431.2 2.3 fusion.19
  433.9 2.0 fusion.20
  435.9 2.2 fusion.6.refs_2_
  441.1 2.9 collective-permute-done.35
  444.7 1.8 collective-permute-start.36
  446.5 5.1 collective-permute-done.36
  456.0 1.8 fusion.14
  463.4 2.1 broadcast_select_fusion.52
  470.7 2.7 fusion.21
  476.9 5.2 collective-permute-done.41.refs_1_
  482.1 3.1 collective-permute-done.40.refs_0_
  485.1 2.5 fusion.23
  489.3 3.6 fusion.11.refs_3_
  500.7 3.4 collective-permute-done.46
  505.8 3.7 collective-permute-done.47
  510.3 2.4 collective-permute-start.48
  525.4 4.3 multiply_add_fusion.2
  529.8 3.3 multiply_add_fusion
  (453 shorter events, 128.5 us)
Async XLA Ops:
  7.2 95.0 %all-gather.4.cloned.1.call-start = ((), (), s32[]{:S(2)}) async-start(), calls=%async_computation.3 | async-start | bytes 6488064 | tf_op jit(solution)/shard_map/all_gather | solution.py:788
  10.7 8.4 %collective-permute-start.6 = (bf16[64,1408]{1,0:T(8,128)(2,1)S(1)}, bf16[64,1408]{1,0:T(8,128)(2,1)S(1)}, u32[]{:S(2)}, u32[]{:S(2)}) collective-permute-start(bf16[64,1408]{1,0:T(8,128)(2,1)S(1)} %get-tuple-element.226), channel_id=1, source_target_pairs={{0,1},{1,0},{2,3},{3,2},{4,5},{5,4},{6,7},{7,6},{8,9},{9,8},{10,11... | collective-permute-start | bytes 540680 | tf_op jit(solution)/shard_map/ppermute | solution.py:626
  13.8 9.9 %collective-permute-start.7 = (bf16[64,1408]{1,0:T(8,128)(2,1)S(1)}, bf16[64,1408]{1,0:T(8,128)(2,1)S(1)}, u32[]{:S(2)}, u32[]{:S(2)}) collective-permute-start(bf16[64,1408]{1,0:T(8,128)(2,1)S(1)} %get-tuple-element.225), channel_id=1, source_target_pairs={{0,2},{1,3},{2,0},{3,1},{4,6},{5,7},{6,4},{7,5},{8,10},{9,11},{10,... | collective-permute-start | bytes 540680 | tf_op jit(solution)/shard_map/ppermute | solution.py:626
  15.3 8.4 %collective-permute-start.8 = (bf16[64,1408]{1,0:T(8,128)(2,1)S(1)}, bf16[64,1408]{1,0:T(8,128)(2,1)S(1)}, u32[]{:S(2)}, u32[]{:S(2)}) collective-permute-start(bf16[64,1408]{1,0:T(8,128)(2,1)S(1)} %get-tuple-element.224), channel_id=1, source_target_pairs={{0,3},{1,2},{2,1},{3,0},{4,7},{5,6},{6,5},{7,4},{8,11},{9,10},{10,... | collective-permute-start | bytes 540680 | tf_op jit(solution)/shard_map/ppermute | solution.py:626
  27.7 146.6 %all-gather.6.cloned.1.call-start = ((), (), s32[]{:S(2)}) async-start(), calls=%async_computation.4 | async-start | bytes 4718592 | tf_op jit(solution)/shard_map/all_gather | solution.py:793
  27.8 23.8 %collective-permute-start.4 = (bf16[256,2048]{1,0:T(8,128)(2,1)S(1)}, bf16[256,2048]{1,0:T(8,128)(2,1)S(1)}, u32[]{:S(2)}, u32[]{:S(2)}) collective-permute-start(bf16[256,2048]{1,0:T(8,128)(2,1)S(1)} %copy-done.13), channel_id=1, source_target_pairs={{0,2},{1,3},{2,0},{3,1},{4,6},{5,7},{6,4},{7,5},{8,10},{9,11},{10,... | collective-permute-start | bytes 3145736 | tf_op jit(solution)/shard_map/ppermute | solution.py:626
  29.4 22.6 %collective-permute-start.5 = (bf16[256,2048]{1,0:T(8,128)(2,1)S(1)}, bf16[256,2048]{1,0:T(8,128)(2,1)}, u32[]{:S(2)}, u32[]{:S(2)}) collective-permute-start(bf16[256,2048]{1,0:T(8,128)(2,1)S(1)} %copy-done.12), channel_id=1, source_target_pairs={{0,1},{1,0},{2,3},{3,2},{4,5},{5,4},{6,7},{7,6},{8,9},{9,8},{10,11... | collective-permute-start | bytes 3145736 | tf_op jit(solution)/shard_map/ppermute | solution.py:626
  53.8 9.0 %collective-permute-start.10 = (bf16[64,2048]{1,0:T(8,128)(2,1)S(1)}, bf16[64,2048]{1,0:T(8,128)(2,1)S(1)}, u32[]{:S(2)}, u32[]{:S(2)}) collective-permute-start(bf16[64,2048]{1,0:T(8,128)(2,1)S(1)} %get-tuple-element.210), channel_id=1, source_target_pairs={{0,2},{1,3},{2,0},{3,1},{4,6},{5,7},{6,4},{7,5},{8,10},{9,11},{10,... | collective-permute-start | bytes 786440 | tf_op jit(solution)/shard_map/ppermute | solution.py:626
  54.7 8.3 %collective-permute-start.11 = (bf16[64,2048]{1,0:T(8,128)(2,1)S(1)}, bf16[64,2048]{1,0:T(8,128)(2,1)S(1)}, u32[]{:S(2)}, u32[]{:S(2)}) collective-permute-start(bf16[64,2048]{1,0:T(8,128)(2,1)S(1)} %get-tuple-element.209), channel_id=1, source_target_pairs={{0,1},{1,0},{2,3},{3,2},{4,5},{5,4},{6,7},{7,6},{8,9},{9,8},{10,11... | collective-permute-start | bytes 786440 | tf_op jit(solution)/shard_map/ppermute | solution.py:626
  56.2 10.6 %collective-permute-start.9 = (bf16[64,2048]{1,0:T(8,128)(2,1)S(1)}, bf16[64,2048]{1,0:T(8,128)(2,1)S(1)}, u32[]{:S(2)}, u32[]{:S(2)}) collective-permute-start(bf16[64,2048]{1,0:T(8,128)(2,1)S(1)} %get-tuple-element.211), channel_id=1, source_target_pairs={{0,3},{1,2},{2,1},{3,0},{4,7},{5,6},{6,5},{7,4},{8,11},{9,10},{10,... | collective-permute-start | bytes 786440 | tf_op jit(solution)/shard_map/ppermute | solution.py:626
  69.0 127.6 %all-gather.8.cloned.1.call-start = ((), (), s32[]{:S(2)}) async-start(), calls=%async_computation.5 | async-start | bytes 4718592 | tf_op jit(solution)/shard_map/all_gather | solution.py:794
  69.7 325.6 %reduce-scatter.6.cloned.1.call-start = ((), (), s32[]{:S(2)}) async-start(), calls=%async_computation.7 | async-start | bytes 4718592 | tf_op jit(solution)/shard_map/reduce_scatter | solution.py:824
  69.8 22.2 %collective-permute-start = (bf16[256,2048]{1,0:T(8,128)(2,1)S(1)}, bf16[256,2048]{1,0:T(8,128)(2,1)S(1)}, u32[]{:S(2)}, u32[]{:S(2)}) collective-permute-start(bf16[256,2048]{1,0:T(8,128)(2,1)S(1)} %copy-done.13), channel_id=1, source_target_pairs={{0,1},{1,0},{2,3},{3,2},{4,5},{5,4},{6,7},{7,6},{8,9},{9,8},{10,11... | collective-permute-start | bytes 3145736 | tf_op jit(solution)/shard_map/ppermute | solution.py:626
  71.5 24.5 %collective-permute-start.2 = (bf16[256,2048]{1,0:T(8,128)(2,1)S(1)}, bf16[256,2048]{1,0:T(8,128)(2,1)}, u32[]{:S(2)}, u32[]{:S(2)}) collective-permute-start(bf16[256,2048]{1,0:T(8,128)(2,1)S(1)} %copy-done.12), channel_id=1, source_target_pairs={{0,2},{1,3},{2,0},{3,1},{4,6},{5,7},{6,4},{7,5},{8,10},{9,11},{10,... | collective-permute-start | bytes 3145736 | tf_op jit(solution)/shard_map/ppermute | solution.py:626
  92.0 27.1 %collective-permute-start.1 = (bf16[256,2048]{1,0:T(8,128)(2,1)S(1)}, bf16[256,2048]{1,0:T(8,128)(2,1)S(1)}, u32[]{:S(2)}, u32[]{:S(2)}) collective-permute-start(bf16[256,2048]{1,0:T(8,128)(2,1)S(1)} %collective-permute-done.refs_3_), channel_id=1, source_target_pairs={{0,2},{1,3},{2,0},{3,1},{4,6},{5,7},{6,4},{7,5},{8,10},{9,11},{10,... | collective-permute-start | bytes 3145736 | tf_op jit(solution)/shard_map/ppermute | solution.py:626
  96.1 23.1 %collective-permute-start.3 = (bf16[256,2048]{1,0:T(8,128)(2,1)}, bf16[256,2048]{1,0:T(8,128)(2,1)S(1)}, u32[]{:S(2)}, u32[]{:S(2)}) collective-permute-start(bf16[256,2048]{1,0:T(8,128)(2,1)} %collective-permute-done.2.refs_6_), channel_id=1, source_target_pairs={{0,1},{1,0},{2,3},{3,2},{4,5},{5,4},{6,7},{7,6},{8,9},{9,8},{10,11... | collective-permute-start | bytes 3145736 | tf_op jit(solution)/shard_map/ppermute | solution.py:626
  120.4 53.9 %collective-permute-start.16 = (bf16[256,2048]{1,0:T(8,128)(2,1)}, bf16[256,2048]{1,0:T(8,128)(2,1)S(1)}, u32[]{:S(2)}, u32[]{:S(2)}) collective-permute-start(bf16[256,2048]{1,0:T(8,128)(2,1)} %get-tuple-element.98.refs_4_), channel_id=1, source_target_pairs={{0,2},{1,3},{2,0},{3,1},{4,6},{5,7},{6,4},{7,5},{8,10},{9,11},{10,... | collective-permute-start | bytes 3145736 | tf_op jit(solution)/shard_map/ppermute | solution.py:626
  121.0 56.3 %collective-permute-start.12 = (bf16[256,2048]{1,0:T(8,128)(2,1)}, bf16[256,2048]{1,0:T(8,128)(2,1)S(1)}, u32[]{:S(2)}, u32[]{:S(2)}) collective-permute-start(bf16[256,2048]{1,0:T(8,128)(2,1)} %get-tuple-element.95.refs_0_), channel_id=1, source_target_pairs={{0,1},{1,0},{2,3},{3,2},{4,5},{5,4},{6,7},{7,6},{8,9},{9,8},{10,11... | collective-permute-start | bytes 3145736 | tf_op jit(solution)/shard_map/ppermute | solution.py:626
  125.3 67.0 %collective-permute-start.15 = (bf16[256,2048]{1,0:T(8,128)(2,1)}, bf16[256,2048]{1,0:T(8,128)(2,1)}, u32[]{:S(2)}, u32[]{:S(2)}) collective-permute-start(bf16[256,2048]{1,0:T(8,128)(2,1)} %get-tuple-element.98.refs_4_), channel_id=1, source_target_pairs={{0,1},{1,0},{2,3},{3,2},{4,5},{5,4},{6,7},{7,6},{8,9},{9,8},{10,11... | collective-permute-start | bytes 3145736 | tf_op jit(solution)/shard_map/ppermute | solution.py:626
  125.5 69.1 %collective-permute-start.13 = (bf16[256,2048]{1,0:T(8,128)(2,1)}, bf16[256,2048]{1,0:T(8,128)(2,1)S(1)}, u32[]{:S(2)}, u32[]{:S(2)}) collective-permute-start(bf16[256,2048]{1,0:T(8,128)(2,1)} %get-tuple-element.95.refs_0_), channel_id=1, source_target_pairs={{0,2},{1,3},{2,0},{3,1},{4,6},{5,7},{6,4},{7,5},{8,10},{9,11},{10,... | collective-permute-start | bytes 3145736 | tf_op jit(solution)/shard_map/ppermute | solution.py:626
  175.3 18.4 %collective-permute-start.17 = (bf16[256,2048]{1,0:T(8,128)(2,1)}, bf16[256,2048]{1,0:T(8,128)(2,1)S(1)}, u32[]{:S(2)}, u32[]{:S(2)}) collective-permute-start(bf16[256,2048]{1,0:T(8,128)(2,1)} %after.30.refs_6_), channel_id=1, source_target_pairs={{0,1},{1,0},{2,3},{3,2},{4,5},{5,4},{6,7},{7,6},{8,9},{9,8},{10,11... | collective-permute-start | bytes 3145736 | tf_op jit(solution)/shard_map/ppermute | solution.py:626
  178.3 17.2 %collective-permute-start.14 = (bf16[256,2048]{1,0:T(8,128)(2,1)}, bf16[256,2048]{1,0:T(8,128)(2,1)S(1)}, u32[]{:S(2)}, u32[]{:S(2)}) collective-permute-start(bf16[256,2048]{1,0:T(8,128)(2,1)} %after.28.refs_1_), channel_id=1, source_target_pairs={{0,2},{1,3},{2,0},{3,1},{4,6},{5,7},{6,4},{7,5},{8,10},{9,11},{10,... | collective-permute-start | bytes 3145736 | tf_op jit(solution)/shard_map/ppermute | solution.py:626
  219.5 5.2 collective-permute-start.20
  264.1 131.2 %reduce-scatter.4.cloned.1.call-start = ((), (), s32[]{:S(2)}) async-start(), calls=%async_computation.6 | async-start | bytes 4718592 | tf_op jit(solution)/shard_map/reduce_scatter | solution.py:824
  278.2 185.2 %reduce-scatter.8.cloned.1.call-start = ((), (), s32[]{:S(2)}) async-start(), calls=%async_computation.8 | async-start | bytes 6488064 | tf_op jit(solution)/shard_map/reduce_scatter | solution.py:824
  278.2 51.7 %collective-permute-start.21 = (bf16[2,2,128,2048]{3,2,1,0:T(8,128)(2,1)}, bf16[2,2,128,2048]{3,2,1,0:T(8,128)(2,1)S(1)}, u32[]{:S(2)}, u32[]{:S(2)}) collective-permute-start(bf16[2,2,128,2048]{3,2,1,0:T(8,128)(2,1)} %get-tuple-element.104), channel_id=1, source_target_pairs={{0,1},{1,0},{2,3},{3,2},{4,5},{5,4},{6,7},{7,6},{8,9},{9,8},{10,11... | collective-permute-start | bytes 6291464 | tf_op jit(solution)/shard_map/ppermute | solution.py:626
  279.5 50.4 %collective-permute-start.22 = (bf16[2,2,128,2048]{3,2,1,0:T(8,128)(2,1)}, bf16[2,2,128,2048]{3,2,1,0:T(8,128)(2,1)}, u32[]{:S(2)}, u32[]{:S(2)}) collective-permute-start(bf16[2,2,128,2048]{3,2,1,0:T(8,128)(2,1)} %get-tuple-element.105), channel_id=1, source_target_pairs={{0,2},{1,3},{2,0},{3,1},{4,6},{5,7},{6,4},{7,5},{8,10},{9,11},{10,... | collective-permute-start | bytes 6291464 | tf_op jit(solution)/shard_map/ppermute | solution.py:626
  327.7 39.7 %collective-permute-start.25 = (bf16[1,2,128,2048]{3,2,1,0:T(8,128)(2,1)}, bf16[1,2,128,2048]{3,2,1,0:T(8,128)(2,1)S(1)}, u32[]{:S(2)}, u32[]{:S(2)}) collective-permute-start(bf16[1,2,128,2048]{3,2,1,0:T(8,128)(2,1)} %get-tuple-element.114.refs_2_.refs_0_), channel_id=1, source_target_pairs={{0,1},{1,0},{2,3},{3,2},{4,5},{5,4},{6,7},{7,6},{8,9},{9,8},{10,11... | collective-permute-start | bytes 3145736 | tf_op jit(solution)/shard_map/ppermute | solution.py:626
  328.9 38.5 %collective-permute-start.26 = (bf16[1,2,128,2048]{3,2,1,0:T(8,128)(2,1)}, bf16[1,2,128,2048]{3,2,1,0:T(8,128)(2,1)}, u32[]{:S(2)}, u32[]{:S(2)}) collective-permute-start(bf16[1,2,128,2048]{3,2,1,0:T(8,128)(2,1)} %get-tuple-element.118.refs_1_), channel_id=1, source_target_pairs={{0,2},{1,3},{2,0},{3,1},{4,6},{5,7},{6,4},{7,5},{8,10},{9,11},{10,... | collective-permute-start | bytes 3145736 | tf_op jit(solution)/shard_map/ppermute | solution.py:626
  333.4 34.0 %collective-permute-start.24 = (bf16[2,1,128,2048]{3,2,1,0:T(8,128)(2,1)S(1)}, bf16[2,1,128,2048]{3,2,1,0:T(8,128)(2,1)S(1)}, u32[]{:S(2)}, u32[]{:S(2)}) collective-permute-start(bf16[2,1,128,2048]{3,2,1,0:T(8,128)(2,1)S(1)} %add_convert_fusion.3.refs_3_), channel_id=1, source_target_pairs={{0,1},{1,0},{2,3},{3,2},{4,5},{5,4},{6,7},{7,6},{8,9},{9,8},{10,11... | collective-permute-start | bytes 3145736 | tf_op jit(solution)/shard_map/ppermute | solution.py:626
  336.3 31.1 %collective-permute-start.23 = (bf16[2,1,128,2048]{3,2,1,0:T(8,128)(2,1)S(1)}, bf16[2,1,128,2048]{3,2,1,0:T(8,128)(2,1)S(1)}, u32[]{:S(2)}, u32[]{:S(2)}) collective-permute-start(bf16[2,1,128,2048]{3,2,1,0:T(8,128)(2,1)S(1)} %add_convert_fusion.4.refs_2_), channel_id=1, source_target_pairs={{0,2},{1,3},{2,0},{3,1},{4,6},{5,7},{6,4},{7,5},{8,10},{9,11},{10,... | collective-permute-start | bytes 3145736 | tf_op jit(solution)/shard_map/ppermute | solution.py:626
  392.0 36.1 %collective-permute-start.31 = (bf16[1,1,128,2048]{3,2,1,0:T(8,128)(2,1)S(1)}, bf16[1,1,128,2048]{3,2,1,0:T(8,128)(2,1)S(1)}, u32[]{:S(2)}, u32[]{:S(2)}) collective-permute-start(bf16[1,1,128,2048]{3,2,1,0:T(8,128)(2,1)S(1)} %add_convert_fusion.16.refs_3_), channel_id=1, source_target_pairs={{0,1},{1,0},{2,3},{3,2},{4,5},{5,4},{6,7},{7,6},{8,9},{9,8},{10,11... | collective-permute-start | bytes 1572872 | tf_op jit(solution)/shard_map/ppermute | solution.py:626
  394.2 33.9 %collective-permute-start.30 = (bf16[1,1,128,2048]{3,2,1,0:T(8,128)(2,1)S(1)}, bf16[1,1,128,2048]{3,2,1,0:T(8,128)(2,1)S(1)}, u32[]{:S(2)}, u32[]{:S(2)}) collective-permute-start(bf16[1,1,128,2048]{3,2,1,0:T(8,128)(2,1)S(1)} %add_convert_fusion.17.refs_2_), channel_id=1, source_target_pairs={{0,2},{1,3},{2,0},{3,1},{4,6},{5,7},{6,4},{7,5},{8,10},{9,11},{10,... | collective-permute-start | bytes 1572872 | tf_op jit(solution)/shard_map/ppermute | solution.py:626
  398.5 6.6 %collective-permute-start.27 = (bf16[64,2048]{1,0:T(8,128)(2,1)}, bf16[64,2048]{1,0:T(8,128)(2,1)S(1)}, u32[]{:S(2)}, u32[]{:S(2)}) collective-permute-start(bf16[64,2048]{1,0:T(8,128)(2,1)} %get-tuple-element.203), channel_id=1, source_target_pairs={{0,1},{1,0},{2,3},{3,2},{4,5},{5,4},{6,7},{7,6},{8,9},{9,8},{10,11... | collective-permute-start | bytes 786440 | tf_op jit(solution)/shard_map/ppermute | solution.py:626
  399.8 9.4 %collective-permute-start.28 = (bf16[64,2048]{1,0:T(8,128)(2,1)}, bf16[64,2048]{1,0:T(8,128)(2,1)S(1)}, u32[]{:S(2)}, u32[]{:S(2)}) collective-permute-start(bf16[64,2048]{1,0:T(8,128)(2,1)} %get-tuple-element.204), channel_id=1, source_target_pairs={{0,2},{1,3},{2,0},{3,1},{4,6},{5,7},{6,4},{7,5},{8,10},{9,11},{10,... | collective-permute-start | bytes 786440 | tf_op jit(solution)/shard_map/ppermute | solution.py:626
  400.8 8.4 %collective-permute-start.29 = (bf16[64,2048]{1,0:T(8,128)(2,1)S(1)}, bf16[64,2048]{1,0:T(8,128)(2,1)S(1)}, u32[]{:S(2)}, u32[]{:S(2)}) collective-permute-start(bf16[64,2048]{1,0:T(8,128)(2,1)S(1)} %get-tuple-element.202), channel_id=1, source_target_pairs={{0,3},{1,2},{2,1},{3,0},{4,7},{5,6},{6,5},{7,4},{8,11},{9,10},{10,... | collective-permute-start | bytes 786440 | tf_op jit(solution)/shard_map/ppermute | solution.py:626
  429.1 30.7 %collective-permute-start.32 = (bf16[1,2,128,2048]{3,2,1,0:T(8,128)(2,1)}, bf16[1,2,128,2048]{3,2,1,0:T(8,128)(2,1)}, u32[]{:S(2)}, u32[]{:S(2)}) collective-permute-start(bf16[1,2,128,2048]{3,2,1,0:T(8,128)(2,1)} %get-tuple-element.130.refs_2_.refs_1_), channel_id=1, source_target_pairs={{0,1},{1,0},{2,3},{3,2},{4,5},{5,4},{6,7},{7,6},{8,9},{9,8},{10,11... | collective-permute-start | bytes 3145736 | tf_op jit(solution)/shard_map/ppermute | solution.py:626
  430.1 8.1 %collective-permute-start.34 = (f32[64,128]{1,0:T(8,128)}, f32[64,128]{1,0:T(8,128)S(1)}, u32[]{:S(2)}, u32[]{:S(2)}) collective-permute-start(f32[64,128]{1,0:T(8,128)} %after.40), channel_id=1, source_target_pairs={{0,4},{4,0},{8,12},{12,8},{16,20},{20,16},{24,28},{28,24},{1,5},{5... | collective-permute-start | bytes 98312 | tf_op jit(solution)/shard_map/ppermute | solution.py:626
  430.1 29.6 %collective-permute-start.33 = (bf16[1,2,128,2048]{3,2,1,0:T(8,128)(2,1)}, bf16[1,2,128,2048]{3,2,1,0:T(8,128)(2,1)}, u32[]{:S(2)}, u32[]{:S(2)}) collective-permute-start(bf16[1,2,128,2048]{3,2,1,0:T(8,128)(2,1)} %get-tuple-element.136), channel_id=1, source_target_pairs={{0,2},{1,3},{2,0},{3,1},{4,6},{5,7},{6,4},{7,5},{8,10},{9,11},{10,... | collective-permute-start | bytes 3145736 | tf_op jit(solution)/shard_map/ppermute | solution.py:626
  438.8 5.2 collective-permute-start.35
  444.7 7.0 %collective-permute-start.36 = (f32[64,128]{1,0:T(8,128)}, f32[64,128]{1,0:T(8,128)}, u32[]{:S(2)}, u32[]{:S(2)}) collective-permute-start(f32[64,128]{1,0:T(8,128)} %add.298), channel_id=1, source_target_pairs={{0,16},{4,20},{8,24},{12,28},{16,0},{20,4},{24,8},{28,12},{1,17},{... | collective-permute-start | bytes 98312 | tf_op jit(solution)/shard_map/ppermute | solution.py:626
  452.4 5.3 collective-permute-start.37
  453.4 5.0 collective-permute-start.38
  467.0 15.0 %collective-permute-start.41 = (bf16[1,1,128,2048]{3,2,1,0:T(8,128)(2,1)S(1)}, bf16[1,1,128,2048]{3,2,1,0:T(8,128)(2,1)}, u32[]{:S(2)}, u32[]{:S(2)}) collective-permute-start(bf16[1,1,128,2048]{3,2,1,0:T(8,128)(2,1)S(1)} %add_convert_fusion.9), channel_id=1, source_target_pairs={{0,1},{1,0},{2,3},{3,2},{4,5},{5,4},{6,7},{7,6},{8,9},{9,8},{10,11... | collective-permute-start | bytes 1572872 | tf_op jit(solution)/shard_map/ppermute | solution.py:626
  469.6 15.6 %collective-permute-start.40 = (bf16[1,1,128,2048]{3,2,1,0:T(8,128)(2,1)S(1)}, bf16[1,1,128,2048]{3,2,1,0:T(8,128)(2,1)}, u32[]{:S(2)}, u32[]{:S(2)}) collective-permute-start(bf16[1,1,128,2048]{3,2,1,0:T(8,128)(2,1)S(1)} %add_convert_fusion.10), channel_id=1, source_target_pairs={{0,2},{1,3},{2,0},{3,1},{4,6},{5,7},{6,4},{7,5},{8,10},{9,11},{10,... | collective-permute-start | bytes 1572872 | tf_op jit(solution)/shard_map/ppermute | solution.py:626
  473.4 19.5 %collective-permute-start.42 = (bf16[64,1408]{1,0:T(8,128)(2,1)}, bf16[64,1408]{1,0:T(8,128)(2,1)}, u32[]{:S(2)}, u32[]{:S(2)}) collective-permute-start(bf16[64,1408]{1,0:T(8,128)(2,1)} %get-tuple-element.222.refs_3_), channel_id=1, source_target_pairs={{0,1},{1,0},{2,3},{3,2},{4,5},{5,4},{6,7},{7,6},{8,9},{9,8},{10,11... | collective-permute-start | bytes 540680 | tf_op jit(solution)/shard_map/ppermute | solution.py:626
  474.3 18.6 %collective-permute-start.43 = (bf16[64,1408]{1,0:T(8,128)(2,1)}, bf16[64,1408]{1,0:T(8,128)(2,1)}, u32[]{:S(2)}, u32[]{:S(2)}) collective-permute-start(bf16[64,1408]{1,0:T(8,128)(2,1)} %get-tuple-element.223.refs_4_), channel_id=1, source_target_pairs={{0,2},{1,3},{2,0},{3,1},{4,6},{5,7},{6,4},{7,5},{8,10},{9,11},{10,... | collective-permute-start | bytes 540680 | tf_op jit(solution)/shard_map/ppermute | solution.py:626
  475.3 17.6 %collective-permute-start.44 = (bf16[64,1408]{1,0:T(8,128)(2,1)}, bf16[64,1408]{1,0:T(8,128)(2,1)}, u32[]{:S(2)}, u32[]{:S(2)}) collective-permute-start(bf16[64,1408]{1,0:T(8,128)(2,1)} %get-tuple-element.220.refs_5_), channel_id=1, source_target_pairs={{0,3},{1,2},{2,1},{3,0},{4,7},{5,6},{6,5},{7,4},{8,11},{9,10},{10,... | collective-permute-start | bytes 540680 | tf_op jit(solution)/shard_map/ppermute | solution.py:626
  (100 other events, 384.4 us)
Sparse Core Ops, SparseCore 0:
  27.8 60.7 all-gather.3
  90.8 45.8 all-gather.5
  138.3 45.7 all-gather.7
  264.2 50.2 reduce-scatter.5
  316.7 48.1 reduce-scatter.3
  388.7 66.4 reduce-scatter.7

commit v5 on v4

--- a/solution.py
+++ b/solution.py
@@ -622,6 +622,120 @@
         **arbitrary("back_project"),
     )(dz, px, w_z, w_x)
 
+
+def shard_kernel(spot, *refs, n, hl):
+    fronts, backs, (weight, gain, shard_in, shard_out, last) = refs[:n], refs[n : 2 * n], refs[2 * n :]
+    rank, own = spot[0], spot[1]
+    width = hl * HEADDIM
+    rows = weight.shape[0]
+    lane = iota2((rows, LANES), 1)
+    square = jnp.zeros((rows, LANES), F32)
+    scaled = jnp.zeros((rows, LANES), F32)
+    shared = [jnp.zeros((rows, LANES), F32) for _ in range(2 * STATE // LANES + 1)]
+    for mask in range(n):
+        at = (rank ^ mask) * width
+        for lo in range(0, width, LANES):
+            spot_z = pl.multiple_of(at + lo, LANES)
+            spot_x = pl.multiple_of(INNER + at + lo, LANES)
+            out = fronts[mask][:, lo : lo + LANES].astype(F32)
+            z = fronts[mask][:, width + lo : width + lo + LANES].astype(F32)
+            x = backs[mask][:, lo : lo + LANES].astype(F32)
+            shard_out[:, pl.ds(spot_z, LANES)] = out
+            shard_in[:, pl.ds(spot_z, LANES)] = z
+            shard_in[:, pl.ds(spot_x, LANES)] = x
+            square += out * out + z * z + x * x
+            scaled += weight[:, pl.ds(spot_z, LANES)].astype(BF).astype(F32) * z
+            scaled += weight[:, pl.ds(spot_x, LANES)].astype(BF).astype(F32) * x
+        for at_lane in range(2 * STATE // LANES):
+            lo = width + at_lane * LANES
+            shared[at_lane] += backs[mask][:, lo : lo + LANES].astype(F32)
+        steps = jnp.where(lane < hl, backs[mask][:, width + 2 * STATE :].astype(F32), 0.0)
+        shared[-1] += pltpu.roll(steps, (rank ^ mask) * hl, 1)
+    for at_lane, one in enumerate(shared):
+        lo = 2 * INNER + at_lane * LANES
+        wide = min(LANES, weight.shape[1] - lo)
+        one = one[:, :wide]
+        shard_in[:, lo : lo + wide] = one
+        square += jnp.concatenate([one * one, jnp.zeros((rows, LANES - wide), F32)], axis=1) if wide < LANES else one * one
+        part = weight[:, lo : lo + wide].astype(BF).astype(F32) * one
+        scaled += jnp.concatenate([part, jnp.zeros((rows, LANES - wide), F32)], axis=1) if wide < LANES else part
+    d_gain = jnp.sum(scaled, axis=1, keepdims=True) / gain[:, 0:1]
+    start = own * rows
+    line = jnp.sum(jnp.where(lane == start % LANES + iota2((rows, LANES), 0), d_gain, 0.0), axis=0, keepdims=True)
+    total = jnp.sum(jnp.sum(square, axis=0, keepdims=True), axis=1, keepdims=True)
+    row, col = iota2(last.shape, 0), iota2(last.shape, 1)
+    last[...] = jnp.where(row == start // LANES, line, 0.0) + jnp.where((row == D // LANES) & (col == 0), total, 0.0)
+
+
+def shards(spot, fronts, backs, weight, gain, hl):
+    rows = weight.shape[0]
+    return pl.pallas_call(
+        functools.partial(shard_kernel, n=len(fronts), hl=hl),
+        grid_spec=pltpu.PrefetchScalarGridSpec(
+            num_scalar_prefetch=1,
+            grid=(1,),
+            in_specs=[pl.BlockSpec(one.shape, lambda i, spot: (0, 0)) for one in (*fronts, *backs, weight, gain)],
+            out_specs=[
+                pl.BlockSpec(weight.shape, lambda i, spot: (0, 0)),
+                pl.BlockSpec((rows, INNER), lambda i, spot: (0, 0)),
+                pl.BlockSpec((D // LANES + 8, LANES), lambda i, spot: (0, 0)),
+            ],
+        ),
+        out_shape=[
+            jax.ShapeDtypeStruct(weight.shape, F32),
+            jax.ShapeDtypeStruct((rows, INNER), F32),
+            jax.ShapeDtypeStruct((D // LANES + 8, LANES), F32),
+        ],
+        **arbitrary("shards"),
+    )(spot, *fronts, *backs, weight, gain)
+
+
+def small_kernel(conv_0, conv_1, vec_0, vec_1, skip_0, skip_1, gain, out):
+    width = gain.shape[1]
+    out[...] = jnp.zeros(out.shape, F32)
+    for tap in range(CONV + 1):
+        rows = slice(tap * 8, tap * 8 + 8)
+        out[tap : tap + 1, :] = jnp.sum(conv_0[rows, :] + conv_1[rows, :], axis=0, keepdims=True)
+    out[5:6, :width] = jnp.sum(gain[...], axis=0, keepdims=True)
+    out[6:7, :width] = jnp.sum(skip_0[...] + skip_1[...], axis=0, keepdims=True)
+    vec = vec_0[...] + vec_1[...]
+    head, lane = iota2((SLOT, LANES), 0), iota2((SLOT, LANES), 1)
+    line = jnp.where(lane == head, vec[:, 0:1], jnp.where(lane == SLOT + head, vec[:, 1:2], 0.0))
+    out[7:8, :LANES] = jnp.sum(line, axis=0, keepdims=True)
+
+
+def small_gradients(*parts):
+    return pl.pallas_call(
+        small_kernel,
+        out_shape=jax.ShapeDtypeStruct((8, parts[0].shape[1]), F32),
+        name="small_gradients",
+    )(*parts)
+
+
+def place_kernel(spot, *refs, width):
+    *pieces, out = refs
+    shared = 0.0
+    for mask, piece in enumerate(pieces):
+        at = (spot[0] ^ mask) * width
+        for lo in range(0, width, LANES):
+            out[:, pl.ds(pl.multiple_of(at + lo, LANES), LANES)] = piece[:, lo : lo + LANES]
+        shared = shared + piece[:, width:]
+    out[:, INNER:] = shared
+
+
+def place_small(spot, pieces, width):
+    return pl.pallas_call(
+        functools.partial(place_kernel, width=width),
+        grid_spec=pltpu.PrefetchScalarGridSpec(
+            num_scalar_prefetch=1,
+            grid=(1,),
+            in_specs=[pl.BlockSpec(one.shape, lambda i, spot: (0, 0)) for one in pieces],
+            out_specs=pl.BlockSpec((8, CH), lambda i, spot: (0, 0)),
+        ),
+        out_shape=jax.ShapeDtypeStruct((8, CH), F32),
+        **arbitrary("place_small"),
+    )(spot, *pieces)
+
 def swapped(value, axis, mask):
     return lax.ppermute(value, axis, [(i, i ^ mask) for i in range(lax.axis_size(axis))])
 
@@ -715,13 +829,6 @@
     return entries, [swapped(one, "seq", mask) for mask, one in enumerate(entries) if mask]
 
 
-def sum_all(value):
-    for axis in ("dp", "seq"):
-        for bit in axis_bits(axis):
-            value = value + swapped(value, axis, bit)
-    return value
-
-
 def sum_pieces(value):
     n = value.shape[-2]
     total = value
@@ -743,6 +850,7 @@
                out_weight, out_m, out_v, packed, packed_m, packed_v):
     n = lax.axis_size("seq")
     rank = lax.axis_index("seq")
+    own = lax.axis_index("dp") * n + rank
     place = rank.astype(jnp.int32).reshape(1)
     ndev = n * lax.axis_size("dp")
     hl = HEADS // n
@@ -803,7 +911,7 @@
     late = [micro * n + at for micro in range(MICRO) for at in range(n) if at & (last := micro_order(micro, "seq")[-1]) and at != last]
     soon = [at for at in range(MICRO * n) if at not in late]
     soon.sort(key=lambda at: (at % n).bit_count())
-    earlier = in_project([more[at] for at in soon], soon, MICRO * n, w_x, done=(aux, masks))
+    earlier = in_project([more[at] for at in soon], soon, MICRO * n, w_x, done=(aux, masks, conv_loc))
     late_pieces = after([more[at] for at in late], earlier[0])
     proj_x, hidden = in_project(late_pieces, late, MICRO * n, w_x, earlier)
 
@@ -819,7 +927,6 @@
     sums = sum_pieces(sums.reshape(MICRO, n, 8 * BLOCK)).reshape(-1, BLOCK)
     first_bits = tuple(micro_order(half, "seq")[0] for half in range(2))
     normed, dy, dz, d_gain_out, *out_part = out_project(z, dn, y, sums, gain, w_o, first_bits)
-    d_gain_out = jnp.sum(d_gain_out, axis=0)
 
     scatter = lambda a: lax.psum_scatter(a, "dp", scatter_dimension=0, tiled=True)
     split = lambda a: [a[q * rows : (q + 1) * rows] for q in range(n)]
@@ -844,59 +951,47 @@
     part_x = dot(hidden, jnp.concatenate([px_0, px_1], axis=0), TN).astype(BF)
     got_x = scatter(part_x)
     hid_got, sent = stages_0.send([part_x])
-    [got_o, got_z] = after([got_o, got_z], px_1)
+    spot = jnp.stack([rank, own]).astype(jnp.int32)
+    own_gain = lax.dynamic_slice_in_dim(gain_in, own * rows, rows)[:, None]
+    first_bit, *more_bits = axis_bits("dp")
+    small = small_gradients(conv_0, conv_1, vec_0, vec_1, skip_0, skip_1, d_gain_out)
+    small = small + swapped(small, "dp", first_bit)
+    [px_1] = after([px_1], part_x, *sent, small)
+    hid_1 = through_in(1, px_1)
+    [got_o, got_z] = after([got_o, got_z], part_x)
     sent_oz, got_oz = exchange(split(jnp.concatenate([got_o, got_z], axis=1)), rank)
-    [px_1] = after([px_1], part_x, *sent, *got_oz)
-    hid_1 = after(through_in(1, px_1), *hid_got)
+    [small] = after([small], hid_1[0], *got_oz)
+    for bit in more_bits:
+        small = small + swapped(small, "dp", bit)
+    small = [small] + [swapped(small, "seq", mask) for mask in range(1, n)]
+    hid_1 = after(hid_1, *hid_got, *small[1:])
     stages_1 = scatter_stages(hid_1)
     hid_got, hid_sent = next(stages_1)
-    output = (tok + finish(out_stages, [hid_1[0]]).astype(F32)).astype(BF)
-
-    d_conv = (conv_0 + conv_1).reshape(CONV + 1, 8, -1).sum(axis=1)
-    d_skip = jnp.sum((skip_0 + skip_1).reshape(8, hl, HEADDIM), axis=(0, 2))
-    d_vec = vec_0 + vec_1
-    head_rows = jnp.concatenate([d_vec[:hl, 0], d_skip, d_vec[:hl, 1]])
-    small = jnp.concatenate([d_conv.reshape(-1), d_gain_out, head_rows])
-    small_size = small.shape[0]
-    small = jnp.pad(small, (0, -small_size % 1024)).reshape(-1, LANES)
-    [small] = after([small], hid_1[0])
-    for bit in axis_bits("dp"):
-        small = small + swapped(small, "dp", bit)
-    small = [small] + after([swapped(small, "seq", mask) for mask in range(1, n)], *hid_got)
-    small = jnp.stack(turned(small, rank)).reshape(n, -1)[:, :small_size]
-    conv_all = small[:, : (CONV + 1) * (xw + bc)].reshape(n, CONV + 1, xw + bc)
-    conv_tot = jnp.concatenate(
-        [conv_all[:, :, :xw].transpose(1, 0, 2).reshape(CONV + 1, INNER), jnp.sum(conv_all[:, :, xw:], axis=0)], axis=1
-    )
-    gain_out_tot = small[:, (CONV + 1) * (xw + bc) : small_size - 3 * hl].reshape(-1)
-    heads_tot = small[:, small_size - 3 * hl :].reshape(n, 3, hl).transpose(1, 0, 2).reshape(-1)
-
-    [got_x] = after([got_x], conv_tot, output)
+    small = place_small(spot, small, xw)
+    conv_tot, gain_out_tot = small[: CONV + 1], small[5, :INNER]
+    skip_tot = jnp.sum(small[6, :INNER].reshape(HEADS, HEADDIM), axis=1)
+    by_head = small[7, :INNER].reshape(n, xw)
+    a_log_tot, dt_bias_tot = by_head[:, :hl].reshape(-1), by_head[:, SLOT : SLOT + hl].reshape(-1)
+    shard_conv = lax.dynamic_slice_in_dim(conv_tot, own * cw, cw, 1)
+    conv_sq = jnp.sum(conv_tot * conv_tot)
+
+    [got_x] = after([got_x], small)
     sent_x, got_x = exchange(split(got_x), rank)
-    d_hidden = jnp.concatenate([finish(stages_0, [hid_1[0]]), finish(stages_1, sent_x)], axis=0).astype(F32)
+    shard_in, shard_out, last = shards(spot, sent_oz[:1] + got_oz, sent_x[:1] + got_x, in_weight, own_gain, hl)
+    shard_out = shard_out.T
+    output = (tok + finish(out_stages, [small]).astype(F32)).astype(BF)
+    d_hidden = jnp.concatenate([finish(stages_0, [hid_1[0]]), finish(stages_1, got_x)], axis=0).astype(F32)
     dh = d_hidden * gain_in
     d_tok = r_in * (dh - tok * (r_in * r_in) * jnp.mean(dh * tok, axis=-1, keepdims=True))
     input_grad = (cotangent.astype(F32) + d_tok).astype(BF)
-    got_x = after(got_x, input_grad)
-    got_oz, got_x = (turned(sent[:1] + got, rank) for sent, got in ((sent_oz, got_oz), (sent_x, got_x)))
-
-    together = lambda parts, lo, hi: jnp.concatenate([one[:, lo:hi] for one in parts], axis=1).astype(F32)
-    g_bc = sum(one[:, xw : xw + bc].astype(F32) for one in got_x)
-    shard_in = jnp.concatenate(
-        [together(got_oz, xw, 2 * xw), together(got_x, 0, xw), g_bc, together(got_x, xw + bc, xw + bc + hl)], axis=1
-    )
-    shard_out = together(got_oz, 0, xw).T
-
-    own = lax.axis_index("dp") * n + rank
-    own_gain = lax.dynamic_slice_in_dim(gain_in, own * rows, rows)
-    d_gain_in = jnp.sum(in_low.astype(F32) * shard_in, axis=1) / own_gain
-    partial_sq = jnp.sum(shard_in * shard_in) + jnp.sum(shard_out * shard_out)
-    last = lax.dynamic_update_slice(jnp.zeros((D + 1024,), F32), d_gain_in, (own * rows,))
-    last = lax.dynamic_update_slice(last, partial_sq[None], (D,))
-    last = sum_all(last.reshape(-1, LANES)).reshape(-1)
-    vec_tot = jnp.concatenate([heads_tot, last[:D], gain_out_tot])
-    shard_conv = lax.dynamic_slice_in_dim(conv_tot, own * cw, cw, 1)
-    grad_norm = jnp.sqrt(last[D] + jnp.sum(conv_tot * conv_tot) + jnp.sum(vec_tot * vec_tot))
+
+    stages = [(axis, bit) for axis in ("dp", "seq") for bit in axis_bits(axis)]
+    for axis, bit in stages[:-1]:
+        last = last + swapped(last, axis, bit)
+    [last] = after([last], input_grad)
+    last = last + swapped(last, *stages[-1])
+    vec_tot = jnp.concatenate([a_log_tot, skip_tot, dt_bias_tot, last[: D // LANES].reshape(-1), gain_out_tot])
+    grad_norm = jnp.sqrt(last[D // LANES, 0] + conv_sq + jnp.sum(vec_tot * vec_tot))
     clip = jnp.minimum(1.0, CLIP_NORM / (grad_norm + 1e-06))
     in_new = adamw(in_weight, shard_in, in_m, in_v, clip, WEIGHT_DECAY)
     conv_new = adamw(conv_weight, shard_conv, conv_m, conv_v, clip, WEIGHT_DECAY)

time: 549 us -> 537 us (0.978)
  local copies, waits for them, and re-layouts: 47.5 us -> 37.3 us
  other arithmetic: 67.4 us -> 58 us
  Pallas kernels: 197 us -> 206 us
    pallas_call x0 -> x3, Pallas kernels: none -> 9.3 us  [the longest x1 5.34 us: shards(): pl.pallas_call(functools.partial(shard_kernel, n=len(fronts), hl=hl), gri...]
    reduce_scatter x3, waiting for transfers between devices: 0.01 us -> 8.09 us  [per_device(): lax.psum_scatter(a, 'dp', scatter_dimension=0, tiled=True)]
    unnamed x195 -> x152, local copies, waits for them, and re-layouts: 22.2 us -> 15.8 us
    ppermute x50, waiting for transfers between devices: 93.5 us -> 88 us  [swapped(): lax.ppermute(value, axis, [(i, i ^ mask) for i in range(lax.axis_size(axi...]
  transfers between devices with their start and end apart: 56 -> 56, of which waited for: 24 -> 27; matrix products, arithmetic and copies ran while one was open for 20% -> 19% of each run, Pallas kernels for 28% -> 31%
where the time goes in v5:
time: 537 us; the launch traced here: 530 us
  Pallas kernels  206 us (38%)
  waiting for transfers between devices  96.8 us (18%)
  matrix products  61.2 us (11%)
  other arithmetic  58 us (11%)
  starting transfers between devices  52 us (10%)
  local copies, waits for them, and re-layouts  37.3 us (7%)
  between operations  18.6 us (3%)
    ppermute x50, waiting for transfers between devices, swapped(): lax.ppermute(value, axis, [(i, i ^ mask) for i in range(lax.axis_size(axi...  88 us
    dot_general x4, matrix products, dot(): return lax.dot_general(a, b, (dims, ((), ())), preferred_element_type=out)  61.2 us
    pallas_call x2, Pallas kernels, scan_backward(): pl.pallas_call(functools.partial(backward_kernel, hl=hl), grid_spec=grid_...  60.1 us
    ppermute x50, starting transfers between devices, swapped(): lax.ppermute(value, axis, [(i, i ^ mask) for i in range(lax.axis_size(axi...  51.7 us
    pallas_call x2, Pallas kernels, back_project(): pl.pallas_call(functools.partial(back_kernel, n=n, bits=bits), grid=(n,),...  34.9 us
    pallas_call x1, Pallas kernels, scan_forward(): pl.pallas_call(functools.partial(forward_kernel, hl=hl), grid_spec=grid_s...  32.8 us
    pallas_call x2, Pallas kernels, in_project(): pl.pallas_call(functools.partial(in_kernel, count=count), grid_spec=pltpu...  26 us
    pallas_call x1, Pallas kernels, out_project(): pl.pallas_call(functools.partial(out_kernel, n=n, bits=bits), grid=(token...  23.8 us
  transfers between devices with their start and end apart: 56, of which 27 were waited for; matrix products, arithmetic and copies ran while one was open for 19% of the time, Pallas kernels for 31%

profile of v5, /device:TPU:0, one launch (start us, length us, event | category | flops | bytes accessed | tf_op | source)
XLA Modules:
  0.0 530.1 jit_solution(14071345963987756995)
XLA Ops:
  7.2 1.7 convert_element_type.242
  10.7 3.0 collective-permute-start.6
  19.2 4.4 collective-permute-done.7.refs_1_
  33.7 17.9 %collective-permute-done.4.refs_4_.refs_2_ = bf16[256,2048]{1,0:T(8,128)(2,1)S(1)} collective-permute-done((bf16[256,2048]{1,0:T(8,128)(2,1)S(1)}, bf16[256,2048]{1,0:T(8,128)(2,1)S(1)}, u32[]{:S(2)}, u32[]{:S(2)}) %collective-permute-start.4) | collective-permute-done | bytes 1048608 | tf_op jit(solution)/shard_map/ppermute | solution.py:740
  57.4 5.5 %collective-permute-done.10 = bf16[64,2048]{1,0:T(8,128)(2,1)S(1)} collective-permute-done((bf16[64,2048]{1,0:T(8,128)(2,1)S(1)}, bf16[64,2048]{1,0:T(8,128)(2,1)S(1)}, u32[]{:S(2)}, u32[]{:S(2)}) %collective-permute-start.10) | collective-permute-done | bytes 262176 | tf_op jit(solution)/shard_map/ppermute | solution.py:740
  63.0 3.7 collective-permute-done.9
  69.7 1.8 collective-permute-start
  74.3 17.8 %collective-permute-done.refs_3_ = bf16[256,2048]{1,0:T(8,128)(2,1)} collective-permute-done((bf16[256,2048]{1,0:T(8,128)(2,1)S(1)}, bf16[256,2048]{1,0:T(8,128)(2,1)}, u32[]{:S(2)}, u32[]{:S(2)}) %collective-permute-start) | collective-permute-done | bytes 1048608 | tf_op jit(solution)/shard_map/ppermute | solution.py:740
  92.1 3.7 collective-permute-done.2.refs_6_
  96.7 3.2 slice_bitcast_fusion.2
  102.8 16.9 %in_project.2 = (bf16[2048,1408]{1,0:T(8,128)(2,1)}, bf16[2048,2048]{1,0:T(8,128)(2,1)}) custom-call(s32[6]{0:T(128)} %constant.29.clone.refs_0_, bf16[256,2048]{1,0:T(8,128)(2,1)} %get-tuple-element.172.refs_3_.refs_1_, bf16[256,2048]{1,0:T(8,128)(2,1)} %get-tuple-element.171.refs_4_.refs_2_, bf16[256,2048]{1,0:T(8,128)(2,1)} %collective-permute-done.refs_3_, ...), custom_call_target="tpu_custom_call" | custom-call | tf_op jit(solution)/shard_map/in_project/pallas_call | solution.py:507
  127.8 9.1 %in_project.3 = (bf16[2048,1408]{1,0:T(8,128)(2,1)}, bf16[2048,2048]{1,0:T(8,128)(2,1)}) custom-call(s32[2]{0:T(128)} %constant.30.clone.refs_0_, bf16[256,2048]{1,0:T(8,128)(2,1)} %get-tuple-element.86.refs_1_.refs_2_, bf16[256,2048]{1,0:T(8,128)(2,1)} %get-tuple-element.87.refs_2_.refs_3_, ...), custom_call_target="tpu_custom_call", output_to_operand_aliasing={{0}: (4, {}), {1}: (5, {})} | custom-call | tf_op jit(solution)/shard_map/in_project/pallas_call | solution.py:507
  137.5 32.8 %scan_forward.1 = (bf16[2048,1024]{1,0:T(8,128)(2,1)}, bf16[8,1024,128]{2,1,0:T(8,128)(2,1)}, bf16[2048,1280]{1,0:T(8,128)(2,1)}, bf16[2048,1280]{1,0:T(8,128)(2,1)}) custom-call(s32[1]{0:T(128)} %bitcast.19.place, bf16[2048,1408]{1,0:T(8,128)(2,1)} %get-tuple-element.90.proj.refs_1_, f32[8,1280]{1,0:T(8,128)} %fusion.26.refs_10_.conv_w, ...), custom_call_target="tpu_custom_call" | custom-call | tf_op jit(solution)/shard_map/scan_forward/pallas_call | solution.py:355
  171.3 2.0 collective-permute-start.17
  174.5 13.8 %convolution_convert_fusion.1.refs_8_.z_in = bf16[2048,1024]{1,0:T(8,128)(2,1)} fusion(bf16[2048,2048]{1,0:T(8,128)(2,1)} %get-tuple-element.89, bf16[2048,1024]{1,0:T(8,128)(2,1)} %after.25.w_z), kind=kOutput, calls=%fused_computation.20 | convolution fusion | flops 8592031744 | bytes 16777216 | tf_op jit(solution)/shard_map/dot_general | solution.py:34
  193.0 19.2 %gate_forward.1 = (bf16[2048,1024]{1,0:T(8,128)(2,1)}, bf16[2048,2048]{1,0:T(8,128)(2,1)}, f32[64,256]{1,0:T(8,128)}) custom-call(bf16[256,2048]{1,0:T(8,128)(2,1)} %get-tuple-element.92.refs_0_, bf16[256,2048]{1,0:T(8,128)(2,1)} %after.27.refs_1_, bf16[256,2048]{1,0:T(8,128)(2,1)} %get-tuple-element.93.refs_2_, ...), custom_call_target="tpu_custom_call" | custom-call | tf_op jit(solution)/shard_map/gate_forward/pallas_call | solution.py:545
  222.3 23.8 %out_project.1 = (bf16[2048,1024]{1,0:T(8,128)(2,1)}, bf16[2048,1024]{1,0:T(8,128)(2,1)}, bf16[2048,1024]{1,0:T(8,128)(2,1)}, f32[8,1024]{1,0:T(8,128)}, bf16[2,...) custom-call(bf16[2048,1024]{1,0:T(8,128)(2,1)} %convolution_convert_, ...), custom_call_target="tpu_custom_call" | custom-call | tf_op jit(solution)/shard_map/out_project/pallas_call | solution.py:593
  246.0 14.0 %convolution_convert_fusion.2.refs_1_ = bf16[2048,1024]{1,0:T(8,128)(2,1)} fusion(bf16[2048,2048]{1,0:T(8,128)(2,1)} %get-tuple-element.89, bf16[2048,1024]{1,0:T(8,128)(2,1)} %get-tuple-element.103.dz), kind=kOutput, calls=%fused_computation.21 | convolution fusion | flops 8592031744 | bytes 16777216 | tf_op jit(solution)/shard_map/dot_general | solution.py:34
  260.1 14.0 %convolution_convert_fusion.3.refs_0_ = bf16[2048,1024]{1,0:T(8,128)(2,1)} fusion(bf16[2048,2048]{1,0:T(8,128)(2,1)} %get-tuple-element.108, bf16[2048,1024]{1,0:T(8,128)(2,1)} %get-tuple-element.109), kind=kOutput, calls=%fused_computation.22 | convolution fusion | flops 8592031744 | bytes 16777216 | tf_op jit(solution)/shard_map/dot_general | solution.py:34
  276.0 30.0 %scan_backward.2 = (bf16[1024,1408]{1,0:T(8,128)(2,1)}, f32[40,1280]{1,0:T(8,128)}, f32[16,128]{1,0:T(8,128)}, f32[8,1024]{1,0:T(8,128)}) custom-call(s32[1]{0:T(128)} %bitcast.19.place, bf16[2048,1408]{1,0:T(8,128)(2,1)} %get-tuple-element.90.proj.refs_1_, f32[8,1280]{1,0:T(8,128)} %fusion.26.refs_10_.conv_w, f32[8,1024]{1,0:T(8,128)} %broadcast_in_dim.30.skip, ...), custom_call_target="tpu_custom_call" | custom-call | tf_op jit(solution)/shard_map/scan_backward/pallas_call | solution.py:417
  306.0 17.5 %back_project.2 = (bf16[1,2,128,2048]{3,2,1,0:T(8,128)(2,1)}, bf16[1,2,128,2048]{3,2,1,0:T(8,128)(2,1)}, bf16[1,2,128,2048]{3,2,1,0:T(8,128)(2,1)}, bf16[1,2,128,2048]{3,2,1,0:T(8,128)(2,1)}) custom-call(bf16[2048,1024]{1,0:T(8,128)(2,1)} %get-tuple-element.103.dz, bf16[1024,1408]{1,0:T(8,128)(2,1)} %get-tuple-element.110.px, bf16[2048,1024]{1,0:T(8,128)(2,1)} %after.25.w_z, ...), custom_call_target="tpu_custom_call" | custom-call | tf_op jit(solution)/shard_map/back_project/pallas_call | solution.py:615
  325.9 2.1 add_convert_fusion.3.refs_3_
  331.9 30.1 %scan_backward.3 = (bf16[1024,1408]{1,0:T(8,128)(2,1)}, f32[40,1280]{1,0:T(8,128)}, f32[16,128]{1,0:T(8,128)}, f32[8,1024]{1,0:T(8,128)}) custom-call(s32[1]{0:T(128)} %bitcast.19.place, bf16[2048,1408]{1,0:T(8,128)(2,1)} %get-tuple-element.90.proj.refs_1_, f32[8,1280]{1,0:T(8,128)} %fusion.26.refs_10_.conv_w, f32[8,1024]{1,0:T(8,128)} %broadcast_in_dim.30.skip, ...), custom_call_target="tpu_custom_call" | custom-call | tf_op jit(solution)/shard_map/scan_backward/pallas_call | solution.py:417
  363.7 19.4 %convolution_convert_fusion.refs_2_.refs_1_ = bf16[2048,1408]{1,0:T(8,128)(2,1)} fusion(bf16[2048,2048]{1,0:T(8,128)(2,1)} %get-tuple-element.89, bf16[1024,1408]{1,0:T(8,128)(2,1)} %after.32.refs_0_, bf16[1024,1408]{1,0:T(8,128)(2,1)} %get-tuple-element.110.px), kind=kOutput, calls=%fused_computation.5 | convolution fusion | flops 11825577984 | bytes 19922944 | tf_op jit(solution)/shard_map/dot_general | solution.py:34
  383.1 1.8 small_gradients.1
  386.1 2.0 add_convert_fusion.16.refs_3_
  398.0 17.5 %back_project.3 = (bf16[1,2,128,2048]{3,2,1,0:T(8,128)(2,1)}, bf16[1,2,128,2048]{3,2,1,0:T(8,128)(2,1)}, bf16[1,2,128,2048]{3,2,1,0:T(8,128)(2,1)}, bf16[1,2,128,2048]{3,2,1,0:T(8,128)(2,1)}) custom-call(bf16[2048,1024]{1,0:T(8,128)(2,1)} %get-tuple-element.103.dz, bf16[1024,1408]{1,0:T(8,128)(2,1)} %after.34.px, bf16[2048,1024]{1,0:T(8,128)(2,1)} %after.25.w_z, ...), custom_call_target="tpu_custom_call" | custom-call | tf_op jit(solution)/shard_map/back_project/pallas_call | solution.py:615
  418.1 3.9 collective-permute-done.31
  422.8 1.7 collective-permute-start.32
  425.1 4.6 collective-permute-done.32
  434.9 2.2 collective-permute-done.35.refs_3_.refs_8_
  439.7 2.2 place_small.1.refs_2_.refs_1_
  441.9 8.1 %reduce-scatter.8.cloned.1.call-done.refs_0_ = bf16[256,1408]{1,0:T(8,128)(2,1)} async-done(((bf16[2048,1408]{1,0:T(8,128)(2,1)}), bf16[256,1408]{1,0:T(8,128)(2,1)}) %reduce-scatter.8.cloned.1.call-update) | async-done | bytes 720912 | tf_op jit(solution)/shard_map/reduce_scatter | solution.py:931
  450.0 2.2 broadcast_select_fusion.36
  455.6 5.1 fusion.15
  460.8 3.2 collective-permute-done.40.refs_2_.refs_5_
  464.0 2.5 collective-permute-done.41.refs_3_.refs_6_
  467.2 5.3 %shards.1 = (f32[64,8512]{1,0:T(8,128)}, f32[64,4096]{1,0:T(8,128)}, f32[24,128]{1,0:T(8,128)}) custom-call(s32[2]{0:T(128)} %pad_add_fusion.spot, bf16[64,2048]{1,0:T(8,128)(2,1)} %get-tuple-element.189.refs_0_, bf16[64,2048]{1,0:T(8,128)(2,1)} %copy-done.48, bf16[64,2048]{1,0:T(8,128)(2,1)} %copy-done.49, bf16[64,2048]{1,0:T(8,128)(2,1)} %copy-done.50, ...), custom_call_target="tpu_custom_call" | custom-call | tf_op jit(solution)/shard_map/shards/pallas_call | solution.py:672
  473.6 2.3 add_convert_fusion.9
  477.0 2.0 add_convert_fusion.10
  481.8 2.0 collective-permute-done.46
  485.3 3.1 collective-permute-done.47
  489.4 2.7 collective-permute-done.48
  493.4 2.2 fusion.20
  497.8 5.2 fusion.11
  505.1 1.9 collective-permute-done.49
  512.3 4.2 multiply_add_fusion.2
  517.4 3.9 multiply_add_fusion
  (378 shorter events, 112.2 us)
Async XLA Ops:
  7.2 92.7 %all-gather.4.cloned.1.call-start = ((), (), s32[]{:S(2)}) async-start(), calls=%async_computation.3 | async-start | bytes 6488064 | tf_op jit(solution)/shard_map/all_gather | solution.py:896
  10.7 8.4 %collective-permute-start.6 = (bf16[64,1408]{1,0:T(8,128)(2,1)S(1)}, bf16[64,1408]{1,0:T(8,128)(2,1)S(1)}, u32[]{:S(2)}, u32[]{:S(2)}) collective-permute-start(bf16[64,1408]{1,0:T(8,128)(2,1)S(1)} %get-tuple-element.208), channel_id=1, source_target_pairs={{0,1},{1,0},{2,3},{3,2},{4,5},{5,4},{6,7},{7,6},{8,9},{9,8},{10,11... | collective-permute-start | bytes 540680 | tf_op jit(solution)/shard_map/ppermute | solution.py:740
  13.8 9.9 %collective-permute-start.7 = (bf16[64,1408]{1,0:T(8,128)(2,1)S(1)}, bf16[64,1408]{1,0:T(8,128)(2,1)S(1)}, u32[]{:S(2)}, u32[]{:S(2)}) collective-permute-start(bf16[64,1408]{1,0:T(8,128)(2,1)S(1)} %get-tuple-element.207), channel_id=1, source_target_pairs={{0,2},{1,3},{2,0},{3,1},{4,6},{5,7},{6,4},{7,5},{8,10},{9,11},{10,... | collective-permute-start | bytes 540680 | tf_op jit(solution)/shard_map/ppermute | solution.py:740
  15.3 8.4 %collective-permute-start.8 = (bf16[64,1408]{1,0:T(8,128)(2,1)S(1)}, bf16[64,1408]{1,0:T(8,128)(2,1)S(1)}, u32[]{:S(2)}, u32[]{:S(2)}) collective-permute-start(bf16[64,1408]{1,0:T(8,128)(2,1)S(1)} %get-tuple-element.206), channel_id=1, source_target_pairs={{0,3},{1,2},{2,1},{3,0},{4,7},{5,6},{6,5},{7,4},{8,11},{9,10},{10,... | collective-permute-start | bytes 540680 | tf_op jit(solution)/shard_map/ppermute | solution.py:740
  27.7 142.6 %all-gather.6.cloned.1.call-start = ((), (), s32[]{:S(2)}) async-start(), calls=%async_computation.4 | async-start | bytes 4718592 | tf_op jit(solution)/shard_map/all_gather | solution.py:901
  27.8 23.8 %collective-permute-start.4 = (bf16[256,2048]{1,0:T(8,128)(2,1)S(1)}, bf16[256,2048]{1,0:T(8,128)(2,1)S(1)}, u32[]{:S(2)}, u32[]{:S(2)}) collective-permute-start(bf16[256,2048]{1,0:T(8,128)(2,1)S(1)} %copy-done.10), channel_id=1, source_target_pairs={{0,2},{1,3},{2,0},{3,1},{4,6},{5,7},{6,4},{7,5},{8,10},{9,11},{10,... | collective-permute-start | bytes 3145736 | tf_op jit(solution)/shard_map/ppermute | solution.py:740
  29.4 22.6 %collective-permute-start.5 = (bf16[256,2048]{1,0:T(8,128)(2,1)S(1)}, bf16[256,2048]{1,0:T(8,128)(2,1)}, u32[]{:S(2)}, u32[]{:S(2)}) collective-permute-start(bf16[256,2048]{1,0:T(8,128)(2,1)S(1)} %copy-done.9), channel_id=1, source_target_pairs={{0,1},{1,0},{2,3},{3,2},{4,5},{5,4},{6,7},{7,6},{8,9},{9,8},{10,11... | collective-permute-start | bytes 3145736 | tf_op jit(solution)/shard_map/ppermute | solution.py:740
  53.8 9.0 %collective-permute-start.10 = (bf16[64,2048]{1,0:T(8,128)(2,1)S(1)}, bf16[64,2048]{1,0:T(8,128)(2,1)S(1)}, u32[]{:S(2)}, u32[]{:S(2)}) collective-permute-start(bf16[64,2048]{1,0:T(8,128)(2,1)S(1)} %get-tuple-element.196), channel_id=1, source_target_pairs={{0,2},{1,3},{2,0},{3,1},{4,6},{5,7},{6,4},{7,5},{8,10},{9,11},{10,... | collective-permute-start | bytes 786440 | tf_op jit(solution)/shard_map/ppermute | solution.py:740
  54.7 8.3 %collective-permute-start.11 = (bf16[64,2048]{1,0:T(8,128)(2,1)S(1)}, bf16[64,2048]{1,0:T(8,128)(2,1)S(1)}, u32[]{:S(2)}, u32[]{:S(2)}) collective-permute-start(bf16[64,2048]{1,0:T(8,128)(2,1)S(1)} %get-tuple-element.195), channel_id=1, source_target_pairs={{0,1},{1,0},{2,3},{3,2},{4,5},{5,4},{6,7},{7,6},{8,9},{9,8},{10,11... | collective-permute-start | bytes 786440 | tf_op jit(solution)/shard_map/ppermute | solution.py:740
  56.2 10.6 %collective-permute-start.9 = (bf16[64,2048]{1,0:T(8,128)(2,1)S(1)}, bf16[64,2048]{1,0:T(8,128)(2,1)S(1)}, u32[]{:S(2)}, u32[]{:S(2)}) collective-permute-start(bf16[64,2048]{1,0:T(8,128)(2,1)S(1)} %get-tuple-element.197), channel_id=1, source_target_pairs={{0,3},{1,2},{2,1},{3,0},{4,7},{5,6},{6,5},{7,4},{8,11},{9,10},{10,... | collective-permute-start | bytes 786440 | tf_op jit(solution)/shard_map/ppermute | solution.py:740
  69.0 123.5 %all-gather.8.cloned.1.call-start = ((), (), s32[]{:S(2)}) async-start(), calls=%async_computation.5 | async-start | bytes 4718592 | tf_op jit(solution)/shard_map/all_gather | solution.py:902
  69.7 319.3 %reduce-scatter.6.cloned.1.call-start = ((), (), s32[]{:S(2)}) async-start(), calls=%async_computation.7 | async-start | bytes 4718592 | tf_op jit(solution)/shard_map/reduce_scatter | solution.py:931
  69.7 22.3 %collective-permute-start = (bf16[256,2048]{1,0:T(8,128)(2,1)S(1)}, bf16[256,2048]{1,0:T(8,128)(2,1)}, u32[]{:S(2)}, u32[]{:S(2)}) collective-permute-start(bf16[256,2048]{1,0:T(8,128)(2,1)S(1)} %copy-done.10), channel_id=1, source_target_pairs={{0,1},{1,0},{2,3},{3,2},{4,5},{5,4},{6,7},{7,6},{8,9},{9,8},{10,11... | collective-permute-start | bytes 3145736 | tf_op jit(solution)/shard_map/ppermute | solution.py:740
  71.5 24.3 %collective-permute-start.2 = (bf16[256,2048]{1,0:T(8,128)(2,1)S(1)}, bf16[256,2048]{1,0:T(8,128)(2,1)}, u32[]{:S(2)}, u32[]{:S(2)}) collective-permute-start(bf16[256,2048]{1,0:T(8,128)(2,1)S(1)} %copy-done.9), channel_id=1, source_target_pairs={{0,2},{1,3},{2,0},{3,1},{4,6},{5,7},{6,4},{7,5},{8,10},{9,11},{10,... | collective-permute-start | bytes 3145736 | tf_op jit(solution)/shard_map/ppermute | solution.py:740
  92.1 27.7 %collective-permute-start.1 = (bf16[256,2048]{1,0:T(8,128)(2,1)}, bf16[256,2048]{1,0:T(8,128)(2,1)S(1)}, u32[]{:S(2)}, u32[]{:S(2)}) collective-permute-start(bf16[256,2048]{1,0:T(8,128)(2,1)} %collective-permute-done.refs_3_), channel_id=1, source_target_pairs={{0,2},{1,3},{2,0},{3,1},{4,6},{5,7},{6,4},{7,5},{8,10},{9,11},{10,... | collective-permute-start | bytes 3145736 | tf_op jit(solution)/shard_map/ppermute | solution.py:740
  95.8 23.9 %collective-permute-start.3 = (bf16[256,2048]{1,0:T(8,128)(2,1)}, bf16[256,2048]{1,0:T(8,128)(2,1)S(1)}, u32[]{:S(2)}, u32[]{:S(2)}) collective-permute-start(bf16[256,2048]{1,0:T(8,128)(2,1)} %collective-permute-done.2.refs_6_), channel_id=1, source_target_pairs={{0,1},{1,0},{2,3},{3,2},{4,5},{5,4},{6,7},{7,6},{8,9},{9,8},{10,11... | collective-permute-start | bytes 3145736 | tf_op jit(solution)/shard_map/ppermute | solution.py:740
  121.1 49.2 %collective-permute-start.16 = (bf16[256,2048]{1,0:T(8,128)(2,1)}, bf16[256,2048]{1,0:T(8,128)(2,1)S(1)}, u32[]{:S(2)}, u32[]{:S(2)}) collective-permute-start(bf16[256,2048]{1,0:T(8,128)(2,1)} %get-tuple-element.95.refs_4_), channel_id=1, source_target_pairs={{0,2},{1,3},{2,0},{3,1},{4,6},{5,7},{6,4},{7,5},{8,10},{9,11},{10,... | collective-permute-start | bytes 3145736 | tf_op jit(solution)/shard_map/ppermute | solution.py:740
  121.9 51.5 %collective-permute-start.12 = (bf16[256,2048]{1,0:T(8,128)(2,1)}, bf16[256,2048]{1,0:T(8,128)(2,1)S(1)}, u32[]{:S(2)}, u32[]{:S(2)}) collective-permute-start(bf16[256,2048]{1,0:T(8,128)(2,1)} %get-tuple-element.92.refs_0_), channel_id=1, source_target_pairs={{0,1},{1,0},{2,3},{3,2},{4,5},{5,4},{6,7},{7,6},{8,9},{9,8},{10,11... | collective-permute-start | bytes 3145736 | tf_op jit(solution)/shard_map/ppermute | solution.py:740
  125.9 62.4 %collective-permute-start.15 = (bf16[256,2048]{1,0:T(8,128)(2,1)}, bf16[256,2048]{1,0:T(8,128)(2,1)}, u32[]{:S(2)}, u32[]{:S(2)}) collective-permute-start(bf16[256,2048]{1,0:T(8,128)(2,1)} %get-tuple-element.95.refs_4_), channel_id=1, source_target_pairs={{0,1},{1,0},{2,3},{3,2},{4,5},{5,4},{6,7},{7,6},{8,9},{9,8},{10,11... | collective-permute-start | bytes 3145736 | tf_op jit(solution)/shard_map/ppermute | solution.py:740
  126.4 63.8 %collective-permute-start.13 = (bf16[256,2048]{1,0:T(8,128)(2,1)}, bf16[256,2048]{1,0:T(8,128)(2,1)S(1)}, u32[]{:S(2)}, u32[]{:S(2)}) collective-permute-start(bf16[256,2048]{1,0:T(8,128)(2,1)} %get-tuple-element.92.refs_0_), channel_id=1, source_target_pairs={{0,2},{1,3},{2,0},{3,1},{4,6},{5,7},{6,4},{7,5},{8,10},{9,11},{10,... | collective-permute-start | bytes 3145736 | tf_op jit(solution)/shard_map/ppermute | solution.py:740
  171.3 18.0 %collective-permute-start.17 = (bf16[256,2048]{1,0:T(8,128)(2,1)}, bf16[256,2048]{1,0:T(8,128)(2,1)S(1)}, u32[]{:S(2)}, u32[]{:S(2)}) collective-permute-start(bf16[256,2048]{1,0:T(8,128)(2,1)} %after.29.refs_6_), channel_id=1, source_target_pairs={{0,1},{1,0},{2,3},{3,2},{4,5},{5,4},{6,7},{7,6},{8,9},{9,8},{10,11... | collective-permute-start | bytes 3145736 | tf_op jit(solution)/shard_map/ppermute | solution.py:740
  174.3 17.1 %collective-permute-start.14 = (bf16[256,2048]{1,0:T(8,128)(2,1)}, bf16[256,2048]{1,0:T(8,128)(2,1)S(1)}, u32[]{:S(2)}, u32[]{:S(2)}) collective-permute-start(bf16[256,2048]{1,0:T(8,128)(2,1)} %after.27.refs_1_), channel_id=1, source_target_pairs={{0,2},{1,3},{2,0},{3,1},{4,6},{5,7},{6,4},{7,5},{8,10},{9,11},{10,... | collective-permute-start | bytes 3145736 | tf_op jit(solution)/shard_map/ppermute | solution.py:740
  215.4 5.2 collective-permute-start.20
  260.0 129.0 %reduce-scatter.4.cloned.1.call-start = ((), (), s32[]{:S(2)}) async-start(), calls=%async_computation.6 | async-start | bytes 4718592 | tf_op jit(solution)/shard_map/reduce_scatter | solution.py:931
  274.1 175.9 %reduce-scatter.8.cloned.1.call-start = ((), (), s32[]{:S(2)}) async-start(), calls=%async_computation.8 | async-start | bytes 6488064 | tf_op jit(solution)/shard_map/reduce_scatter | solution.py:931
  274.1 51.7 %collective-permute-start.21 = (bf16[2,2,128,2048]{3,2,1,0:T(8,128)(2,1)}, bf16[2,2,128,2048]{3,2,1,0:T(8,128)(2,1)}, u32[]{:S(2)}, u32[]{:S(2)}) collective-permute-start(bf16[2,2,128,2048]{3,2,1,0:T(8,128)(2,1)} %get-tuple-element.101), channel_id=1, source_target_pairs={{0,1},{1,0},{2,3},{3,2},{4,5},{5,4},{6,7},{7,6},{8,9},{9,8},{10,11... | collective-permute-start | bytes 6291464 | tf_op jit(solution)/shard_map/ppermute | solution.py:740
  275.5 50.4 %collective-permute-start.22 = (bf16[2,2,128,2048]{3,2,1,0:T(8,128)(2,1)}, bf16[2,2,128,2048]{3,2,1,0:T(8,128)(2,1)}, u32[]{:S(2)}, u32[]{:S(2)}) collective-permute-start(bf16[2,2,128,2048]{3,2,1,0:T(8,128)(2,1)} %get-tuple-element.102), channel_id=1, source_target_pairs={{0,2},{1,3},{2,0},{3,1},{4,6},{5,7},{6,4},{7,5},{8,10},{9,11},{10,... | collective-permute-start | bytes 6291464 | tf_op jit(solution)/shard_map/ppermute | solution.py:740
  323.5 38.5 %collective-permute-start.26 = (bf16[1,2,128,2048]{3,2,1,0:T(8,128)(2,1)}, bf16[1,2,128,2048]{3,2,1,0:T(8,128)(2,1)S(1)}, u32[]{:S(2)}, u32[]{:S(2)}) collective-permute-start(bf16[1,2,128,2048]{3,2,1,0:T(8,128)(2,1)} %get-tuple-element.111.refs_2_.refs_0_), channel_id=1, source_target_pairs={{0,1},{1,0},{2,3},{3,2},{4,5},{5,4},{6,7},{7,6},{8,9},{9,8},{10,11... | collective-permute-start | bytes 3145736 | tf_op jit(solution)/shard_map/ppermute | solution.py:740
  324.8 37.2 %collective-permute-start.27 = (bf16[1,2,128,2048]{3,2,1,0:T(8,128)(2,1)}, bf16[1,2,128,2048]{3,2,1,0:T(8,128)(2,1)S(1)}, u32[]{:S(2)}, u32[]{:S(2)}) collective-permute-start(bf16[1,2,128,2048]{3,2,1,0:T(8,128)(2,1)} %get-tuple-element.116.refs_1_), channel_id=1, source_target_pairs={{0,2},{1,3},{2,0},{3,1},{4,6},{5,7},{6,4},{7,5},{8,10},{9,11},{10,... | collective-permute-start | bytes 3145736 | tf_op jit(solution)/shard_map/ppermute | solution.py:740
  328.0 34.0 %collective-permute-start.24 = (bf16[2,1,128,2048]{3,2,1,0:T(8,128)(2,1)S(1)}, bf16[2,1,128,2048]{3,2,1,0:T(8,128)(2,1)S(1)}, u32[]{:S(2)}, u32[]{:S(2)}) collective-permute-start(bf16[2,1,128,2048]{3,2,1,0:T(8,128)(2,1)S(1)} %add_convert_fusion.3.refs_3_), channel_id=1, source_target_pairs={{0,1},{1,0},{2,3},{3,2},{4,5},{5,4},{6,7},{7,6},{8,9},{9,8},{10,11... | collective-permute-start | bytes 3145736 | tf_op jit(solution)/shard_map/ppermute | solution.py:740
  330.9 31.9 %collective-permute-start.23 = (bf16[2,1,128,2048]{3,2,1,0:T(8,128)(2,1)S(1)}, bf16[2,1,128,2048]{3,2,1,0:T(8,128)(2,1)}, u32[]{:S(2)}, u32[]{:S(2)}) collective-permute-start(bf16[2,1,128,2048]{3,2,1,0:T(8,128)(2,1)S(1)} %add_convert_fusion.4.refs_2_), channel_id=1, source_target_pairs={{0,2},{1,3},{2,0},{3,1},{4,6},{5,7},{6,4},{7,5},{8,10},{9,11},{10,... | collective-permute-start | bytes 3145736 | tf_op jit(solution)/shard_map/ppermute | solution.py:740
  384.9 11.3 %collective-permute-start.25 = (f32[8,1280]{1,0:T(8,128)}, f32[8,1280]{1,0:T(8,128)S(1)}, u32[]{:S(2)}, u32[]{:S(2)}) collective-permute-start(f32[8,1280]{1,0:T(8,128)} %small_gradients.1), channel_id=1, source_target_pairs={{0,4},{4,0},{8,12},{12,8},{16,20},{20,16},{24,28},{28,24},{1,5},{5... | collective-permute-start | bytes 122888 | tf_op jit(solution)/shard_map/ppermute | solution.py:740
  388.1 45.9 %collective-permute-start.37 = (bf16[1,1,128,2048]{3,2,1,0:T(8,128)(2,1)}, bf16[1,1,128,2048]{3,2,1,0:T(8,128)(2,1)S(1)}, u32[]{:S(2)}, u32[]{:S(2)}) collective-permute-start(bf16[1,1,128,2048]{3,2,1,0:T(8,128)(2,1)} %add_convert_fusion.16.refs_3_), channel_id=1, source_target_pairs={{0,1},{1,0},{2,3},{3,2},{4,5},{5,4},{6,7},{7,6},{8,9},{9,8},{10,11... | collective-permute-start | bytes 1572872 | tf_op jit(solution)/shard_map/ppermute | solution.py:740
  392.5 23.0 %collective-permute-start.28 = (bf16[64,2048]{1,0:T(8,128)(2,1)}, bf16[64,2048]{1,0:T(8,128)(2,1)S(1)}, u32[]{:S(2)}, u32[]{:S(2)}) collective-permute-start(bf16[64,2048]{1,0:T(8,128)(2,1)} %get-tuple-element.190), channel_id=1, source_target_pairs={{0,1},{1,0},{2,3},{3,2},{4,5},{5,4},{6,7},{7,6},{8,9},{9,8},{10,11... | collective-permute-start | bytes 786440 | tf_op jit(solution)/shard_map/ppermute | solution.py:740
  393.8 21.8 %collective-permute-start.29 = (bf16[64,2048]{1,0:T(8,128)(2,1)}, bf16[64,2048]{1,0:T(8,128)(2,1)S(1)}, u32[]{:S(2)}, u32[]{:S(2)}) collective-permute-start(bf16[64,2048]{1,0:T(8,128)(2,1)} %get-tuple-element.191), channel_id=1, source_target_pairs={{0,2},{1,3},{2,0},{3,1},{4,6},{5,7},{6,4},{7,5},{8,10},{9,11},{10,... | collective-permute-start | bytes 786440 | tf_op jit(solution)/shard_map/ppermute | solution.py:740
  394.8 20.7 %collective-permute-start.30 = (bf16[64,2048]{1,0:T(8,128)(2,1)}, bf16[64,2048]{1,0:T(8,128)(2,1)S(1)}, u32[]{:S(2)}, u32[]{:S(2)}) collective-permute-start(bf16[64,2048]{1,0:T(8,128)(2,1)} %get-tuple-element.192), channel_id=1, source_target_pairs={{0,3},{1,2},{2,1},{3,0},{4,7},{5,6},{6,5},{7,4},{8,11},{9,10},{10,... | collective-permute-start | bytes 786440 | tf_op jit(solution)/shard_map/ppermute | solution.py:740
  396.2 37.8 %collective-permute-start.36 = (bf16[1,1,128,2048]{3,2,1,0:T(8,128)(2,1)S(1)}, bf16[1,1,128,2048]{3,2,1,0:T(8,128)(2,1)S(1)}, u32[]{:S(2)}, u32[]{:S(2)}) collective-permute-start(bf16[1,1,128,2048]{3,2,1,0:T(8,128)(2,1)S(1)} %add_convert_fusion.17.refs_2_), channel_id=1, source_target_pairs={{0,2},{1,3},{2,0},{3,1},{4,6},{5,7},{6,4},{7,5},{8,10},{9,11},{10,... | collective-permute-start | bytes 1572872 | tf_op jit(solution)/shard_map/ppermute | solution.py:740
  416.4 5.6 %collective-permute-start.31 = (f32[8,1280]{1,0:T(8,128)}, f32[8,1280]{1,0:T(8,128)S(1)}, u32[]{:S(2)}, u32[]{:S(2)}) collective-permute-start(f32[8,1280]{1,0:T(8,128)} %after.36), channel_id=1, source_target_pairs={{0,8},{4,12},{8,0},{12,4},{16,24},{20,28},{24,16},{28,20},{1,9},{5... | collective-permute-start | bytes 122888 | tf_op jit(solution)/shard_map/ppermute | solution.py:740
  422.8 6.8 %collective-permute-start.32 = (f32[8,1280]{1,0:T(8,128)S(1)}, f32[8,1280]{1,0:T(8,128)S(1)}, u32[]{:S(2)}, u32[]{:S(2)}) collective-permute-start(f32[8,1280]{1,0:T(8,128)S(1)} %add.262), channel_id=1, source_target_pairs={{0,16},{4,20},{8,24},{12,28},{16,0},{20,4},{24,8},{28,12},{1,17},{... | collective-permute-start | bytes 122888 | tf_op jit(solution)/shard_map/ppermute | solution.py:740
  431.8 5.3 collective-permute-start.35
  437.7 34.8 %collective-permute-start.38 = (bf16[1,2,128,2048]{3,2,1,0:T(8,128)(2,1)}, bf16[1,2,128,2048]{3,2,1,0:T(8,128)(2,1)S(1)}, u32[]{:S(2)}, u32[]{:S(2)}) collective-permute-start(bf16[1,2,128,2048]{3,2,1,0:T(8,128)(2,1)} %get-tuple-element.136.refs_2_), channel_id=1, source_target_pairs={{0,1},{1,0},{2,3},{3,2},{4,5},{5,4},{6,7},{7,6},{8,9},{9,8},{10,11... | collective-permute-start | bytes 3145736 | tf_op jit(solution)/shard_map/ppermute | solution.py:740
  438.5 34.1 %collective-permute-start.39 = (bf16[1,2,128,2048]{3,2,1,0:T(8,128)(2,1)}, bf16[1,2,128,2048]{3,2,1,0:T(8,128)(2,1)}, u32[]{:S(2)}, u32[]{:S(2)}) collective-permute-start(bf16[1,2,128,2048]{3,2,1,0:T(8,128)(2,1)} %get-tuple-element.140), channel_id=1, source_target_pairs={{0,2},{1,3},{2,0},{3,1},{4,6},{5,7},{6,4},{7,5},{8,10},{9,11},{10,... | collective-permute-start | bytes 3145736 | tf_op jit(solution)/shard_map/ppermute | solution.py:740
  452.1 11.9 %collective-permute-start.40 = (bf16[64,1408]{1,0:T(8,128)(2,1)}, bf16[64,1408]{1,0:T(8,128)(2,1)S(1)}, u32[]{:S(2)}, u32[]{:S(2)}) collective-permute-start(bf16[64,1408]{1,0:T(8,128)(2,1)} %get-tuple-element.203), channel_id=1, source_target_pairs={{0,1},{1,0},{2,3},{3,2},{4,5},{5,4},{6,7},{7,6},{8,9},{9,8},{10,11... | collective-permute-start | bytes 540680 | tf_op jit(solution)/shard_map/ppermute | solution.py:740
  453.6 12.9 %collective-permute-start.41 = (bf16[64,1408]{1,0:T(8,128)(2,1)}, bf16[64,1408]{1,0:T(8,128)(2,1)S(1)}, u32[]{:S(2)}, u32[]{:S(2)}) collective-permute-start(bf16[64,1408]{1,0:T(8,128)(2,1)} %get-tuple-element.204), channel_id=1, source_target_pairs={{0,2},{1,3},{2,0},{3,1},{4,6},{5,7},{6,4},{7,5},{8,10},{9,11},{10,... | collective-permute-start | bytes 540680 | tf_op jit(solution)/shard_map/ppermute | solution.py:740
  455.1 11.6 %collective-permute-start.42 = (bf16[64,1408]{1,0:T(8,128)(2,1)}, bf16[64,1408]{1,0:T(8,128)(2,1)}, u32[]{:S(2)}, u32[]{:S(2)}) collective-permute-start(bf16[64,1408]{1,0:T(8,128)(2,1)} %get-tuple-element.205), channel_id=1, source_target_pairs={{0,3},{1,2},{2,1},{3,0},{4,7},{5,6},{6,5},{7,4},{8,11},{9,10},{10,... | collective-permute-start | bytes 540680 | tf_op jit(solution)/shard_map/ppermute | solution.py:740
  472.6 7.5 %collective-permute-start.45 = (f32[24,128]{1,0:T(8,128)}, f32[24,128]{1,0:T(8,128)S(1)}, u32[]{:S(2)}, u32[]{:S(2)}) collective-permute-start(f32[24,128]{1,0:T(8,128)} %get-tuple-element.146), channel_id=1, source_target_pairs={{0,4},{4,0},{8,12},{12,8},{16,20},{20,16},{24,28},{28,24},{1,5},{5... | collective-permute-start | bytes 36872 | tf_op jit(solution)/shard_map/ppermute | solution.py:740
  475.8 16.8 %collective-permute-start.44 = (bf16[1,1,128,2048]{3,2,1,0:T(8,128)(2,1)}, bf16[1,1,128,2048]{3,2,1,0:T(8,128)(2,1)}, u32[]{:S(2)}, u32[]{:S(2)}) collective-permute-start(bf16[1,1,128,2048]{3,2,1,0:T(8,128)(2,1)} %add_convert_fusion.9), channel_id=1, source_target_pairs={{0,1},{1,0},{2,3},{3,2},{4,5},{5,4},{6,7},{7,6},{8,9},{9,8},{10,11... | collective-permute-start | bytes 1572872 | tf_op jit(solution)/shard_map/ppermute | solution.py:740
  479.0 14.4 %collective-permute-start.43 = (bf16[1,1,128,2048]{3,2,1,0:T(8,128)(2,1)}, bf16[1,1,128,2048]{3,2,1,0:T(8,128)(2,1)}, u32[]{:S(2)}, u32[]{:S(2)}) collective-permute-start(bf16[1,1,128,2048]{3,2,1,0:T(8,128)(2,1)} %add_convert_fusion.10), channel_id=1, source_target_pairs={{0,2},{1,3},{2,0},{3,1},{4,6},{5,7},{6,4},{7,5},{8,10},{9,11},{10,... | collective-permute-start | bytes 1572872 | tf_op jit(solution)/shard_map/ppermute | solution.py:740
  (79 other events, 347.4 us)
Sparse Core Ops, SparseCore 0:
  27.8 60.7 all-gather.3
  90.8 45.8 all-gather.5
  138.3 45.8 all-gather.7
  260.2 49.9 reduce-scatter.5
  312.4 48.1 reduce-scatter.3
  383.2 66.6 reduce-scatter.7

commit v6 on v5

--- a/solution.py
+++ b/solution.py
@@ -181,13 +181,12 @@
 
 
 def backward_kernel(place, proj, conv_w, skip, heads, aux, masks, act, slope, dy, s_in, *refs, hl):
-    dproj, dconv, dvec, dskip, dwin, grad_s, dcb, colsum, dkeep, right, carried, later_w, spreads, picks, sums, used, into = refs[-17:]
+    dproj, dco, dvec, dskip, dwin, grad_s, dcb, colsum, dkeep, right, carried, later_w, spreads, picks, sums, used, into = refs[-17:]
     width = hl * HEADDIM
     conv_width = width + 2 * STATE
 
     @pl.when(pl.program_id(0) == 0)
     def _():
-        dconv[...] = jnp.zeros(dconv.shape, F32)
         dvec[...] = jnp.zeros(dvec.shape, F32)
         dskip[...] = jnp.zeros(dskip.shape, F32)
         dwin[BLOCK : BLOCK + 8, :] = jnp.zeros((8, conv_width), F32)
@@ -284,16 +283,36 @@
     for lo in range(0, conv_width, LANES):
         hi = lo + LANES
         own = dwin[0:BLOCK, lo:hi]
+        dco[:, lo:hi] = own.astype(BF)
+        grad = conv_w[CONV - 1 : CONV, lo:hi] * own
+        for tap in range(CONV - 1):
+            ahead = CONV - 1 - tap
+            grad += conv_w[tap : tap + 1, lo:hi] * (dwin[ahead : ahead + BLOCK, lo:hi] * valid[tap])
+        dproj[:, lo:hi] = grad.astype(BF)
+    dwin[BLOCK : BLOCK + 8, :] = dwin[0:8, :]
+
+
+def taps_kernel(place, proj, aux, dco, dconv, dwin):
+    conv_width = dco.shape[1]
+
+    @pl.when(pl.program_id(0) == 0)
+    def _():
+        dconv[...] = jnp.zeros(dconv.shape, F32)
+        dwin[BLOCK : BLOCK + 8, :] = jnp.zeros((8, conv_width), F32)
+
+    aux_v = aux[...]
+    valid = [spread(aux_v, 4 + tap) for tap in range(CONV - 1)]
+    for lo in range(0, conv_width, LANES):
+        hi = lo + LANES
+        own = dco[:, lo:hi].astype(F32)
+        dwin[0:BLOCK, lo:hi] = own
         value = proj[:, lo:hi].astype(F32)
-        grad = conv_w[CONV - 1 : CONV, lo:hi] * own
         dconv[CONV * 8 : CONV * 8 + 8, lo:hi] += tree(own)
         dconv[(CONV - 1) * 8 : CONV * 8, lo:hi] += tree(own * value)
         for tap in range(CONV - 1):
             ahead = CONV - 1 - tap
             moved = dwin[ahead : ahead + BLOCK, lo:hi] * valid[tap]
-            grad += conv_w[tap : tap + 1, lo:hi] * moved
             dconv[tap * 8 : tap * 8 + 8, lo:hi] += tree(moved * value)
-        dproj[:, lo:hi] = grad.astype(BF)
     dwin[BLOCK : BLOCK + 8, :] = dwin[0:8, :]
 
 
@@ -394,7 +413,7 @@
         + [pl.BlockSpec(memory_space=pl.ANY)] * len(done),
         out_specs=[
             pl.BlockSpec((BLOCK, full), lambda j, place: ((nb - 1 - j) ^ place[0], 0)),
-            pl.BlockSpec((8 * (CONV + 1), conv_width), whole),
+            pl.BlockSpec((BLOCK, conv_width), lambda j, place: ((nb - 1 - j) ^ place[0], 0)),
             pl.BlockSpec((SLOT, LANES), whole),
             pl.BlockSpec((8, width), whole),
         ],
@@ -419,13 +438,36 @@
         grid_spec=grid_spec,
         out_shape=[
             jax.ShapeDtypeStruct((tokens, full), BF),
-            jax.ShapeDtypeStruct((8 * (CONV + 1), conv_width), F32),
+            jax.ShapeDtypeStruct((tokens, conv_width), BF),
             jax.ShapeDtypeStruct((SLOT, LANES), F32),
             jax.ShapeDtypeStruct((8, width), F32),
         ],
         compiler_params=pltpu.CompilerParams(vmem_limit_bytes=VMEM, dimension_semantics=("arbitrary",)),
         name="scan_backward",
     )(place, proj, conv_w, skip, heads, aux, masks, act, slope, dy, states, *done)
+
+
+def tap_gradients(place, micro, proj, aux, dco):
+    tokens, conv_width = dco.shape
+    nb = tokens // BLOCK
+    grid_spec = pltpu.PrefetchScalarGridSpec(
+        num_scalar_prefetch=1,
+        grid=(nb,),
+        in_specs=[
+            pl.BlockSpec((BLOCK, proj.shape[1]), lambda j, place: (micro * nb + ((nb - 1 - j) ^ place[0]), 0)),
+            pl.BlockSpec((BLOCK, 8), lambda j, place: (micro * nb + nb - 1 - j, 0)),
+            pl.BlockSpec((BLOCK, conv_width), lambda j, place: ((nb - 1 - j) ^ place[0], 0)),
+        ],
+        out_specs=pl.BlockSpec((8 * (CONV + 1), conv_width), lambda j, place: (0, 0)),
+        scratch_shapes=[pltpu.VMEM((BLOCK + 8, conv_width), F32)],
+    )
+    return pl.pallas_call(
+        taps_kernel,
+        grid_spec=grid_spec,
+        out_shape=jax.ShapeDtypeStruct((8 * (CONV + 1), conv_width), F32),
+        compiler_params=pltpu.CompilerParams(vmem_limit_bytes=VMEM, dimension_semantics=("arbitrary",)),
+        name="tap_gradients",
+    )(place, proj, aux, dco)
 
 
 def fetch(pieces, buffer, sems, step):
@@ -941,32 +983,35 @@
         place, micro, proj_x, conv_loc, skip, heads, aux, masks, act, slope, dy, states, hl, *done
     )
 
-    px_0, conv_0, vec_0, skip_0 = scan_back(0, part_o, part_z)
+    px_0, dco_0, vec_0, skip_0 = scan_back(0, part_o, part_z)
     hid_0 = through_in(0, px_0)
     out_got, out_sent = out_stages.send([hid_0[0]])
     stages_0 = scatter_stages(hid_0)
     hid_got, sent = next(stages_0)
-    px_1, conv_1, vec_1, skip_1 = scan_back(1, *sent, *out_sent)
+    px_1, dco_1, vec_1, skip_1 = scan_back(1, *sent, *out_sent)
     [px_1] = after([px_1], *hid_got, *out_got)
     part_x = dot(hidden, jnp.concatenate([px_0, px_1], axis=0), TN).astype(BF)
     got_x = scatter(part_x)
     hid_got, sent = stages_0.send([part_x])
     spot = jnp.stack([rank, own]).astype(jnp.int32)
     own_gain = lax.dynamic_slice_in_dim(gain_in, own * rows, rows)[:, None]
-    first_bit, *more_bits = axis_bits("dp")
-    small = small_gradients(conv_0, conv_1, vec_0, vec_1, skip_0, skip_1, d_gain_out)
-    small = small + swapped(small, "dp", first_bit)
-    [px_1] = after([px_1], part_x, *sent, small)
+    [px_1] = after([px_1], part_x, *sent)
     hid_1 = through_in(1, px_1)
     [got_o, got_z] = after([got_o, got_z], part_x)
     sent_oz, got_oz = exchange(split(jnp.concatenate([got_o, got_z], axis=1)), rank)
-    [small] = after([small], hid_1[0], *got_oz)
-    for bit in more_bits:
+    dco_0, dco_1 = after([dco_0, dco_1], hid_1[0], *got_oz)
+    conv_0, conv_1 = (tap_gradients(place, micro, proj_x, aux, one) for micro, one in enumerate((dco_0, dco_1)))
+    stages_1 = scatter_stages(after(hid_1, *hid_got))
+    hid_got, _ = next(stages_1)
+    small = small_gradients(conv_0, conv_1, vec_0, vec_1, skip_0, skip_1, d_gain_out)
+    [small] = after([small], *hid_got)
+    for bit in axis_bits("dp"):
         small = small + swapped(small, "dp", bit)
-    small = [small] + [swapped(small, "seq", mask) for mask in range(1, n)]
-    hid_1 = after(hid_1, *hid_got, *small[1:])
-    stages_1 = scatter_stages(hid_1)
-    hid_got, hid_sent = next(stages_1)
+    _, hid_sent = stages_1.send(None)
+    [got_x] = after([got_x], small, *hid_sent)
+    sent_x, got_x = exchange(split(got_x), rank)
+    [small] = after([small], *sent_x)
+    small = [small] + after([swapped(small, "seq", mask) for mask in range(1, n)], *got_x)
     small = place_small(spot, small, xw)
     conv_tot, gain_out_tot = small[: CONV + 1], small[5, :INNER]
     skip_tot = jnp.sum(small[6, :INNER].reshape(HEADS, HEADDIM), axis=1)
@@ -974,22 +1019,17 @@
     a_log_tot, dt_bias_tot = by_head[:, :hl].reshape(-1), by_head[:, SLOT : SLOT + hl].reshape(-1)
     shard_conv = lax.dynamic_slice_in_dim(conv_tot, own * cw, cw, 1)
     conv_sq = jnp.sum(conv_tot * conv_tot)
-
-    [got_x] = after([got_x], small)
-    sent_x, got_x = exchange(split(got_x), rank)
     shard_in, shard_out, last = shards(spot, sent_oz[:1] + got_oz, sent_x[:1] + got_x, in_weight, own_gain, hl)
     shard_out = shard_out.T
-    output = (tok + finish(out_stages, [small]).astype(F32)).astype(BF)
-    d_hidden = jnp.concatenate([finish(stages_0, [hid_1[0]]), finish(stages_1, got_x)], axis=0).astype(F32)
+    output = (tok + finish(out_stages, got_x).astype(F32)).astype(BF)
+    d_hidden = jnp.concatenate([finish(stages_0, [hid_1[0]]), finish(stages_1)], axis=0).astype(F32)
     dh = d_hidden * gain_in
     d_tok = r_in * (dh - tok * (r_in * r_in) * jnp.mean(dh * tok, axis=-1, keepdims=True))
     input_grad = (cotangent.astype(F32) + d_tok).astype(BF)
 
-    stages = [(axis, bit) for axis in ("dp", "seq") for bit in axis_bits(axis)]
-    for axis, bit in stages[:-1]:
+    stages = [(axis, bit) for axis in ("seq", "dp") for bit in axis_bits(axis)]
+    for axis, bit in stages:
         last = last + swapped(last, axis, bit)
-    [last] = after([last], input_grad)
-    last = last + swapped(last, *stages[-1])
     vec_tot = jnp.concatenate([a_log_tot, skip_tot, dt_bias_tot, last[: D // LANES].reshape(-1), gain_out_tot])
     grad_norm = jnp.sqrt(last[D // LANES, 0] + conv_sq + jnp.sum(vec_tot * vec_tot))
     clip = jnp.minimum(1.0, CLIP_NORM / (grad_norm + 1e-06))

time: 537 us -> 528 us (0.983)
  waiting for transfers between devices: 96.8 us -> 79.8 us
  Pallas kernels: 206 us -> 214 us
    pallas_call x0 -> x2, Pallas kernels: none -> 13.8 us  [tap_gradients(): pl.pallas_call(taps_kernel, grid_spec=grid_spec, out_shape=jax.ShapeDtype...]
    ppermute x50, waiting for transfers between devices: 88 us -> 79 us  [swapped(): lax.ppermute(value, axis, [(i, i ^ mask) for i in range(lax.axis_size(axi...]
    reduce_scatter x3, waiting for transfers between devices: 8.09 us -> 0.02 us  [per_device(): lax.psum_scatter(a, 'dp', scatter_dimension=0, tiled=True)]
    pallas_call x2, Pallas kernels: 60.1 us -> 54.1 us  [scan_backward(): pl.pallas_call(functools.partial(backward_kernel, hl=hl), grid_spec=grid_...]
    unnamed x152 -> x154, local copies, waits for them, and re-layouts: 15.8 us -> 15.3 us
  transfers between devices with their start and end apart: 56 -> 56, of which waited for: 27 -> 23; matrix products, arithmetic and copies ran while one was open for 19% -> 20% of each run, Pallas kernels for 31% -> 33%
where the time goes in v6:
time: 528 us; the launch traced here: 521 us
  Pallas kernels  214 us (41%)
  waiting for transfers between devices  79.8 us (15%)
  matrix products  60.9 us (12%)
  other arithmetic  56.5 us (11%)
  starting transfers between devices  53.3 us (10%)
  local copies, waits for them, and re-layouts  37.2 us (7%)
  between operations  18.7 us (4%)
    ppermute x50, waiting for transfers between devices, swapped(): lax.ppermute(value, axis, [(i, i ^ mask) for i in range(lax.axis_size(axi...  79 us
    dot_general x4, matrix products, dot(): return lax.dot_general(a, b, (dims, ((), ())), preferred_element_type=out)  60.9 us
    pallas_call x2, Pallas kernels, scan_backward(): pl.pallas_call(functools.partial(backward_kernel, hl=hl), grid_spec=grid_...  54.1 us
    ppermute x50, starting transfers between devices, swapped(): lax.ppermute(value, axis, [(i, i ^ mask) for i in range(lax.axis_size(axi...  53.1 us
    pallas_call x2, Pallas kernels, back_project(): pl.pallas_call(functools.partial(back_kernel, n=n, bits=bits), grid=(n,),...  35.3 us
    pallas_call x1, Pallas kernels, scan_forward(): pl.pallas_call(functools.partial(forward_kernel, hl=hl), grid_spec=grid_s...  32.8 us
    pallas_call x2, Pallas kernels, in_project(): pl.pallas_call(functools.partial(in_kernel, count=count), grid_spec=pltpu...  26 us
    pallas_call x1, Pallas kernels, out_project(): pl.pallas_call(functools.partial(out_kernel, n=n, bits=bits), grid=(token...  23.8 us
  transfers between devices with their start and end apart: 56, of which 23 were waited for; matrix products, arithmetic and copies ran while one was open for 20% of the time, Pallas kernels for 33%

profile of v6, /device:TPU:0, one launch (start us, length us, event | category | flops | bytes accessed | tf_op | source)
XLA Modules:
  0.0 520.9 jit_solution(8308964643002705636)
XLA Ops:
  7.2 1.7 convert_element_type.242
  10.7 3.0 collective-permute-start.6
  19.2 4.4 collective-permute-done.7.refs_1_
  33.7 17.9 %collective-permute-done.4.refs_4_.refs_2_ = bf16[256,2048]{1,0:T(8,128)(2,1)S(1)} collective-permute-done((bf16[256,2048]{1,0:T(8,128)(2,1)S(1)}, bf16[256,2048]{1,0:T(8,128)(2,1)S(1)}, u32[]{:S(2)}, u32[]{:S(2)}) %collective-permute-start.4) | collective-permute-done | bytes 1048608 | tf_op jit(solution)/shard_map/ppermute | solution.py:782
  57.4 5.5 %collective-permute-done.10 = bf16[64,2048]{1,0:T(8,128)(2,1)S(1)} collective-permute-done((bf16[64,2048]{1,0:T(8,128)(2,1)S(1)}, bf16[64,2048]{1,0:T(8,128)(2,1)S(1)}, u32[]{:S(2)}, u32[]{:S(2)}) %collective-permute-start.10) | collective-permute-done | bytes 262176 | tf_op jit(solution)/shard_map/ppermute | solution.py:782
  63.0 3.7 collective-permute-done.9
  69.7 1.8 collective-permute-start
  74.3 17.8 %collective-permute-done.refs_3_ = bf16[256,2048]{1,0:T(8,128)(2,1)} collective-permute-done((bf16[256,2048]{1,0:T(8,128)(2,1)S(1)}, bf16[256,2048]{1,0:T(8,128)(2,1)}, u32[]{:S(2)}, u32[]{:S(2)}) %collective-permute-start) | collective-permute-done | bytes 1048608 | tf_op jit(solution)/shard_map/ppermute | solution.py:782
  92.1 3.7 collective-permute-done.2.refs_6_
  96.7 3.2 slice_bitcast_fusion.2
  102.8 16.9 %in_project.2 = (bf16[2048,1408]{1,0:T(8,128)(2,1)}, bf16[2048,2048]{1,0:T(8,128)(2,1)}) custom-call(s32[6]{0:T(128)} %constant.29.clone.refs_0_, bf16[256,2048]{1,0:T(8,128)(2,1)} %get-tuple-element.174.refs_3_.refs_1_, bf16[256,2048]{1,0:T(8,128)(2,1)} %get-tuple-element.173.refs_4_.refs_2_, bf16[256,2048]{1,0:T(8,128)(2,1)} %collective-permute-done.refs_3_, ...), custom_call_target="tpu_custom_call" | custom-call | tf_op jit(solution)/shard_map/in_project/pallas_call | solution.py:549
  127.8 9.1 %in_project.3 = (bf16[2048,1408]{1,0:T(8,128)(2,1)}, bf16[2048,2048]{1,0:T(8,128)(2,1)}) custom-call(s32[2]{0:T(128)} %constant.30.clone.refs_0_, bf16[256,2048]{1,0:T(8,128)(2,1)} %get-tuple-element.87.refs_1_.refs_2_, bf16[256,2048]{1,0:T(8,128)(2,1)} %get-tuple-element.88.refs_2_.refs_3_, ...), custom_call_target="tpu_custom_call", output_to_operand_aliasing={{0}: (4, {}), {1}: (5, {})} | custom-call | tf_op jit(solution)/shard_map/in_project/pallas_call | solution.py:549
  137.5 32.8 %scan_forward.1 = (bf16[2048,1024]{1,0:T(8,128)(2,1)}, bf16[8,1024,128]{2,1,0:T(8,128)(2,1)}, bf16[2048,1280]{1,0:T(8,128)(2,1)}, bf16[2048,1280]{1,0:T(8,128)(2,1)}) custom-call(s32[1]{0:T(128)} %bitcast.19.place, bf16[2048,1408]{1,0:T(8,128)(2,1)} %get-tuple-element.91.proj.refs_1_, f32[8,1280]{1,0:T(8,128)} %fusion.26.refs_10_.conv_w, ...), custom_call_target="tpu_custom_call" | custom-call | tf_op jit(solution)/shard_map/scan_forward/pallas_call | solution.py:374
  171.3 2.0 collective-permute-start.17
  174.5 13.8 %convolution_convert_fusion.1.refs_8_.z_in = bf16[2048,1024]{1,0:T(8,128)(2,1)} fusion(bf16[2048,2048]{1,0:T(8,128)(2,1)} %get-tuple-element.90, bf16[2048,1024]{1,0:T(8,128)(2,1)} %after.25.w_z), kind=kOutput, calls=%fused_computation.20 | convolution fusion | flops 8592031744 | bytes 16777216 | tf_op jit(solution)/shard_map/dot_general | solution.py:34
  193.1 19.2 %gate_forward.1 = (bf16[2048,1024]{1,0:T(8,128)(2,1)}, bf16[2048,2048]{1,0:T(8,128)(2,1)}, f32[64,256]{1,0:T(8,128)}) custom-call(bf16[256,2048]{1,0:T(8,128)(2,1)} %get-tuple-element.93.refs_0_, bf16[256,2048]{1,0:T(8,128)(2,1)} %after.27.refs_1_, bf16[256,2048]{1,0:T(8,128)(2,1)} %get-tuple-element.94.refs_2_, ...), custom_call_target="tpu_custom_call" | custom-call | tf_op jit(solution)/shard_map/gate_forward/pallas_call | solution.py:587
  222.3 23.8 %out_project.1 = (bf16[2048,1024]{1,0:T(8,128)(2,1)}, bf16[2048,1024]{1,0:T(8,128)(2,1)}, bf16[2048,1024]{1,0:T(8,128)(2,1)}, f32[8,1024]{1,0:T(8,128)}, bf16[2,...) custom-call(bf16[2048,1024]{1,0:T(8,128)(2,1)} %convolution_convert_, ...), custom_call_target="tpu_custom_call" | custom-call | tf_op jit(solution)/shard_map/out_project/pallas_call | solution.py:635
  246.0 14.0 %convolution_convert_fusion.2.refs_1_ = bf16[2048,1024]{1,0:T(8,128)(2,1)} fusion(bf16[2048,2048]{1,0:T(8,128)(2,1)} %get-tuple-element.90, bf16[2048,1024]{1,0:T(8,128)(2,1)} %get-tuple-element.104.dz), kind=kOutput, calls=%fused_computation.21 | convolution fusion | flops 8592031744 | bytes 16777216 | tf_op jit(solution)/shard_map/dot_general | solution.py:34
  260.1 14.0 %convolution_convert_fusion.3.refs_0_ = bf16[2048,1024]{1,0:T(8,128)(2,1)} fusion(bf16[2048,2048]{1,0:T(8,128)(2,1)} %get-tuple-element.109, bf16[2048,1024]{1,0:T(8,128)(2,1)} %get-tuple-element.110), kind=kOutput, calls=%fused_computation.22 | convolution fusion | flops 8592031744 | bytes 16777216 | tf_op jit(solution)/shard_map/dot_general | solution.py:34
  276.0 27.0 %scan_backward.2 = (bf16[1024,1408]{1,0:T(8,128)(2,1)}, bf16[1024,1280]{1,0:T(8,128)(2,1)}, f32[16,128]{1,0:T(8,128)}, f32[8,1024]{1,0:T(8,128)}) custom-call(s32[1]{0:T(128)} %bitcast.19.place, bf16[2048,1408]{1,0:T(8,128)(2,1)} %get-tuple-element.91.proj.refs_1_, f32[8,1280]{1,0:T(8,128)} %fusion.26.refs_10_.conv_w, f32[8,1024]{1,0:T(8,128)} %broadcast_in_dim.30.skip, ...), custom_call_target="tpu_custom_call" | custom-call | tf_op jit(solution)/shard_map/scan_backward/pallas_call | solution.py:436
  303.0 17.4 %back_project.2 = (bf16[1,2,128,2048]{3,2,1,0:T(8,128)(2,1)}, bf16[1,2,128,2048]{3,2,1,0:T(8,128)(2,1)}, bf16[1,2,128,2048]{3,2,1,0:T(8,128)(2,1)}, bf16[1,2,128,2048]{3,2,1,0:T(8,128)(2,1)}) custom-call(bf16[2048,1024]{1,0:T(8,128)(2,1)} %get-tuple-element.104.dz, bf16[1024,1408]{1,0:T(8,128)(2,1)} %get-tuple-element.111.px, bf16[2048,1024]{1,0:T(8,128)(2,1)} %after.25.w_z, ...), custom_call_target="tpu_custom_call" | custom-call | tf_op jit(solution)/shard_map/back_project/pallas_call | solution.py:657
  322.8 2.1 add_convert_fusion.3.refs_3_
  326.2 1.6 add_convert_fusion.4.refs_2_
  328.9 27.1 %scan_backward.3 = (bf16[1024,1408]{1,0:T(8,128)(2,1)}, bf16[1024,1280]{1,0:T(8,128)(2,1)}, f32[16,128]{1,0:T(8,128)}, f32[8,1024]{1,0:T(8,128)}) custom-call(s32[1]{0:T(128)} %bitcast.19.place, bf16[2048,1408]{1,0:T(8,128)(2,1)} %get-tuple-element.91.proj.refs_1_, f32[8,1280]{1,0:T(8,128)} %fusion.26.refs_10_.conv_w, f32[8,1024]{1,0:T(8,128)} %broadcast_in_dim.30.skip, ...), custom_call_target="tpu_custom_call" | custom-call | tf_op jit(solution)/shard_map/scan_backward/pallas_call | solution.py:436
  356.0 2.8 collective-permute-done.24.refs_4_.refs_1_
  359.8 19.1 %convolution_convert_fusion.refs_2_.refs_1_ = bf16[2048,1408]{1,0:T(8,128)(2,1)} fusion(bf16[2048,2048]{1,0:T(8,128)(2,1)} %get-tuple-element.90, bf16[1024,1408]{1,0:T(8,128)(2,1)} %after.32.refs_0_, bf16[1024,1408]{1,0:T(8,128)(2,1)} %get-tuple-element.111.px), kind=kOutput, calls=%fused_computation.5 | convolution fusion | flops 11825577984 | bytes 19922944 | tf_op jit(solution)/shard_map/dot_general | solution.py:34
  390.2 1.6 collective-permute-start.29
  391.8 17.9 %back_project.3 = (bf16[1,2,128,2048]{3,2,1,0:T(8,128)(2,1)}, bf16[1,2,128,2048]{3,2,1,0:T(8,128)(2,1)}, bf16[1,2,128,2048]{3,2,1,0:T(8,128)(2,1)}, bf16[1,2,128,2048]{3,2,1,0:T(8,128)(2,1)}) custom-call(bf16[2048,1024]{1,0:T(8,128)(2,1)} %get-tuple-element.104.dz, bf16[1024,1408]{1,0:T(8,128)(2,1)} %after.34.px, bf16[2048,1024]{1,0:T(8,128)(2,1)} %after.25.w_z, ...), custom_call_target="tpu_custom_call" | custom-call | tf_op jit(solution)/shard_map/back_project/pallas_call | solution.py:657
  415.8 6.9 %tap_gradients.3.conv_1 = f32[40,1280]{1,0:T(8,128)} custom-call(s32[1]{0:T(128)} %bitcast.19.place, bf16[2048,1408]{1,0:T(8,128)(2,1)} %get-tuple-element.91.proj.refs_1_, f32[2048,8]{1,0:T(8,128)} %copy.116.refs_8_.aux, bf16[1024,1280]{1,0:T(8,128)(2,1)} %get-tuple-element.128.dco), custom_call_target="tpu_custom_call" | custom-call | tf_op jit(solution)/shard_map/tap_gradients/pallas_call | solution.py:464
  422.7 6.9 %tap_gradients.2.conv_0 = f32[40,1280]{1,0:T(8,128)} custom-call(s32[1]{0:T(128)} %bitcast.19.place, bf16[2048,1408]{1,0:T(8,128)(2,1)} %get-tuple-element.91.proj.refs_1_, f32[2048,8]{1,0:T(8,128)} %copy.116.refs_8_.aux, bf16[1024,1280]{1,0:T(8,128)(2,1)} %get-tuple-element.127.dco), custom_call_target="tpu_custom_call" | custom-call | tf_op jit(solution)/shard_map/tap_gradients/pallas_call | solution.py:464
  429.6 1.9 small_gradients.1.refs_0_
  436.1 1.7 collective-permute-start.35
  441.5 1.6 collective-permute-start.36
  443.1 1.9 fusion.18
  449.5 3.2 collective-permute-done.41
  453.7 2.1 broadcast_select_fusion.36
  457.4 1.9 collective-permute-start.39
  461.5 2.1 collective-permute-done.37.refs_2_.refs_5_.refs_3_
  464.5 2.3 collective-permute-done.38.refs_3_.refs_6_.refs_4_
  467.5 5.3 %shards.1 = (f32[64,8512]{1,0:T(8,128)}, f32[64,4096]{1,0:T(8,128)}, f32[24,128]{1,0:T(8,128)}) custom-call(s32[2]{0:T(128)} %pad_add_fusion.spot, bf16[64,2048]{1,0:T(8,128)(2,1)} %get-tuple-element.191.refs_0_, bf16[64,2048]{1,0:T(8,128)(2,1)} %copy-done.49, bf16[64,2048]{1,0:T(8,128)(2,1)} %copy-done.50, bf16[64,2048]{1,0:T(8,128)(2,1)} %copy-done.51, ...), custom_call_target="tpu_custom_call" | custom-call | tf_op jit(solution)/shard_map/shards/pallas_call | solution.py:714
  474.0 4.4 fusion.15
  479.4 5.3 %fusion.11 = (bf16[2,256,2048]{2,1,0:T(8,128)(2,1)}, bf16[2,256,2048]{2,1,0:T(8,128)(2,1)}) fusion(bf16[2,256,2048]{2,1,0:T(8,128)(2,1)S(1)} %copy-done.1, bf16[2,256,2048]{2,1,0:T(8,128)(2,1)S(1)} %copy-done.12, f32[2,256]{1,0:T(2,128)S(1)} %copy-done.70, f32[2,256]{1,0:T(2,128)S(1)} %copy-done.69, f32[2048]{0:T(1024)S(1)} %copy-done.57, ...), kind=kLoop, calls=%fused_computation.17 | loop fusion | flops 24117248 | bytes 12597248 | tf_op jit(solution)/shard_map/convert_element_type | solution.py:1028
  485.4 2.2 place_small.1
  490.7 2.2 collective-permute-done.45
  492.9 2.2 collective-permute-start.46
  495.6 1.9 collective-permute-done.46
  501.4 4.2 multiply_add_fusion.2
  506.5 5.5 %multiply_add_fusion = (f32[64,8512]{1,0:T(8,128)}, f32[64,8512]{1,0:T(8,128)}, f32[64,8512]{1,0:T(8,128)}) fusion(f32[64,8512]{1,0:T(8,128)S(1)} %copy-done.2, f32[64,8512]{1,0:T(8,128)} %get-tuple-element.149, f32[]{:T(128)S(6)} %min.3, f32[64,8512]{1,0:T(8,128)S(1)} %copy-done.34, f32[64,8512]{1,0:T(8,128)S(1)} %copy-done.35), kind=kLoop, calls=%fused_computation.25 | loop fusion | flops 8716288 | bytes 15253508 | tf_op jit(solution)/shard_map/add | solution.py:1042
  (383 shorter events, 111.4 us)
Async XLA Ops:
  7.2 92.7 %all-gather.4.cloned.1.call-start = ((), (), s32[]{:S(2)}) async-start(), calls=%async_computation.3 | async-start | bytes 6488064 | tf_op jit(solution)/shard_map/all_gather | solution.py:938
  10.7 8.4 %collective-permute-start.6 = (bf16[64,1408]{1,0:T(8,128)(2,1)S(1)}, bf16[64,1408]{1,0:T(8,128)(2,1)S(1)}, u32[]{:S(2)}, u32[]{:S(2)}) collective-permute-start(bf16[64,1408]{1,0:T(8,128)(2,1)S(1)} %get-tuple-element.210), channel_id=1, source_target_pairs={{0,1},{1,0},{2,3},{3,2},{4,5},{5,4},{6,7},{7,6},{8,9},{9,8},{10,11... | collective-permute-start | bytes 540680 | tf_op jit(solution)/shard_map/ppermute | solution.py:782
  13.8 9.9 %collective-permute-start.7 = (bf16[64,1408]{1,0:T(8,128)(2,1)S(1)}, bf16[64,1408]{1,0:T(8,128)(2,1)S(1)}, u32[]{:S(2)}, u32[]{:S(2)}) collective-permute-start(bf16[64,1408]{1,0:T(8,128)(2,1)S(1)} %get-tuple-element.209), channel_id=1, source_target_pairs={{0,2},{1,3},{2,0},{3,1},{4,6},{5,7},{6,4},{7,5},{8,10},{9,11},{10,... | collective-permute-start | bytes 540680 | tf_op jit(solution)/shard_map/ppermute | solution.py:782
  15.3 8.4 %collective-permute-start.8 = (bf16[64,1408]{1,0:T(8,128)(2,1)S(1)}, bf16[64,1408]{1,0:T(8,128)(2,1)S(1)}, u32[]{:S(2)}, u32[]{:S(2)}) collective-permute-start(bf16[64,1408]{1,0:T(8,128)(2,1)S(1)} %get-tuple-element.208), channel_id=1, source_target_pairs={{0,3},{1,2},{2,1},{3,0},{4,7},{5,6},{6,5},{7,4},{8,11},{9,10},{10,... | collective-permute-start | bytes 540680 | tf_op jit(solution)/shard_map/ppermute | solution.py:782
  27.7 142.6 %all-gather.6.cloned.1.call-start = ((), (), s32[]{:S(2)}) async-start(), calls=%async_computation.4 | async-start | bytes 4718592 | tf_op jit(solution)/shard_map/all_gather | solution.py:943
  27.8 23.8 %collective-permute-start.4 = (bf16[256,2048]{1,0:T(8,128)(2,1)S(1)}, bf16[256,2048]{1,0:T(8,128)(2,1)S(1)}, u32[]{:S(2)}, u32[]{:S(2)}) collective-permute-start(bf16[256,2048]{1,0:T(8,128)(2,1)S(1)} %copy-done.10), channel_id=1, source_target_pairs={{0,2},{1,3},{2,0},{3,1},{4,6},{5,7},{6,4},{7,5},{8,10},{9,11},{10,... | collective-permute-start | bytes 3145736 | tf_op jit(solution)/shard_map/ppermute | solution.py:782
  29.4 22.6 %collective-permute-start.5 = (bf16[256,2048]{1,0:T(8,128)(2,1)S(1)}, bf16[256,2048]{1,0:T(8,128)(2,1)}, u32[]{:S(2)}, u32[]{:S(2)}) collective-permute-start(bf16[256,2048]{1,0:T(8,128)(2,1)S(1)} %copy-done.9), channel_id=1, source_target_pairs={{0,1},{1,0},{2,3},{3,2},{4,5},{5,4},{6,7},{7,6},{8,9},{9,8},{10,11... | collective-permute-start | bytes 3145736 | tf_op jit(solution)/shard_map/ppermute | solution.py:782
  53.8 9.0 %collective-permute-start.10 = (bf16[64,2048]{1,0:T(8,128)(2,1)S(1)}, bf16[64,2048]{1,0:T(8,128)(2,1)S(1)}, u32[]{:S(2)}, u32[]{:S(2)}) collective-permute-start(bf16[64,2048]{1,0:T(8,128)(2,1)S(1)} %get-tuple-element.198), channel_id=1, source_target_pairs={{0,2},{1,3},{2,0},{3,1},{4,6},{5,7},{6,4},{7,5},{8,10},{9,11},{10,... | collective-permute-start | bytes 786440 | tf_op jit(solution)/shard_map/ppermute | solution.py:782
  54.7 8.3 %collective-permute-start.11 = (bf16[64,2048]{1,0:T(8,128)(2,1)S(1)}, bf16[64,2048]{1,0:T(8,128)(2,1)S(1)}, u32[]{:S(2)}, u32[]{:S(2)}) collective-permute-start(bf16[64,2048]{1,0:T(8,128)(2,1)S(1)} %get-tuple-element.197), channel_id=1, source_target_pairs={{0,1},{1,0},{2,3},{3,2},{4,5},{5,4},{6,7},{7,6},{8,9},{9,8},{10,11... | collective-permute-start | bytes 786440 | tf_op jit(solution)/shard_map/ppermute | solution.py:782
  56.2 10.6 %collective-permute-start.9 = (bf16[64,2048]{1,0:T(8,128)(2,1)S(1)}, bf16[64,2048]{1,0:T(8,128)(2,1)S(1)}, u32[]{:S(2)}, u32[]{:S(2)}) collective-permute-start(bf16[64,2048]{1,0:T(8,128)(2,1)S(1)} %get-tuple-element.199), channel_id=1, source_target_pairs={{0,3},{1,2},{2,1},{3,0},{4,7},{5,6},{6,5},{7,4},{8,11},{9,10},{10,... | collective-permute-start | bytes 786440 | tf_op jit(solution)/shard_map/ppermute | solution.py:782
  69.0 123.5 %all-gather.8.cloned.1.call-start = ((), (), s32[]{:S(2)}) async-start(), calls=%async_computation.5 | async-start | bytes 4718592 | tf_op jit(solution)/shard_map/all_gather | solution.py:944
  69.7 315.5 %reduce-scatter.8.cloned.1.call-start = ((), (), s32[]{:S(2)}) async-start(), calls=%async_computation.8 | async-start | bytes 4718592 | tf_op jit(solution)/shard_map/reduce_scatter | solution.py:973
  69.7 22.3 %collective-permute-start = (bf16[256,2048]{1,0:T(8,128)(2,1)S(1)}, bf16[256,2048]{1,0:T(8,128)(2,1)}, u32[]{:S(2)}, u32[]{:S(2)}) collective-permute-start(bf16[256,2048]{1,0:T(8,128)(2,1)S(1)} %copy-done.10), channel_id=1, source_target_pairs={{0,1},{1,0},{2,3},{3,2},{4,5},{5,4},{6,7},{7,6},{8,9},{9,8},{10,11... | collective-permute-start | bytes 3145736 | tf_op jit(solution)/shard_map/ppermute | solution.py:782
  71.5 24.3 %collective-permute-start.2 = (bf16[256,2048]{1,0:T(8,128)(2,1)S(1)}, bf16[256,2048]{1,0:T(8,128)(2,1)}, u32[]{:S(2)}, u32[]{:S(2)}) collective-permute-start(bf16[256,2048]{1,0:T(8,128)(2,1)S(1)} %copy-done.9), channel_id=1, source_target_pairs={{0,2},{1,3},{2,0},{3,1},{4,6},{5,7},{6,4},{7,5},{8,10},{9,11},{10,... | collective-permute-start | bytes 3145736 | tf_op jit(solution)/shard_map/ppermute | solution.py:782
  92.1 27.7 %collective-permute-start.1 = (bf16[256,2048]{1,0:T(8,128)(2,1)}, bf16[256,2048]{1,0:T(8,128)(2,1)S(1)}, u32[]{:S(2)}, u32[]{:S(2)}) collective-permute-start(bf16[256,2048]{1,0:T(8,128)(2,1)} %collective-permute-done.refs_3_), channel_id=1, source_target_pairs={{0,2},{1,3},{2,0},{3,1},{4,6},{5,7},{6,4},{7,5},{8,10},{9,11},{10,... | collective-permute-start | bytes 3145736 | tf_op jit(solution)/shard_map/ppermute | solution.py:782
  95.8 24.0 %collective-permute-start.3 = (bf16[256,2048]{1,0:T(8,128)(2,1)}, bf16[256,2048]{1,0:T(8,128)(2,1)S(1)}, u32[]{:S(2)}, u32[]{:S(2)}) collective-permute-start(bf16[256,2048]{1,0:T(8,128)(2,1)} %collective-permute-done.2.refs_6_), channel_id=1, source_target_pairs={{0,1},{1,0},{2,3},{3,2},{4,5},{5,4},{6,7},{7,6},{8,9},{9,8},{10,11... | collective-permute-start | bytes 3145736 | tf_op jit(solution)/shard_map/ppermute | solution.py:782
  121.1 49.2 %collective-permute-start.16 = (bf16[256,2048]{1,0:T(8,128)(2,1)}, bf16[256,2048]{1,0:T(8,128)(2,1)S(1)}, u32[]{:S(2)}, u32[]{:S(2)}) collective-permute-start(bf16[256,2048]{1,0:T(8,128)(2,1)} %get-tuple-element.96.refs_4_), channel_id=1, source_target_pairs={{0,2},{1,3},{2,0},{3,1},{4,6},{5,7},{6,4},{7,5},{8,10},{9,11},{10,... | collective-permute-start | bytes 3145736 | tf_op jit(solution)/shard_map/ppermute | solution.py:782
  121.9 51.5 %collective-permute-start.12 = (bf16[256,2048]{1,0:T(8,128)(2,1)}, bf16[256,2048]{1,0:T(8,128)(2,1)S(1)}, u32[]{:S(2)}, u32[]{:S(2)}) collective-permute-start(bf16[256,2048]{1,0:T(8,128)(2,1)} %get-tuple-element.93.refs_0_), channel_id=1, source_target_pairs={{0,1},{1,0},{2,3},{3,2},{4,5},{5,4},{6,7},{7,6},{8,9},{9,8},{10,11... | collective-permute-start | bytes 3145736 | tf_op jit(solution)/shard_map/ppermute | solution.py:782
  125.9 62.4 %collective-permute-start.15 = (bf16[256,2048]{1,0:T(8,128)(2,1)}, bf16[256,2048]{1,0:T(8,128)(2,1)}, u32[]{:S(2)}, u32[]{:S(2)}) collective-permute-start(bf16[256,2048]{1,0:T(8,128)(2,1)} %get-tuple-element.96.refs_4_), channel_id=1, source_target_pairs={{0,1},{1,0},{2,3},{3,2},{4,5},{5,4},{6,7},{7,6},{8,9},{9,8},{10,11... | collective-permute-start | bytes 3145736 | tf_op jit(solution)/shard_map/ppermute | solution.py:782
  126.4 63.9 %collective-permute-start.13 = (bf16[256,2048]{1,0:T(8,128)(2,1)}, bf16[256,2048]{1,0:T(8,128)(2,1)S(1)}, u32[]{:S(2)}, u32[]{:S(2)}) collective-permute-start(bf16[256,2048]{1,0:T(8,128)(2,1)} %get-tuple-element.93.refs_0_), channel_id=1, source_target_pairs={{0,2},{1,3},{2,0},{3,1},{4,6},{5,7},{6,4},{7,5},{8,10},{9,11},{10,... | collective-permute-start | bytes 3145736 | tf_op jit(solution)/shard_map/ppermute | solution.py:782
  171.3 18.0 %collective-permute-start.17 = (bf16[256,2048]{1,0:T(8,128)(2,1)}, bf16[256,2048]{1,0:T(8,128)(2,1)S(1)}, u32[]{:S(2)}, u32[]{:S(2)}) collective-permute-start(bf16[256,2048]{1,0:T(8,128)(2,1)} %after.29.refs_6_), channel_id=1, source_target_pairs={{0,1},{1,0},{2,3},{3,2},{4,5},{5,4},{6,7},{7,6},{8,9},{9,8},{10,11... | collective-permute-start | bytes 3145736 | tf_op jit(solution)/shard_map/ppermute | solution.py:782
  174.4 17.1 %collective-permute-start.14 = (bf16[256,2048]{1,0:T(8,128)(2,1)}, bf16[256,2048]{1,0:T(8,128)(2,1)S(1)}, u32[]{:S(2)}, u32[]{:S(2)}) collective-permute-start(bf16[256,2048]{1,0:T(8,128)(2,1)} %after.27.refs_1_), channel_id=1, source_target_pairs={{0,2},{1,3},{2,0},{3,1},{4,6},{5,7},{6,4},{7,5},{8,10},{9,11},{10,... | collective-permute-start | bytes 3145736 | tf_op jit(solution)/shard_map/ppermute | solution.py:782
  260.0 125.2 %reduce-scatter.6.cloned.1.call-start = ((), (), s32[]{:S(2)}) async-start(), calls=%async_computation.7 | async-start | bytes 4718592 | tf_op jit(solution)/shard_map/reduce_scatter | solution.py:973
  274.1 179.6 %reduce-scatter.4.cloned.1.call-start = ((), (), s32[]{:S(2)}) async-start(), calls=%async_computation.6 | async-start | bytes 6488064 | tf_op jit(solution)/shard_map/reduce_scatter | solution.py:973
  274.1 48.7 %collective-permute-start.21 = (bf16[2,2,128,2048]{3,2,1,0:T(8,128)(2,1)}, bf16[2,2,128,2048]{3,2,1,0:T(8,128)(2,1)}, u32[]{:S(2)}, u32[]{:S(2)}) collective-permute-start(bf16[2,2,128,2048]{3,2,1,0:T(8,128)(2,1)} %get-tuple-element.102), channel_id=1, source_target_pairs={{0,1},{1,0},{2,3},{3,2},{4,5},{5,4},{6,7},{7,6},{8,9},{9,8},{10,11... | collective-permute-start | bytes 6291464 | tf_op jit(solution)/shard_map/ppermute | solution.py:782
  275.5 47.4 %collective-permute-start.22 = (bf16[2,2,128,2048]{3,2,1,0:T(8,128)(2,1)}, bf16[2,2,128,2048]{3,2,1,0:T(8,128)(2,1)}, u32[]{:S(2)}, u32[]{:S(2)}) collective-permute-start(bf16[2,2,128,2048]{3,2,1,0:T(8,128)(2,1)} %get-tuple-element.103), channel_id=1, source_target_pairs={{0,2},{1,3},{2,0},{3,1},{4,6},{5,7},{6,4},{7,5},{8,10},{9,11},{10,... | collective-permute-start | bytes 6291464 | tf_op jit(solution)/shard_map/ppermute | solution.py:782
  320.4 35.5 %collective-permute-start.25 = (bf16[1,2,128,2048]{3,2,1,0:T(8,128)(2,1)}, bf16[1,2,128,2048]{3,2,1,0:T(8,128)(2,1)S(1)}, u32[]{:S(2)}, u32[]{:S(2)}) collective-permute-start(bf16[1,2,128,2048]{3,2,1,0:T(8,128)(2,1)} %get-tuple-element.112.refs_2_.refs_0_), channel_id=1, source_target_pairs={{0,1},{1,0},{2,3},{3,2},{4,5},{5,4},{6,7},{7,6},{8,9},{9,8},{10,11... | collective-permute-start | bytes 3145736 | tf_op jit(solution)/shard_map/ppermute | solution.py:782
  321.8 34.2 %collective-permute-start.26 = (bf16[1,2,128,2048]{3,2,1,0:T(8,128)(2,1)}, bf16[1,2,128,2048]{3,2,1,0:T(8,128)(2,1)S(1)}, u32[]{:S(2)}, u32[]{:S(2)}) collective-permute-start(bf16[1,2,128,2048]{3,2,1,0:T(8,128)(2,1)} %get-tuple-element.116.refs_1_), channel_id=1, source_target_pairs={{0,2},{1,3},{2,0},{3,1},{4,6},{5,7},{6,4},{7,5},{8,10},{9,11},{10,... | collective-permute-start | bytes 3145736 | tf_op jit(solution)/shard_map/ppermute | solution.py:782
  325.0 33.8 %collective-permute-start.24 = (bf16[2,1,128,2048]{3,2,1,0:T(8,128)(2,1)S(1)}, bf16[2,1,128,2048]{3,2,1,0:T(8,128)(2,1)S(1)}, u32[]{:S(2)}, u32[]{:S(2)}) collective-permute-start(bf16[2,1,128,2048]{3,2,1,0:T(8,128)(2,1)S(1)} %add_convert_fusion.3.refs_3_), channel_id=1, source_target_pairs={{0,1},{1,0},{2,3},{3,2},{4,5},{5,4},{6,7},{7,6},{8,9},{9,8},{10,11... | collective-permute-start | bytes 3145736 | tf_op jit(solution)/shard_map/ppermute | solution.py:782
  327.9 31.9 %collective-permute-start.23 = (bf16[2,1,128,2048]{3,2,1,0:T(8,128)(2,1)S(1)}, bf16[2,1,128,2048]{3,2,1,0:T(8,128)(2,1)}, u32[]{:S(2)}, u32[]{:S(2)}) collective-permute-start(bf16[2,1,128,2048]{3,2,1,0:T(8,128)(2,1)S(1)} %add_convert_fusion.4.refs_2_), channel_id=1, source_target_pairs={{0,2},{1,3},{2,0},{3,1},{4,6},{5,7},{6,4},{7,5},{8,10},{9,11},{10,... | collective-permute-start | bytes 3145736 | tf_op jit(solution)/shard_map/ppermute | solution.py:782
  381.4 28.3 %collective-permute-start.31 = (bf16[1,1,128,2048]{3,2,1,0:T(8,128)(2,1)S(1)}, bf16[1,1,128,2048]{3,2,1,0:T(8,128)(2,1)S(1)}, u32[]{:S(2)}, u32[]{:S(2)}) collective-permute-start(bf16[1,1,128,2048]{3,2,1,0:T(8,128)(2,1)S(1)} %add_convert_fusion.16.refs_3_), channel_id=1, source_target_pairs={{0,1},{1,0},{2,3},{3,2},{4,5},{5,4},{6,7},{7,6},{8,9},{9,8},{10,11... | collective-permute-start | bytes 1572872 | tf_op jit(solution)/shard_map/ppermute | solution.py:782
  383.8 26.9 %collective-permute-start.30 = (bf16[1,1,128,2048]{3,2,1,0:T(8,128)(2,1)S(1)}, bf16[1,1,128,2048]{3,2,1,0:T(8,128)(2,1)S(1)}, u32[]{:S(2)}, u32[]{:S(2)}) collective-permute-start(bf16[1,1,128,2048]{3,2,1,0:T(8,128)(2,1)S(1)} %add_convert_fusion.17.refs_2_), channel_id=1, source_target_pairs={{0,2},{1,3},{2,0},{3,1},{4,6},{5,7},{6,4},{7,5},{8,10},{9,11},{10,... | collective-permute-start | bytes 1572872 | tf_op jit(solution)/shard_map/ppermute | solution.py:782
  388.4 23.1 %collective-permute-start.27 = (bf16[64,2048]{1,0:T(8,128)(2,1)}, bf16[64,2048]{1,0:T(8,128)(2,1)S(1)}, u32[]{:S(2)}, u32[]{:S(2)}) collective-permute-start(bf16[64,2048]{1,0:T(8,128)(2,1)} %get-tuple-element.192), channel_id=1, source_target_pairs={{0,1},{1,0},{2,3},{3,2},{4,5},{5,4},{6,7},{7,6},{8,9},{9,8},{10,11... | collective-permute-start | bytes 786440 | tf_op jit(solution)/shard_map/ppermute | solution.py:782
  389.4 22.0 %collective-permute-start.28 = (bf16[64,2048]{1,0:T(8,128)(2,1)S(1)}, bf16[64,2048]{1,0:T(8,128)(2,1)S(1)}, u32[]{:S(2)}, u32[]{:S(2)}) collective-permute-start(bf16[64,2048]{1,0:T(8,128)(2,1)S(1)} %get-tuple-element.193), channel_id=1, source_target_pairs={{0,2},{1,3},{2,0},{3,1},{4,6},{5,7},{6,4},{7,5},{8,10},{9,11},{10,... | collective-permute-start | bytes 786440 | tf_op jit(solution)/shard_map/ppermute | solution.py:782
  390.2 21.3 %collective-permute-start.29 = (bf16[64,2048]{1,0:T(8,128)(2,1)S(1)}, bf16[64,2048]{1,0:T(8,128)(2,1)S(1)}, u32[]{:S(2)}, u32[]{:S(2)}) collective-permute-start(bf16[64,2048]{1,0:T(8,128)(2,1)S(1)} %get-tuple-element.194), channel_id=1, source_target_pairs={{0,3},{1,2},{2,1},{3,0},{4,7},{5,6},{6,5},{7,4},{8,11},{9,10},{10,... | collective-permute-start | bytes 786440 | tf_op jit(solution)/shard_map/ppermute | solution.py:782
  412.4 19.1 %collective-permute-start.32 = (bf16[1,2,128,2048]{3,2,1,0:T(8,128)(2,1)}, bf16[1,2,128,2048]{3,2,1,0:T(8,128)(2,1)}, u32[]{:S(2)}, u32[]{:S(2)}) collective-permute-start(bf16[1,2,128,2048]{3,2,1,0:T(8,128)(2,1)} %get-tuple-element.137), channel_id=1, source_target_pairs={{0,1},{1,0},{2,3},{3,2},{4,5},{5,4},{6,7},{7,6},{8,9},{9,8},{10,11... | collective-permute-start | bytes 3145736 | tf_op jit(solution)/shard_map/ppermute | solution.py:782
  413.6 18.0 %collective-permute-start.33 = (bf16[1,2,128,2048]{3,2,1,0:T(8,128)(2,1)}, bf16[1,2,128,2048]{3,2,1,0:T(8,128)(2,1)S(1)}, u32[]{:S(2)}, u32[]{:S(2)}) collective-permute-start(bf16[1,2,128,2048]{3,2,1,0:T(8,128)(2,1)} %get-tuple-element.138), channel_id=1, source_target_pairs={{0,2},{1,3},{2,0},{3,1},{4,6},{5,7},{6,4},{7,5},{8,10},{9,11},{10,... | collective-permute-start | bytes 3145736 | tf_op jit(solution)/shard_map/ppermute | solution.py:782
  434.0 14.2 %collective-permute-start.40 = (bf16[1,1,128,2048]{3,2,1,0:T(8,128)(2,1)S(1)}, bf16[1,1,128,2048]{3,2,1,0:T(8,128)(2,1)S(1)}, u32[]{:S(2)}, u32[]{:S(2)}) collective-permute-start(bf16[1,1,128,2048]{3,2,1,0:T(8,128)(2,1)S(1)} %add_convert_fusion.15.refs_2_), channel_id=1, source_target_pairs={{0,2},{1,3},{2,0},{3,1},{4,6},{5,7},{6,4},{7,5},{8,10},{9,11},{10,... | collective-permute-start | bytes 1572872 | tf_op jit(solution)/shard_map/ppermute | solution.py:782
  436.1 5.4 %collective-permute-start.35 = (f32[8,1280]{1,0:T(8,128)S(1)}, f32[8,1280]{1,0:T(8,128)S(1)}, u32[]{:S(2)}, u32[]{:S(2)}) collective-permute-start(f32[8,1280]{1,0:T(8,128)S(1)} %add.260), channel_id=1, source_target_pairs={{0,8},{4,12},{8,0},{12,4},{16,24},{20,28},{24,16},{28,20},{1,9},{5... | collective-permute-start | bytes 122888 | tf_op jit(solution)/shard_map/ppermute | solution.py:782
  438.9 13.7 %collective-permute-start.41 = (bf16[1,1,128,2048]{3,2,1,0:T(8,128)(2,1)S(1)}, bf16[1,1,128,2048]{3,2,1,0:T(8,128)(2,1)S(1)}, u32[]{:S(2)}, u32[]{:S(2)}) collective-permute-start(bf16[1,1,128,2048]{3,2,1,0:T(8,128)(2,1)S(1)} %add_convert_fusion.14.refs_3_), channel_id=1, source_target_pairs={{0,1},{1,0},{2,3},{3,2},{4,5},{5,4},{6,7},{7,6},{8,9},{9,8},{10,11... | collective-permute-start | bytes 1572872 | tf_op jit(solution)/shard_map/ppermute | solution.py:782
  455.9 7.7 %collective-permute-start.37 = (bf16[64,1408]{1,0:T(8,128)(2,1)}, bf16[64,1408]{1,0:T(8,128)(2,1)S(1)}, u32[]{:S(2)}, u32[]{:S(2)}) collective-permute-start(bf16[64,1408]{1,0:T(8,128)(2,1)} %get-tuple-element.205.refs_2_), channel_id=1, source_target_pairs={{0,1},{1,0},{2,3},{3,2},{4,5},{5,4},{6,7},{7,6},{8,9},{9,8},{10,11... | collective-permute-start | bytes 540680 | tf_op jit(solution)/shard_map/ppermute | solution.py:782
  456.8 10.0 %collective-permute-start.38 = (bf16[64,1408]{1,0:T(8,128)(2,1)}, bf16[64,1408]{1,0:T(8,128)(2,1)S(1)}, u32[]{:S(2)}, u32[]{:S(2)}) collective-permute-start(bf16[64,1408]{1,0:T(8,128)(2,1)} %get-tuple-element.206.refs_3_), channel_id=1, source_target_pairs={{0,2},{1,3},{2,0},{3,1},{4,6},{5,7},{6,4},{7,5},{8,10},{9,11},{10,... | collective-permute-start | bytes 540680 | tf_op jit(solution)/shard_map/ppermute | solution.py:782
  457.4 9.4 %collective-permute-start.39 = (bf16[64,1408]{1,0:T(8,128)(2,1)}, bf16[64,1408]{1,0:T(8,128)(2,1)}, u32[]{:S(2)}, u32[]{:S(2)}) collective-permute-start(bf16[64,1408]{1,0:T(8,128)(2,1)} %get-tuple-element.207.refs_4_), channel_id=1, source_target_pairs={{0,3},{1,2},{2,1},{3,0},{4,7},{5,6},{6,5},{7,4},{8,11},{9,10},{10,... | collective-permute-start | bytes 540680 | tf_op jit(solution)/shard_map/ppermute | solution.py:782
  459.9 24.8 %collective-permute-start.47 = (f32[8,1280]{1,0:T(8,128)}, f32[8,1280]{1,0:T(8,128)S(1)}, u32[]{:S(2)}, u32[]{:S(2)}) collective-permute-start(f32[8,1280]{1,0:T(8,128)} %after.42.refs_0_), channel_id=1, source_target_pairs={{0,1},{1,0},{2,3},{3,2},{4,5},{5,4},{6,7},{7,6},{8,9},{9,8},{10,11... | collective-permute-start | bytes 122888 | tf_op jit(solution)/shard_map/ppermute | solution.py:782
  460.9 23.9 %collective-permute-start.48 = (f32[8,1280]{1,0:T(8,128)}, f32[8,1280]{1,0:T(8,128)}, u32[]{:S(2)}, u32[]{:S(2)}) collective-permute-start(f32[8,1280]{1,0:T(8,128)} %after.42.refs_0_), channel_id=1, source_target_pairs={{0,2},{1,3},{2,0},{3,1},{4,6},{5,7},{6,4},{7,5},{8,10},{9,11},{10,... | collective-permute-start | bytes 122888 | tf_op jit(solution)/shard_map/ppermute | solution.py:782
  463.6 21.2 %collective-permute-start.49 = (f32[8,1280]{1,0:T(8,128)}, f32[8,1280]{1,0:T(8,128)}, u32[]{:S(2)}, u32[]{:S(2)}) collective-permute-start(f32[8,1280]{1,0:T(8,128)} %after.42.refs_0_), channel_id=1, source_target_pairs={{0,3},{1,2},{2,1},{3,0},{4,7},{5,6},{6,5},{7,4},{8,11},{9,10},{10,... | collective-permute-start | bytes 122888 | tf_op jit(solution)/shard_map/ppermute | solution.py:782
  472.8 5.6 %collective-permute-start.42 = (f32[24,128]{1,0:T(8,128)}, f32[24,128]{1,0:T(8,128)S(1)}, u32[]{:S(2)}, u32[]{:S(2)}) collective-permute-start(f32[24,128]{1,0:T(8,128)} %get-tuple-element.145), channel_id=1, source_target_pairs={{0,1},{1,0},{2,3},{3,2},{4,5},{5,4},{6,7},{7,6},{8,9},{9,8},{10,11... | collective-permute-start | bytes 36872 | tf_op jit(solution)/shard_map/ppermute | solution.py:782
  478.4 9.1 %collective-permute-start.43 = (f32[24,128]{1,0:T(8,128)S(1)}, f32[24,128]{1,0:T(8,128)S(1)}, u32[]{:S(2)}, u32[]{:S(2)}) collective-permute-start(f32[24,128]{1,0:T(8,128)S(1)} %add.280), channel_id=1, source_target_pairs={{0,2},{1,3},{2,0},{3,1},{4,6},{5,7},{6,4},{7,5},{8,10},{9,11},{10,... | collective-permute-start | bytes 36872 | tf_op jit(solution)/shard_map/ppermute | solution.py:782
  (79 other events, 393.3 us)
Sparse Core Ops, SparseCore 0:
  27.8 60.7 all-gather.3
  90.8 45.8 all-gather.5
  138.3 45.8 all-gather.7
  260.2 49.9 reduce-scatter.7
  312.4 48.1 reduce-scatter.5
  379.1 66.2 reduce-scatter.3

commit v7 on v6

--- a/solution.py
+++ b/solution.py
@@ -578,7 +578,9 @@
     ones = jnp.ones((8, gz.shape[1]), BF)
     first = dot(ones, (gz * gz).astype(BF), NT)
     second = dot(ones, (dn * gain[0:1, :] * gz).astype(BF), NT)
-    sums[...] = jnp.where(iota2((8, BLOCK), 0) == 0, first, second)
+    step = pl.program_id(0)
+    sums[pl.ds(step, 1), :] = first[0:1]
+    sums[pl.ds(count + step, 1), :] = second[0:1]
 
 
 def gate_forward(pieces, z, w_o, y, gain):
@@ -588,11 +590,11 @@
         functools.partial(gate_kernel, count=count),
         grid=(count,),
         in_specs=[pl.BlockSpec(memory_space=pl.ANY)] * count + [by_rows(width), fixed(w_o), by_rows(width), fixed(gain)],
-        out_specs=[by_rows(width), by_rows(depth), pl.BlockSpec((8, BLOCK), lambda i: (i, 0))],
+        out_specs=[by_rows(width), by_rows(depth), pl.BlockSpec((2 * count, BLOCK), lambda i: (0, 0))],
         out_shape=[
             jax.ShapeDtypeStruct((count * BLOCK, width), BF),
             jax.ShapeDtypeStruct((count * BLOCK, depth), BF),
-            jax.ShapeDtypeStruct((count * 8, BLOCK), F32),
+            jax.ShapeDtypeStruct((2 * count, BLOCK), F32),
         ],
         scratch_shapes=[pltpu.VMEM((2, BLOCK, depth), BF), pltpu.SemaphoreType.DMA((2,))],
         **arbitrary("gate_forward"),
@@ -605,8 +607,8 @@
     def _():
         dgain[...] = jnp.zeros(dgain.shape, F32)
 
-    scale = lax.rsqrt(sums[0:1, :] / INNER + NORM_EPS)
-    slope = scale * scale * scale * sums[1:2, :] / INNER
+    scale = lax.rsqrt(sums[pl.ds(step, 1), :] / INNER + NORM_EPS)
+    slope = scale * scale * scale * sums[pl.ds(MICRO * n + step, 1), :] / INNER
     row = iota2((LANES, BLOCK), 0)
     columns = jnp.where(row == 0, scale, jnp.where(row == 1, slope, 0.0)).T
     scale, slope = columns[:, 0:1], columns[:, 1:2]
@@ -635,7 +637,7 @@
     return pl.pallas_call(
         functools.partial(out_kernel, n=n, bits=bits),
         grid=(tokens // BLOCK,),
-        in_specs=[one, one, one, pl.BlockSpec((8, BLOCK), lambda i: (i, 0)), fixed(gain), fixed(w_o)],
+        in_specs=[one, one, one, fixed(sums), fixed(gain), fixed(w_o)],
         out_specs=[one, one, one, pl.BlockSpec((8, width), lambda i: (0, 0))] + places,
         out_shape=[jax.ShapeDtypeStruct((tokens, width), BF)] * 3 + [jax.ShapeDtypeStruct((8, width), F32)] + shapes,
         scratch_shapes=scratch,
@@ -966,7 +968,7 @@
     [w_z] = after([w_z], y)
     z = dot(hidden, w_z, NN).astype(BF)
     dn, cot, sums = gate_forward(cot, z, w_o, y, gain)
-    sums = sum_pieces(sums.reshape(MICRO, n, 8 * BLOCK)).reshape(-1, BLOCK)
+    sums = sum_pieces(sums.reshape(2, MICRO, n, piece)).reshape(-1, BLOCK)
     first_bits = tuple(micro_order(half, "seq")[0] for half in range(2))
     normed, dy, dz, d_gain_out, *out_part = out_project(z, dn, y, sums, gain, w_o, first_bits)
 
@@ -1005,10 +1007,11 @@
     hid_got, _ = next(stages_1)
     small = small_gradients(conv_0, conv_1, vec_0, vec_1, skip_0, skip_1, d_gain_out)
     [small] = after([small], *hid_got)
+    output = (tok + finish(out_stages, [small]).astype(F32)).astype(BF)
     for bit in axis_bits("dp"):
         small = small + swapped(small, "dp", bit)
     _, hid_sent = stages_1.send(None)
-    [got_x] = after([got_x], small, *hid_sent)
+    [got_x] = after([got_x], small, output, *hid_sent)
     sent_x, got_x = exchange(split(got_x), rank)
     [small] = after([small], *sent_x)
     small = [small] + after([swapped(small, "seq", mask) for mask in range(1, n)], *got_x)
@@ -1021,8 +1024,7 @@
     conv_sq = jnp.sum(conv_tot * conv_tot)
     shard_in, shard_out, last = shards(spot, sent_oz[:1] + got_oz, sent_x[:1] + got_x, in_weight, own_gain, hl)
     shard_out = shard_out.T
-    output = (tok + finish(out_stages, got_x).astype(F32)).astype(BF)
-    d_hidden = jnp.concatenate([finish(stages_0, [hid_1[0]]), finish(stages_1)], axis=0).astype(F32)
+    d_hidden = jnp.concatenate([finish(stages_0, [hid_1[0]]), finish(stages_1, got_x)], axis=0).astype(F32)
     dh = d_hidden * gain_in
     d_tok = r_in * (dh - tok * (r_in * r_in) * jnp.mean(dh * tok, axis=-1, keepdims=True))
     input_grad = (cotangent.astype(F32) + d_tok).astype(BF)

time: 528 us -> 523 us (level)
  waiting for transfers between devices: 79.8 us -> 72.3 us
    ppermute x50, waiting for transfers between devices: 79 us -> 71.5 us  [swapped(): lax.ppermute(value, axis, [(i, i ^ mask) for i in range(lax.axis_size(axi...]
    unnamed x154 -> x170, local copies, waits for them, and re-layouts: 15.3 us -> 17.5 us
  transfers between devices with their start and end apart: 56 -> 56, of which waited for: 23 -> 22; matrix products, arithmetic and copies ran while one was open for 20% -> 21% of each run, Pallas kernels for 33% -> 33%
where the time goes in v7:
time: 523 us; the launch traced here: 517 us
  Pallas kernels  214 us (41%)
  waiting for transfers between devices  72.3 us (14%)
  matrix products  60.9 us (12%)
  other arithmetic  56.1 us (11%)
  starting transfers between devices  55 us (11%)
  local copies, waits for them, and re-layouts  39.1 us (7%)
  between operations  18.7 us (4%)
    ppermute x50, waiting for transfers between devices, swapped(): lax.ppermute(value, axis, [(i, i ^ mask) for i in range(lax.axis_size(axi...  71.5 us
    dot_general x4, matrix products, dot(): return lax.dot_general(a, b, (dims, ((), ())), preferred_element_type=out)  60.9 us
    ppermute x50, starting transfers between devices, swapped(): lax.ppermute(value, axis, [(i, i ^ mask) for i in range(lax.axis_size(axi...  54.7 us
    pallas_call x2, Pallas kernels, scan_backward(): pl.pallas_call(functools.partial(backward_kernel, hl=hl), grid_spec=grid_...  54.1 us
    pallas_call x2, Pallas kernels, back_project(): pl.pallas_call(functools.partial(back_kernel, n=n, bits=bits), grid=(n,),...  35.3 us
    pallas_call x1, Pallas kernels, scan_forward(): pl.pallas_call(functools.partial(forward_kernel, hl=hl), grid_spec=grid_s...  32.8 us
    pallas_call x2, Pallas kernels, in_project(): pl.pallas_call(functools.partial(in_kernel, count=count), grid_spec=pltpu...  26 us
    pallas_call x1, Pallas kernels, out_project(): pl.pallas_call(functools.partial(out_kernel, n=n, bits=bits), grid=(token...  23.8 us
  transfers between devices with their start and end apart: 56, of which 22 were waited for; matrix products, arithmetic and copies ran while one was open for 21% of the time, Pallas kernels for 33%

profile of v7, /device:TPU:0, one launch (start us, length us, event | category | flops | bytes accessed | tf_op | source)
XLA Modules:
  0.0 516.5 jit_solution(3760809753324945407)
XLA Ops:
  7.2 1.7 convert_element_type.242
  10.8 3.0 collective-permute-start.6
  19.3 4.4 collective-permute-done.7.refs_1_
  33.8 17.9 %collective-permute-done.4.refs_4_.refs_2_ = bf16[256,2048]{1,0:T(8,128)(2,1)S(1)} collective-permute-done((bf16[256,2048]{1,0:T(8,128)(2,1)S(1)}, bf16[256,2048]{1,0:T(8,128)(2,1)S(1)}, u32[]{:S(2)}, u32[]{:S(2)}) %collective-permute-start.4) | collective-permute-done | bytes 1048608 | tf_op jit(solution)/shard_map/ppermute | solution.py:784
  57.5 5.5 %collective-permute-done.10 = bf16[64,2048]{1,0:T(8,128)(2,1)S(1)} collective-permute-done((bf16[64,2048]{1,0:T(8,128)(2,1)S(1)}, bf16[64,2048]{1,0:T(8,128)(2,1)S(1)}, u32[]{:S(2)}, u32[]{:S(2)}) %collective-permute-start.10) | collective-permute-done | bytes 262176 | tf_op jit(solution)/shard_map/ppermute | solution.py:784
  63.1 3.7 collective-permute-done.9
  69.9 1.8 collective-permute-start
  74.4 17.8 %collective-permute-done.refs_3_ = bf16[256,2048]{1,0:T(8,128)(2,1)} collective-permute-done((bf16[256,2048]{1,0:T(8,128)(2,1)S(1)}, bf16[256,2048]{1,0:T(8,128)(2,1)}, u32[]{:S(2)}, u32[]{:S(2)}) %collective-permute-start) | collective-permute-done | bytes 1048608 | tf_op jit(solution)/shard_map/ppermute | solution.py:784
  92.2 3.7 collective-permute-done.2.refs_6_
  96.8 3.2 slice_bitcast_fusion.2
  102.9 16.9 %in_project.2 = (bf16[2048,1408]{1,0:T(8,128)(2,1)}, bf16[2048,2048]{1,0:T(8,128)(2,1)}) custom-call(s32[6]{0:T(128)} %constant.29.clone.refs_0_, bf16[256,2048]{1,0:T(8,128)(2,1)} %get-tuple-element.176.refs_3_.refs_1_, bf16[256,2048]{1,0:T(8,128)(2,1)} %get-tuple-element.175.refs_4_.refs_2_, bf16[256,2048]{1,0:T(8,128)(2,1)} %collective-permute-done.refs_3_, ...), custom_call_target="tpu_custom_call" | custom-call | tf_op jit(solution)/shard_map/in_project/pallas_call | solution.py:549
  127.8 9.1 %in_project.3 = (bf16[2048,1408]{1,0:T(8,128)(2,1)}, bf16[2048,2048]{1,0:T(8,128)(2,1)}) custom-call(s32[2]{0:T(128)} %constant.30.clone.refs_0_, bf16[256,2048]{1,0:T(8,128)(2,1)} %get-tuple-element.89.refs_1_.refs_2_, bf16[256,2048]{1,0:T(8,128)(2,1)} %get-tuple-element.90.refs_2_.refs_3_, ...), custom_call_target="tpu_custom_call", output_to_operand_aliasing={{0}: (4, {}), {1}: (5, {})} | custom-call | tf_op jit(solution)/shard_map/in_project/pallas_call | solution.py:549
  137.6 32.8 %scan_forward.1 = (bf16[2048,1024]{1,0:T(8,128)(2,1)}, bf16[8,1024,128]{2,1,0:T(8,128)(2,1)}, bf16[2048,1280]{1,0:T(8,128)(2,1)}, bf16[2048,1280]{1,0:T(8,128)(2,1)}) custom-call(s32[1]{0:T(128)} %bitcast.19.place, bf16[2048,1408]{1,0:T(8,128)(2,1)} %get-tuple-element.93.proj.refs_1_, f32[8,1280]{1,0:T(8,128)} %fusion.26.refs_10_.conv_w, ...), custom_call_target="tpu_custom_call" | custom-call | tf_op jit(solution)/shard_map/scan_forward/pallas_call | solution.py:374
  171.4 2.0 collective-permute-start.17
  174.6 13.8 %convolution_convert_fusion.1.refs_8_.z_in = bf16[2048,1024]{1,0:T(8,128)(2,1)} fusion(bf16[2048,2048]{1,0:T(8,128)(2,1)} %get-tuple-element.92, bf16[2048,1024]{1,0:T(8,128)(2,1)} %after.26.w_z), kind=kOutput, calls=%fused_computation.20 | convolution fusion | flops 8592031744 | bytes 16777216 | tf_op jit(solution)/shard_map/dot_general | solution.py:34
  193.1 19.2 %gate_forward.1 = (bf16[2048,1024]{1,0:T(8,128)(2,1)}, bf16[2048,2048]{1,0:T(8,128)(2,1)}, f32[16,256]{1,0:T(8,128)}) custom-call(bf16[256,2048]{1,0:T(8,128)(2,1)} %get-tuple-element.95.refs_0_, bf16[256,2048]{1,0:T(8,128)(2,1)} %after.28.refs_1_, bf16[256,2048]{1,0:T(8,128)(2,1)} %get-tuple-element.96.refs_2_, ...), custom_call_target="tpu_custom_call" | custom-call | tf_op jit(solution)/shard_map/gate_forward/pallas_call | solution.py:589
  221.5 23.8 %out_project.1 = (bf16[2048,1024]{1,0:T(8,128)(2,1)}, bf16[2048,1024]{1,0:T(8,128)(2,1)}, bf16[2048,1024]{1,0:T(8,128)(2,1)}, f32[8,1024]{1,0:T(8,128)}, bf16[2,...) custom-call(bf16[2048,1024]{1,0:T(8,128)(2,1)} %convolution_convert_, ...), custom_call_target="tpu_custom_call" | custom-call | tf_op jit(solution)/shard_map/out_project/pallas_call | solution.py:637
  245.3 14.0 %convolution_convert_fusion.2.refs_1_ = bf16[2048,1024]{1,0:T(8,128)(2,1)} fusion(bf16[2048,2048]{1,0:T(8,128)(2,1)} %get-tuple-element.92, bf16[2048,1024]{1,0:T(8,128)(2,1)} %get-tuple-element.106.dz), kind=kOutput, calls=%fused_computation.21 | convolution fusion | flops 8592031744 | bytes 16777216 | tf_op jit(solution)/shard_map/dot_general | solution.py:34
  259.4 14.0 %convolution_convert_fusion.3.refs_0_ = bf16[2048,1024]{1,0:T(8,128)(2,1)} fusion(bf16[2048,2048]{1,0:T(8,128)(2,1)} %get-tuple-element.111, bf16[2048,1024]{1,0:T(8,128)(2,1)} %get-tuple-element.112), kind=kOutput, calls=%fused_computation.22 | convolution fusion | flops 8592031744 | bytes 16777216 | tf_op jit(solution)/shard_map/dot_general | solution.py:34
  275.1 27.0 %scan_backward.2 = (bf16[1024,1408]{1,0:T(8,128)(2,1)}, bf16[1024,1280]{1,0:T(8,128)(2,1)}, f32[16,128]{1,0:T(8,128)}, f32[8,1024]{1,0:T(8,128)}) custom-call(s32[1]{0:T(128)} %bitcast.19.place, bf16[2048,1408]{1,0:T(8,128)(2,1)} %get-tuple-element.93.proj.refs_1_, f32[8,1280]{1,0:T(8,128)} %fusion.26.refs_10_.conv_w, f32[8,1024]{1,0:T(8,128)} %broadcast_in_dim.30.skip, ...), custom_call_target="tpu_custom_call" | custom-call | tf_op jit(solution)/shard_map/scan_backward/pallas_call | solution.py:436
  302.1 17.4 %back_project.2 = (bf16[1,2,128,2048]{3,2,1,0:T(8,128)(2,1)}, bf16[1,2,128,2048]{3,2,1,0:T(8,128)(2,1)}, bf16[1,2,128,2048]{3,2,1,0:T(8,128)(2,1)}, bf16[1,2,128,2048]{3,2,1,0:T(8,128)(2,1)}) custom-call(bf16[2048,1024]{1,0:T(8,128)(2,1)} %get-tuple-element.106.dz, bf16[1024,1408]{1,0:T(8,128)(2,1)} %get-tuple-element.113.px, bf16[2048,1024]{1,0:T(8,128)(2,1)} %after.26.w_z, ...), custom_call_target="tpu_custom_call" | custom-call | tf_op jit(solution)/shard_map/back_project/pallas_call | solution.py:659
  322.1 2.1 add_convert_fusion.3.refs_3_
  325.5 1.6 add_convert_fusion.4.refs_2_
  328.1 27.1 %scan_backward.3 = (bf16[1024,1408]{1,0:T(8,128)(2,1)}, bf16[1024,1280]{1,0:T(8,128)(2,1)}, f32[16,128]{1,0:T(8,128)}, f32[8,1024]{1,0:T(8,128)}) custom-call(s32[1]{0:T(128)} %bitcast.19.place, bf16[2048,1408]{1,0:T(8,128)(2,1)} %get-tuple-element.93.proj.refs_1_, f32[8,1280]{1,0:T(8,128)} %fusion.26.refs_10_.conv_w, f32[8,1024]{1,0:T(8,128)} %broadcast_in_dim.30.skip, ...), custom_call_target="tpu_custom_call" | custom-call | tf_op jit(solution)/shard_map/scan_backward/pallas_call | solution.py:436
  355.2 2.7 collective-permute-done.24.refs_4_.refs_1_
  358.9 19.2 %convolution_convert_fusion.refs_2_.refs_1_ = bf16[2048,1408]{1,0:T(8,128)(2,1)} fusion(bf16[2048,2048]{1,0:T(8,128)(2,1)} %get-tuple-element.92, bf16[1024,1408]{1,0:T(8,128)(2,1)} %after.33.refs_0_, bf16[1024,1408]{1,0:T(8,128)(2,1)} %get-tuple-element.113.px), kind=kOutput, calls=%fused_computation.5 | convolution fusion | flops 11825577984 | bytes 19922944 | tf_op jit(solution)/shard_map/dot_general | solution.py:34
  382.8 1.7 collective-permute-start.30
  391.1 17.9 %back_project.3 = (bf16[1,2,128,2048]{3,2,1,0:T(8,128)(2,1)}, bf16[1,2,128,2048]{3,2,1,0:T(8,128)(2,1)}, bf16[1,2,128,2048]{3,2,1,0:T(8,128)(2,1)}, bf16[1,2,128,2048]{3,2,1,0:T(8,128)(2,1)}) custom-call(bf16[2048,1024]{1,0:T(8,128)(2,1)} %get-tuple-element.106.dz, bf16[1024,1408]{1,0:T(8,128)(2,1)} %after.35.px, bf16[2048,1024]{1,0:T(8,128)(2,1)} %after.26.w_z, ...), custom_call_target="tpu_custom_call" | custom-call | tf_op jit(solution)/shard_map/back_project/pallas_call | solution.py:659
  414.9 6.9 %tap_gradients.3.conv_1 = f32[40,1280]{1,0:T(8,128)} custom-call(s32[1]{0:T(128)} %bitcast.19.place, bf16[2048,1408]{1,0:T(8,128)(2,1)} %get-tuple-element.93.proj.refs_1_, f32[2048,8]{1,0:T(8,128)} %copy.118.refs_8_.aux, bf16[1024,1280]{1,0:T(8,128)(2,1)} %get-tuple-element.130.dco), custom_call_target="tpu_custom_call" | custom-call | tf_op jit(solution)/shard_map/tap_gradients/pallas_call | solution.py:464
  421.7 6.9 %tap_gradients.2.conv_0 = f32[40,1280]{1,0:T(8,128)} custom-call(s32[1]{0:T(128)} %bitcast.19.place, bf16[2048,1408]{1,0:T(8,128)(2,1)} %get-tuple-element.93.proj.refs_1_, f32[2048,8]{1,0:T(8,128)} %copy.118.refs_8_.aux, bf16[1024,1280]{1,0:T(8,128)(2,1)} %get-tuple-element.129.dco), custom_call_target="tpu_custom_call" | custom-call | tf_op jit(solution)/shard_map/tap_gradients/pallas_call | solution.py:464
  428.7 1.8 small_gradients.1.refs_0_
  434.1 2.1 fusion.15
  436.3 1.9 fusion.16
  444.3 2.1 collective-permute-start.38
  446.4 2.2 fusion.6.refs_2_
  449.8 2.2 broadcast_select_fusion.36
  455.5 3.2 fusion.18
  459.9 3.3 collective-permute-done.40.refs_3_.refs_6_.refs_4_
  464.6 1.7 collective-permute-start.49
  466.2 5.5 %shards.1 = (f32[64,8512]{1,0:T(8,128)}, f32[64,4096]{1,0:T(8,128)}, f32[24,128]{1,0:T(8,128)}) custom-call(s32[2]{0:T(128)} %pad_add_fusion.spot, bf16[64,2048]{1,0:T(8,128)(2,1)} %get-tuple-element.193.refs_0_, bf16[64,2048]{1,0:T(8,128)(2,1)} %copy-done.56, bf16[64,2048]{1,0:T(8,128)(2,1)} %copy-done.57, bf16[64,2048]{1,0:T(8,128)(2,1)} %copy-done.58, ...), custom_call_target="tpu_custom_call" | custom-call | tf_op jit(solution)/shard_map/shards/pallas_call | solution.py:716
  472.2 2.3 fusion.20
  477.1 3.6 fusion.11
  481.3 2.2 place_small.1
  487.0 1.9 collective-permute-done.45
  488.9 2.1 collective-permute-start.46
  491.4 2.1 collective-permute-done.46
  497.4 3.9 multiply_add_fusion.2
  502.1 5.5 %multiply_add_fusion = (f32[64,8512]{1,0:T(8,128)}, f32[64,8512]{1,0:T(8,128)}, f32[64,8512]{1,0:T(8,128)}) fusion(f32[64,8512]{1,0:T(8,128)S(1)} %copy-done.2, f32[64,8512]{1,0:T(8,128)} %get-tuple-element.153, f32[]{:T(128)S(6)} %min.3, f32[64,8512]{1,0:T(8,128)S(1)} %copy-done.31, f32[64,8512]{1,0:T(8,128)S(1)} %copy-done.32), kind=kLoop, calls=%fused_computation.25 | loop fusion | flops 8716288 | bytes 15253508 | tf_op jit(solution)/shard_map/add | solution.py:1044
  (401 shorter events, 109.5 us)
Async XLA Ops:
  7.2 92.8 %all-gather.4.cloned.1.call-start = ((), (), s32[]{:S(2)}) async-start(), calls=%async_computation.3 | async-start | bytes 6488064 | tf_op jit(solution)/shard_map/all_gather | solution.py:940
  10.8 8.5 %collective-permute-start.6 = (bf16[64,1408]{1,0:T(8,128)(2,1)S(1)}, bf16[64,1408]{1,0:T(8,128)(2,1)S(1)}, u32[]{:S(2)}, u32[]{:S(2)}) collective-permute-start(bf16[64,1408]{1,0:T(8,128)(2,1)S(1)} %get-tuple-element.212), channel_id=1, source_target_pairs={{0,1},{1,0},{2,3},{3,2},{4,5},{5,4},{6,7},{7,6},{8,9},{9,8},{10,11... | collective-permute-start | bytes 540680 | tf_op jit(solution)/shard_map/ppermute | solution.py:784
  13.8 9.9 %collective-permute-start.7 = (bf16[64,1408]{1,0:T(8,128)(2,1)S(1)}, bf16[64,1408]{1,0:T(8,128)(2,1)S(1)}, u32[]{:S(2)}, u32[]{:S(2)}) collective-permute-start(bf16[64,1408]{1,0:T(8,128)(2,1)S(1)} %get-tuple-element.211), channel_id=1, source_target_pairs={{0,2},{1,3},{2,0},{3,1},{4,6},{5,7},{6,4},{7,5},{8,10},{9,11},{10,... | collective-permute-start | bytes 540680 | tf_op jit(solution)/shard_map/ppermute | solution.py:784
  15.3 8.4 %collective-permute-start.8 = (bf16[64,1408]{1,0:T(8,128)(2,1)S(1)}, bf16[64,1408]{1,0:T(8,128)(2,1)S(1)}, u32[]{:S(2)}, u32[]{:S(2)}) collective-permute-start(bf16[64,1408]{1,0:T(8,128)(2,1)S(1)} %get-tuple-element.210), channel_id=1, source_target_pairs={{0,3},{1,2},{2,1},{3,0},{4,7},{5,6},{6,5},{7,4},{8,11},{9,10},{10,... | collective-permute-start | bytes 540680 | tf_op jit(solution)/shard_map/ppermute | solution.py:784
  27.9 142.6 %all-gather.6.cloned.1.call-start = ((), (), s32[]{:S(2)}) async-start(), calls=%async_computation.4 | async-start | bytes 4718592 | tf_op jit(solution)/shard_map/all_gather | solution.py:945
  27.9 23.8 %collective-permute-start.4 = (bf16[256,2048]{1,0:T(8,128)(2,1)S(1)}, bf16[256,2048]{1,0:T(8,128)(2,1)S(1)}, u32[]{:S(2)}, u32[]{:S(2)}) collective-permute-start(bf16[256,2048]{1,0:T(8,128)(2,1)S(1)} %copy-done.9), channel_id=1, source_target_pairs={{0,2},{1,3},{2,0},{3,1},{4,6},{5,7},{6,4},{7,5},{8,10},{9,11},{10,... | collective-permute-start | bytes 3145736 | tf_op jit(solution)/shard_map/ppermute | solution.py:784
  29.5 22.6 %collective-permute-start.5 = (bf16[256,2048]{1,0:T(8,128)(2,1)S(1)}, bf16[256,2048]{1,0:T(8,128)(2,1)}, u32[]{:S(2)}, u32[]{:S(2)}) collective-permute-start(bf16[256,2048]{1,0:T(8,128)(2,1)S(1)} %copy-done.8), channel_id=1, source_target_pairs={{0,1},{1,0},{2,3},{3,2},{4,5},{5,4},{6,7},{7,6},{8,9},{9,8},{10,11... | collective-permute-start | bytes 3145736 | tf_op jit(solution)/shard_map/ppermute | solution.py:784
  53.9 9.0 %collective-permute-start.10 = (bf16[64,2048]{1,0:T(8,128)(2,1)S(1)}, bf16[64,2048]{1,0:T(8,128)(2,1)S(1)}, u32[]{:S(2)}, u32[]{:S(2)}) collective-permute-start(bf16[64,2048]{1,0:T(8,128)(2,1)S(1)} %get-tuple-element.200), channel_id=1, source_target_pairs={{0,2},{1,3},{2,0},{3,1},{4,6},{5,7},{6,4},{7,5},{8,10},{9,11},{10,... | collective-permute-start | bytes 786440 | tf_op jit(solution)/shard_map/ppermute | solution.py:784
  54.8 8.3 %collective-permute-start.11 = (bf16[64,2048]{1,0:T(8,128)(2,1)S(1)}, bf16[64,2048]{1,0:T(8,128)(2,1)S(1)}, u32[]{:S(2)}, u32[]{:S(2)}) collective-permute-start(bf16[64,2048]{1,0:T(8,128)(2,1)S(1)} %get-tuple-element.199), channel_id=1, source_target_pairs={{0,1},{1,0},{2,3},{3,2},{4,5},{5,4},{6,7},{7,6},{8,9},{9,8},{10,11... | collective-permute-start | bytes 786440 | tf_op jit(solution)/shard_map/ppermute | solution.py:784
  56.3 10.6 %collective-permute-start.9 = (bf16[64,2048]{1,0:T(8,128)(2,1)S(1)}, bf16[64,2048]{1,0:T(8,128)(2,1)S(1)}, u32[]{:S(2)}, u32[]{:S(2)}) collective-permute-start(bf16[64,2048]{1,0:T(8,128)(2,1)S(1)} %get-tuple-element.201), channel_id=1, source_target_pairs={{0,3},{1,2},{2,1},{3,0},{4,7},{5,6},{6,5},{7,4},{8,11},{9,10},{10,... | collective-permute-start | bytes 786440 | tf_op jit(solution)/shard_map/ppermute | solution.py:784
  69.1 123.4 %all-gather.8.cloned.1.call-start = ((), (), s32[]{:S(2)}) async-start(), calls=%async_computation.5 | async-start | bytes 4718592 | tf_op jit(solution)/shard_map/all_gather | solution.py:946
  69.8 314.7 %reduce-scatter.6.cloned.1.call-start = ((), (), s32[]{:S(2)}) async-start(), calls=%async_computation.7 | async-start | bytes 4718592 | tf_op jit(solution)/shard_map/reduce_scatter | solution.py:975
  69.9 22.3 %collective-permute-start = (bf16[256,2048]{1,0:T(8,128)(2,1)S(1)}, bf16[256,2048]{1,0:T(8,128)(2,1)}, u32[]{:S(2)}, u32[]{:S(2)}) collective-permute-start(bf16[256,2048]{1,0:T(8,128)(2,1)S(1)} %copy-done.9), channel_id=1, source_target_pairs={{0,1},{1,0},{2,3},{3,2},{4,5},{5,4},{6,7},{7,6},{8,9},{9,8},{10,11... | collective-permute-start | bytes 3145736 | tf_op jit(solution)/shard_map/ppermute | solution.py:784
  71.6 24.3 %collective-permute-start.2 = (bf16[256,2048]{1,0:T(8,128)(2,1)S(1)}, bf16[256,2048]{1,0:T(8,128)(2,1)}, u32[]{:S(2)}, u32[]{:S(2)}) collective-permute-start(bf16[256,2048]{1,0:T(8,128)(2,1)S(1)} %copy-done.8), channel_id=1, source_target_pairs={{0,2},{1,3},{2,0},{3,1},{4,6},{5,7},{6,4},{7,5},{8,10},{9,11},{10,... | collective-permute-start | bytes 3145736 | tf_op jit(solution)/shard_map/ppermute | solution.py:784
  92.2 27.7 %collective-permute-start.1 = (bf16[256,2048]{1,0:T(8,128)(2,1)}, bf16[256,2048]{1,0:T(8,128)(2,1)S(1)}, u32[]{:S(2)}, u32[]{:S(2)}) collective-permute-start(bf16[256,2048]{1,0:T(8,128)(2,1)} %collective-permute-done.refs_3_), channel_id=1, source_target_pairs={{0,2},{1,3},{2,0},{3,1},{4,6},{5,7},{6,4},{7,5},{8,10},{9,11},{10,... | collective-permute-start | bytes 3145736 | tf_op jit(solution)/shard_map/ppermute | solution.py:784
  96.0 23.9 %collective-permute-start.3 = (bf16[256,2048]{1,0:T(8,128)(2,1)}, bf16[256,2048]{1,0:T(8,128)(2,1)S(1)}, u32[]{:S(2)}, u32[]{:S(2)}) collective-permute-start(bf16[256,2048]{1,0:T(8,128)(2,1)} %collective-permute-done.2.refs_6_), channel_id=1, source_target_pairs={{0,1},{1,0},{2,3},{3,2},{4,5},{5,4},{6,7},{7,6},{8,9},{9,8},{10,11... | collective-permute-start | bytes 3145736 | tf_op jit(solution)/shard_map/ppermute | solution.py:784
  121.2 49.3 %collective-permute-start.16 = (bf16[256,2048]{1,0:T(8,128)(2,1)}, bf16[256,2048]{1,0:T(8,128)(2,1)S(1)}, u32[]{:S(2)}, u32[]{:S(2)}) collective-permute-start(bf16[256,2048]{1,0:T(8,128)(2,1)} %get-tuple-element.98.refs_4_), channel_id=1, source_target_pairs={{0,2},{1,3},{2,0},{3,1},{4,6},{5,7},{6,4},{7,5},{8,10},{9,11},{10,... | collective-permute-start | bytes 3145736 | tf_op jit(solution)/shard_map/ppermute | solution.py:784
  122.0 51.4 %collective-permute-start.12 = (bf16[256,2048]{1,0:T(8,128)(2,1)}, bf16[256,2048]{1,0:T(8,128)(2,1)S(1)}, u32[]{:S(2)}, u32[]{:S(2)}) collective-permute-start(bf16[256,2048]{1,0:T(8,128)(2,1)} %get-tuple-element.95.refs_0_), channel_id=1, source_target_pairs={{0,1},{1,0},{2,3},{3,2},{4,5},{5,4},{6,7},{7,6},{8,9},{9,8},{10,11... | collective-permute-start | bytes 3145736 | tf_op jit(solution)/shard_map/ppermute | solution.py:784
  126.0 62.4 %collective-permute-start.15 = (bf16[256,2048]{1,0:T(8,128)(2,1)}, bf16[256,2048]{1,0:T(8,128)(2,1)}, u32[]{:S(2)}, u32[]{:S(2)}) collective-permute-start(bf16[256,2048]{1,0:T(8,128)(2,1)} %get-tuple-element.98.refs_4_), channel_id=1, source_target_pairs={{0,1},{1,0},{2,3},{3,2},{4,5},{5,4},{6,7},{7,6},{8,9},{9,8},{10,11... | collective-permute-start | bytes 3145736 | tf_op jit(solution)/shard_map/ppermute | solution.py:784
  126.5 63.8 %collective-permute-start.13 = (bf16[256,2048]{1,0:T(8,128)(2,1)}, bf16[256,2048]{1,0:T(8,128)(2,1)S(1)}, u32[]{:S(2)}, u32[]{:S(2)}) collective-permute-start(bf16[256,2048]{1,0:T(8,128)(2,1)} %get-tuple-element.95.refs_0_), channel_id=1, source_target_pairs={{0,2},{1,3},{2,0},{3,1},{4,6},{5,7},{6,4},{7,5},{8,10},{9,11},{10,... | collective-permute-start | bytes 3145736 | tf_op jit(solution)/shard_map/ppermute | solution.py:784
  171.4 18.0 %collective-permute-start.17 = (bf16[256,2048]{1,0:T(8,128)(2,1)}, bf16[256,2048]{1,0:T(8,128)(2,1)S(1)}, u32[]{:S(2)}, u32[]{:S(2)}) collective-permute-start(bf16[256,2048]{1,0:T(8,128)(2,1)} %after.30.refs_6_), channel_id=1, source_target_pairs={{0,1},{1,0},{2,3},{3,2},{4,5},{5,4},{6,7},{7,6},{8,9},{9,8},{10,11... | collective-permute-start | bytes 3145736 | tf_op jit(solution)/shard_map/ppermute | solution.py:784
  174.4 17.1 %collective-permute-start.14 = (bf16[256,2048]{1,0:T(8,128)(2,1)}, bf16[256,2048]{1,0:T(8,128)(2,1)S(1)}, u32[]{:S(2)}, u32[]{:S(2)}) collective-permute-start(bf16[256,2048]{1,0:T(8,128)(2,1)} %after.28.refs_1_), channel_id=1, source_target_pairs={{0,2},{1,3},{2,0},{3,1},{4,6},{5,7},{6,4},{7,5},{8,10},{9,11},{10,... | collective-permute-start | bytes 3145736 | tf_op jit(solution)/shard_map/ppermute | solution.py:784
  259.3 125.2 %reduce-scatter.4.cloned.1.call-start = ((), (), s32[]{:S(2)}) async-start(), calls=%async_computation.6 | async-start | bytes 4718592 | tf_op jit(solution)/shard_map/reduce_scatter | solution.py:975
  273.3 176.4 %reduce-scatter.8.cloned.1.call-start = ((), (), s32[]{:S(2)}) async-start(), calls=%async_computation.8 | async-start | bytes 6488064 | tf_op jit(solution)/shard_map/reduce_scatter | solution.py:975
  273.4 48.7 %collective-permute-start.21 = (bf16[2,2,128,2048]{3,2,1,0:T(8,128)(2,1)}, bf16[2,2,128,2048]{3,2,1,0:T(8,128)(2,1)}, u32[]{:S(2)}, u32[]{:S(2)}) collective-permute-start(bf16[2,2,128,2048]{3,2,1,0:T(8,128)(2,1)} %get-tuple-element.104), channel_id=1, source_target_pairs={{0,1},{1,0},{2,3},{3,2},{4,5},{5,4},{6,7},{7,6},{8,9},{9,8},{10,11... | collective-permute-start | bytes 6291464 | tf_op jit(solution)/shard_map/ppermute | solution.py:784
  274.7 47.4 %collective-permute-start.22 = (bf16[2,2,128,2048]{3,2,1,0:T(8,128)(2,1)}, bf16[2,2,128,2048]{3,2,1,0:T(8,128)(2,1)}, u32[]{:S(2)}, u32[]{:S(2)}) collective-permute-start(bf16[2,2,128,2048]{3,2,1,0:T(8,128)(2,1)} %get-tuple-element.105), channel_id=1, source_target_pairs={{0,2},{1,3},{2,0},{3,1},{4,6},{5,7},{6,4},{7,5},{8,10},{9,11},{10,... | collective-permute-start | bytes 6291464 | tf_op jit(solution)/shard_map/ppermute | solution.py:784
  319.6 35.6 %collective-permute-start.25 = (bf16[1,2,128,2048]{3,2,1,0:T(8,128)(2,1)}, bf16[1,2,128,2048]{3,2,1,0:T(8,128)(2,1)S(1)}, u32[]{:S(2)}, u32[]{:S(2)}) collective-permute-start(bf16[1,2,128,2048]{3,2,1,0:T(8,128)(2,1)} %get-tuple-element.114.refs_2_.refs_0_), channel_id=1, source_target_pairs={{0,1},{1,0},{2,3},{3,2},{4,5},{5,4},{6,7},{7,6},{8,9},{9,8},{10,11... | collective-permute-start | bytes 3145736 | tf_op jit(solution)/shard_map/ppermute | solution.py:784
  320.9 34.3 %collective-permute-start.26 = (bf16[1,2,128,2048]{3,2,1,0:T(8,128)(2,1)}, bf16[1,2,128,2048]{3,2,1,0:T(8,128)(2,1)S(1)}, u32[]{:S(2)}, u32[]{:S(2)}) collective-permute-start(bf16[1,2,128,2048]{3,2,1,0:T(8,128)(2,1)} %get-tuple-element.119.refs_1_), channel_id=1, source_target_pairs={{0,2},{1,3},{2,0},{3,1},{4,6},{5,7},{6,4},{7,5},{8,10},{9,11},{10,... | collective-permute-start | bytes 3145736 | tf_op jit(solution)/shard_map/ppermute | solution.py:784
  324.2 33.8 %collective-permute-start.24 = (bf16[2,1,128,2048]{3,2,1,0:T(8,128)(2,1)S(1)}, bf16[2,1,128,2048]{3,2,1,0:T(8,128)(2,1)S(1)}, u32[]{:S(2)}, u32[]{:S(2)}) collective-permute-start(bf16[2,1,128,2048]{3,2,1,0:T(8,128)(2,1)S(1)} %add_convert_fusion.3.refs_3_), channel_id=1, source_target_pairs={{0,1},{1,0},{2,3},{3,2},{4,5},{5,4},{6,7},{7,6},{8,9},{9,8},{10,11... | collective-permute-start | bytes 3145736 | tf_op jit(solution)/shard_map/ppermute | solution.py:784
  327.1 31.7 %collective-permute-start.23 = (bf16[2,1,128,2048]{3,2,1,0:T(8,128)(2,1)S(1)}, bf16[2,1,128,2048]{3,2,1,0:T(8,128)(2,1)}, u32[]{:S(2)}, u32[]{:S(2)}) collective-permute-start(bf16[2,1,128,2048]{3,2,1,0:T(8,128)(2,1)S(1)} %add_convert_fusion.4.refs_2_), channel_id=1, source_target_pairs={{0,2},{1,3},{2,0},{3,1},{4,6},{5,7},{6,4},{7,5},{8,10},{9,11},{10,... | collective-permute-start | bytes 3145736 | tf_op jit(solution)/shard_map/ppermute | solution.py:784
  380.5 28.5 %collective-permute-start.31 = (bf16[1,1,128,2048]{3,2,1,0:T(8,128)(2,1)S(1)}, bf16[1,1,128,2048]{3,2,1,0:T(8,128)(2,1)S(1)}, u32[]{:S(2)}, u32[]{:S(2)}) collective-permute-start(bf16[1,1,128,2048]{3,2,1,0:T(8,128)(2,1)S(1)} %add_convert_fusion.16.refs_3_), channel_id=1, source_target_pairs={{0,1},{1,0},{2,3},{3,2},{4,5},{5,4},{6,7},{7,6},{8,9},{9,8},{10,11... | collective-permute-start | bytes 1572872 | tf_op jit(solution)/shard_map/ppermute | solution.py:784
  382.8 27.0 %collective-permute-start.30 = (bf16[1,1,128,2048]{3,2,1,0:T(8,128)(2,1)S(1)}, bf16[1,1,128,2048]{3,2,1,0:T(8,128)(2,1)S(1)}, u32[]{:S(2)}, u32[]{:S(2)}) collective-permute-start(bf16[1,1,128,2048]{3,2,1,0:T(8,128)(2,1)S(1)} %add_convert_fusion.17.refs_2_), channel_id=1, source_target_pairs={{0,2},{1,3},{2,0},{3,1},{4,6},{5,7},{6,4},{7,5},{8,10},{9,11},{10,... | collective-permute-start | bytes 1572872 | tf_op jit(solution)/shard_map/ppermute | solution.py:784
  387.6 23.0 %collective-permute-start.27 = (bf16[64,2048]{1,0:T(8,128)(2,1)}, bf16[64,2048]{1,0:T(8,128)(2,1)S(1)}, u32[]{:S(2)}, u32[]{:S(2)}) collective-permute-start(bf16[64,2048]{1,0:T(8,128)(2,1)} %get-tuple-element.194), channel_id=1, source_target_pairs={{0,1},{1,0},{2,3},{3,2},{4,5},{5,4},{6,7},{7,6},{8,9},{9,8},{10,11... | collective-permute-start | bytes 786440 | tf_op jit(solution)/shard_map/ppermute | solution.py:784
  388.7 21.9 %collective-permute-start.28 = (bf16[64,2048]{1,0:T(8,128)(2,1)S(1)}, bf16[64,2048]{1,0:T(8,128)(2,1)S(1)}, u32[]{:S(2)}, u32[]{:S(2)}) collective-permute-start(bf16[64,2048]{1,0:T(8,128)(2,1)S(1)} %get-tuple-element.195), channel_id=1, source_target_pairs={{0,2},{1,3},{2,0},{3,1},{4,6},{5,7},{6,4},{7,5},{8,10},{9,11},{10,... | collective-permute-start | bytes 786440 | tf_op jit(solution)/shard_map/ppermute | solution.py:784
  389.5 21.2 %collective-permute-start.29 = (bf16[64,2048]{1,0:T(8,128)(2,1)S(1)}, bf16[64,2048]{1,0:T(8,128)(2,1)S(1)}, u32[]{:S(2)}, u32[]{:S(2)}) collective-permute-start(bf16[64,2048]{1,0:T(8,128)(2,1)S(1)} %get-tuple-element.196), channel_id=1, source_target_pairs={{0,3},{1,2},{2,1},{3,0},{4,7},{5,6},{6,5},{7,4},{8,11},{9,10},{10,... | collective-permute-start | bytes 786440 | tf_op jit(solution)/shard_map/ppermute | solution.py:784
  411.5 18.9 %collective-permute-start.32 = (bf16[1,2,128,2048]{3,2,1,0:T(8,128)(2,1)}, bf16[1,2,128,2048]{3,2,1,0:T(8,128)(2,1)S(1)}, u32[]{:S(2)}, u32[]{:S(2)}) collective-permute-start(bf16[1,2,128,2048]{3,2,1,0:T(8,128)(2,1)} %get-tuple-element.139), channel_id=1, source_target_pairs={{0,1},{1,0},{2,3},{3,2},{4,5},{5,4},{6,7},{7,6},{8,9},{9,8},{10,11... | collective-permute-start | bytes 3145736 | tf_op jit(solution)/shard_map/ppermute | solution.py:784
  412.7 17.7 %collective-permute-start.33 = (bf16[1,2,128,2048]{3,2,1,0:T(8,128)(2,1)}, bf16[1,2,128,2048]{3,2,1,0:T(8,128)(2,1)S(1)}, u32[]{:S(2)}, u32[]{:S(2)}) collective-permute-start(bf16[1,2,128,2048]{3,2,1,0:T(8,128)(2,1)} %get-tuple-element.140), channel_id=1, source_target_pairs={{0,2},{1,3},{2,0},{3,1},{4,6},{5,7},{6,4},{7,5},{8,10},{9,11},{10,... | collective-permute-start | bytes 3145736 | tf_op jit(solution)/shard_map/ppermute | solution.py:784
  432.5 7.6 %collective-permute-start.36 = (f32[8,1280]{1,0:T(8,128)}, f32[8,1280]{1,0:T(8,128)S(1)}, u32[]{:S(2)}, u32[]{:S(2)}) collective-permute-start(f32[8,1280]{1,0:T(8,128)} %after.39.refs_2_), channel_id=1, source_target_pairs={{0,4},{4,0},{8,12},{12,8},{16,20},{20,16},{24,28},{28,24},{1,5},{5... | collective-permute-start | bytes 122888 | tf_op jit(solution)/shard_map/ppermute | solution.py:784
  439.2 32.5 %collective-permute-start.35 = (bf16[1,1,128,2048]{3,2,1,0:T(8,128)(2,1)}, bf16[1,1,128,2048]{3,2,1,0:T(8,128)(2,1)}, u32[]{:S(2)}, u32[]{:S(2)}) collective-permute-start(bf16[1,1,128,2048]{3,2,1,0:T(8,128)(2,1)} %add_convert_fusion.9.refs_4_), channel_id=1, source_target_pairs={{0,1},{1,0},{2,3},{3,2},{4,5},{5,4},{6,7},{7,6},{8,9},{9,8},{10,11... | collective-permute-start | bytes 1572872 | tf_op jit(solution)/shard_map/ppermute | solution.py:784
  442.7 29.5 %collective-permute-start.34 = (bf16[1,1,128,2048]{3,2,1,0:T(8,128)(2,1)}, bf16[1,1,128,2048]{3,2,1,0:T(8,128)(2,1)}, u32[]{:S(2)}, u32[]{:S(2)}) collective-permute-start(bf16[1,1,128,2048]{3,2,1,0:T(8,128)(2,1)} %add_convert_fusion.10.refs_3_), channel_id=1, source_target_pairs={{0,2},{1,3},{2,0},{3,1},{4,6},{5,7},{6,4},{7,5},{8,10},{9,11},{10,... | collective-permute-start | bytes 1572872 | tf_op jit(solution)/shard_map/ppermute | solution.py:784
  444.3 4.9 collective-permute-start.38
  452.0 7.0 %collective-permute-start.39 = (bf16[64,1408]{1,0:T(8,128)(2,1)}, bf16[64,1408]{1,0:T(8,128)(2,1)S(1)}, u32[]{:S(2)}, u32[]{:S(2)}) collective-permute-start(bf16[64,1408]{1,0:T(8,128)(2,1)} %get-tuple-element.207.refs_2_), channel_id=1, source_target_pairs={{0,1},{1,0},{2,3},{3,2},{4,5},{5,4},{6,7},{7,6},{8,9},{9,8},{10,11... | collective-permute-start | bytes 540680 | tf_op jit(solution)/shard_map/ppermute | solution.py:784
  453.1 10.1 %collective-permute-start.40 = (bf16[64,1408]{1,0:T(8,128)(2,1)}, bf16[64,1408]{1,0:T(8,128)(2,1)S(1)}, u32[]{:S(2)}, u32[]{:S(2)}) collective-permute-start(bf16[64,1408]{1,0:T(8,128)(2,1)} %get-tuple-element.208.refs_3_), channel_id=1, source_target_pairs={{0,2},{1,3},{2,0},{3,1},{4,6},{5,7},{6,4},{7,5},{8,10},{9,11},{10,... | collective-permute-start | bytes 540680 | tf_op jit(solution)/shard_map/ppermute | solution.py:784
  454.3 10.2 %collective-permute-start.41 = (bf16[64,1408]{1,0:T(8,128)(2,1)}, bf16[64,1408]{1,0:T(8,128)(2,1)}, u32[]{:S(2)}, u32[]{:S(2)}) collective-permute-start(bf16[64,1408]{1,0:T(8,128)(2,1)} %get-tuple-element.209.refs_4_), channel_id=1, source_target_pairs={{0,3},{1,2},{2,1},{3,0},{4,7},{5,6},{6,5},{7,4},{8,11},{9,10},{10,... | collective-permute-start | bytes 540680 | tf_op jit(solution)/shard_map/ppermute | solution.py:784
  459.0 21.7 %collective-permute-start.47 = (f32[8,1280]{1,0:T(8,128)}, f32[8,1280]{1,0:T(8,128)S(1)}, u32[]{:S(2)}, u32[]{:S(2)}) collective-permute-start(f32[8,1280]{1,0:T(8,128)} %after.44.refs_0_), channel_id=1, source_target_pairs={{0,1},{1,0},{2,3},{3,2},{4,5},{5,4},{6,7},{7,6},{8,9},{9,8},{10,11... | collective-permute-start | bytes 122888 | tf_op jit(solution)/shard_map/ppermute | solution.py:784
  463.2 17.5 %collective-permute-start.48 = (f32[8,1280]{1,0:T(8,128)}, f32[8,1280]{1,0:T(8,128)}, u32[]{:S(2)}, u32[]{:S(2)}) collective-permute-start(f32[8,1280]{1,0:T(8,128)} %after.44.refs_0_), channel_id=1, source_target_pairs={{0,2},{1,3},{2,0},{3,1},{4,6},{5,7},{6,4},{7,5},{8,10},{9,11},{10,... | collective-permute-start | bytes 122888 | tf_op jit(solution)/shard_map/ppermute | solution.py:784
  464.6 16.2 %collective-permute-start.49 = (f32[8,1280]{1,0:T(8,128)}, f32[8,1280]{1,0:T(8,128)}, u32[]{:S(2)}, u32[]{:S(2)}) collective-permute-start(f32[8,1280]{1,0:T(8,128)} %after.44.refs_0_), channel_id=1, source_target_pairs={{0,3},{1,2},{2,1},{3,0},{4,7},{5,6},{6,5},{7,4},{8,11},{9,10},{10,... | collective-permute-start | bytes 122888 | tf_op jit(solution)/shard_map/ppermute | solution.py:784
  475.6 7.9 %collective-permute-start.43 = (f32[24,128]{1,0:T(8,128)S(1)}, f32[24,128]{1,0:T(8,128)S(1)}, u32[]{:S(2)}, u32[]{:S(2)}) collective-permute-start(f32[24,128]{1,0:T(8,128)S(1)} %add.280), channel_id=1, source_target_pairs={{0,2},{1,3},{2,0},{3,1},{4,6},{5,7},{6,4},{7,5},{8,10},{9,11},{10,... | collective-permute-start | bytes 36872 | tf_op jit(solution)/shard_map/ppermute | solution.py:784
  (87 other events, 370.4 us)
Sparse Core Ops, SparseCore 0:
  28.0 60.7 all-gather.3
  90.9 45.8 all-gather.5
  138.4 45.7 all-gather.7
  259.4 49.9 reduce-scatter.5
  311.6 48.1 reduce-scatter.3
  378.2 65.3 reduce-scatter.7

commit v8 on v7

--- a/solution.py
+++ b/solution.py
@@ -1001,7 +1001,7 @@
     hid_1 = through_in(1, px_1)
     [got_o, got_z] = after([got_o, got_z], part_x)
     sent_oz, got_oz = exchange(split(jnp.concatenate([got_o, got_z], axis=1)), rank)
-    dco_0, dco_1 = after([dco_0, dco_1], hid_1[0], *got_oz)
+    dco_0, dco_1 = after([dco_0, dco_1], hid_1[0])
     conv_0, conv_1 = (tap_gradients(place, micro, proj_x, aux, one) for micro, one in enumerate((dco_0, dco_1)))
     stages_1 = scatter_stages(after(hid_1, *hid_got))
     hid_got, _ = next(stages_1)
@@ -1011,7 +1011,7 @@
     for bit in axis_bits("dp"):
         small = small + swapped(small, "dp", bit)
     _, hid_sent = stages_1.send(None)
-    [got_x] = after([got_x], small, output, *hid_sent)
+    [got_x] = after([got_x], output, *hid_sent, *got_oz)
     sent_x, got_x = exchange(split(got_x), rank)
     [small] = after([small], *sent_x)
     small = [small] + after([swapped(small, "seq", mask) for mask in range(1, n)], *got_x)

time: 523 us -> 533 us (1.019)
  waiting for transfers between devices: 72.3 us -> 82.2 us
    ppermute x50, waiting for transfers between devices: 71.5 us -> 81.4 us  [swapped(): lax.ppermute(value, axis, [(i, i ^ mask) for i in range(lax.axis_size(axi...]
    unnamed x170 -> x164, local copies, waits for them, and re-layouts: 17.5 us -> 15.5 us
  transfers between devices with their start and end apart: 56 -> 56, of which waited for: 22 -> 20; matrix products, arithmetic and copies ran while one was open for 21% -> 21% of each run, Pallas kernels for 33% -> 33%
where the time goes in v8:
time: 533 us; the launch traced here: 526 us
  Pallas kernels  215 us (40%)
  waiting for transfers between devices  82.2 us (15%)
  matrix products  60.8 us (11%)
  other arithmetic  58.1 us (11%)
  starting transfers between devices  54.8 us (10%)
  local copies, waits for them, and re-layouts  37.1 us (7%)
  between operations  18.7 us (4%)
    ppermute x50, waiting for transfers between devices, swapped(): lax.ppermute(value, axis, [(i, i ^ mask) for i in range(lax.axis_size(axi...  81.4 us
    dot_general x4, matrix products, dot(): return lax.dot_general(a, b, (dims, ((), ())), preferred_element_type=out)  60.8 us
    ppermute x50, starting transfers between devices, swapped(): lax.ppermute(value, axis, [(i, i ^ mask) for i in range(lax.axis_size(axi...  54.5 us
    pallas_call x2, Pallas kernels, scan_backward(): pl.pallas_call(functools.partial(backward_kernel, hl=hl), grid_spec=grid_...  54.1 us
    pallas_call x2, Pallas kernels, back_project(): pl.pallas_call(functools.partial(back_kernel, n=n, bits=bits), grid=(n,),...  35.3 us
    pallas_call x1, Pallas kernels, scan_forward(): pl.pallas_call(functools.partial(forward_kernel, hl=hl), grid_spec=grid_s...  32.8 us
    pallas_call x2, Pallas kernels, in_project(): pl.pallas_call(functools.partial(in_kernel, count=count), grid_spec=pltpu...  26 us
    pallas_call x1, Pallas kernels, out_project(): pl.pallas_call(functools.partial(out_kernel, n=n, bits=bits), grid=(token...  23.8 us
  transfers between devices with their start and end apart: 56, of which 20 were waited for; matrix products, arithmetic and copies ran while one was open for 21% of the time, Pallas kernels for 33%

profile of v8, /device:TPU:0, one launch (start us, length us, event | category | flops | bytes accessed | tf_op | source)
XLA Modules:
  0.0 526.3 jit_solution(1320776296910949259)
XLA Ops:
  7.2 1.7 convert_element_type.242
  10.8 3.0 collective-permute-start.6
  19.3 4.4 collective-permute-done.7.refs_1_
  33.8 17.9 %collective-permute-done.4.refs_4_.refs_2_ = bf16[256,2048]{1,0:T(8,128)(2,1)S(1)} collective-permute-done((bf16[256,2048]{1,0:T(8,128)(2,1)S(1)}, bf16[256,2048]{1,0:T(8,128)(2,1)S(1)}, u32[]{:S(2)}, u32[]{:S(2)}) %collective-permute-start.4) | collective-permute-done | bytes 1048608 | tf_op jit(solution)/shard_map/ppermute | solution.py:784
  57.5 5.5 %collective-permute-done.10 = bf16[64,2048]{1,0:T(8,128)(2,1)S(1)} collective-permute-done((bf16[64,2048]{1,0:T(8,128)(2,1)S(1)}, bf16[64,2048]{1,0:T(8,128)(2,1)S(1)}, u32[]{:S(2)}, u32[]{:S(2)}) %collective-permute-start.10) | collective-permute-done | bytes 262176 | tf_op jit(solution)/shard_map/ppermute | solution.py:784
  63.1 3.7 collective-permute-done.9
  69.9 1.8 collective-permute-start
  74.4 17.8 %collective-permute-done.refs_3_ = bf16[256,2048]{1,0:T(8,128)(2,1)} collective-permute-done((bf16[256,2048]{1,0:T(8,128)(2,1)S(1)}, bf16[256,2048]{1,0:T(8,128)(2,1)}, u32[]{:S(2)}, u32[]{:S(2)}) %collective-permute-start) | collective-permute-done | bytes 1048608 | tf_op jit(solution)/shard_map/ppermute | solution.py:784
  92.3 3.7 collective-permute-done.2.refs_6_
  96.8 3.2 slice_bitcast_fusion.2
  102.9 16.9 %in_project.2 = (bf16[2048,1408]{1,0:T(8,128)(2,1)}, bf16[2048,2048]{1,0:T(8,128)(2,1)}) custom-call(s32[6]{0:T(128)} %constant.29.clone.refs_0_, bf16[256,2048]{1,0:T(8,128)(2,1)} %get-tuple-element.176.refs_3_.refs_1_, bf16[256,2048]{1,0:T(8,128)(2,1)} %get-tuple-element.175.refs_4_.refs_2_, bf16[256,2048]{1,0:T(8,128)(2,1)} %collective-permute-done.refs_3_, ...), custom_call_target="tpu_custom_call" | custom-call | tf_op jit(solution)/shard_map/in_project/pallas_call | solution.py:549
  127.9 9.1 %in_project.3 = (bf16[2048,1408]{1,0:T(8,128)(2,1)}, bf16[2048,2048]{1,0:T(8,128)(2,1)}) custom-call(s32[2]{0:T(128)} %constant.30.clone.refs_0_, bf16[256,2048]{1,0:T(8,128)(2,1)} %get-tuple-element.89.refs_1_.refs_2_, bf16[256,2048]{1,0:T(8,128)(2,1)} %get-tuple-element.90.refs_2_.refs_3_, ...), custom_call_target="tpu_custom_call", output_to_operand_aliasing={{0}: (4, {}), {1}: (5, {})} | custom-call | tf_op jit(solution)/shard_map/in_project/pallas_call | solution.py:549
  137.6 32.8 %scan_forward.1 = (bf16[2048,1024]{1,0:T(8,128)(2,1)}, bf16[8,1024,128]{2,1,0:T(8,128)(2,1)}, bf16[2048,1280]{1,0:T(8,128)(2,1)}, bf16[2048,1280]{1,0:T(8,128)(2,1)}) custom-call(s32[1]{0:T(128)} %bitcast.19.place, bf16[2048,1408]{1,0:T(8,128)(2,1)} %get-tuple-element.93.proj.refs_1_, f32[8,1280]{1,0:T(8,128)} %fusion.26.refs_10_.conv_w, ...), custom_call_target="tpu_custom_call" | custom-call | tf_op jit(solution)/shard_map/scan_forward/pallas_call | solution.py:374
  171.4 2.0 collective-permute-start.17
  174.6 13.8 %convolution_convert_fusion.1.refs_8_.z_in = bf16[2048,1024]{1,0:T(8,128)(2,1)} fusion(bf16[2048,2048]{1,0:T(8,128)(2,1)} %get-tuple-element.92, bf16[2048,1024]{1,0:T(8,128)(2,1)} %after.26.w_z), kind=kOutput, calls=%fused_computation.20 | convolution fusion | flops 8592031744 | bytes 16777216 | tf_op jit(solution)/shard_map/dot_general | solution.py:34
  193.2 19.2 %gate_forward.1 = (bf16[2048,1024]{1,0:T(8,128)(2,1)}, bf16[2048,2048]{1,0:T(8,128)(2,1)}, f32[16,256]{1,0:T(8,128)}) custom-call(bf16[256,2048]{1,0:T(8,128)(2,1)} %get-tuple-element.95.refs_0_, bf16[256,2048]{1,0:T(8,128)(2,1)} %after.28.refs_1_, bf16[256,2048]{1,0:T(8,128)(2,1)} %get-tuple-element.96.refs_2_, ...), custom_call_target="tpu_custom_call" | custom-call | tf_op jit(solution)/shard_map/gate_forward/pallas_call | solution.py:589
  221.4 23.8 %out_project.1 = (bf16[2048,1024]{1,0:T(8,128)(2,1)}, bf16[2048,1024]{1,0:T(8,128)(2,1)}, bf16[2048,1024]{1,0:T(8,128)(2,1)}, f32[8,1024]{1,0:T(8,128)}, bf16[2,...) custom-call(bf16[2048,1024]{1,0:T(8,128)(2,1)} %convolution_convert_, ...), custom_call_target="tpu_custom_call" | custom-call | tf_op jit(solution)/shard_map/out_project/pallas_call | solution.py:637
  245.2 14.0 %convolution_convert_fusion.2.refs_1_ = bf16[2048,1024]{1,0:T(8,128)(2,1)} fusion(bf16[2048,2048]{1,0:T(8,128)(2,1)} %get-tuple-element.92, bf16[2048,1024]{1,0:T(8,128)(2,1)} %get-tuple-element.106.dz), kind=kOutput, calls=%fused_computation.21 | convolution fusion | flops 8592031744 | bytes 16777216 | tf_op jit(solution)/shard_map/dot_general | solution.py:34
  259.3 14.0 %convolution_convert_fusion.3.refs_0_ = bf16[2048,1024]{1,0:T(8,128)(2,1)} fusion(bf16[2048,2048]{1,0:T(8,128)(2,1)} %get-tuple-element.111, bf16[2048,1024]{1,0:T(8,128)(2,1)} %get-tuple-element.112), kind=kOutput, calls=%fused_computation.22 | convolution fusion | flops 8592031744 | bytes 16777216 | tf_op jit(solution)/shard_map/dot_general | solution.py:34
  275.2 27.0 %scan_backward.2 = (bf16[1024,1408]{1,0:T(8,128)(2,1)}, bf16[1024,1280]{1,0:T(8,128)(2,1)}, f32[16,128]{1,0:T(8,128)}, f32[8,1024]{1,0:T(8,128)}) custom-call(s32[1]{0:T(128)} %bitcast.19.place, bf16[2048,1408]{1,0:T(8,128)(2,1)} %get-tuple-element.93.proj.refs_1_, f32[8,1280]{1,0:T(8,128)} %fusion.26.refs_10_.conv_w, f32[8,1024]{1,0:T(8,128)} %broadcast_in_dim.30.skip, ...), custom_call_target="tpu_custom_call" | custom-call | tf_op jit(solution)/shard_map/scan_backward/pallas_call | solution.py:436
  302.2 17.4 %back_project.2 = (bf16[1,2,128,2048]{3,2,1,0:T(8,128)(2,1)}, bf16[1,2,128,2048]{3,2,1,0:T(8,128)(2,1)}, bf16[1,2,128,2048]{3,2,1,0:T(8,128)(2,1)}, bf16[1,2,128,2048]{3,2,1,0:T(8,128)(2,1)}) custom-call(bf16[2048,1024]{1,0:T(8,128)(2,1)} %get-tuple-element.106.dz, bf16[1024,1408]{1,0:T(8,128)(2,1)} %get-tuple-element.113.px, bf16[2048,1024]{1,0:T(8,128)(2,1)} %after.26.w_z, ...), custom_call_target="tpu_custom_call" | custom-call | tf_op jit(solution)/shard_map/back_project/pallas_call | solution.py:659
  322.0 2.1 add_convert_fusion.3.refs_3_
  328.0 27.1 %scan_backward.3 = (bf16[1024,1408]{1,0:T(8,128)(2,1)}, bf16[1024,1280]{1,0:T(8,128)(2,1)}, f32[16,128]{1,0:T(8,128)}, f32[8,1024]{1,0:T(8,128)}) custom-call(s32[1]{0:T(128)} %bitcast.19.place, bf16[2048,1408]{1,0:T(8,128)(2,1)} %get-tuple-element.93.proj.refs_1_, f32[8,1280]{1,0:T(8,128)} %fusion.26.refs_10_.conv_w, f32[8,1024]{1,0:T(8,128)} %broadcast_in_dim.30.skip, ...), custom_call_target="tpu_custom_call" | custom-call | tf_op jit(solution)/shard_map/scan_backward/pallas_call | solution.py:436
  355.1 2.8 collective-permute-done.24.refs_4_.refs_1_
  358.9 19.1 %convolution_convert_fusion.refs_2_.refs_1_ = bf16[2048,1408]{1,0:T(8,128)(2,1)} fusion(bf16[2048,2048]{1,0:T(8,128)(2,1)} %get-tuple-element.92, bf16[1024,1408]{1,0:T(8,128)(2,1)} %after.33.refs_0_, bf16[1024,1408]{1,0:T(8,128)(2,1)} %get-tuple-element.113.px), kind=kOutput, calls=%fused_computation.5 | convolution fusion | flops 11825577984 | bytes 19922944 | tf_op jit(solution)/shard_map/dot_general | solution.py:34
  384.3 17.8 %back_project.3 = (bf16[1,2,128,2048]{3,2,1,0:T(8,128)(2,1)}, bf16[1,2,128,2048]{3,2,1,0:T(8,128)(2,1)}, bf16[1,2,128,2048]{3,2,1,0:T(8,128)(2,1)}, bf16[1,2,128,2048]{3,2,1,0:T(8,128)(2,1)}) custom-call(bf16[2048,1024]{1,0:T(8,128)(2,1)} %get-tuple-element.106.dz, bf16[1024,1408]{1,0:T(8,128)(2,1)} %after.35.px, bf16[2048,1024]{1,0:T(8,128)(2,1)} %after.26.w_z, ...), custom_call_target="tpu_custom_call" | custom-call | tf_op jit(solution)/shard_map/back_project/pallas_call | solution.py:659
  407.7 6.9 %tap_gradients.3.conv_1 = f32[40,1280]{1,0:T(8,128)} custom-call(s32[1]{0:T(128)} %bitcast.19.place, bf16[2048,1408]{1,0:T(8,128)(2,1)} %get-tuple-element.93.proj.refs_1_, f32[2048,8]{1,0:T(8,128)} %copy.118.refs_8_.aux, bf16[1024,1280]{1,0:T(8,128)(2,1)} %get-tuple-element.128.dco), custom_call_target="tpu_custom_call" | custom-call | tf_op jit(solution)/shard_map/tap_gradients/pallas_call | solution.py:464
  414.6 6.9 %tap_gradients.2.conv_0 = f32[40,1280]{1,0:T(8,128)} custom-call(s32[1]{0:T(128)} %bitcast.19.place, bf16[2048,1408]{1,0:T(8,128)(2,1)} %get-tuple-element.93.proj.refs_1_, f32[2048,8]{1,0:T(8,128)} %copy.118.refs_8_.aux, bf16[1024,1280]{1,0:T(8,128)(2,1)} %get-tuple-element.127.dco), custom_call_target="tpu_custom_call" | custom-call | tf_op jit(solution)/shard_map/tap_gradients/pallas_call | solution.py:464
  421.5 1.9 small_gradients.1.refs_0_
  425.4 2.1 add_convert_fusion.9.refs_3_
  428.5 2.2 fusion.15
  431.1 2.0 fusion.16
  433.1 2.2 fusion.6.refs_1_
  445.5 3.7 collective-permute-done.33.refs_4_.refs_1_
  449.2 2.3 collective-permute-start.46
  451.5 4.7 collective-permute-done.34.refs_5_.refs_2_
  456.2 2.1 broadcast_select_fusion.36
  461.8 3.2 fusion.18
  467.2 6.2 %collective-permute-done.37.refs_3_.refs_6_.refs_4_ = bf16[64,1408]{1,0:T(8,128)(2,1)S(1)} collective-permute-done((bf16[64,1408]{1,0:T(8,128)(2,1)}, bf16[64,1408]{1,0:T(8,128)(2,1)S(1)}, u32[]{:S(2)}, u32[]{:S(2)}) %collective-permute-start.37) | collective-permute-done | bytes 180256 | tf_op jit(solution)/shard_map/ppermute | solution.py:784
  475.8 5.5 %shards.1 = (f32[64,8512]{1,0:T(8,128)}, f32[64,4096]{1,0:T(8,128)}, f32[24,128]{1,0:T(8,128)}) custom-call(s32[2]{0:T(128)} %pad_add_fusion.spot, bf16[64,2048]{1,0:T(8,128)(2,1)} %get-tuple-element.193.refs_0_, bf16[64,2048]{1,0:T(8,128)(2,1)} %copy-done.58, bf16[64,2048]{1,0:T(8,128)(2,1)} %collective-permute-done.34.refs_5_.refs_2_, ...), custom_call_target="tpu_custom_call" | custom-call | tf_op jit(solution)/shard_map/shards/pallas_call | solution.py:716
  482.4 2.3 fusion.20
  486.9 3.6 fusion.11
  491.1 2.2 place_small.1
  496.5 2.1 collective-permute-done.42
  498.7 2.2 collective-permute-start.43
  501.3 1.9 collective-permute-done.43
  507.2 3.9 multiply_add_fusion.2
  511.9 5.5 %multiply_add_fusion = (f32[64,8512]{1,0:T(8,128)}, f32[64,8512]{1,0:T(8,128)}, f32[64,8512]{1,0:T(8,128)}) fusion(f32[64,8512]{1,0:T(8,128)S(1)} %copy-done.2, f32[64,8512]{1,0:T(8,128)} %get-tuple-element.153, f32[]{:T(128)S(6)} %min.3, f32[64,8512]{1,0:T(8,128)S(1)} %copy-done.30, f32[64,8512]{1,0:T(8,128)S(1)} %copy-done.31), kind=kLoop, calls=%fused_computation.25 | loop fusion | flops 8716288 | bytes 15253508 | tf_op jit(solution)/shard_map/add | solution.py:1044
  (395 shorter events, 110.2 us)
Async XLA Ops:
  7.2 92.8 %all-gather.4.cloned.1.call-start = ((), (), s32[]{:S(2)}) async-start(), calls=%async_computation.3 | async-start | bytes 6488064 | tf_op jit(solution)/shard_map/all_gather | solution.py:940
  10.8 8.5 %collective-permute-start.6 = (bf16[64,1408]{1,0:T(8,128)(2,1)S(1)}, bf16[64,1408]{1,0:T(8,128)(2,1)S(1)}, u32[]{:S(2)}, u32[]{:S(2)}) collective-permute-start(bf16[64,1408]{1,0:T(8,128)(2,1)S(1)} %get-tuple-element.212), channel_id=1, source_target_pairs={{0,1},{1,0},{2,3},{3,2},{4,5},{5,4},{6,7},{7,6},{8,9},{9,8},{10,11... | collective-permute-start | bytes 540680 | tf_op jit(solution)/shard_map/ppermute | solution.py:784
  13.8 9.9 %collective-permute-start.7 = (bf16[64,1408]{1,0:T(8,128)(2,1)S(1)}, bf16[64,1408]{1,0:T(8,128)(2,1)S(1)}, u32[]{:S(2)}, u32[]{:S(2)}) collective-permute-start(bf16[64,1408]{1,0:T(8,128)(2,1)S(1)} %get-tuple-element.211), channel_id=1, source_target_pairs={{0,2},{1,3},{2,0},{3,1},{4,6},{5,7},{6,4},{7,5},{8,10},{9,11},{10,... | collective-permute-start | bytes 540680 | tf_op jit(solution)/shard_map/ppermute | solution.py:784
  15.4 8.4 %collective-permute-start.8 = (bf16[64,1408]{1,0:T(8,128)(2,1)S(1)}, bf16[64,1408]{1,0:T(8,128)(2,1)S(1)}, u32[]{:S(2)}, u32[]{:S(2)}) collective-permute-start(bf16[64,1408]{1,0:T(8,128)(2,1)S(1)} %get-tuple-element.210), channel_id=1, source_target_pairs={{0,3},{1,2},{2,1},{3,0},{4,7},{5,6},{6,5},{7,4},{8,11},{9,10},{10,... | collective-permute-start | bytes 540680 | tf_op jit(solution)/shard_map/ppermute | solution.py:784
  27.9 142.6 %all-gather.6.cloned.1.call-start = ((), (), s32[]{:S(2)}) async-start(), calls=%async_computation.4 | async-start | bytes 4718592 | tf_op jit(solution)/shard_map/all_gather | solution.py:945
  27.9 23.8 %collective-permute-start.4 = (bf16[256,2048]{1,0:T(8,128)(2,1)S(1)}, bf16[256,2048]{1,0:T(8,128)(2,1)S(1)}, u32[]{:S(2)}, u32[]{:S(2)}) collective-permute-start(bf16[256,2048]{1,0:T(8,128)(2,1)S(1)} %copy-done.9), channel_id=1, source_target_pairs={{0,2},{1,3},{2,0},{3,1},{4,6},{5,7},{6,4},{7,5},{8,10},{9,11},{10,... | collective-permute-start | bytes 3145736 | tf_op jit(solution)/shard_map/ppermute | solution.py:784
  29.5 22.6 %collective-permute-start.5 = (bf16[256,2048]{1,0:T(8,128)(2,1)S(1)}, bf16[256,2048]{1,0:T(8,128)(2,1)}, u32[]{:S(2)}, u32[]{:S(2)}) collective-permute-start(bf16[256,2048]{1,0:T(8,128)(2,1)S(1)} %copy-done.8), channel_id=1, source_target_pairs={{0,1},{1,0},{2,3},{3,2},{4,5},{5,4},{6,7},{7,6},{8,9},{9,8},{10,11... | collective-permute-start | bytes 3145736 | tf_op jit(solution)/shard_map/ppermute | solution.py:784
  53.9 9.0 %collective-permute-start.10 = (bf16[64,2048]{1,0:T(8,128)(2,1)S(1)}, bf16[64,2048]{1,0:T(8,128)(2,1)S(1)}, u32[]{:S(2)}, u32[]{:S(2)}) collective-permute-start(bf16[64,2048]{1,0:T(8,128)(2,1)S(1)} %get-tuple-element.200), channel_id=1, source_target_pairs={{0,2},{1,3},{2,0},{3,1},{4,6},{5,7},{6,4},{7,5},{8,10},{9,11},{10,... | collective-permute-start | bytes 786440 | tf_op jit(solution)/shard_map/ppermute | solution.py:784
  54.8 8.3 %collective-permute-start.11 = (bf16[64,2048]{1,0:T(8,128)(2,1)S(1)}, bf16[64,2048]{1,0:T(8,128)(2,1)S(1)}, u32[]{:S(2)}, u32[]{:S(2)}) collective-permute-start(bf16[64,2048]{1,0:T(8,128)(2,1)S(1)} %get-tuple-element.199), channel_id=1, source_target_pairs={{0,1},{1,0},{2,3},{3,2},{4,5},{5,4},{6,7},{7,6},{8,9},{9,8},{10,11... | collective-permute-start | bytes 786440 | tf_op jit(solution)/shard_map/ppermute | solution.py:784
  56.3 10.6 %collective-permute-start.9 = (bf16[64,2048]{1,0:T(8,128)(2,1)S(1)}, bf16[64,2048]{1,0:T(8,128)(2,1)S(1)}, u32[]{:S(2)}, u32[]{:S(2)}) collective-permute-start(bf16[64,2048]{1,0:T(8,128)(2,1)S(1)} %get-tuple-element.201), channel_id=1, source_target_pairs={{0,3},{1,2},{2,1},{3,0},{4,7},{5,6},{6,5},{7,4},{8,11},{9,10},{10,... | collective-permute-start | bytes 786440 | tf_op jit(solution)/shard_map/ppermute | solution.py:784
  69.1 123.5 %all-gather.8.cloned.1.call-start = ((), (), s32[]{:S(2)}) async-start(), calls=%async_computation.5 | async-start | bytes 4718592 | tf_op jit(solution)/shard_map/all_gather | solution.py:946
  69.8 367.0 %reduce-scatter.8.cloned.1.call-start = ((), (), s32[]{:S(2)}) async-start(), calls=%async_computation.8 | async-start | bytes 4718592 | tf_op jit(solution)/shard_map/reduce_scatter | solution.py:975
  69.9 22.3 %collective-permute-start = (bf16[256,2048]{1,0:T(8,128)(2,1)S(1)}, bf16[256,2048]{1,0:T(8,128)(2,1)}, u32[]{:S(2)}, u32[]{:S(2)}) collective-permute-start(bf16[256,2048]{1,0:T(8,128)(2,1)S(1)} %copy-done.9), channel_id=1, source_target_pairs={{0,1},{1,0},{2,3},{3,2},{4,5},{5,4},{6,7},{7,6},{8,9},{9,8},{10,11... | collective-permute-start | bytes 3145736 | tf_op jit(solution)/shard_map/ppermute | solution.py:784
  71.7 24.3 %collective-permute-start.2 = (bf16[256,2048]{1,0:T(8,128)(2,1)S(1)}, bf16[256,2048]{1,0:T(8,128)(2,1)}, u32[]{:S(2)}, u32[]{:S(2)}) collective-permute-start(bf16[256,2048]{1,0:T(8,128)(2,1)S(1)} %copy-done.8), channel_id=1, source_target_pairs={{0,2},{1,3},{2,0},{3,1},{4,6},{5,7},{6,4},{7,5},{8,10},{9,11},{10,... | collective-permute-start | bytes 3145736 | tf_op jit(solution)/shard_map/ppermute | solution.py:784
  92.2 27.7 %collective-permute-start.1 = (bf16[256,2048]{1,0:T(8,128)(2,1)}, bf16[256,2048]{1,0:T(8,128)(2,1)S(1)}, u32[]{:S(2)}, u32[]{:S(2)}) collective-permute-start(bf16[256,2048]{1,0:T(8,128)(2,1)} %collective-permute-done.refs_3_), channel_id=1, source_target_pairs={{0,2},{1,3},{2,0},{3,1},{4,6},{5,7},{6,4},{7,5},{8,10},{9,11},{10,... | collective-permute-start | bytes 3145736 | tf_op jit(solution)/shard_map/ppermute | solution.py:784
  96.0 23.9 %collective-permute-start.3 = (bf16[256,2048]{1,0:T(8,128)(2,1)}, bf16[256,2048]{1,0:T(8,128)(2,1)S(1)}, u32[]{:S(2)}, u32[]{:S(2)}) collective-permute-start(bf16[256,2048]{1,0:T(8,128)(2,1)} %collective-permute-done.2.refs_6_), channel_id=1, source_target_pairs={{0,1},{1,0},{2,3},{3,2},{4,5},{5,4},{6,7},{7,6},{8,9},{9,8},{10,11... | collective-permute-start | bytes 3145736 | tf_op jit(solution)/shard_map/ppermute | solution.py:784
  121.2 49.3 %collective-permute-start.16 = (bf16[256,2048]{1,0:T(8,128)(2,1)}, bf16[256,2048]{1,0:T(8,128)(2,1)S(1)}, u32[]{:S(2)}, u32[]{:S(2)}) collective-permute-start(bf16[256,2048]{1,0:T(8,128)(2,1)} %get-tuple-element.98.refs_4_), channel_id=1, source_target_pairs={{0,2},{1,3},{2,0},{3,1},{4,6},{5,7},{6,4},{7,5},{8,10},{9,11},{10,... | collective-permute-start | bytes 3145736 | tf_op jit(solution)/shard_map/ppermute | solution.py:784
  122.0 51.5 %collective-permute-start.12 = (bf16[256,2048]{1,0:T(8,128)(2,1)}, bf16[256,2048]{1,0:T(8,128)(2,1)S(1)}, u32[]{:S(2)}, u32[]{:S(2)}) collective-permute-start(bf16[256,2048]{1,0:T(8,128)(2,1)} %get-tuple-element.95.refs_0_), channel_id=1, source_target_pairs={{0,1},{1,0},{2,3},{3,2},{4,5},{5,4},{6,7},{7,6},{8,9},{9,8},{10,11... | collective-permute-start | bytes 3145736 | tf_op jit(solution)/shard_map/ppermute | solution.py:784
  126.0 62.4 %collective-permute-start.15 = (bf16[256,2048]{1,0:T(8,128)(2,1)}, bf16[256,2048]{1,0:T(8,128)(2,1)}, u32[]{:S(2)}, u32[]{:S(2)}) collective-permute-start(bf16[256,2048]{1,0:T(8,128)(2,1)} %get-tuple-element.98.refs_4_), channel_id=1, source_target_pairs={{0,1},{1,0},{2,3},{3,2},{4,5},{5,4},{6,7},{7,6},{8,9},{9,8},{10,11... | collective-permute-start | bytes 3145736 | tf_op jit(solution)/shard_map/ppermute | solution.py:784
  126.5 63.8 %collective-permute-start.13 = (bf16[256,2048]{1,0:T(8,128)(2,1)}, bf16[256,2048]{1,0:T(8,128)(2,1)S(1)}, u32[]{:S(2)}, u32[]{:S(2)}) collective-permute-start(bf16[256,2048]{1,0:T(8,128)(2,1)} %get-tuple-element.95.refs_0_), channel_id=1, source_target_pairs={{0,2},{1,3},{2,0},{3,1},{4,6},{5,7},{6,4},{7,5},{8,10},{9,11},{10,... | collective-permute-start | bytes 3145736 | tf_op jit(solution)/shard_map/ppermute | solution.py:784
  171.4 18.0 %collective-permute-start.17 = (bf16[256,2048]{1,0:T(8,128)(2,1)}, bf16[256,2048]{1,0:T(8,128)(2,1)S(1)}, u32[]{:S(2)}, u32[]{:S(2)}) collective-permute-start(bf16[256,2048]{1,0:T(8,128)(2,1)} %after.30.refs_6_), channel_id=1, source_target_pairs={{0,1},{1,0},{2,3},{3,2},{4,5},{5,4},{6,7},{7,6},{8,9},{9,8},{10,11... | collective-permute-start | bytes 3145736 | tf_op jit(solution)/shard_map/ppermute | solution.py:784
  174.5 17.1 %collective-permute-start.14 = (bf16[256,2048]{1,0:T(8,128)(2,1)}, bf16[256,2048]{1,0:T(8,128)(2,1)S(1)}, u32[]{:S(2)}, u32[]{:S(2)}) collective-permute-start(bf16[256,2048]{1,0:T(8,128)(2,1)} %after.28.refs_1_), channel_id=1, source_target_pairs={{0,2},{1,3},{2,0},{3,1},{4,6},{5,7},{6,4},{7,5},{8,10},{9,11},{10,... | collective-permute-start | bytes 3145736 | tf_op jit(solution)/shard_map/ppermute | solution.py:784
  259.2 177.6 %reduce-scatter.6.cloned.1.call-start = ((), (), s32[]{:S(2)}) async-start(), calls=%async_computation.7 | async-start | bytes 4718592 | tf_op jit(solution)/shard_map/reduce_scatter | solution.py:975
  273.3 182.9 %reduce-scatter.4.cloned.1.call-start = ((), (), s32[]{:S(2)}) async-start(), calls=%async_computation.6 | async-start | bytes 6488064 | tf_op jit(solution)/shard_map/reduce_scatter | solution.py:975
  273.3 48.7 %collective-permute-start.21 = (bf16[2,2,128,2048]{3,2,1,0:T(8,128)(2,1)}, bf16[2,2,128,2048]{3,2,1,0:T(8,128)(2,1)}, u32[]{:S(2)}, u32[]{:S(2)}) collective-permute-start(bf16[2,2,128,2048]{3,2,1,0:T(8,128)(2,1)} %get-tuple-element.104), channel_id=1, source_target_pairs={{0,1},{1,0},{2,3},{3,2},{4,5},{5,4},{6,7},{7,6},{8,9},{9,8},{10,11... | collective-permute-start | bytes 6291464 | tf_op jit(solution)/shard_map/ppermute | solution.py:784
  274.6 47.4 %collective-permute-start.22 = (bf16[2,2,128,2048]{3,2,1,0:T(8,128)(2,1)}, bf16[2,2,128,2048]{3,2,1,0:T(8,128)(2,1)}, u32[]{:S(2)}, u32[]{:S(2)}) collective-permute-start(bf16[2,2,128,2048]{3,2,1,0:T(8,128)(2,1)} %get-tuple-element.105), channel_id=1, source_target_pairs={{0,2},{1,3},{2,0},{3,1},{4,6},{5,7},{6,4},{7,5},{8,10},{9,11},{10,... | collective-permute-start | bytes 6291464 | tf_op jit(solution)/shard_map/ppermute | solution.py:784
  319.6 35.5 %collective-permute-start.25 = (bf16[1,2,128,2048]{3,2,1,0:T(8,128)(2,1)}, bf16[1,2,128,2048]{3,2,1,0:T(8,128)(2,1)S(1)}, u32[]{:S(2)}, u32[]{:S(2)}) collective-permute-start(bf16[1,2,128,2048]{3,2,1,0:T(8,128)(2,1)} %get-tuple-element.114.refs_2_.refs_0_), channel_id=1, source_target_pairs={{0,1},{1,0},{2,3},{3,2},{4,5},{5,4},{6,7},{7,6},{8,9},{9,8},{10,11... | collective-permute-start | bytes 3145736 | tf_op jit(solution)/shard_map/ppermute | solution.py:784
  321.0 34.2 %collective-permute-start.26 = (bf16[1,2,128,2048]{3,2,1,0:T(8,128)(2,1)}, bf16[1,2,128,2048]{3,2,1,0:T(8,128)(2,1)S(1)}, u32[]{:S(2)}, u32[]{:S(2)}) collective-permute-start(bf16[1,2,128,2048]{3,2,1,0:T(8,128)(2,1)} %get-tuple-element.119.refs_1_), channel_id=1, source_target_pairs={{0,2},{1,3},{2,0},{3,1},{4,6},{5,7},{6,4},{7,5},{8,10},{9,11},{10,... | collective-permute-start | bytes 3145736 | tf_op jit(solution)/shard_map/ppermute | solution.py:784
  324.1 33.8 %collective-permute-start.24 = (bf16[2,1,128,2048]{3,2,1,0:T(8,128)(2,1)S(1)}, bf16[2,1,128,2048]{3,2,1,0:T(8,128)(2,1)S(1)}, u32[]{:S(2)}, u32[]{:S(2)}) collective-permute-start(bf16[2,1,128,2048]{3,2,1,0:T(8,128)(2,1)S(1)} %add_convert_fusion.3.refs_3_), channel_id=1, source_target_pairs={{0,1},{1,0},{2,3},{3,2},{4,5},{5,4},{6,7},{7,6},{8,9},{9,8},{10,11... | collective-permute-start | bytes 3145736 | tf_op jit(solution)/shard_map/ppermute | solution.py:784
  327.1 31.7 %collective-permute-start.23 = (bf16[2,1,128,2048]{3,2,1,0:T(8,128)(2,1)S(1)}, bf16[2,1,128,2048]{3,2,1,0:T(8,128)(2,1)}, u32[]{:S(2)}, u32[]{:S(2)}) collective-permute-start(bf16[2,1,128,2048]{3,2,1,0:T(8,128)(2,1)S(1)} %add_convert_fusion.4.refs_2_), channel_id=1, source_target_pairs={{0,2},{1,3},{2,0},{3,1},{4,6},{5,7},{6,4},{7,5},{8,10},{9,11},{10,... | collective-permute-start | bytes 3145736 | tf_op jit(solution)/shard_map/ppermute | solution.py:784
  380.4 21.8 %collective-permute-start.28 = (bf16[1,1,128,2048]{3,2,1,0:T(8,128)(2,1)S(1)}, bf16[1,1,128,2048]{3,2,1,0:T(8,128)(2,1)S(1)}, u32[]{:S(2)}, u32[]{:S(2)}) collective-permute-start(bf16[1,1,128,2048]{3,2,1,0:T(8,128)(2,1)S(1)} %add_convert_fusion.16.refs_3_), channel_id=1, source_target_pairs={{0,1},{1,0},{2,3},{3,2},{4,5},{5,4},{6,7},{7,6},{8,9},{9,8},{10,11... | collective-permute-start | bytes 1572872 | tf_op jit(solution)/shard_map/ppermute | solution.py:784
  382.7 20.4 %collective-permute-start.27 = (bf16[1,1,128,2048]{3,2,1,0:T(8,128)(2,1)S(1)}, bf16[1,1,128,2048]{3,2,1,0:T(8,128)(2,1)S(1)}, u32[]{:S(2)}, u32[]{:S(2)}) collective-permute-start(bf16[1,1,128,2048]{3,2,1,0:T(8,128)(2,1)S(1)} %add_convert_fusion.17.refs_2_), channel_id=1, source_target_pairs={{0,2},{1,3},{2,0},{3,1},{4,6},{5,7},{6,4},{7,5},{8,10},{9,11},{10,... | collective-permute-start | bytes 1572872 | tf_op jit(solution)/shard_map/ppermute | solution.py:784
  404.1 19.3 %collective-permute-start.29 = (bf16[1,2,128,2048]{3,2,1,0:T(8,128)(2,1)}, bf16[1,2,128,2048]{3,2,1,0:T(8,128)(2,1)S(1)}, u32[]{:S(2)}, u32[]{:S(2)}) collective-permute-start(bf16[1,2,128,2048]{3,2,1,0:T(8,128)(2,1)} %get-tuple-element.137), channel_id=1, source_target_pairs={{0,1},{1,0},{2,3},{3,2},{4,5},{5,4},{6,7},{7,6},{8,9},{9,8},{10,11... | collective-permute-start | bytes 3145736 | tf_op jit(solution)/shard_map/ppermute | solution.py:784
  405.4 18.0 %collective-permute-start.30 = (bf16[1,2,128,2048]{3,2,1,0:T(8,128)(2,1)}, bf16[1,2,128,2048]{3,2,1,0:T(8,128)(2,1)S(1)}, u32[]{:S(2)}, u32[]{:S(2)}) collective-permute-start(bf16[1,2,128,2048]{3,2,1,0:T(8,128)(2,1)} %get-tuple-element.138), channel_id=1, source_target_pairs={{0,2},{1,3},{2,0},{3,1},{4,6},{5,7},{6,4},{7,5},{8,10},{9,11},{10,... | collective-permute-start | bytes 3145736 | tf_op jit(solution)/shard_map/ppermute | solution.py:784
  425.4 9.8 %collective-permute-start.44 = (f32[8,1280]{1,0:T(8,128)}, f32[8,1280]{1,0:T(8,128)S(1)}, u32[]{:S(2)}, u32[]{:S(2)}) collective-permute-start(f32[8,1280]{1,0:T(8,128)} %after.38.refs_2_), channel_id=1, source_target_pairs={{0,4},{4,0},{8,12},{12,8},{16,20},{20,16},{24,28},{28,24},{1,5},{5... | collective-permute-start | bytes 122888 | tf_op jit(solution)/shard_map/ppermute | solution.py:784
  427.6 53.7 %collective-permute-start.32 = (bf16[1,1,128,2048]{3,2,1,0:T(8,128)(2,1)}, bf16[1,1,128,2048]{3,2,1,0:T(8,128)(2,1)}, u32[]{:S(2)}, u32[]{:S(2)}) collective-permute-start(bf16[1,1,128,2048]{3,2,1,0:T(8,128)(2,1)} %add_convert_fusion.9.refs_3_), channel_id=1, source_target_pairs={{0,1},{1,0},{2,3},{3,2},{4,5},{5,4},{6,7},{7,6},{8,9},{9,8},{10,11... | collective-permute-start | bytes 1572872 | tf_op jit(solution)/shard_map/ppermute | solution.py:784
  435.2 9.2 %collective-permute-start.45 = (f32[8,1280]{1,0:T(8,128)S(1)}, f32[8,1280]{1,0:T(8,128)S(1)}, u32[]{:S(2)}, u32[]{:S(2)}) collective-permute-start(f32[8,1280]{1,0:T(8,128)S(1)} %add.282), channel_id=1, source_target_pairs={{0,8},{4,12},{8,0},{12,4},{16,24},{20,28},{24,16},{28,20},{1,9},{5... | collective-permute-start | bytes 122888 | tf_op jit(solution)/shard_map/ppermute | solution.py:784
  440.0 9.2 %collective-permute-start.33 = (bf16[64,2048]{1,0:T(8,128)(2,1)S(1)}, bf16[64,2048]{1,0:T(8,128)(2,1)S(1)}, u32[]{:S(2)}, u32[]{:S(2)}) collective-permute-start(bf16[64,2048]{1,0:T(8,128)(2,1)S(1)} %get-tuple-element.194), channel_id=1, source_target_pairs={{0,1},{1,0},{2,3},{3,2},{4,5},{5,4},{6,7},{7,6},{8,9},{9,8},{10,11... | collective-permute-start | bytes 786440 | tf_op jit(solution)/shard_map/ppermute | solution.py:784
  441.2 15.0 %collective-permute-start.34 = (bf16[64,2048]{1,0:T(8,128)(2,1)S(1)}, bf16[64,2048]{1,0:T(8,128)(2,1)}, u32[]{:S(2)}, u32[]{:S(2)}) collective-permute-start(bf16[64,2048]{1,0:T(8,128)(2,1)S(1)} %get-tuple-element.195), channel_id=1, source_target_pairs={{0,2},{1,3},{2,0},{3,1},{4,6},{5,7},{6,4},{7,5},{8,10},{9,11},{10,... | collective-permute-start | bytes 786440 | tf_op jit(solution)/shard_map/ppermute | solution.py:784
  442.3 13.9 %collective-permute-start.35 = (bf16[64,2048]{1,0:T(8,128)(2,1)S(1)}, bf16[64,2048]{1,0:T(8,128)(2,1)}, u32[]{:S(2)}, u32[]{:S(2)}) collective-permute-start(bf16[64,2048]{1,0:T(8,128)(2,1)S(1)} %get-tuple-element.196), channel_id=1, source_target_pairs={{0,3},{1,2},{2,1},{3,0},{4,7},{5,6},{6,5},{7,4},{8,11},{9,10},{10,... | collective-permute-start | bytes 786440 | tf_op jit(solution)/shard_map/ppermute | solution.py:784
  444.4 38.0 %collective-permute-start.31 = (bf16[1,1,128,2048]{3,2,1,0:T(8,128)(2,1)}, bf16[1,1,128,2048]{3,2,1,0:T(8,128)(2,1)}, u32[]{:S(2)}, u32[]{:S(2)}) collective-permute-start(bf16[1,1,128,2048]{3,2,1,0:T(8,128)(2,1)} %add_convert_fusion.10.refs_2_), channel_id=1, source_target_pairs={{0,2},{1,3},{2,0},{3,1},{4,6},{5,7},{6,4},{7,5},{8,10},{9,11},{10,... | collective-permute-start | bytes 1572872 | tf_op jit(solution)/shard_map/ppermute | solution.py:784
  449.2 11.0 %collective-permute-start.46 = (f32[8,1280]{1,0:T(8,128)S(1)}, f32[8,1280]{1,0:T(8,128)}, u32[]{:S(2)}, u32[]{:S(2)}) collective-permute-start(f32[8,1280]{1,0:T(8,128)S(1)} %add.283), channel_id=1, source_target_pairs={{0,16},{4,20},{8,24},{12,28},{16,0},{20,4},{24,8},{28,12},{1,17},{... | collective-permute-start | bytes 122888 | tf_op jit(solution)/shard_map/ppermute | solution.py:784
  458.3 8.1 %collective-permute-start.36 = (bf16[64,1408]{1,0:T(8,128)(2,1)}, bf16[64,1408]{1,0:T(8,128)(2,1)S(1)}, u32[]{:S(2)}, u32[]{:S(2)}) collective-permute-start(bf16[64,1408]{1,0:T(8,128)(2,1)} %get-tuple-element.207.refs_2_), channel_id=1, source_target_pairs={{0,1},{1,0},{2,3},{3,2},{4,5},{5,4},{6,7},{7,6},{8,9},{9,8},{10,11... | collective-permute-start | bytes 540680 | tf_op jit(solution)/shard_map/ppermute | solution.py:784
  459.1 14.3 %collective-permute-start.37 = (bf16[64,1408]{1,0:T(8,128)(2,1)}, bf16[64,1408]{1,0:T(8,128)(2,1)S(1)}, u32[]{:S(2)}, u32[]{:S(2)}) collective-permute-start(bf16[64,1408]{1,0:T(8,128)(2,1)} %get-tuple-element.208.refs_3_), channel_id=1, source_target_pairs={{0,2},{1,3},{2,0},{3,1},{4,6},{5,7},{6,4},{7,5},{8,10},{9,11},{10,... | collective-permute-start | bytes 540680 | tf_op jit(solution)/shard_map/ppermute | solution.py:784
  460.2 14.3 %collective-permute-start.38 = (bf16[64,1408]{1,0:T(8,128)(2,1)}, bf16[64,1408]{1,0:T(8,128)(2,1)}, u32[]{:S(2)}, u32[]{:S(2)}) collective-permute-start(bf16[64,1408]{1,0:T(8,128)(2,1)} %get-tuple-element.209.refs_4_), channel_id=1, source_target_pairs={{0,3},{1,2},{2,1},{3,0},{4,7},{5,6},{6,5},{7,4},{8,11},{9,10},{10,... | collective-permute-start | bytes 540680 | tf_op jit(solution)/shard_map/ppermute | solution.py:784
  466.4 24.1 %collective-permute-start.47 = (f32[8,1280]{1,0:T(8,128)}, f32[8,1280]{1,0:T(8,128)S(1)}, u32[]{:S(2)}, u32[]{:S(2)}) collective-permute-start(f32[8,1280]{1,0:T(8,128)} %after.44.refs_0_), channel_id=1, source_target_pairs={{0,1},{1,0},{2,3},{3,2},{4,5},{5,4},{6,7},{7,6},{8,9},{9,8},{10,11... | collective-permute-start | bytes 122888 | tf_op jit(solution)/shard_map/ppermute | solution.py:784
  473.4 17.1 %collective-permute-start.48 = (f32[8,1280]{1,0:T(8,128)}, f32[8,1280]{1,0:T(8,128)}, u32[]{:S(2)}, u32[]{:S(2)}) collective-permute-start(f32[8,1280]{1,0:T(8,128)} %after.44.refs_0_), channel_id=1, source_target_pairs={{0,2},{1,3},{2,0},{3,1},{4,6},{5,7},{6,4},{7,5},{8,10},{9,11},{10,... | collective-permute-start | bytes 122888 | tf_op jit(solution)/shard_map/ppermute | solution.py:784
  474.5 16.0 %collective-permute-start.49 = (f32[8,1280]{1,0:T(8,128)}, f32[8,1280]{1,0:T(8,128)}, u32[]{:S(2)}, u32[]{:S(2)}) collective-permute-start(f32[8,1280]{1,0:T(8,128)} %after.44.refs_0_), channel_id=1, source_target_pairs={{0,3},{1,2},{2,1},{3,0},{4,7},{5,6},{6,5},{7,4},{8,11},{9,10},{10,... | collective-permute-start | bytes 122888 | tf_op jit(solution)/shard_map/ppermute | solution.py:784
  (84 other events, 382.6 us)
Sparse Core Ops, SparseCore 0:
  28.0 60.7 all-gather.3
  90.9 45.8 all-gather.5
  138.4 45.7 all-gather.7
  259.3 50.0 reduce-scatter.7
  311.5 48.1 reduce-scatter.5
  378.2 66.2 reduce-scatter.3
